TPU v7x, 32 devices: a whole 2x2x4 slice. The times are simulated.
32 devices in a mesh: batch: 2 (over x), seq: 16 (over z, y, core).
Axes of the slice: x: 2, y: 2, z: 4, core: 2. Of those that a mesh axis runs over, the one named last changes fastest.
Arguments:
- query_gate: float32 [4, 4096, 128], P('batch', 'seq'), may hold values from -6 to 6
- key_gate: float32 [4, 4096, 128], P('batch', 'seq'), may hold values from -6 to 6
- value_input: float32 [4, 4096, 128], P('batch', 'seq'), may hold values from -6 to 6
- filters: float32 [128, 4096], P('seq'), may hold values from -1 to 1, as said below
- skip_gain: float32 [128], replicated, may hold values from 0.5 to 1.5
- cotangent: float32 [4, 4096, 128], P('batch', 'seq'), may hold values from -6 to 6
Outputs:
- output: float32 [4, 4096, 128], P('batch', 'seq')
- query_grad: float32 [4, 4096, 128], P('batch', 'seq')
- key_grad: float32 [4, 4096, 128], P('batch', 'seq')
- value_grad: float32 [4, 4096, 128], P('batch', 'seq')
- filter_grad: float32 [128, 4096], P('seq', 'batch')
Inputs may be any that keep to these rules, and one draw needn't show every extreme that they name: `filters`: each channel's filter has a sum of squares of one.
All inputs are finite; a program needn't handle non-finite values.
Results may differ from a plain program's by a relative error of at most 0.0001.
Values sent between devices are 32-bit elements; how exact they have to be, the bound alone decides.
No kernel may reach another device: no remote copies, remote signals or barrier semaphores. Data moves between devices by JAX's collectives and lax.ppermute only.
A program may use at most 128 MiB of HBM per device.

v0:
```python
import math

import jax
import jax.numpy as jnp
import ml_dtypes
import numpy as np
from jax import lax
from jax.experimental import pallas as pl
from jax.experimental.pallas import tpu as pltpu
from jax.sharding import PartitionSpec as P

VMEM_BYTES = 48 * 1024 * 1024
ROW_CHUNK = 128


def add(a, b):
    if a is None:
        return b
    if b is None:
        return a
    return a + b


def sub(a, b):
    if b is None:
        return a
    if a is None:
        return -b
    return a - b


def scale(a, factor):
    if a is None or factor == 1.0:
        return a
    if factor == -1.0:
        return -a
    return a * factor


def turn(x, step, period):
    if x is None:
        return None
    re, im = x
    step = step % period
    if (4 * step) % period == 0:
        quarter = 4 * step // period
        if quarter == 0:
            return (re, im)
        if quarter == 1:
            return (im, scale(re, -1.0))
        if quarter == 2:
            return (scale(re, -1.0), scale(im, -1.0))
        return (scale(im, -1.0), re)
    angle = -2.0 * math.pi * step / period
    c, s = math.cos(angle), math.sin(angle)
    if (8 * step) % period == 0:
        root = math.sqrt(0.5)
        total, difference = add(re, im), sub(re, im)
        if c * s > 0:
            return (scale(difference, math.copysign(root, c)), scale(total, math.copysign(root, c)))
        return (scale(total, math.copysign(root, c)), scale(sub(im, re), math.copysign(root, c)))
    return (sub(scale(re, c), scale(im, s)), add(scale(re, s), scale(im, c)))


def complex_add(x, y):
    if x is None:
        return y
    if y is None:
        return x
    return (add(x[0], y[0]), add(x[1], y[1]))


def complex_sub(x, y):
    if y is None:
        return x
    if x is None:
        return (scale(y[0], -1.0), scale(y[1], -1.0))
    return (sub(x[0], y[0]), sub(x[1], y[1]))


def small_dft(values):
    size = len(values)
    if size == 1:
        return list(values)
    even = small_dft(values[0::2])
    odd = small_dft(values[1::2])
    odd = [turn(value, step, size) for step, value in enumerate(odd)]
    return [complex_add(e, o) for e, o in zip(even, odd)] + [
        complex_sub(e, o) for e, o in zip(even, odd)
    ]


def factors_of(size):
    first = 1
    while first * first < size:
        first *= 2
    return (size // first, first)


def across_rows(load, emit, count, kept, store, fetch):
    first, second = factors_of(count)
    for b in range(second):
        values = small_dft([load(second * a + b) for a in range(first)])
        for p, value in enumerate(values):
            store(b, p, turn(value, b * p, count))
    for p in range(first):
        values = small_dft([fetch(b, p) for b in range(second)])
        for q, value in enumerate(values):
            k1 = p + first * q
            if k1 < kept:
                emit(k1, value)


def tables(count, lanes):
    k1 = np.arange(count)[:, None]
    n2 = np.arange(lanes)[None, :]
    phase = -2.0 * np.pi * ((k1 * n2) % (count * lanes)) / (count * lanes)
    twist = np.concatenate([np.cos(phase), np.sin(phase)], axis=1).astype(np.float32)
    j = np.arange(lanes)
    phase = -2.0 * np.pi * ((j[:, None] * j[None, :]) % lanes) / lanes
    c, s = np.cos(phase), np.sin(phase)
    matrix = np.block([[c, s], [-s, c]]).astype(np.float32)
    high = matrix.astype(ml_dtypes.bfloat16)
    low = (matrix - high.astype(np.float32)).astype(ml_dtypes.bfloat16)
    return twist, np.concatenate([high, high, low], axis=0)


def lane_dft(x, matrix):
    high = x.astype(jnp.bfloat16)
    low = (x - high.astype(jnp.float32)).astype(jnp.bfloat16)
    return jnp.dot(
        jnp.concatenate([high, low, high], axis=1), matrix, preferred_element_type=jnp.float32
    )


def gate_kernel(query_ref, key_ref, value_ref, cotangent_ref, sent_ref):
    shards, _, batch, channels, tokens = sent_ref.shape
    for b in range(batch):
        mixed = key_ref[b] * value_ref[b]
        upstream = cotangent_ref[b] * query_ref[b]
        sent_ref[:, 0, b] = jnp.transpose(mixed).reshape(shards, channels, tokens)
        sent_ref[:, 1, b] = jnp.transpose(upstream).reshape(shards, channels, tokens)


def spectral_kernel(
    lag_scale, held_ref, filter_ref, twist_ref, matrix_ref, back_ref, lag_ref,
    middle, turned, filter_spec, mixed_spec, upstream_spec,
):
    shards, _, batch, channels, tokens = held_ref.shape
    count, width = twist_ref.shape
    lanes = width // 2
    length = shards * tokens
    live = count // 2
    pieces = tokens // lanes
    groups = lag_ref.shape[0]
    me = lax.axis_index("batch")

    def store(b, p, value):
        first, _ = factors_of(count)
        row = b * first + p
        re, im = value
        middle[row, :, :lanes] = jnp.zeros_like(im) if re is None else re
        middle[row, :, lanes:] = jnp.zeros_like(re) if im is None else im

    def fetch(b, p):
        first, _ = factors_of(count)
        row = b * first + p
        return (middle[row, :, :lanes], middle[row, :, lanes:])

    def place(k1, value):
        c, s = twist_ref[k1 : k1 + 1, :lanes], twist_ref[k1 : k1 + 1, lanes:]
        turned[k1, :, :lanes] = value[0] * c - value[1] * s
        turned[k1, :, lanes:] = value[0] * s + value[1] * c

    per_chunk = ROW_CHUNK // channels

    def chunks():
        for start in range(0, count, per_chunk):
            yield slice(start, min(start + per_chunk, count))

    def flat(x):
        return x.reshape(x.shape[0] * channels, width)

    def forward(load, spec):
        across_rows(load, place, count, count, store, fetch)
        for part in chunks():
            out = lane_dft(flat(turned[part]), matrix_ref[...])
            spec[part] = out.reshape(-1, channels, width)

    def inverse(product, emit):
        for part in chunks():
            re, im = product(part)
            x = jnp.concatenate([flat2(re), flat2(im)], axis=1)
            turned[part] = lane_dft(x, matrix_ref[...]).reshape(-1, channels, width)

        def load(k1):
            c, s = twist_ref[k1 : k1 + 1, :lanes], twist_ref[k1 : k1 + 1, lanes:]
            re, im = turned[k1, :, :lanes], turned[k1, :, lanes:]
            return (re * c - im * s, re * s + im * c)

        across_rows(load, emit, count, live, store, fetch)

    def flat2(x):
        return x.reshape(x.shape[0] * channels, lanes)

    def parts(spec, part):
        return spec[part, :, :lanes], spec[part, :, lanes:]

    def load_filter(n1):
        if n1 >= live:
            return None
        return (filter_ref[:, n1 * lanes : (n1 + 1) * lanes] * (0.5 / length), None)

    forward(load_filter, filter_spec)
    for pair in range(batch // 2):

        def load_kind(kind):
            def load(n1):
                if n1 >= live:
                    return None
                shard, piece = n1 // pieces, n1 % pieces
                span = slice(piece * lanes, (piece + 1) * lanes)
                return (
                    held_ref[shard, kind, 2 * pair, :, span],
                    held_ref[shard, kind, 2 * pair + 1, :, span],
                )

            return load

        def emit_kind(kind):
            def emit(n1, value):
                shard, piece = n1 // pieces, n1 % pieces
                span = slice(piece * lanes, (piece + 1) * lanes)
                back_ref[shard, kind, 2 * pair, :, span] = value[0]
                back_ref[shard, kind, 2 * pair + 1, :, span] = -value[1]

            return emit

        def convolve(part):
            fr, fi = parts(filter_spec, part)
            mr, mi = parts(mixed_spec, part)
            return (fr * mr - fi * mi, -(fr * mi + fi * mr))

        def correlate(part):
            fr, fi = parts(filter_spec, part)
            ur, ui = parts(upstream_spec, part)
            return (fr * ur + fi * ui, fi * ur - fr * ui)

        def lags(part):
            mr, mi = parts(mixed_spec, part)
            ur, ui = parts(upstream_spec, part)
            return (mr * ur + mi * ui, mi * ur - mr * ui)

        def emit_lag(n1, value):
            at = n1 * lanes
            share = length // groups
            slot = lax.rem(at // share - me + groups, groups)
            span = slice(at % share, at % share + lanes)
            if pair == 0:
                lag_ref[slot, :, span] = value[0] * lag_scale
            else:
                lag_ref[slot, :, span] += value[0] * lag_scale

        forward(load_kind(0), mixed_spec)
        inverse(convolve, emit_kind(0))
        forward(load_kind(1), upstream_spec)
        inverse(correlate, emit_kind(1))
        inverse(lags, emit_lag)


def output_kernel(
    query_ref, key_ref, value_ref, cotangent_ref, skip_ref, home_ref,
    output_ref, query_grad_ref, key_grad_ref, value_grad_ref,
):
    shards, _, batch, channels, tokens = home_ref.shape
    skip = skip_ref[...]
    for b in range(batch):
        query, key, value, cotangent = query_ref[b], key_ref[b], value_ref[b], cotangent_ref[b]
        convolved = jnp.transpose(home_ref[:, 0, b].reshape(shards * channels, tokens))
        hidden = convolved + skip * (key * value)
        output_ref[b] = query * hidden
        query_grad_ref[b] = cotangent * hidden
        back = jnp.transpose(home_ref[:, 1, b].reshape(shards * channels, tokens))
        mixed_grad = back + skip * (cotangent * query)
        key_grad_ref[b] = mixed_grad * value
        value_grad_ref[b] = mixed_grad * key


def per_device(query_gate, key_gate, value_input, filters, skip_gain, cotangent, *, shards, groups):
    batch, tokens, all_channels = query_gate.shape
    channels, length = filters.shape
    lanes = 128 if 2 * length // 128 <= 64 else tokens
    count = 2 * length // lanes
    twist, matrix = tables(count, lanes)
    params = pltpu.CompilerParams(vmem_limit_bytes=VMEM_BYTES)
    swap = jax.ShapeDtypeStruct((shards, 2, batch, channels, tokens), jnp.float32)
    sent = pl.pallas_call(gate_kernel, out_shape=swap, compiler_params=params, name="gate")(
        query_gate, key_gate, value_input, cotangent
    )
    held = lax.all_to_all(sent, "seq", split_axis=0, concat_axis=0, tiled=True)
    block = pltpu.VMEM((count, channels, 2 * lanes), jnp.float32)

    def body(*refs):
        spectral_kernel(1.0 / (2.0 * length * math.sqrt(length)), *refs)

    back, lag = pl.pallas_call(
        body,
        out_shape=(swap, jax.ShapeDtypeStruct((groups, channels, length // groups), jnp.float32)),
        scratch_shapes=[block] * 5,
        compiler_params=params,
        name="spectral",
    )(held, filters, twist, matrix)
    filter_grad = lag[0]
    for step in range(1, groups):
        pairs = [(source, (source + step) % groups) for source in range(groups)]
        filter_grad = filter_grad + lax.ppermute(lag[step], "batch", pairs)
    home = lax.all_to_all(back, "seq", split_axis=0, concat_axis=0, tiled=True)
    token_out = jax.ShapeDtypeStruct(query_gate.shape, jnp.float32)
    output, query_grad, key_grad, value_grad = pl.pallas_call(
        output_kernel, out_shape=(token_out,) * 4, compiler_params=params, name="outputs"
    )(query_gate, key_gate, value_input, cotangent, skip_gain.reshape(1, all_channels), home)
    return (output, query_grad, key_grad, value_grad, filter_grad)


def solution(mesh):
    in_specs = (
        P("batch", "seq", None),
        P("batch", "seq", None),
        P("batch", "seq", None),
        P("seq", None),
        P(),
        P("batch", "seq", None),
    )
    out_specs = (
        P("batch", "seq", None),
        P("batch", "seq", None),
        P("batch", "seq", None),
        P("batch", "seq", None),
        P("seq", "batch"),
    )
    shards, groups = mesh.shape["seq"], mesh.shape["batch"]

    def whole(*arrays):
        return per_device(*arrays, shards=shards, groups=groups)

    return jax.shard_map(whole, mesh=mesh, in_specs=in_specs, out_specs=out_specs, check_vma=False)
```

profile of v0, /device:TPU:0, one launch (start us, length us, event | category | flops | bytes accessed | tf_op | source)
XLA Modules:
  0.0 49.3 jit_solution(5646450250763580366)
XLA Ops:
  0.6 0.0 copy-start
  0.6 0.9 %copy-done = f32[2,256,128]{2,1,0:T(8,128)S(1)} copy-done((f32[2,256,128]{2,1,0:T(8,128)S(1)}, f32[2,256,128]{2,1,0:T(8,128)}, u32[]{:S(2)}) %copy-start) | copy-done | bytes 262168
  1.6 0.0 copy-start.2
  1.6 0.9 %copy-done.2 = f32[2,256,128]{2,1,0:T(8,128)S(1)} copy-done((f32[2,256,128]{2,1,0:T(8,128)S(1)}, f32[2,256,128]{2,1,0:T(8,128)}, u32[]{:S(2)}) %copy-start.2) | copy-done | bytes 262168
  2.5 0.0 copy-start.4
  2.5 0.9 %copy-done.4 = f32[2,256,128]{2,1,0:T(8,128)S(1)} copy-done((f32[2,256,128]{2,1,0:T(8,128)S(1)}, f32[2,256,128]{2,1,0:T(8,128)}, u32[]{:S(2)}) %copy-start.4) | copy-done | bytes 262168
  3.5 0.0 copy-start.6
  3.5 0.9 %copy-done.6 = f32[2,256,128]{2,1,0:T(8,128)S(1)} copy-done((f32[2,256,128]{2,1,0:T(8,128)S(1)}, f32[2,256,128]{2,1,0:T(8,128)}, u32[]{:S(2)}) %copy-start.6) | copy-done | bytes 262168
  4.4 0.2 gate.1
  4.6 0.0 copy-start.8
  4.7 0.0 copy-start.9
  4.7 0.0 copy-start.10
  4.7 21.8 %all_to_all.10.refs_0_ = f32[16,2,2,8,256]{4,3,2,1,0:T(8,128)S(1)} all-to-all(f32[16,2,2,8,256]{4,3,2,1,0:T(8,128)S(1)} %gate.1), channel_id=1, replica_groups=mesh['batch'=2,'seq'=16] {'seq'}, dimensions={0} | all-to-all | bytes 1048576 | tf_op jit(solution)/shard_map/all_to_all | solution.py:300
  26.5 0.0 copy-done.8
  26.5 0.0 copy-done.9
  26.5 0.0 copy-done.10
  26.5 2.9 %spectral.1 = (f32[16,2,2,8,256]{4,3,2,1,0:T(8,128)}, f32[2,8,2048]{2,1,0:T(8,128)S(1)}) custom-call(f32[16,2,2,8,256]{4,3,2,1,0:T(8,128)S(1)} %all_to_all.10.refs_0_, f32[8,4096]{1,0:T(8,128)S(1)} %copy-done.9, f32[64,256]{1,0:T(8,128)S(1)} %copy-done.10, bf16[768,256]{1,0:T(8,128)(2,1)S(1)} %copy-done.8), custom_call_target="tpu_custom_call" | custom-call | tf_op jit(solution)/shard_map/spectral/pallas_call | solution.py:306
  29.4 0.0 copy-start.3
  29.4 0.0 copy-start.5
  29.4 0.0 copy-start.7
  29.4 4.2 %all-to-all-start.1 = ((f32[16,2,2,8,256]{4,3,2,1,0:T(8,128)}), f32[16,2,2,8,256]{4,3,2,1,0:T(8,128)S(1)}, u32[]{:S(2)}, u32[]{:S(2)}) async-start(f32[16,2,2,8,256]{4,3,2,1,0:T(8,128)} %get-tuple-element.11), calls=%async_computation.1 | async-start | bytes 1048576 | tf_op jit(solution)/shard_map/all_to_all | solution.py:317
  33.6 0.0 copy-start.1
  33.6 1.6 %collective-permute-start = (f32[8,2048]{1,0:T(8,128)S(1)}, f32[8,2048]{1,0:T(8,128)S(1)}, u32[]{:S(2)}, u32[]{:S(2)}) collective-permute-start(f32[8,2048]{1,0:T(8,128)S(1)} %slice_bitcast_fusion), channel_id=1, source_target_pairs={{0,16},{16,0},{1,17},{17,1},{2,18},{18,2},{3,19},{19,3},{4,20},{20... | collective-permute-start | bytes 196616 | tf_op jit(solution)/shard_map/ppermute | solution.py:316
  35.2 2.9 %collective-permute-done = f32[8,2048]{1,0:T(8,128)S(1)} collective-permute-done((f32[8,2048]{1,0:T(8,128)S(1)}, f32[8,2048]{1,0:T(8,128)S(1)}, u32[]{:S(2)}, u32[]{:S(2)}) %collective-permute-start) | collective-permute-done | bytes 65568 | tf_op jit(solution)/shard_map/ppermute | solution.py:316
  38.1 0.6 %bitcast_add_fusion = f32[8,2048]{1,0:T(8,128)} fusion(f32[8,2048]{1,0:T(8,128)S(1)} %collective-permute-done, f32[2,8,2048]{2,1,0:T(8,128)S(1)} %get-tuple-element.16), kind=kLoop, calls=%fused_computation | loop fusion | flops 16384 | bytes 196608 | tf_op jit(solution)/shard_map/add | solution.py:316
  38.8 0.0 copy-start.11
  38.8 9.3 %all-to-all-done.1.home_ref = f32[16,2,2,8,256]{4,3,2,1,0:T(8,128)S(1)} async-done(((f32[16,2,2,8,256]{4,3,2,1,0:T(8,128)}), f32[16,2,2,8,256]{4,3,2,1,0:T(8,128)S(1)}, u32[]{:S(2)}, u32[]{:S(2)}) %all-to-all-start.1) | async-done | bytes 524320 | tf_op jit(solution)/shard_map/all_to_all | solution.py:317
  48.1 0.0 copy-done.3
  48.1 0.0 copy-done.5
  48.1 0.0 copy-done.7
  48.1 0.0 copy-done.1
  48.1 0.0 copy-done.11
  48.1 1.1 %outputs.1 = (f32[2,256,128]{2,1,0:T(8,128)}, f32[2,256,128]{2,1,0:T(8,128)}, f32[2,256,128]{2,1,0:T(8,128)}, f32[2,256,128]{2,1,0:T(8,128)}) custom-call(f32[2,256,128]{2,1,0:T(8,128)S(1)} %copy-done.1, f32[2,256,128]{2,1,0:T(8,128)S(1)} %copy-done.3, f32[2,256,128]{2,1,0:T(8,128)S(1)} %copy-done.5, f32[2,256,128]{2,1,0:T(8,128)S(1)} %copy-done.7, ...), custom_call_target="tpu_custom_call" | custom-call | tf_op jit(solution)/shard_map/outputs/pallas_call | solution.py:319
  (1 shorter events, 0.0 us)
Async XLA Ops:
  0.6 1.0 %copy-start = (f32[2,256,128]{2,1,0:T(8,128)S(1)}, f32[2,256,128]{2,1,0:T(8,128)}, u32[]{:S(2)}) copy-start(f32[2,256,128]{2,1,0:T(8,128)} %query_ref.3) | copy-start | bytes 786436
  1.6 0.9 %copy-start.2 = (f32[2,256,128]{2,1,0:T(8,128)S(1)}, f32[2,256,128]{2,1,0:T(8,128)}, u32[]{:S(2)}) copy-start(f32[2,256,128]{2,1,0:T(8,128)} %key_ref.3) | copy-start | bytes 786436
  2.5 0.9 %copy-start.4 = (f32[2,256,128]{2,1,0:T(8,128)S(1)}, f32[2,256,128]{2,1,0:T(8,128)}, u32[]{:S(2)}) copy-start(f32[2,256,128]{2,1,0:T(8,128)} %value_ref.3) | copy-start | bytes 786436
  3.5 0.9 %copy-start.6 = (f32[2,256,128]{2,1,0:T(8,128)S(1)}, f32[2,256,128]{2,1,0:T(8,128)}, u32[]{:S(2)}) copy-start(f32[2,256,128]{2,1,0:T(8,128)} %cotangent_ref.3) | copy-start | bytes 786436
  4.6 21.8 %copy-start.8 = (bf16[768,256]{1,0:T(8,128)(2,1)S(1)}, bf16[768,256]{1,0:T(8,128)(2,1)}, u32[]{:S(2)}) copy-start(bf16[768,256]{1,0:T(8,128)(2,1)} %constant.5.clone.refs_3_) | copy-start | bytes 1179652
  4.7 21.8 %copy-start.9 = (f32[8,4096]{1,0:T(8,128)S(1)}, f32[8,4096]{1,0:T(8,128)}, u32[]{:S(2)}) copy-start(f32[8,4096]{1,0:T(8,128)} %refs_1_.1) | copy-start | bytes 393220
  4.7 21.8 %copy-start.10 = (f32[64,256]{1,0:T(8,128)S(1)}, f32[64,256]{1,0:T(8,128)}, u32[]{:S(2)}) copy-start(f32[64,256]{1,0:T(8,128)} %constant.4.clone.refs_2_) | copy-start | bytes 196612
  29.4 18.7 %copy-start.3 = (f32[2,256,128]{2,1,0:T(8,128)S(1)}, f32[2,256,128]{2,1,0:T(8,128)}, u32[]{:S(2)}) copy-start(f32[2,256,128]{2,1,0:T(8,128)} %key_ref.3) | copy-start | bytes 786436
  29.4 18.7 %copy-start.5 = (f32[2,256,128]{2,1,0:T(8,128)S(1)}, f32[2,256,128]{2,1,0:T(8,128)}, u32[]{:S(2)}) copy-start(f32[2,256,128]{2,1,0:T(8,128)} %value_ref.3) | copy-start | bytes 786436
  29.4 18.7 %copy-start.7 = (f32[2,256,128]{2,1,0:T(8,128)S(1)}, f32[2,256,128]{2,1,0:T(8,128)}, u32[]{:S(2)}) copy-start(f32[2,256,128]{2,1,0:T(8,128)} %cotangent_ref.3) | copy-start | bytes 786436
  29.4 18.7 %all-to-all-start.1 = ((f32[16,2,2,8,256]{4,3,2,1,0:T(8,128)}), f32[16,2,2,8,256]{4,3,2,1,0:T(8,128)S(1)}, u32[]{:S(2)}, u32[]{:S(2)}) async-start(f32[16,2,2,8,256]{4,3,2,1,0:T(8,128)} %get-tuple-element.11), calls=%async_computation.1 | async-start | bytes 1048576 | tf_op jit(solution)/shard_map/all_to_all | solution.py:317
  33.6 14.5 %copy-start.1 = (f32[2,256,128]{2,1,0:T(8,128)S(1)}, f32[2,256,128]{2,1,0:T(8,128)}, u32[]{:S(2)}) copy-start(f32[2,256,128]{2,1,0:T(8,128)} %query_ref.3) | copy-start | bytes 786436
  33.6 4.5 %collective-permute-start = (f32[8,2048]{1,0:T(8,128)S(1)}, f32[8,2048]{1,0:T(8,128)S(1)}, u32[]{:S(2)}, u32[]{:S(2)}) collective-permute-start(f32[8,2048]{1,0:T(8,128)S(1)} %slice_bitcast_fusion), channel_id=1, source_target_pairs={{0,16},{16,0},{1,17},{17,1},{2,18},{18,2},{3,19},{19,3},{4,20},{20... | collective-permute-start | bytes 196616 | tf_op jit(solution)/shard_map/ppermute | solution.py:316
  38.8 9.3 %copy-start.11 = (f32[128]{0:T(128)S(1)}, f32[128]{0:T(128)}, u32[]{:S(2)}) copy-start(f32[128]{0:T(128)} %param.12) | copy-start | bytes 1540
where the time goes:
time: 49.7 us; the launch traced here: 49.3 us
  blocking collectives  21.8 us (44%)
  waiting for transfers between devices  12.2 us (25%)
  starting transfers between devices  5.79 us (12%)
  Pallas kernels  4.24 us (9%)
  local copies, waits for them, and re-layouts  3.84 us (8%)
  between operations  0.73 us (1%)
  other arithmetic  0.64 us (1%)
    all_to_all x1, blocking collectives, per_device(): held = lax.all_to_all(sent, 'seq', split_axis=0, concat_axis=0, tiled=True)  21.8 us
    all_to_all x1, waiting for transfers between devices, per_device(): home = lax.all_to_all(back, 'seq', split_axis=0, concat_axis=0, tiled=True)  9.31 us
    all_to_all x1, starting transfers between devices, per_device(): home = lax.all_to_all(back, 'seq', split_axis=0, concat_axis=0, tiled=True)  4.23 us
    unnamed x24, local copies, waits for them, and re-layouts  3.83 us
    ppermute x1, waiting for transfers between devices, per_device(): filter_grad = filter_grad + lax.ppermute(lag[step], 'batch', pairs)  2.94 us
    pallas_call x1, Pallas kernels, per_device(): pl.pallas_call(body, out_shape=(swap, jax.ShapeDtypeStruct((groups, chann...  2.89 us
    ppermute x1, starting transfers between devices, per_device(): filter_grad = filter_grad + lax.ppermute(lag[step], 'batch', pairs)  1.55 us
    pallas_call x1, Pallas kernels, per_device(): pl.pallas_call(output_kernel, out_shape=(token_out,) * 4, compiler_params...  1.15 us
  transfers between devices with their start and end apart: 2, of which 2 were waited for; matrix products, arithmetic and copies ran while one was open for 1% of the time, Pallas kernels for 0%

commit v1 on v0

--- a/solution.py
+++ b/solution.py
@@ -133,27 +133,46 @@
     )
 
 
-def gate_kernel(query_ref, key_ref, value_ref, cotangent_ref, sent_ref):
-    shards, _, batch, channels, tokens = sent_ref.shape
+def gate_kernel(query_hbm, key_hbm, value_hbm, cotangent_hbm, *refs):
+    *sent, held, turned, sems = refs
+    shards = len(sent)
+    _, batch, channels, tokens = sent[0].shape
+    me = lax.axis_index("seq")
+    sources = (key_hbm, value_hbm, cotangent_hbm, query_hbm)
+
+    def copy(b, i):
+        return pltpu.make_async_copy(sources[i].at[b], held.at[i, b], sems.at[i, b])
+
     for b in range(batch):
-        mixed = key_ref[b] * value_ref[b]
-        upstream = cotangent_ref[b] * query_ref[b]
-        sent_ref[:, 0, b] = jnp.transpose(mixed).reshape(shards, channels, tokens)
-        sent_ref[:, 1, b] = jnp.transpose(upstream).reshape(shards, channels, tokens)
+        for i in range(4):
+            copy(b, i).start()
+    for b in range(batch):
+        for kind in range(2):
+            copy(b, 2 * kind).wait()
+            copy(b, 2 * kind + 1).wait()
+            product = held[2 * kind, b] * held[2 * kind + 1, b]
+            turned[:, kind, b] = jnp.transpose(product).reshape(shards, channels, tokens)
+    for step in range(shards):
+        sent[step][...] = turned[me ^ step]
 
 
 def spectral_kernel(
-    lag_scale, held_ref, filter_ref, twist_ref, matrix_ref, back_ref, lag_ref,
-    middle, turned, filter_spec, mixed_spec, upstream_spec,
+    shards, lag_scale, filter_ref, twist_ref, matrix_ref, *refs
 ):
-    shards, _, batch, channels, tokens = held_ref.shape
+    received, refs = refs[:shards], refs[shards:]
+    returned, refs = refs[:shards], refs[shards:]
+    lag_ref, held_ref, back_ref, middle, turned, filter_spec, mixed_spec, upstream_spec = refs
+    _, _, batch, channels, tokens = held_ref.shape
     count, width = twist_ref.shape
     lanes = width // 2
     length = shards * tokens
     live = count // 2
     pieces = tokens // lanes
     groups = lag_ref.shape[0]
-    me = lax.axis_index("batch")
+    group = lax.axis_index("batch")
+    me = lax.axis_index("seq")
+    for step in range(shards):
+        held_ref[me ^ step] = received[step][...]
 
     def store(b, p, value):
         first, _ = factors_of(count)
@@ -254,7 +273,7 @@
         def emit_lag(n1, value):
             at = n1 * lanes
             share = length // groups
-            slot = lax.rem(at // share - me + groups, groups)
+            slot = lax.rem(at // share - group + groups, groups)
             span = slice(at % share, at % share + lanes)
             if pair == 0:
                 lag_ref[slot, :, span] = value[0] * lag_scale
@@ -266,24 +285,38 @@
         forward(load_kind(1), upstream_spec)
         inverse(correlate, emit_kind(1))
         inverse(lags, emit_lag)
-
-
-def output_kernel(
-    query_ref, key_ref, value_ref, cotangent_ref, skip_ref, home_ref,
-    output_ref, query_grad_ref, key_grad_ref, value_grad_ref,
-):
-    shards, _, batch, channels, tokens = home_ref.shape
+    for step in range(shards):
+        returned[step][...] = back_ref[me ^ step]
+
+
+def output_kernel(query_ref, key_ref, value_ref, cotangent_ref, skip_ref, *refs):
+    *home, output_ref, query_grad_ref, key_grad_ref, value_grad_ref, turned = refs
+    _, batch, channels, tokens = home[0].shape
+    me = lax.axis_index("seq")
+    for step, block in enumerate(home):
+        turned[me ^ step] = block[...]
     skip = skip_ref[...]
+
+    def columns(kind, b):
+        return jnp.transpose(turned[:, kind, b].reshape(len(home) * channels, tokens))
+
     for b in range(batch):
         query, key, value, cotangent = query_ref[b], key_ref[b], value_ref[b], cotangent_ref[b]
-        convolved = jnp.transpose(home_ref[:, 0, b].reshape(shards * channels, tokens))
-        hidden = convolved + skip * (key * value)
+        hidden = columns(0, b) + skip * (key * value)
         output_ref[b] = query * hidden
         query_grad_ref[b] = cotangent * hidden
-        back = jnp.transpose(home_ref[:, 1, b].reshape(shards * channels, tokens))
-        mixed_grad = back + skip * (cotangent * query)
+        mixed_grad = columns(1, b) + skip * (cotangent * query)
         key_grad_ref[b] = mixed_grad * value
         value_grad_ref[b] = mixed_grad * key
+
+
+def exchange(blocks):
+    shards = len(blocks)
+    received = [blocks[0]] + [None] * (shards - 1)
+    for step in range(shards - 1, 0, -1):
+        pairs = [(source, source ^ step) for source in range(shards)]
+        received[step] = lax.ppermute(blocks[step], "seq", pairs)
+    return received
 
 
 def per_device(query_gate, key_gate, value_input, filters, skip_gain, cotangent, *, shards, groups):
@@ -293,32 +326,50 @@
     count = 2 * length // lanes
     twist, matrix = tables(count, lanes)
     params = pltpu.CompilerParams(vmem_limit_bytes=VMEM_BYTES)
-    swap = jax.ShapeDtypeStruct((shards, 2, batch, channels, tokens), jnp.float32)
-    sent = pl.pallas_call(gate_kernel, out_shape=swap, compiler_params=params, name="gate")(
-        query_gate, key_gate, value_input, cotangent
-    )
-    held = lax.all_to_all(sent, "seq", split_axis=0, concat_axis=0, tiled=True)
-    block = pltpu.VMEM((count, channels, 2 * lanes), jnp.float32)
+    block = jax.ShapeDtypeStruct((2, batch, channels, tokens), jnp.float32)
+    swap = pltpu.VMEM((shards, 2, batch, channels, tokens), jnp.float32)
+    sent = pl.pallas_call(
+        gate_kernel,
+        out_shape=(block,) * shards,
+        in_specs=[pl.BlockSpec(memory_space=pltpu.HBM)] * 4,
+        scratch_shapes=[
+            pltpu.VMEM((4, batch, tokens, all_channels), jnp.float32),
+            swap,
+            pltpu.SemaphoreType.DMA((4, batch)),
+        ],
+        compiler_params=params,
+        name="gate",
+    )(*(
+        pltpu.with_memory_space_constraint(x, pltpu.HBM)
+        for x in (query_gate, key_gate, value_input, cotangent)
+    ))
+    received = exchange(sent)
+    spectrum = pltpu.VMEM((count, channels, 2 * lanes), jnp.float32)
 
     def body(*refs):
-        spectral_kernel(1.0 / (2.0 * length * math.sqrt(length)), *refs)
-
-    back, lag = pl.pallas_call(
+        spectral_kernel(shards, 1.0 / (2.0 * length * math.sqrt(length)), *refs)
+
+    *returned, lag = pl.pallas_call(
         body,
-        out_shape=(swap, jax.ShapeDtypeStruct((groups, channels, length // groups), jnp.float32)),
-        scratch_shapes=[block] * 5,
+        out_shape=(block,) * shards
+        + (jax.ShapeDtypeStruct((groups, channels, length // groups), jnp.float32),),
+        scratch_shapes=[swap] * 2 + [spectrum] * 5,
         compiler_params=params,
         name="spectral",
-    )(held, filters, twist, matrix)
+    )(filters, twist, matrix, *received)
+    home = exchange(returned)
     filter_grad = lag[0]
     for step in range(1, groups):
         pairs = [(source, (source + step) % groups) for source in range(groups)]
         filter_grad = filter_grad + lax.ppermute(lag[step], "batch", pairs)
-    home = lax.all_to_all(back, "seq", split_axis=0, concat_axis=0, tiled=True)
     token_out = jax.ShapeDtypeStruct(query_gate.shape, jnp.float32)
     output, query_grad, key_grad, value_grad = pl.pallas_call(
-        output_kernel, out_shape=(token_out,) * 4, compiler_params=params, name="outputs"
-    )(query_gate, key_gate, value_input, cotangent, skip_gain.reshape(1, all_channels), home)
+        output_kernel,
+        out_shape=(token_out,) * 4,
+        scratch_shapes=[swap],
+        compiler_params=params,
+        name="outputs",
+    )(query_gate, key_gate, value_input, cotangent, skip_gain.reshape(1, all_channels), *home)
     return (output, query_grad, key_grad, value_grad, filter_grad)
 
 

time: 49.7 us -> 59.9 us (1.21)
  starting transfers between devices: 5.79 us -> 43.7 us
  blocking collectives: 21.8 us -> 0 us
  waiting for transfers between devices: 12.2 us -> 8.72 us
  local copies, waits for them, and re-layouts: 3.84 us -> 0.68 us
  Pallas kernels: 4.24 us -> 5.23 us
    ppermute x0 -> x30, starting transfers between devices: none -> 42.2 us  [exchange(): received[step] = lax.ppermute(blocks[step], 'seq', pairs)]
    all_to_all x1 -> x0, blocking collectives: 21.8 us -> none  [per_device(): held = lax.all_to_all(sent, 'seq', split_axis=0, concat_axis=0, tiled=True)]
    all_to_all x1 -> x0, waiting for transfers between devices: 9.31 us -> none  [per_device(): home = lax.all_to_all(back, 'seq', split_axis=0, concat_axis=0, tiled=True)]
    ppermute x0 -> x30, waiting for transfers between devices: none -> 8.72 us  [exchange(): received[step] = lax.ppermute(blocks[step], 'seq', pairs)]
    all_to_all x1 -> x0, starting transfers between devices: 4.23 us -> none  [per_device(): home = lax.all_to_all(back, 'seq', split_axis=0, concat_axis=0, tiled=True)]
    unnamed x24 -> x16, local copies, waits for them, and re-layouts: 3.83 us -> 0.68 us
    ppermute x1, waiting for transfers between devices: 2.94 us -> 0.01 us  [per_device(): filter_grad = filter_grad + lax.ppermute(lag[step], 'batch', pairs)]
    pallas_call x3, Pallas kernels: 4.24 us -> 5.23 us  [the longest x1 2.46 us: per_device(): pl.pallas_call(body, out_shape=(block,) * shards + (jax.ShapeDtypeStruct(...]
  transfers between devices with their start and end apart: 2 -> 31, of which waited for: 2 -> 6; matrix products, arithmetic and copies ran while one was open for 1% -> 0% of each run, Pallas kernels for 0% -> 2%
where the time goes in v1:
time: 59.9 us; the launch traced here: 59.8 us
  starting transfers between devices  43.7 us (73%)
  waiting for transfers between devices  8.72 us (15%)
  Pallas kernels  5.23 us (9%)
  between operations  0.76 us (1%)
  local copies, waits for them, and re-layouts  0.68 us (1%)
  other arithmetic  0.64 us (1%)
    ppermute x30, starting transfers between devices, exchange(): received[step] = lax.ppermute(blocks[step], 'seq', pairs)  42.2 us
    ppermute x30, waiting for transfers between devices, exchange(): received[step] = lax.ppermute(blocks[step], 'seq', pairs)  8.72 us
    pallas_call x1, Pallas kernels, per_device(): pl.pallas_call(body, out_shape=(block,) * shards + (jax.ShapeDtypeStruct(...  2.46 us
    pallas_call x1, Pallas kernels, per_device(): pl.pallas_call(gate_kernel, out_shape=(block,) * shards, in_specs=[pl.Blo...  1.58 us
    ppermute x1, starting transfers between devices, per_device(): filter_grad = filter_grad + lax.ppermute(lag[step], 'batch', pairs)  1.55 us
  transfers between devices with their start and end apart: 31, of which 6 were waited for; matrix products, arithmetic and copies ran while one was open for 0% of the time, Pallas kernels for 2%

profile of v1, /device:TPU:0, one launch (start us, length us, event | category | flops | bytes accessed | tf_op | source)
XLA Modules:
  0.0 59.8 jit_solution(7858771875367915754)
XLA Ops:
  0.6 0.0 copy-start.4
  0.7 0.0 copy-start.6
  0.7 1.6 %gate.1 = (f32[2,2,8,256]{3,2,1,0:T(8,128)S(1)}, f32[2,2,8,256]{3,2,1,0:T(8,128)S(1)}, f32[2,2,8,256]{3,2,1,0:T(8,128)S(1)}, f32[2,2,8,256]{3,2,1,0:T(8,128)S(1)...) custom-call(f32[2,256,128]{2,1,0:T(8,128)} %query_ref.1, ...), custom_call_target="tpu_custom_call" | custom-call | tf_op jit(solution)/shard_map/gate/pallas_call | solution.py:331
  2.3 0.5 collective-permute-start
  2.8 2.6 %collective-permute-start.1 = (f32[2,2,8,256]{3,2,1,0:T(8,128)S(1)}, f32[2,2,8,256]{3,2,1,0:T(8,128)S(1)}, u32[]{:S(2)}, u32[]{:S(2)}) collective-permute-start(f32[2,2,8,256]{3,2,1,0:T(8,128)S(1)} %get-tuple-element.44), channel_id=1, source_target_pairs={{0,2},{1,3},{2,0},{3,1},{4,6},{5,7},{6,4},{7,5},{8,10},{9,11},{10,... | collective-permute-start | bytes 98312 | tf_op jit(solution)/shard_map/ppermute | solution.py:318
  5.4 0.1 collective-permute-start.2
  5.4 1.8 %collective-permute-start.3 = (f32[2,2,8,256]{3,2,1,0:T(8,128)S(1)}, f32[2,2,8,256]{3,2,1,0:T(8,128)S(1)}, u32[]{:S(2)}, u32[]{:S(2)}) collective-permute-start(f32[2,2,8,256]{3,2,1,0:T(8,128)S(1)} %get-tuple-element.46), channel_id=1, source_target_pairs={{0,4},{1,5},{2,6},{3,7},{4,0},{5,1},{6,2},{7,3},{8,12},{9,13},{10,... | collective-permute-start | bytes 98312 | tf_op jit(solution)/shard_map/ppermute | solution.py:318
  7.2 0.0 collective-permute-start.4
  7.2 0.0 collective-permute-done.refs_4_
  7.2 2.6 %collective-permute-start.5 = (f32[2,2,8,256]{3,2,1,0:T(8,128)S(1)}, f32[2,2,8,256]{3,2,1,0:T(8,128)S(1)}, u32[]{:S(2)}, u32[]{:S(2)}) collective-permute-start(f32[2,2,8,256]{3,2,1,0:T(8,128)S(1)} %get-tuple-element.48), channel_id=1, source_target_pairs={{0,6},{1,7},{2,4},{3,5},{4,2},{5,3},{6,0},{7,1},{8,14},{9,15},{10,... | collective-permute-start | bytes 98312 | tf_op jit(solution)/shard_map/ppermute | solution.py:318
  9.9 0.0 collective-permute-done.1.refs_5_
  9.9 0.1 collective-permute-start.6
  10.0 0.0 collective-permute-done.2.refs_6_
  10.0 2.6 %collective-permute-start.7 = (f32[2,2,8,256]{3,2,1,0:T(8,128)S(1)}, f32[2,2,8,256]{3,2,1,0:T(8,128)S(1)}, u32[]{:S(2)}, u32[]{:S(2)}) collective-permute-start(f32[2,2,8,256]{3,2,1,0:T(8,128)S(1)} %get-tuple-element.50), channel_id=1, source_target_pairs={{0,8},{1,9},{2,10},{3,11},{4,12},{5,13},{6,14},{7,15},{8,0},{9,1},... | collective-permute-start | bytes 98312 | tf_op jit(solution)/shard_map/ppermute | solution.py:318
  12.6 0.0 collective-permute-done.3.refs_7_
  12.6 0.3 collective-permute-start.8
  13.0 0.0 collective-permute-done.4.refs_8_
  13.0 3.2 %collective-permute-start.9 = (f32[2,2,8,256]{3,2,1,0:T(8,128)S(1)}, f32[2,2,8,256]{3,2,1,0:T(8,128)S(1)}, u32[]{:S(2)}, u32[]{:S(2)}) collective-permute-start(f32[2,2,8,256]{3,2,1,0:T(8,128)S(1)} %get-tuple-element.52), channel_id=1, source_target_pairs={{0,10},{1,11},{2,8},{3,9},{4,14},{5,15},{6,12},{7,13},{8,2},{9,3},... | collective-permute-start | bytes 98312 | tf_op jit(solution)/shard_map/ppermute | solution.py:318
  16.2 0.0 collective-permute-done.5.refs_9_
  16.2 0.1 collective-permute-start.10
  16.3 0.0 collective-permute-done.6.refs_10_
  16.3 3.5 %collective-permute-start.11 = (f32[2,2,8,256]{3,2,1,0:T(8,128)S(1)}, f32[2,2,8,256]{3,2,1,0:T(8,128)S(1)}, u32[]{:S(2)}, u32[]{:S(2)}) collective-permute-start(f32[2,2,8,256]{3,2,1,0:T(8,128)S(1)} %get-tuple-element.54), channel_id=1, source_target_pairs={{0,12},{1,13},{2,14},{3,15},{4,8},{5,9},{6,10},{7,11},{8,4},{9,5},... | collective-permute-start | bytes 98312 | tf_op jit(solution)/shard_map/ppermute | solution.py:318
  19.9 0.0 collective-permute-done.7.refs_11_
  19.9 0.2 collective-permute-start.12
  20.1 0.0 collective-permute-done.8.refs_12_
  20.1 4.2 %collective-permute-start.13 = (f32[2,2,8,256]{3,2,1,0:T(8,128)S(1)}, f32[2,2,8,256]{3,2,1,0:T(8,128)S(1)}, u32[]{:S(2)}, u32[]{:S(2)}) collective-permute-start(f32[2,2,8,256]{3,2,1,0:T(8,128)S(1)} %get-tuple-element.56), channel_id=1, source_target_pairs={{0,14},{1,15},{2,12},{3,13},{4,10},{5,11},{6,8},{7,9},{8,6},{9,7},... | collective-permute-start | bytes 98312 | tf_op jit(solution)/shard_map/ppermute | solution.py:318
  24.3 0.0 collective-permute-done.9.refs_13_
  24.3 0.1 collective-permute-start.14
  24.4 0.0 collective-permute-done.10.refs_14_
  24.4 0.0 collective-permute-done.11.refs_15_
  24.4 0.7 %collective-permute-done.12.refs_16_ = f32[2,2,8,256]{3,2,1,0:T(8,128)S(1)} collective-permute-done((f32[2,2,8,256]{3,2,1,0:T(8,128)S(1)}, f32[2,2,8,256]{3,2,1,0:T(8,128)S(1)}, u32[]{:S(2)}, u32[]{:S(2)}) %collective-permute-start.12) | collective-permute-done | bytes 32800 | tf_op jit(solution)/shard_map/ppermute | solution.py:318
  25.1 2.0 %collective-permute-done.13.refs_17_ = f32[2,2,8,256]{3,2,1,0:T(8,128)S(1)} collective-permute-done((f32[2,2,8,256]{3,2,1,0:T(8,128)S(1)}, f32[2,2,8,256]{3,2,1,0:T(8,128)S(1)}, u32[]{:S(2)}, u32[]{:S(2)}) %collective-permute-start.13) | collective-permute-done | bytes 32800 | tf_op jit(solution)/shard_map/ppermute | solution.py:318
  27.1 3.2 %collective-permute-done.14.refs_18_ = f32[2,2,8,256]{3,2,1,0:T(8,128)S(1)} collective-permute-done((f32[2,2,8,256]{3,2,1,0:T(8,128)S(1)}, f32[2,2,8,256]{3,2,1,0:T(8,128)S(1)}, u32[]{:S(2)}, u32[]{:S(2)}) %collective-permute-start.14) | collective-permute-done | bytes 32800 | tf_op jit(solution)/shard_map/ppermute | solution.py:318
  30.4 0.0 copy-start
  30.4 0.0 copy-start.1
  30.4 0.0 copy-start.2
  30.4 0.0 copy-start.3
  30.4 2.5 %spectral.1 = (f32[2,2,8,256]{3,2,1,0:T(8,128)S(1)}, f32[2,2,8,256]{3,2,1,0:T(8,128)S(1)}, f32[2,2,8,256]{3,2,1,0:T(8,128)S(1)}, f32[2,2,8,256]{3,2,1,0:T(8,128)...) custom-call(f32[8,4096]{1,0:T(8,128)S(1)} %copy-done.5, ...), custom_call_target="tpu_custom_call" | custom-call | tf_op jit(solution)/shard_map/spectral/pallas_call | solution.py:352
  32.9 0.2 collective-permute-start.15
  33.1 0.5 collective-permute-start.16
  33.6 1.2 %collective-permute-start.17 = (f32[2,2,8,256]{3,2,1,0:T(8,128)S(1)}, f32[2,2,8,256]{3,2,1,0:T(8,128)S(1)}, u32[]{:S(2)}, u32[]{:S(2)}) collective-permute-start(f32[2,2,8,256]{3,2,1,0:T(8,128)S(1)} %get-tuple-element.61), channel_id=1, source_target_pairs={{0,3},{1,2},{2,1},{3,0},{4,7},{5,6},{6,5},{7,4},{8,11},{9,10},{10,... | collective-permute-start | bytes 98312 | tf_op jit(solution)/shard_map/ppermute | solution.py:318
  34.8 0.0 collective-permute-start.18
  34.8 1.8 %collective-permute-start.19 = (f32[2,2,8,256]{3,2,1,0:T(8,128)S(1)}, f32[2,2,8,256]{3,2,1,0:T(8,128)S(1)}, u32[]{:S(2)}, u32[]{:S(2)}) collective-permute-start(f32[2,2,8,256]{3,2,1,0:T(8,128)S(1)} %get-tuple-element.63), channel_id=1, source_target_pairs={{0,5},{1,4},{2,7},{3,6},{4,1},{5,0},{6,3},{7,2},{8,13},{9,12},{10,... | collective-permute-start | bytes 98312 | tf_op jit(solution)/shard_map/ppermute | solution.py:318
  36.6 0.0 collective-permute-done.15.refs_1_
  36.6 0.2 collective-permute-start.20
  36.9 0.4 collective-permute-done.16.refs_2_
  37.3 1.9 %collective-permute-start.21 = (f32[2,2,8,256]{3,2,1,0:T(8,128)S(1)}, f32[2,2,8,256]{3,2,1,0:T(8,128)S(1)}, u32[]{:S(2)}, u32[]{:S(2)}) collective-permute-start(f32[2,2,8,256]{3,2,1,0:T(8,128)S(1)} %get-tuple-element.65), channel_id=1, source_target_pairs={{0,7},{1,6},{2,5},{3,4},{4,3},{5,2},{6,1},{7,0},{8,15},{9,14},{10,... | collective-permute-start | bytes 98312 | tf_op jit(solution)/shard_map/ppermute | solution.py:318
  39.2 0.0 collective-permute-done.17.refs_3_
  39.2 2.7 %collective-permute-start.23 = (f32[2,2,8,256]{3,2,1,0:T(8,128)S(1)}, f32[2,2,8,256]{3,2,1,0:T(8,128)S(1)}, u32[]{:S(2)}, u32[]{:S(2)}) collective-permute-start(f32[2,2,8,256]{3,2,1,0:T(8,128)S(1)} %get-tuple-element.67), channel_id=1, source_target_pairs={{0,9},{1,8},{2,11},{3,10},{4,13},{5,12},{6,15},{7,14},{8,1},{9,0},... | collective-permute-start | bytes 98312 | tf_op jit(solution)/shard_map/ppermute | solution.py:318
  41.9 0.0 collective-permute-done.19.refs_5_
  41.9 0.3 collective-permute-start.24
  42.2 0.0 collective-permute-done.20.refs_6_
  42.2 3.2 %collective-permute-start.25 = (f32[2,2,8,256]{3,2,1,0:T(8,128)S(1)}, f32[2,2,8,256]{3,2,1,0:T(8,128)S(1)}, u32[]{:S(2)}, u32[]{:S(2)}) collective-permute-start(f32[2,2,8,256]{3,2,1,0:T(8,128)S(1)} %get-tuple-element.69), channel_id=1, source_target_pairs={{0,11},{1,10},{2,9},{3,8},{4,15},{5,14},{6,13},{7,12},{8,3},{9,2},... | collective-permute-start | bytes 98312 | tf_op jit(solution)/shard_map/ppermute | solution.py:318
  45.4 1.6 %collective-permute-start.30 = (f32[8,2048]{1,0:T(8,128)S(1)}, f32[8,2048]{1,0:T(8,128)S(1)}, u32[]{:S(2)}, u32[]{:S(2)}) collective-permute-start(f32[8,2048]{1,0:T(8,128)S(1)} %slice_bitcast_fusion), channel_id=1, source_target_pairs={{0,16},{16,0},{1,17},{17,1},{2,18},{18,2},{3,19},{19,3},{4,20},{20... | collective-permute-start | bytes 196616 | tf_op jit(solution)/shard_map/ppermute | solution.py:364
  47.0 0.6 %collective-permute-start.26 = (f32[2,2,8,256]{3,2,1,0:T(8,128)S(1)}, f32[2,2,8,256]{3,2,1,0:T(8,128)S(1)}, u32[]{:S(2)}, u32[]{:S(2)}) collective-permute-start(f32[2,2,8,256]{3,2,1,0:T(8,128)S(1)} %get-tuple-element.70), channel_id=1, source_target_pairs={{0,12},{1,13},{2,14},{3,15},{4,8},{5,9},{6,10},{7,11},{8,4},{9,5},... | collective-permute-start | bytes 98312 | tf_op jit(solution)/shard_map/ppermute | solution.py:318
  47.6 2.7 %collective-permute-start.27 = (f32[2,2,8,256]{3,2,1,0:T(8,128)S(1)}, f32[2,2,8,256]{3,2,1,0:T(8,128)S(1)}, u32[]{:S(2)}, u32[]{:S(2)}) collective-permute-start(f32[2,2,8,256]{3,2,1,0:T(8,128)S(1)} %get-tuple-element.71), channel_id=1, source_target_pairs={{0,13},{1,12},{2,15},{3,14},{4,9},{5,8},{6,11},{7,10},{8,5},{9,4},... | collective-permute-start | bytes 98312 | tf_op jit(solution)/shard_map/ppermute | solution.py:318
  50.3 0.8 %collective-permute-start.28 = (f32[2,2,8,256]{3,2,1,0:T(8,128)S(1)}, f32[2,2,8,256]{3,2,1,0:T(8,128)S(1)}, u32[]{:S(2)}, u32[]{:S(2)}) collective-permute-start(f32[2,2,8,256]{3,2,1,0:T(8,128)S(1)} %get-tuple-element.72), channel_id=1, source_target_pairs={{0,14},{1,15},{2,12},{3,13},{4,10},{5,11},{6,8},{7,9},{8,6},{9,7},... | collective-permute-start | bytes 98312 | tf_op jit(solution)/shard_map/ppermute | solution.py:318
  51.2 0.0 collective-permute-done.25.refs_11_
  51.2 3.8 %collective-permute-start.29 = (f32[2,2,8,256]{3,2,1,0:T(8,128)S(1)}, f32[2,2,8,256]{3,2,1,0:T(8,128)S(1)}, u32[]{:S(2)}, u32[]{:S(2)}) collective-permute-start(f32[2,2,8,256]{3,2,1,0:T(8,128)S(1)} %get-tuple-element.73), channel_id=1, source_target_pairs={{0,15},{1,14},{2,13},{3,12},{4,11},{5,10},{6,9},{7,8},{8,7},{9,6},... | collective-permute-start | bytes 98312 | tf_op jit(solution)/shard_map/ppermute | solution.py:318
  55.0 2.0 %collective-permute-done.28.refs_14_ = f32[2,2,8,256]{3,2,1,0:T(8,128)S(1)} collective-permute-done((f32[2,2,8,256]{3,2,1,0:T(8,128)S(1)}, f32[2,2,8,256]{3,2,1,0:T(8,128)S(1)}, u32[]{:S(2)}, u32[]{:S(2)}) %collective-permute-start.28) | collective-permute-done | bytes 32800 | tf_op jit(solution)/shard_map/ppermute | solution.py:318
  57.0 0.3 collective-permute-done.29.refs_15_
  57.3 0.6 %copy-done.7 = f32[128]{0:T(128)S(1)} copy-done((f32[128]{0:T(128)S(1)}, f32[128]{0:T(128)}, u32[]{:S(2)}) %copy-start.7) | copy-done | bytes 536
  57.9 1.2 %outputs.1 = (f32[2,256,128]{2,1,0:T(8,128)}, f32[2,256,128]{2,1,0:T(8,128)}, f32[2,256,128]{2,1,0:T(8,128)}, f32[2,256,128]{2,1,0:T(8,128)}) custom-call(f32[2,256,128]{2,1,0:T(8,128)S(1)} %copy-done, f32[2,256,128]{2,1,0:T(8,128)S(1)} %copy-done.1, f32[2,256,128]{2,1,0:T(8,128)S(1)} %copy-done.2, f32[2,256,128]{2,1,0:T(8,128)S(1)} %copy-done.3, ...), custom_call_target="tpu_custom_call" | custom-call | tf_op jit(solution)/shard_map/outputs/pallas_call | solution.py:366
  59.1 0.6 %bitcast_add_fusion = f32[8,2048]{1,0:T(8,128)} fusion(f32[8,2048]{1,0:T(8,128)S(1)} %collective-permute-done.30, f32[2,8,2048]{2,1,0:T(8,128)S(1)} %get-tuple-element.78), kind=kLoop, calls=%fused_computation | loop fusion | flops 16384 | bytes 196608 | tf_op jit(solution)/shard_map/add | solution.py:364
  (19 shorter events, 0.0 us)
Async XLA Ops:
  0.6 29.7 %copy-start.4 = (bf16[768,256]{1,0:T(8,128)(2,1)S(1)}, bf16[768,256]{1,0:T(8,128)(2,1)}, u32[]{:S(2)}) copy-start(bf16[768,256]{1,0:T(8,128)(2,1)} %constant.5.clone.refs_2_) | copy-start | bytes 1179652
  0.6 29.7 %copy-start.5 = (f32[8,4096]{1,0:T(8,128)S(1)}, f32[8,4096]{1,0:T(8,128)}, u32[]{:S(2)}) copy-start(f32[8,4096]{1,0:T(8,128)} %refs_0_.1) | copy-start | bytes 393220
  0.7 29.7 %copy-start.6 = (f32[64,256]{1,0:T(8,128)S(1)}, f32[64,256]{1,0:T(8,128)}, u32[]{:S(2)}) copy-start(f32[64,256]{1,0:T(8,128)} %constant.4.clone.refs_1_) | copy-start | bytes 196612
  2.3 5.0 %collective-permute-start = (f32[2,2,8,256]{3,2,1,0:T(8,128)S(1)}, f32[2,2,8,256]{3,2,1,0:T(8,128)S(1)}, u32[]{:S(2)}, u32[]{:S(2)}) collective-permute-start(f32[2,2,8,256]{3,2,1,0:T(8,128)S(1)} %get-tuple-element.43), channel_id=1, source_target_pairs={{0,1},{1,0},{2,3},{3,2},{4,5},{5,4},{6,7},{7,6},{8,9},{9,8},{10,11... | collective-permute-start | bytes 98312 | tf_op jit(solution)/shard_map/ppermute | solution.py:318
  2.8 7.1 %collective-permute-start.1 = (f32[2,2,8,256]{3,2,1,0:T(8,128)S(1)}, f32[2,2,8,256]{3,2,1,0:T(8,128)S(1)}, u32[]{:S(2)}, u32[]{:S(2)}) collective-permute-start(f32[2,2,8,256]{3,2,1,0:T(8,128)S(1)} %get-tuple-element.44), channel_id=1, source_target_pairs={{0,2},{1,3},{2,0},{3,1},{4,6},{5,7},{6,4},{7,5},{8,10},{9,11},{10,... | collective-permute-start | bytes 98312 | tf_op jit(solution)/shard_map/ppermute | solution.py:318
  5.4 4.6 %collective-permute-start.2 = (f32[2,2,8,256]{3,2,1,0:T(8,128)S(1)}, f32[2,2,8,256]{3,2,1,0:T(8,128)S(1)}, u32[]{:S(2)}, u32[]{:S(2)}) collective-permute-start(f32[2,2,8,256]{3,2,1,0:T(8,128)S(1)} %get-tuple-element.45), channel_id=1, source_target_pairs={{0,3},{1,2},{2,1},{3,0},{4,7},{5,6},{6,5},{7,4},{8,11},{9,10},{10,... | collective-permute-start | bytes 98312 | tf_op jit(solution)/shard_map/ppermute | solution.py:318
  5.4 7.2 %collective-permute-start.3 = (f32[2,2,8,256]{3,2,1,0:T(8,128)S(1)}, f32[2,2,8,256]{3,2,1,0:T(8,128)S(1)}, u32[]{:S(2)}, u32[]{:S(2)}) collective-permute-start(f32[2,2,8,256]{3,2,1,0:T(8,128)S(1)} %get-tuple-element.46), channel_id=1, source_target_pairs={{0,4},{1,5},{2,6},{3,7},{4,0},{5,1},{6,2},{7,3},{8,12},{9,13},{10,... | collective-permute-start | bytes 98312 | tf_op jit(solution)/shard_map/ppermute | solution.py:318
  7.2 5.7 %collective-permute-start.4 = (f32[2,2,8,256]{3,2,1,0:T(8,128)S(1)}, f32[2,2,8,256]{3,2,1,0:T(8,128)S(1)}, u32[]{:S(2)}, u32[]{:S(2)}) collective-permute-start(f32[2,2,8,256]{3,2,1,0:T(8,128)S(1)} %get-tuple-element.47), channel_id=1, source_target_pairs={{0,5},{1,4},{2,7},{3,6},{4,1},{5,0},{6,3},{7,2},{8,13},{9,12},{10,... | collective-permute-start | bytes 98312 | tf_op jit(solution)/shard_map/ppermute | solution.py:318
  7.2 9.0 %collective-permute-start.5 = (f32[2,2,8,256]{3,2,1,0:T(8,128)S(1)}, f32[2,2,8,256]{3,2,1,0:T(8,128)S(1)}, u32[]{:S(2)}, u32[]{:S(2)}) collective-permute-start(f32[2,2,8,256]{3,2,1,0:T(8,128)S(1)} %get-tuple-element.48), channel_id=1, source_target_pairs={{0,6},{1,7},{2,4},{3,5},{4,2},{5,3},{6,0},{7,1},{8,14},{9,15},{10,... | collective-permute-start | bytes 98312 | tf_op jit(solution)/shard_map/ppermute | solution.py:318
  9.9 6.4 %collective-permute-start.6 = (f32[2,2,8,256]{3,2,1,0:T(8,128)S(1)}, f32[2,2,8,256]{3,2,1,0:T(8,128)S(1)}, u32[]{:S(2)}, u32[]{:S(2)}) collective-permute-start(f32[2,2,8,256]{3,2,1,0:T(8,128)S(1)} %get-tuple-element.49), channel_id=1, source_target_pairs={{0,7},{1,6},{2,5},{3,4},{4,3},{5,2},{6,1},{7,0},{8,15},{9,14},{10,... | collective-permute-start | bytes 98312 | tf_op jit(solution)/shard_map/ppermute | solution.py:318
  10.0 9.9 %collective-permute-start.7 = (f32[2,2,8,256]{3,2,1,0:T(8,128)S(1)}, f32[2,2,8,256]{3,2,1,0:T(8,128)S(1)}, u32[]{:S(2)}, u32[]{:S(2)}) collective-permute-start(f32[2,2,8,256]{3,2,1,0:T(8,128)S(1)} %get-tuple-element.50), channel_id=1, source_target_pairs={{0,8},{1,9},{2,10},{3,11},{4,12},{5,13},{6,14},{7,15},{8,0},{9,1},... | collective-permute-start | bytes 98312 | tf_op jit(solution)/shard_map/ppermute | solution.py:318
  12.6 7.4 %collective-permute-start.8 = (f32[2,2,8,256]{3,2,1,0:T(8,128)S(1)}, f32[2,2,8,256]{3,2,1,0:T(8,128)S(1)}, u32[]{:S(2)}, u32[]{:S(2)}) collective-permute-start(f32[2,2,8,256]{3,2,1,0:T(8,128)S(1)} %get-tuple-element.51), channel_id=1, source_target_pairs={{0,9},{1,8},{2,11},{3,10},{4,13},{5,12},{6,15},{7,14},{8,1},{9,0},... | collective-permute-start | bytes 98312 | tf_op jit(solution)/shard_map/ppermute | solution.py:318
  13.0 11.3 %collective-permute-start.9 = (f32[2,2,8,256]{3,2,1,0:T(8,128)S(1)}, f32[2,2,8,256]{3,2,1,0:T(8,128)S(1)}, u32[]{:S(2)}, u32[]{:S(2)}) collective-permute-start(f32[2,2,8,256]{3,2,1,0:T(8,128)S(1)} %get-tuple-element.52), channel_id=1, source_target_pairs={{0,10},{1,11},{2,8},{3,9},{4,14},{5,15},{6,12},{7,13},{8,2},{9,3},... | collective-permute-start | bytes 98312 | tf_op jit(solution)/shard_map/ppermute | solution.py:318
  16.2 8.2 %collective-permute-start.10 = (f32[2,2,8,256]{3,2,1,0:T(8,128)S(1)}, f32[2,2,8,256]{3,2,1,0:T(8,128)S(1)}, u32[]{:S(2)}, u32[]{:S(2)}) collective-permute-start(f32[2,2,8,256]{3,2,1,0:T(8,128)S(1)} %get-tuple-element.53), channel_id=1, source_target_pairs={{0,11},{1,10},{2,9},{3,8},{4,15},{5,14},{6,13},{7,12},{8,3},{9,2},... | collective-permute-start | bytes 98312 | tf_op jit(solution)/shard_map/ppermute | solution.py:318
  16.3 8.1 %collective-permute-start.11 = (f32[2,2,8,256]{3,2,1,0:T(8,128)S(1)}, f32[2,2,8,256]{3,2,1,0:T(8,128)S(1)}, u32[]{:S(2)}, u32[]{:S(2)}) collective-permute-start(f32[2,2,8,256]{3,2,1,0:T(8,128)S(1)} %get-tuple-element.54), channel_id=1, source_target_pairs={{0,12},{1,13},{2,14},{3,15},{4,8},{5,9},{6,10},{7,11},{8,4},{9,5},... | collective-permute-start | bytes 98312 | tf_op jit(solution)/shard_map/ppermute | solution.py:318
  19.9 5.3 %collective-permute-start.12 = (f32[2,2,8,256]{3,2,1,0:T(8,128)S(1)}, f32[2,2,8,256]{3,2,1,0:T(8,128)S(1)}, u32[]{:S(2)}, u32[]{:S(2)}) collective-permute-start(f32[2,2,8,256]{3,2,1,0:T(8,128)S(1)} %get-tuple-element.55), channel_id=1, source_target_pairs={{0,13},{1,12},{2,15},{3,14},{4,9},{5,8},{6,11},{7,10},{8,5},{9,4},... | collective-permute-start | bytes 98312 | tf_op jit(solution)/shard_map/ppermute | solution.py:318
  20.1 7.0 %collective-permute-start.13 = (f32[2,2,8,256]{3,2,1,0:T(8,128)S(1)}, f32[2,2,8,256]{3,2,1,0:T(8,128)S(1)}, u32[]{:S(2)}, u32[]{:S(2)}) collective-permute-start(f32[2,2,8,256]{3,2,1,0:T(8,128)S(1)} %get-tuple-element.56), channel_id=1, source_target_pairs={{0,14},{1,15},{2,12},{3,13},{4,10},{5,11},{6,8},{7,9},{8,6},{9,7},... | collective-permute-start | bytes 98312 | tf_op jit(solution)/shard_map/ppermute | solution.py:318
  24.3 6.0 %collective-permute-start.14 = (f32[2,2,8,256]{3,2,1,0:T(8,128)S(1)}, f32[2,2,8,256]{3,2,1,0:T(8,128)S(1)}, u32[]{:S(2)}, u32[]{:S(2)}) collective-permute-start(f32[2,2,8,256]{3,2,1,0:T(8,128)S(1)} %get-tuple-element.57), channel_id=1, source_target_pairs={{0,15},{1,14},{2,13},{3,12},{4,11},{5,10},{6,9},{7,8},{8,7},{9,6},... | collective-permute-start | bytes 98312 | tf_op jit(solution)/shard_map/ppermute | solution.py:318
  30.4 26.9 %copy-start = (f32[2,256,128]{2,1,0:T(8,128)S(1)}, f32[2,256,128]{2,1,0:T(8,128)}, u32[]{:S(2)}) copy-start(f32[2,256,128]{2,1,0:T(8,128)} %query_ref.1) | copy-start | bytes 786436
  30.4 26.9 %copy-start.1 = (f32[2,256,128]{2,1,0:T(8,128)S(1)}, f32[2,256,128]{2,1,0:T(8,128)}, u32[]{:S(2)}) copy-start(f32[2,256,128]{2,1,0:T(8,128)} %key_ref.1) | copy-start | bytes 786436
  30.4 26.9 %copy-start.2 = (f32[2,256,128]{2,1,0:T(8,128)S(1)}, f32[2,256,128]{2,1,0:T(8,128)}, u32[]{:S(2)}) copy-start(f32[2,256,128]{2,1,0:T(8,128)} %value_ref.1) | copy-start | bytes 786436
  30.4 26.9 %copy-start.3 = (f32[2,256,128]{2,1,0:T(8,128)S(1)}, f32[2,256,128]{2,1,0:T(8,128)}, u32[]{:S(2)}) copy-start(f32[2,256,128]{2,1,0:T(8,128)} %cotangent_ref.1) | copy-start | bytes 786436
  32.9 3.7 %collective-permute-start.15 = (f32[2,2,8,256]{3,2,1,0:T(8,128)S(1)}, f32[2,2,8,256]{3,2,1,0:T(8,128)S(1)}, u32[]{:S(2)}, u32[]{:S(2)}) collective-permute-start(f32[2,2,8,256]{3,2,1,0:T(8,128)S(1)} %get-tuple-element.59), channel_id=1, source_target_pairs={{0,1},{1,0},{2,3},{3,2},{4,5},{5,4},{6,7},{7,6},{8,9},{9,8},{10,11... | collective-permute-start | bytes 98312 | tf_op jit(solution)/shard_map/ppermute | solution.py:318
  33.1 4.2 %collective-permute-start.16 = (f32[2,2,8,256]{3,2,1,0:T(8,128)S(1)}, f32[2,2,8,256]{3,2,1,0:T(8,128)S(1)}, u32[]{:S(2)}, u32[]{:S(2)}) collective-permute-start(f32[2,2,8,256]{3,2,1,0:T(8,128)S(1)} %get-tuple-element.60), channel_id=1, source_target_pairs={{0,2},{1,3},{2,0},{3,1},{4,6},{5,7},{6,4},{7,5},{8,10},{9,11},{10,... | collective-permute-start | bytes 98312 | tf_op jit(solution)/shard_map/ppermute | solution.py:318
  33.6 5.6 %collective-permute-start.17 = (f32[2,2,8,256]{3,2,1,0:T(8,128)S(1)}, f32[2,2,8,256]{3,2,1,0:T(8,128)S(1)}, u32[]{:S(2)}, u32[]{:S(2)}) collective-permute-start(f32[2,2,8,256]{3,2,1,0:T(8,128)S(1)} %get-tuple-element.61), channel_id=1, source_target_pairs={{0,3},{1,2},{2,1},{3,0},{4,7},{5,6},{6,5},{7,4},{8,11},{9,10},{10,... | collective-permute-start | bytes 98312 | tf_op jit(solution)/shard_map/ppermute | solution.py:318
  34.8 4.4 %collective-permute-start.18 = (f32[2,2,8,256]{3,2,1,0:T(8,128)S(1)}, f32[2,2,8,256]{3,2,1,0:T(8,128)S(1)}, u32[]{:S(2)}, u32[]{:S(2)}) collective-permute-start(f32[2,2,8,256]{3,2,1,0:T(8,128)S(1)} %get-tuple-element.62), channel_id=1, source_target_pairs={{0,4},{1,5},{2,6},{3,7},{4,0},{5,1},{6,2},{7,3},{8,12},{9,13},{10,... | collective-permute-start | bytes 98312 | tf_op jit(solution)/shard_map/ppermute | solution.py:318
  34.8 7.1 %collective-permute-start.19 = (f32[2,2,8,256]{3,2,1,0:T(8,128)S(1)}, f32[2,2,8,256]{3,2,1,0:T(8,128)S(1)}, u32[]{:S(2)}, u32[]{:S(2)}) collective-permute-start(f32[2,2,8,256]{3,2,1,0:T(8,128)S(1)} %get-tuple-element.63), channel_id=1, source_target_pairs={{0,5},{1,4},{2,7},{3,6},{4,1},{5,0},{6,3},{7,2},{8,13},{9,12},{10,... | collective-permute-start | bytes 98312 | tf_op jit(solution)/shard_map/ppermute | solution.py:318
  36.6 5.6 %collective-permute-start.20 = (f32[2,2,8,256]{3,2,1,0:T(8,128)S(1)}, f32[2,2,8,256]{3,2,1,0:T(8,128)S(1)}, u32[]{:S(2)}, u32[]{:S(2)}) collective-permute-start(f32[2,2,8,256]{3,2,1,0:T(8,128)S(1)} %get-tuple-element.64), channel_id=1, source_target_pairs={{0,6},{1,7},{2,4},{3,5},{4,2},{5,3},{6,0},{7,1},{8,14},{9,15},{10,... | collective-permute-start | bytes 98312 | tf_op jit(solution)/shard_map/ppermute | solution.py:318
  37.3 8.1 %collective-permute-start.21 = (f32[2,2,8,256]{3,2,1,0:T(8,128)S(1)}, f32[2,2,8,256]{3,2,1,0:T(8,128)S(1)}, u32[]{:S(2)}, u32[]{:S(2)}) collective-permute-start(f32[2,2,8,256]{3,2,1,0:T(8,128)S(1)} %get-tuple-element.65), channel_id=1, source_target_pairs={{0,7},{1,6},{2,5},{3,4},{4,3},{5,2},{6,1},{7,0},{8,15},{9,14},{10,... | collective-permute-start | bytes 98312 | tf_op jit(solution)/shard_map/ppermute | solution.py:318
  39.2 7.8 %collective-permute-start.22 = (f32[2,2,8,256]{3,2,1,0:T(8,128)S(1)}, f32[2,2,8,256]{3,2,1,0:T(8,128)S(1)}, u32[]{:S(2)}, u32[]{:S(2)}) collective-permute-start(f32[2,2,8,256]{3,2,1,0:T(8,128)S(1)} %get-tuple-element.66), channel_id=1, source_target_pairs={{0,8},{1,9},{2,10},{3,11},{4,12},{5,13},{6,14},{7,15},{8,0},{9,1},... | collective-permute-start | bytes 98312 | tf_op jit(solution)/shard_map/ppermute | solution.py:318
  39.2 8.4 %collective-permute-start.23 = (f32[2,2,8,256]{3,2,1,0:T(8,128)S(1)}, f32[2,2,8,256]{3,2,1,0:T(8,128)S(1)}, u32[]{:S(2)}, u32[]{:S(2)}) collective-permute-start(f32[2,2,8,256]{3,2,1,0:T(8,128)S(1)} %get-tuple-element.67), channel_id=1, source_target_pairs={{0,9},{1,8},{2,11},{3,10},{4,13},{5,12},{6,15},{7,14},{8,1},{9,0},... | collective-permute-start | bytes 98312 | tf_op jit(solution)/shard_map/ppermute | solution.py:318
  41.9 8.4 %collective-permute-start.24 = (f32[2,2,8,256]{3,2,1,0:T(8,128)S(1)}, f32[2,2,8,256]{3,2,1,0:T(8,128)S(1)}, u32[]{:S(2)}, u32[]{:S(2)}) collective-permute-start(f32[2,2,8,256]{3,2,1,0:T(8,128)S(1)} %get-tuple-element.68), channel_id=1, source_target_pairs={{0,10},{1,11},{2,8},{3,9},{4,14},{5,15},{6,12},{7,13},{8,2},{9,3},... | collective-permute-start | bytes 98312 | tf_op jit(solution)/shard_map/ppermute | solution.py:318
  42.2 8.9 %collective-permute-start.25 = (f32[2,2,8,256]{3,2,1,0:T(8,128)S(1)}, f32[2,2,8,256]{3,2,1,0:T(8,128)S(1)}, u32[]{:S(2)}, u32[]{:S(2)}) collective-permute-start(f32[2,2,8,256]{3,2,1,0:T(8,128)S(1)} %get-tuple-element.69), channel_id=1, source_target_pairs={{0,11},{1,10},{2,9},{3,8},{4,15},{5,14},{6,13},{7,12},{8,3},{9,2},... | collective-permute-start | bytes 98312 | tf_op jit(solution)/shard_map/ppermute | solution.py:318
  45.4 13.7 %collective-permute-start.30 = (f32[8,2048]{1,0:T(8,128)S(1)}, f32[8,2048]{1,0:T(8,128)S(1)}, u32[]{:S(2)}, u32[]{:S(2)}) collective-permute-start(f32[8,2048]{1,0:T(8,128)S(1)} %slice_bitcast_fusion), channel_id=1, source_target_pairs={{0,16},{16,0},{1,17},{17,1},{2,18},{18,2},{3,19},{19,3},{4,20},{20... | collective-permute-start | bytes 196616 | tf_op jit(solution)/shard_map/ppermute | solution.py:364
  47.0 8.0 %collective-permute-start.26 = (f32[2,2,8,256]{3,2,1,0:T(8,128)S(1)}, f32[2,2,8,256]{3,2,1,0:T(8,128)S(1)}, u32[]{:S(2)}, u32[]{:S(2)}) collective-permute-start(f32[2,2,8,256]{3,2,1,0:T(8,128)S(1)} %get-tuple-element.70), channel_id=1, source_target_pairs={{0,12},{1,13},{2,14},{3,15},{4,8},{5,9},{6,10},{7,11},{8,4},{9,5},... | collective-permute-start | bytes 98312 | tf_op jit(solution)/shard_map/ppermute | solution.py:318
  47.6 7.4 %collective-permute-start.27 = (f32[2,2,8,256]{3,2,1,0:T(8,128)S(1)}, f32[2,2,8,256]{3,2,1,0:T(8,128)S(1)}, u32[]{:S(2)}, u32[]{:S(2)}) collective-permute-start(f32[2,2,8,256]{3,2,1,0:T(8,128)S(1)} %get-tuple-element.71), channel_id=1, source_target_pairs={{0,13},{1,12},{2,15},{3,14},{4,9},{5,8},{6,11},{7,10},{8,5},{9,4},... | collective-permute-start | bytes 98312 | tf_op jit(solution)/shard_map/ppermute | solution.py:318
  50.3 6.7 %collective-permute-start.28 = (f32[2,2,8,256]{3,2,1,0:T(8,128)S(1)}, f32[2,2,8,256]{3,2,1,0:T(8,128)S(1)}, u32[]{:S(2)}, u32[]{:S(2)}) collective-permute-start(f32[2,2,8,256]{3,2,1,0:T(8,128)S(1)} %get-tuple-element.72), channel_id=1, source_target_pairs={{0,14},{1,15},{2,12},{3,13},{4,10},{5,11},{6,8},{7,9},{8,6},{9,7},... | collective-permute-start | bytes 98312 | tf_op jit(solution)/shard_map/ppermute | solution.py:318
  51.2 6.1 %collective-permute-start.29 = (f32[2,2,8,256]{3,2,1,0:T(8,128)S(1)}, f32[2,2,8,256]{3,2,1,0:T(8,128)S(1)}, u32[]{:S(2)}, u32[]{:S(2)}) collective-permute-start(f32[2,2,8,256]{3,2,1,0:T(8,128)S(1)} %get-tuple-element.73), channel_id=1, source_target_pairs={{0,15},{1,14},{2,13},{3,12},{4,11},{5,10},{6,9},{7,8},{8,7},{9,6},... | collective-permute-start | bytes 98312 | tf_op jit(solution)/shard_map/ppermute | solution.py:318
  57.3 0.7 %copy-start.7 = (f32[128]{0:T(128)S(1)}, f32[128]{0:T(128)}, u32[]{:S(2)}) copy-start(f32[128]{0:T(128)} %param.12) | copy-start | bytes 1540

commit v2 on v0

v2 whole, which is shorter than its diff:
```python
import functools
import math

import jax
import jax.numpy as jnp
import ml_dtypes
import numpy as np
from jax import lax
from jax.experimental import pallas as pl
from jax.experimental.pallas import tpu as pltpu
from jax.sharding import PartitionSpec as P

VMEM_BYTES = 48 * 1024 * 1024
ROW_CHUNK = 128


def add(a, b):
    if a is None:
        return b
    if b is None:
        return a
    return a + b


def sub(a, b):
    if b is None:
        return a
    if a is None:
        return -b
    return a - b


def scale(a, factor):
    if a is None or factor == 1.0:
        return a
    if factor == -1.0:
        return -a
    return a * factor


def turn(x, step, period):
    if x is None:
        return None
    re, im = x
    step = step % period
    if (4 * step) % period == 0:
        quarter = 4 * step // period
        if quarter == 0:
            return (re, im)
        if quarter == 1:
            return (im, scale(re, -1.0))
        if quarter == 2:
            return (scale(re, -1.0), scale(im, -1.0))
        return (scale(im, -1.0), re)
    angle = -2.0 * math.pi * step / period
    c, s = math.cos(angle), math.sin(angle)
    if (8 * step) % period == 0:
        root = math.sqrt(0.5)
        total, difference = add(re, im), sub(re, im)
        if c * s > 0:
            return (scale(difference, math.copysign(root, c)), scale(total, math.copysign(root, c)))
        return (scale(total, math.copysign(root, c)), scale(sub(im, re), math.copysign(root, c)))
    return (sub(scale(re, c), scale(im, s)), add(scale(re, s), scale(im, c)))


def complex_add(x, y):
    if x is None:
        return y
    if y is None:
        return x
    return (add(x[0], y[0]), add(x[1], y[1]))


def complex_sub(x, y):
    if y is None:
        return x
    if x is None:
        return (scale(y[0], -1.0), scale(y[1], -1.0))
    return (sub(x[0], y[0]), sub(x[1], y[1]))


def small_dft(values):
    size = len(values)
    if size == 1:
        return list(values)
    even = small_dft(values[0::2])
    odd = small_dft(values[1::2])
    odd = [turn(value, step, size) for step, value in enumerate(odd)]
    return [complex_add(e, o) for e, o in zip(even, odd)] + [
        complex_sub(e, o) for e, o in zip(even, odd)
    ]


def factors_of(size):
    first = 1
    while first * first < size:
        first *= 2
    return (size // first, first)


def across_rows(load, emit, count, kept, store, fetch):
    first, second = factors_of(count)
    for b in range(second):
        values = small_dft([load(second * a + b) for a in range(first)])
        for p, value in enumerate(values):
            store(b, p, turn(value, b * p, count))
    for p in range(first):
        values = small_dft([fetch(b, p) for b in range(second)])
        for q, value in enumerate(values):
            k1 = p + first * q
            if k1 < kept:
                emit(k1, value)


def tables(count, lanes):
    k1 = np.arange(count)[:, None]
    n2 = np.arange(lanes)[None, :]
    phase = -2.0 * np.pi * ((k1 * n2) % (count * lanes)) / (count * lanes)
    twist = np.concatenate([np.cos(phase), np.sin(phase)], axis=1).astype(np.float32)
    j = np.arange(lanes)
    phase = -2.0 * np.pi * ((j[:, None] * j[None, :]) % lanes) / lanes
    c, s = np.cos(phase), np.sin(phase)
    matrix = np.block([[c, s], [-s, c]]).astype(np.float32)
    high = matrix.astype(ml_dtypes.bfloat16)
    low = (matrix - high.astype(np.float32)).astype(ml_dtypes.bfloat16)
    return twist, np.concatenate([high, high, low], axis=0)


def lane_dft(x, matrix):
    high = x.astype(jnp.bfloat16)
    low = (x - high.astype(jnp.float32)).astype(jnp.bfloat16)
    return jnp.dot(
        jnp.concatenate([high, low, high], axis=1), matrix, preferred_element_type=jnp.float32
    )


def gate_kernel(query_hbm, key_hbm, value_hbm, cotangent_hbm, mixed_ref, upstream_ref, held, sems):
    shards, batch, channels, tokens = mixed_ref.shape
    sources = (key_hbm, value_hbm, cotangent_hbm, query_hbm)

    def copy(b, i):
        return pltpu.make_async_copy(sources[i].at[b], held.at[i, b], sems.at[i, b])

    for i in range(4):
        for b in range(batch):
            copy(b, i).start()
    for kind, sent in enumerate((mixed_ref, upstream_ref)):
        for b in range(batch):
            copy(b, 2 * kind).wait()
            copy(b, 2 * kind + 1).wait()
            product = held[2 * kind, b] * held[2 * kind + 1, b]
            sent[:, b] = jnp.transpose(product).reshape(shards, channels, tokens)


def transforms(twist_ref, matrix_ref, middle, turned):
    count, channels, width = turned.shape
    lanes = width // 2
    first, _ = factors_of(count)
    per_chunk = ROW_CHUNK // channels
    chunks = [slice(at, min(at + per_chunk, count)) for at in range(0, count, per_chunk)]

    def store(b, p, value):
        re, im = value
        middle[b * first + p, :, :lanes] = jnp.zeros_like(im) if re is None else re
        middle[b * first + p, :, lanes:] = jnp.zeros_like(re) if im is None else im

    def fetch(b, p):
        return (middle[b * first + p, :, :lanes], middle[b * first + p, :, lanes:])

    def twist(k1, value):
        c, s = twist_ref[k1 : k1 + 1, :lanes], twist_ref[k1 : k1 + 1, lanes:]
        return (value[0] * c - value[1] * s, value[0] * s + value[1] * c)

    def place(k1, value):
        turned[k1, :, :lanes], turned[k1, :, lanes:] = twist(k1, value)

    def forward(load, spec):
        across_rows(load, place, count, count, store, fetch)
        for part in chunks:
            x = turned[part].reshape(-1, width)
            spec[part] = lane_dft(x, matrix_ref[...]).reshape(-1, channels, width)

    def inverse(left, right, conjugate_left, emit):
        for part in chunks:
            lr, li = left[part, :, :lanes], left[part, :, lanes:]
            rr, ri = right[part, :, :lanes], right[part, :, lanes:]
            if conjugate_left:
                re, im = lr * rr + li * ri, li * rr - lr * ri
            else:
                re, im = lr * rr - li * ri, -(lr * ri + li * rr)
            x = jnp.concatenate([re.reshape(-1, lanes), im.reshape(-1, lanes)], axis=1)
            turned[part] = lane_dft(x, matrix_ref[...]).reshape(-1, channels, width)

        def load(k1):
            return twist(k1, (turned[k1, :, :lanes], turned[k1, :, lanes:]))

        across_rows(load, emit, count, count // 2, store, fetch)

    return forward, inverse


def token_blocks(ref, lanes, pair, live):
    pieces = ref.shape[3] // lanes

    def where(n1):
        at = n1 % pieces * lanes
        return n1 // pieces, slice(at, at + lanes)

    def load(n1):
        if n1 >= live:
            return None
        shard, span = where(n1)
        return (ref[shard, 2 * pair, :, span], ref[shard, 2 * pair + 1, :, span])

    def emit(n1, value):
        shard, span = where(n1)
        ref[shard, 2 * pair, :, span] = value[0]
        ref[shard, 2 * pair + 1, :, span] = -value[1]

    return load, emit


def filter_kernel(filter_ref, twist_ref, matrix_ref, spec_ref, middle, turned):
    length = filter_ref.shape[1]
    lanes = twist_ref.shape[1] // 2
    forward, _ = transforms(twist_ref, matrix_ref, middle, turned)

    def load(n1):
        if n1 * lanes >= length:
            return None
        return (filter_ref[:, n1 * lanes : (n1 + 1) * lanes] * (0.5 / length), None)

    forward(load, spec_ref)


def convolve_kernel(
    conjugate, held_ref, filter_ref, twist_ref, matrix_ref, back_ref, spec_ref, middle, turned
):
    count, width = twist_ref.shape
    forward, inverse = transforms(twist_ref, matrix_ref, middle, turned)
    for pair in range(spec_ref.shape[0]):
        load, _ = token_blocks(held_ref, width // 2, pair, count // 2)
        _, emit = token_blocks(back_ref, width // 2, pair, count // 2)
        forward(load, spec_ref.at[pair])
        inverse(filter_ref, spec_ref.at[pair], conjugate, emit)


def lag_kernel(scaling, mixed_ref, upstream_ref, twist_ref, matrix_ref, lag_ref, middle, turned):
    lanes = twist_ref.shape[1] // 2
    groups, _, share = lag_ref.shape
    group = lax.axis_index("batch")
    _, inverse = transforms(twist_ref, matrix_ref, middle, turned)
    for pair in range(mixed_ref.shape[0]):

        def emit(n1, value):
            at = n1 * lanes
            slot = lax.rem(at // share - group + groups, groups)
            span = slice(at % share, at % share + lanes)
            if pair == 0:
                lag_ref[slot, :, span] = value[0] * scaling
            else:
                lag_ref[slot, :, span] += value[0] * scaling

        inverse(mixed_ref.at[pair], upstream_ref.at[pair], True, emit)


def output_kernel(
    query_ref, key_ref, value_ref, cotangent_ref, skip_ref, convolved_ref, back_ref,
    output_ref, query_grad_ref, key_grad_ref, value_grad_ref,
):
    shards, batch, channels, tokens = convolved_ref.shape
    skip = skip_ref[...]

    def rows(ref, b):
        return jnp.transpose(ref[:, b].reshape(shards * channels, tokens))

    for b in range(batch):
        query, key, value, cotangent = query_ref[b], key_ref[b], value_ref[b], cotangent_ref[b]
        hidden = rows(convolved_ref, b) + skip * (key * value)
        output_ref[b] = query * hidden
        query_grad_ref[b] = cotangent * hidden
        mixed_grad = rows(back_ref, b) + skip * (cotangent * query)
        key_grad_ref[b] = mixed_grad * value
        value_grad_ref[b] = mixed_grad * key


def exchange(blocks):
    return lax.all_to_all(blocks, "seq", split_axis=0, concat_axis=0, tiled=True)


def per_device(query_gate, key_gate, value_input, filters, skip_gain, cotangent, *, shards, groups):
    batch, tokens, all_channels = query_gate.shape
    channels, length = filters.shape
    lanes = 128 if 2 * length // 128 <= 64 else tokens
    count = 2 * length // lanes
    twist, matrix = tables(count, lanes)

    lane_work = 2 * 3 * count * channels * (2 * lanes) ** 2

    def of(*shape):
        return jax.ShapeDtypeStruct(shape, jnp.float32)

    def call(kernel, name, stages, out_shape, scratch, *arrays, **options):
        return pl.pallas_call(
            kernel,
            out_shape=out_shape,
            scratch_shapes=scratch,
            compiler_params=pltpu.CompilerParams(vmem_limit_bytes=VMEM_BYTES),
            cost_estimate=pl.CostEstimate(
                flops=stages * lane_work, bytes_accessed=stages * 4 * batch * channels * length,
                transcendentals=0,
            ),
            name=name,
            **options,
        )(*arrays)

    swap = of(shards, batch, channels, tokens)
    spectrum = of(batch // 2, count, channels, 2 * lanes)
    work = [pltpu.VMEM((count, channels, 2 * lanes), jnp.float32)] * 2
    mixed, upstream = call(
        gate_kernel,
        "gate", 1,
        (swap, swap),
        [
            pltpu.VMEM((4, batch, tokens, all_channels), jnp.float32),
            pltpu.SemaphoreType.DMA((4, batch)),
        ],
        *(
            pltpu.with_memory_space_constraint(x, pltpu.HBM)
            for x in (query_gate, key_gate, value_input, cotangent)
        ),
        in_specs=[pl.BlockSpec(memory_space=pltpu.HBM)] * 4,
    )
    mixed = exchange(mixed)
    upstream = exchange(upstream)
    filter_spec = call(
        filter_kernel, "filter", 2, of(count, channels, 2 * lanes), work, filters, twist, matrix
    )
    convolved, mixed_spec = call(
        functools.partial(convolve_kernel, False),
        "convolve", 4, (swap, spectrum), work, mixed, filter_spec, twist, matrix,
    )
    convolved = exchange(convolved)
    filter_spec, mixed_spec = lax.optimization_barrier((filter_spec, mixed_spec))
    back, upstream_spec = call(
        functools.partial(convolve_kernel, True),
        "correlate", 4, (swap, spectrum), work, upstream, filter_spec, twist, matrix,
    )
    back = exchange(back)
    lag = call(
        functools.partial(lag_kernel, 1.0 / (2.0 * length * math.sqrt(length))),
        "lags", 2, of(groups, channels, length // groups), work,
        mixed_spec, upstream_spec, twist, matrix,
    )
    filter_grad = lag[0]
    for step in range(1, groups):
        pairs = [(source, (source + step) % groups) for source in range(groups)]
        filter_grad = filter_grad + lax.ppermute(lag[step], "batch", pairs)
    output, query_grad, key_grad, value_grad = call(
        output_kernel,
        "outputs", 2, (of(*query_gate.shape),) * 4, [],
        query_gate, key_gate, value_input, cotangent, skip_gain.reshape(1, all_channels),
        convolved, back,
    )
    return (output, query_grad, key_grad, value_grad, filter_grad)


def solution(mesh):
    in_specs = (
        P("batch", "seq", None),
        P("batch", "seq", None),
        P("batch", "seq", None),
        P("seq", None),
        P(),
        P("batch", "seq", None),
    )
    out_specs = (
        P("batch", "seq", None),
        P("batch", "seq", None),
        P("batch", "seq", None),
        P("batch", "seq", None),
        P("seq", "batch"),
    )
    shards, groups = mesh.shape["seq"], mesh.shape["batch"]

    def whole(*arrays):
        return per_device(*arrays, shards=shards, groups=groups)

    return jax.shard_map(whole, mesh=mesh, in_specs=in_specs, out_specs=out_specs, check_vma=False)
```

time: 49.7 us -> 64.5 us (1.30)
  waiting for transfers between devices: 12.2 us -> 25.1 us
  starting transfers between devices: 5.79 us -> 12.4 us
  blocking collectives: 21.8 us -> 17.4 us
  local copies, waits for them, and re-layouts: 3.84 us -> 0.04 us
  Pallas kernels: 4.24 us -> 7.58 us
    all_to_all x1 -> x3, waiting for transfers between devices: 9.31 us -> 25.1 us  [exchange(): lax.all_to_all(blocks, 'seq', split_axis=0, concat_axis=0, tiled=True)]
    all_to_all x1 -> x3, starting transfers between devices: 4.23 us -> 10.9 us  [exchange(): lax.all_to_all(blocks, 'seq', split_axis=0, concat_axis=0, tiled=True)]
    all_to_all x1, blocking collectives: 21.8 us -> 17.4 us  [exchange(): lax.all_to_all(blocks, 'seq', split_axis=0, concat_axis=0, tiled=True)]
    unnamed x24 -> x16, local copies, waits for them, and re-layouts: 3.83 us -> 0.04 us
    pallas_call x3 -> x6, Pallas kernels: 4.24 us -> 7.58 us  [call(): pl.pallas_call(kernel, out_shape=out_shape, scratch_shapes=scratch, compi...]
    ppermute x1, waiting for transfers between devices: 2.94 us -> 0.01 us  [per_device(): filter_grad = filter_grad + lax.ppermute(lag[step], 'batch', pairs)]
  transfers between devices with their start and end apart: 2 -> 4, of which waited for: 2 -> 3; matrix products, arithmetic and copies ran while one was open for 1% -> 1% of each run, Pallas kernels for 0% -> 4%
where the time goes in v2:
time: 64.5 us; the launch traced here: 63.9 us
  waiting for transfers between devices  25.1 us (39%)
  blocking collectives  17.4 us (27%)
  starting transfers between devices  12.4 us (19%)
  Pallas kernels  7.58 us (12%)
  between operations  0.77 us (1%)
    all_to_all x3, waiting for transfers between devices, exchange(): lax.all_to_all(blocks, 'seq', split_axis=0, concat_axis=0, tiled=True)  25.1 us
    all_to_all x1, blocking collectives, exchange(): lax.all_to_all(blocks, 'seq', split_axis=0, concat_axis=0, tiled=True)  17.4 us
    all_to_all x3, starting transfers between devices, exchange(): lax.all_to_all(blocks, 'seq', split_axis=0, concat_axis=0, tiled=True)  10.9 us
    pallas_call x6, Pallas kernels, call(): pl.pallas_call(kernel, out_shape=out_shape, scratch_shapes=scratch, compi...  7.58 us
    ppermute x1, starting transfers between devices, per_device(): filter_grad = filter_grad + lax.ppermute(lag[step], 'batch', pairs)  1.56 us
  transfers between devices with their start and end apart: 4, of which 3 were waited for; matrix products, arithmetic and copies ran while one was open for 1% of the time, Pallas kernels for 4%

profile of v2, /device:TPU:0, one launch (start us, length us, event | category | flops | bytes accessed | tf_op | source)
XLA Modules:
  0.0 63.9 jit_solution(13584629485350757112)
XLA Ops:
  0.6 2.2 %gate.1 = (f32[16,2,8,256]{3,2,1,0:T(8,128)S(1)}, f32[16,2,8,256]{3,2,1,0:T(8,128)}) custom-call(f32[2,256,128]{2,1,0:T(8,128)} %query_ref.1, f32[2,256,128]{2,1,0:T(8,128)} %key_ref.1, f32[2,256,128]{2,1,0:T(8,128)} %value_ref.1, f32[2,256,128]{2,1,0:T(8,128)} %cotangent_ref.1), custom_call_target="tpu_custom_call" | custom-call | flops 201326592 | bytes 262144 | tf_op jit(solution)/shard_map/gate/pallas_call | solution.py:304
  2.9 0.0 copy-start.7
  2.9 17.4 %all_to_all.20.held_ref = f32[16,2,8,256]{3,2,1,0:T(8,128)S(1)} all-to-all(f32[16,2,8,256]{3,2,1,0:T(8,128)S(1)} %get-tuple-element.17), channel_id=1, replica_groups=mesh['batch'=2,'seq'=16] {'seq'}, dimensions={0} | all-to-all | bytes 524288 | tf_op jit(solution)/shard_map/all_to_all | solution.py:288
  20.2 0.0 copy-start.4
  20.2 0.0 copy-start.5
  20.2 3.7 %all-to-all-start.2 = ((f32[16,2,8,256]{3,2,1,0:T(8,128)}), f32[16,2,8,256]{3,2,1,0:T(8,128)S(1)}, u32[]{:S(2)}, u32[]{:S(2)}) async-start(f32[16,2,8,256]{3,2,1,0:T(8,128)} %get-tuple-element.19), calls=%async_computation.2 | async-start | bytes 524288 | tf_op jit(solution)/shard_map/all_to_all | solution.py:288
  23.9 0.0 copy-done.7
  23.9 0.0 copy-done.4
  23.9 0.0 copy-done.5
  23.9 0.5 filter.1.filter_ref
  24.4 1.6 %convolve.1 = (f32[16,2,8,256]{3,2,1,0:T(8,128)}, f32[1,64,8,256]{3,2,1,0:T(8,128)S(1)}) custom-call(f32[16,2,8,256]{3,2,1,0:T(8,128)S(1)} %all_to_all.20.held_ref, f32[64,8,256]{2,1,0:T(8,128)S(1)} %filter.1.filter_ref, f32[64,256]{1,0:T(8,128)S(1)} %copy-done.5, bf16[768,256]{1,0:T(8,128)(2,1)S(1)} %copy-done.4), custom_call_target="tpu_custom_call" | custom-call | flops 805306368 | bytes 1048576 | tf_op jit(solution)/shard_map/convolve/pallas_call | solution.py:304
  26.1 7.9 %all-to-all-done.2.held_ref = f32[16,2,8,256]{3,2,1,0:T(8,128)S(1)} async-done(((f32[16,2,8,256]{3,2,1,0:T(8,128)}), f32[16,2,8,256]{3,2,1,0:T(8,128)S(1)}, u32[]{:S(2)}, u32[]{:S(2)}) %all-to-all-start.2) | async-done | bytes 262176 | tf_op jit(solution)/shard_map/all_to_all | solution.py:288
  33.9 1.6 %correlate.1 = (f32[16,2,8,256]{3,2,1,0:T(8,128)}, f32[1,64,8,256]{3,2,1,0:T(8,128)S(1)}) custom-call(f32[16,2,8,256]{3,2,1,0:T(8,128)S(1)} %all-to-all-done.2.held_ref, f32[64,8,256]{2,1,0:T(8,128)S(1)} %filter.1.filter_ref, f32[64,256]{1,0:T(8,128)S(1)} %copy-done.5, bf16[768,256]{1,0:T(8,128)(2,1)S(1)} %copy-done.4), custom_call_target="tpu_custom_call" | custom-call | flops 805306368 | bytes 1048576 | tf_op jit(solution)/shard_map/correlate/pallas_call | solution.py:304
  35.5 3.5 %all-to-all-start.3 = ((f32[16,2,8,256]{3,2,1,0:T(8,128)}), f32[16,2,8,256]{3,2,1,0:T(8,128)S(1)}, u32[]{:S(2)}, u32[]{:S(2)}) async-start(f32[16,2,8,256]{3,2,1,0:T(8,128)} %get-tuple-element.22), calls=%async_computation.3 | async-start | bytes 524288 | tf_op jit(solution)/shard_map/all_to_all | solution.py:288
  39.1 0.0 copy-start.3
  39.1 0.5 lags.1
  39.6 0.0 copy-start.2
  39.6 1.6 %collective-permute-start = (f32[8,2048]{1,0:T(8,128)S(1)}, f32[8,2048]{1,0:T(8,128)S(1)}, u32[]{:S(2)}, u32[]{:S(2)}) collective-permute-start(f32[8,2048]{1,0:T(8,128)S(1)} %slice_bitcast_fusion), channel_id=1, source_target_pairs={{0,16},{16,0},{1,17},{17,1},{2,18},{18,2},{3,19},{19,3},{4,20},{20... | collective-permute-start | bytes 196616 | tf_op jit(solution)/shard_map/ppermute | solution.py:358
  41.2 7.9 %all-to-all-done.3.back_ref = f32[16,2,8,256]{3,2,1,0:T(8,128)S(1)} async-done(((f32[16,2,8,256]{3,2,1,0:T(8,128)}), f32[16,2,8,256]{3,2,1,0:T(8,128)S(1)}, u32[]{:S(2)}, u32[]{:S(2)}) %all-to-all-start.3) | async-done | bytes 262176 | tf_op jit(solution)/shard_map/all_to_all | solution.py:288
  49.1 0.0 copy-start
  49.1 0.0 copy-start.1
  49.1 3.7 %all-to-all-start.1 = ((f32[16,2,8,256]{3,2,1,0:T(8,128)}), f32[16,2,8,256]{3,2,1,0:T(8,128)S(1)}, u32[]{:S(2)}, u32[]{:S(2)}) async-start(f32[16,2,8,256]{3,2,1,0:T(8,128)} %get-tuple-element.18), calls=%async_computation.1 | async-start | bytes 524288 | tf_op jit(solution)/shard_map/all_to_all | solution.py:288
  52.7 0.0 collective-permute-done
  52.8 0.6 fusion
  53.4 0.0 copy-start.6
  53.4 9.4 %all-to-all-done.1.convolved_ref = f32[16,2,8,256]{3,2,1,0:T(8,128)S(1)} async-done(((f32[16,2,8,256]{3,2,1,0:T(8,128)}), f32[16,2,8,256]{3,2,1,0:T(8,128)S(1)}, u32[]{:S(2)}, u32[]{:S(2)}) %all-to-all-start.1) | async-done | bytes 262176 | tf_op jit(solution)/shard_map/all_to_all | solution.py:288
  62.8 0.0 copy-done.3
  62.8 0.0 copy-done.2
  62.8 0.0 copy-done
  62.8 0.0 copy-done.1
  62.8 0.0 copy-done.6
  62.8 1.1 %outputs.1 = (f32[2,256,128]{2,1,0:T(8,128)}, f32[2,256,128]{2,1,0:T(8,128)}, f32[2,256,128]{2,1,0:T(8,128)}, f32[2,256,128]{2,1,0:T(8,128)}) custom-call(f32[2,256,128]{2,1,0:T(8,128)S(1)} %copy-done, f32[2,256,128]{2,1,0:T(8,128)S(1)} %copy-done.1, f32[2,256,128]{2,1,0:T(8,128)S(1)} %copy-done.2, f32[2,256,128]{2,1,0:T(8,128)S(1)} %copy-done.3, ...), custom_call_target="tpu_custom_call" | custom-call | flops 402653184 | bytes 524288 | tf_op jit(solution)/shard_map/outputs/pallas_call | solution.py:304
  (1 shorter events, 0.0 us)
Async XLA Ops:
  2.9 21.1 %copy-start.7 = (f32[8,4096]{1,0:T(8,128)S(1)}, f32[8,4096]{1,0:T(8,128)}, u32[]{:S(2)}) copy-start(f32[8,4096]{1,0:T(8,128)} %filter_ref.1) | copy-start | bytes 393220
  20.2 3.7 %copy-start.4 = (bf16[768,256]{1,0:T(8,128)(2,1)S(1)}, bf16[768,256]{1,0:T(8,128)(2,1)}, u32[]{:S(2)}) copy-start(bf16[768,256]{1,0:T(8,128)(2,1)} %constant.5.clone.matrix_ref) | copy-start | bytes 1179652
  20.2 3.7 %copy-start.5 = (f32[64,256]{1,0:T(8,128)S(1)}, f32[64,256]{1,0:T(8,128)}, u32[]{:S(2)}) copy-start(f32[64,256]{1,0:T(8,128)} %constant.4.clone.twist_ref) | copy-start | bytes 196612
  20.2 13.7 %all-to-all-start.2 = ((f32[16,2,8,256]{3,2,1,0:T(8,128)}), f32[16,2,8,256]{3,2,1,0:T(8,128)S(1)}, u32[]{:S(2)}, u32[]{:S(2)}) async-start(f32[16,2,8,256]{3,2,1,0:T(8,128)} %get-tuple-element.19), calls=%async_computation.2 | async-start | bytes 524288 | tf_op jit(solution)/shard_map/all_to_all | solution.py:288
  35.5 13.5 %all-to-all-start.3 = ((f32[16,2,8,256]{3,2,1,0:T(8,128)}), f32[16,2,8,256]{3,2,1,0:T(8,128)S(1)}, u32[]{:S(2)}, u32[]{:S(2)}) async-start(f32[16,2,8,256]{3,2,1,0:T(8,128)} %get-tuple-element.22), calls=%async_computation.3 | async-start | bytes 524288 | tf_op jit(solution)/shard_map/all_to_all | solution.py:288
  39.1 23.7 %copy-start.3 = (f32[2,256,128]{2,1,0:T(8,128)S(1)}, f32[2,256,128]{2,1,0:T(8,128)}, u32[]{:S(2)}) copy-start(f32[2,256,128]{2,1,0:T(8,128)} %cotangent_ref.1) | copy-start | bytes 786436
  39.6 23.2 %copy-start.2 = (f32[2,256,128]{2,1,0:T(8,128)S(1)}, f32[2,256,128]{2,1,0:T(8,128)}, u32[]{:S(2)}) copy-start(f32[2,256,128]{2,1,0:T(8,128)} %value_ref.1) | copy-start | bytes 786436
  39.6 13.1 %collective-permute-start = (f32[8,2048]{1,0:T(8,128)S(1)}, f32[8,2048]{1,0:T(8,128)S(1)}, u32[]{:S(2)}, u32[]{:S(2)}) collective-permute-start(f32[8,2048]{1,0:T(8,128)S(1)} %slice_bitcast_fusion), channel_id=1, source_target_pairs={{0,16},{16,0},{1,17},{17,1},{2,18},{18,2},{3,19},{19,3},{4,20},{20... | collective-permute-start | bytes 196616 | tf_op jit(solution)/shard_map/ppermute | solution.py:358
  49.1 13.7 %copy-start = (f32[2,256,128]{2,1,0:T(8,128)S(1)}, f32[2,256,128]{2,1,0:T(8,128)}, u32[]{:S(2)}) copy-start(f32[2,256,128]{2,1,0:T(8,128)} %query_ref.1) | copy-start | bytes 786436
  49.1 13.7 %copy-start.1 = (f32[2,256,128]{2,1,0:T(8,128)S(1)}, f32[2,256,128]{2,1,0:T(8,128)}, u32[]{:S(2)}) copy-start(f32[2,256,128]{2,1,0:T(8,128)} %key_ref.1) | copy-start | bytes 786436
  49.1 13.7 %all-to-all-start.1 = ((f32[16,2,8,256]{3,2,1,0:T(8,128)}), f32[16,2,8,256]{3,2,1,0:T(8,128)S(1)}, u32[]{:S(2)}, u32[]{:S(2)}) async-start(f32[16,2,8,256]{3,2,1,0:T(8,128)} %get-tuple-element.18), calls=%async_computation.1 | async-start | bytes 524288 | tf_op jit(solution)/shard_map/all_to_all | solution.py:288
  53.4 9.4 %copy-start.6 = (f32[128]{0:T(128)S(1)}, f32[128]{0:T(128)}, u32[]{:S(2)}) copy-start(f32[128]{0:T(128)} %param.12) | copy-start | bytes 1540

commit v3 on v2

--- a/solution.py
+++ b/solution.py
@@ -134,8 +134,13 @@
     )
 
 
-def gate_kernel(query_hbm, key_hbm, value_hbm, cotangent_hbm, mixed_ref, upstream_ref, held, sems):
-    shards, batch, channels, tokens = mixed_ref.shape
+def reversed_order(shards):
+    width = shards.bit_length() - 1
+    return [int(format(place, f"0{width}b")[::-1], 2) if width else 0 for place in range(shards)]
+
+
+def gate_kernel(order, query_hbm, key_hbm, value_hbm, cotangent_hbm, sent_ref, held, sems):
+    shards, _, batch, channels, tokens = sent_ref.shape
     sources = (key_hbm, value_hbm, cotangent_hbm, query_hbm)
 
     def copy(b, i):
@@ -144,12 +149,14 @@
     for i in range(4):
         for b in range(batch):
             copy(b, i).start()
-    for kind, sent in enumerate((mixed_ref, upstream_ref)):
+    for kind in range(2):
         for b in range(batch):
             copy(b, 2 * kind).wait()
             copy(b, 2 * kind + 1).wait()
-            product = held[2 * kind, b] * held[2 * kind + 1, b]
-            sent[:, b] = jnp.transpose(product).reshape(shards, channels, tokens)
+            columns = jnp.transpose(held[2 * kind, b] * held[2 * kind + 1, b])
+            for place, shard in enumerate(order):
+                rows = columns[shard * channels : (shard + 1) * channels]
+                sent_ref[place, kind, b] = rows
 
 
 def transforms(twist_ref, matrix_ref, middle, turned):
@@ -199,23 +206,23 @@
     return forward, inverse
 
 
-def token_blocks(ref, lanes, pair, live):
-    pieces = ref.shape[3] // lanes
+def token_blocks(ref, order, kind, lanes, pair, live):
+    pieces = ref.shape[4] // lanes
 
     def where(n1):
         at = n1 % pieces * lanes
-        return n1 // pieces, slice(at, at + lanes)
+        return order.index(n1 // pieces), slice(at, at + lanes)
 
     def load(n1):
         if n1 >= live:
             return None
-        shard, span = where(n1)
-        return (ref[shard, 2 * pair, :, span], ref[shard, 2 * pair + 1, :, span])
+        place, span = where(n1)
+        return (ref[place, kind, 2 * pair, :, span], ref[place, kind, 2 * pair + 1, :, span])
 
     def emit(n1, value):
-        shard, span = where(n1)
-        ref[shard, 2 * pair, :, span] = value[0]
-        ref[shard, 2 * pair + 1, :, span] = -value[1]
+        place, span = where(n1)
+        ref[place, kind, 2 * pair, :, span] = value[0]
+        ref[place, kind, 2 * pair + 1, :, span] = -value[1]
 
     return load, emit
 
@@ -234,15 +241,16 @@
 
 
 def convolve_kernel(
-    conjugate, held_ref, filter_ref, twist_ref, matrix_ref, back_ref, spec_ref, middle, turned
+    order, held_ref, filter_ref, twist_ref, matrix_ref, back_ref, mixed_ref, upstream_ref, middle, turned
 ):
     count, width = twist_ref.shape
     forward, inverse = transforms(twist_ref, matrix_ref, middle, turned)
-    for pair in range(spec_ref.shape[0]):
-        load, _ = token_blocks(held_ref, width // 2, pair, count // 2)
-        _, emit = token_blocks(back_ref, width // 2, pair, count // 2)
-        forward(load, spec_ref.at[pair])
-        inverse(filter_ref, spec_ref.at[pair], conjugate, emit)
+    for kind, spec_ref in enumerate((mixed_ref, upstream_ref)):
+        for pair in range(spec_ref.shape[0]):
+            load, _ = token_blocks(held_ref, order, kind, width // 2, pair, count // 2)
+            _, emit = token_blocks(back_ref, order, kind, width // 2, pair, count // 2)
+            forward(load, spec_ref.at[pair])
+            inverse(filter_ref, spec_ref.at[pair], kind == 1, emit)
 
 
 def lag_kernel(scaling, mixed_ref, upstream_ref, twist_ref, matrix_ref, lag_ref, middle, turned):
@@ -265,27 +273,24 @@
 
 
 def output_kernel(
-    query_ref, key_ref, value_ref, cotangent_ref, skip_ref, convolved_ref, back_ref,
+    order, query_ref, key_ref, value_ref, cotangent_ref, skip_ref, home_ref,
     output_ref, query_grad_ref, key_grad_ref, value_grad_ref,
 ):
-    shards, batch, channels, tokens = convolved_ref.shape
+    shards, _, batch, _, _ = home_ref.shape
     skip = skip_ref[...]
 
-    def rows(ref, b):
-        return jnp.transpose(ref[:, b].reshape(shards * channels, tokens))
+    def rows(kind, b):
+        blocks = [home_ref[order.index(shard), kind, b] for shard in range(shards)]
+        return jnp.transpose(jnp.concatenate(blocks, axis=0))
 
     for b in range(batch):
         query, key, value, cotangent = query_ref[b], key_ref[b], value_ref[b], cotangent_ref[b]
-        hidden = rows(convolved_ref, b) + skip * (key * value)
+        hidden = rows(0, b) + skip * (key * value)
         output_ref[b] = query * hidden
         query_grad_ref[b] = cotangent * hidden
-        mixed_grad = rows(back_ref, b) + skip * (cotangent * query)
+        mixed_grad = rows(1, b) + skip * (cotangent * query)
         key_grad_ref[b] = mixed_grad * value
         value_grad_ref[b] = mixed_grad * key
-
-
-def exchange(blocks):
-    return lax.all_to_all(blocks, "seq", split_axis=0, concat_axis=0, tiled=True)
 
 
 def per_device(query_gate, key_gate, value_input, filters, skip_gain, cotangent, *, shards, groups):
@@ -294,7 +299,7 @@
     lanes = 128 if 2 * length // 128 <= 64 else tokens
     count = 2 * length // lanes
     twist, matrix = tables(count, lanes)
-
+    order = reversed_order(shards)
     lane_work = 2 * 3 * count * channels * (2 * lanes) ** 2
 
     def of(*shape):
@@ -314,13 +319,17 @@
             **options,
         )(*arrays)
 
-    swap = of(shards, batch, channels, tokens)
+    def exchange(blocks):
+        return lax.all_to_all(
+            blocks, "seq", split_axis=0, concat_axis=0, tiled=True, axis_index_groups=[order]
+        )
+
+    swap = of(shards, 2, batch, channels, tokens)
     spectrum = of(batch // 2, count, channels, 2 * lanes)
     work = [pltpu.VMEM((count, channels, 2 * lanes), jnp.float32)] * 2
-    mixed, upstream = call(
-        gate_kernel,
-        "gate", 1,
-        (swap, swap),
+    sent = call(
+        functools.partial(gate_kernel, order),
+        "gate", 1, swap,
         [
             pltpu.VMEM((4, batch, tokens, all_channels), jnp.float32),
             pltpu.SemaphoreType.DMA((4, batch)),
@@ -331,22 +340,15 @@
         ),
         in_specs=[pl.BlockSpec(memory_space=pltpu.HBM)] * 4,
     )
-    mixed = exchange(mixed)
-    upstream = exchange(upstream)
+    held = exchange(sent)
     filter_spec = call(
         filter_kernel, "filter", 2, of(count, channels, 2 * lanes), work, filters, twist, matrix
     )
-    convolved, mixed_spec = call(
-        functools.partial(convolve_kernel, False),
-        "convolve", 4, (swap, spectrum), work, mixed, filter_spec, twist, matrix,
-    )
-    convolved = exchange(convolved)
-    filter_spec, mixed_spec = lax.optimization_barrier((filter_spec, mixed_spec))
-    back, upstream_spec = call(
-        functools.partial(convolve_kernel, True),
-        "correlate", 4, (swap, spectrum), work, upstream, filter_spec, twist, matrix,
-    )
-    back = exchange(back)
+    back, mixed_spec, upstream_spec = call(
+        functools.partial(convolve_kernel, order),
+        "convolve", 8, (swap, spectrum, spectrum), work, held, filter_spec, twist, matrix,
+    )
+    home = exchange(back)
     lag = call(
         functools.partial(lag_kernel, 1.0 / (2.0 * length * math.sqrt(length))),
         "lags", 2, of(groups, channels, length // groups), work,
@@ -357,10 +359,10 @@
         pairs = [(source, (source + step) % groups) for source in range(groups)]
         filter_grad = filter_grad + lax.ppermute(lag[step], "batch", pairs)
     output, query_grad, key_grad, value_grad = call(
-        output_kernel,
+        functools.partial(output_kernel, order),
         "outputs", 2, (of(*query_gate.shape),) * 4, [],
         query_gate, key_gate, value_input, cotangent, skip_gain.reshape(1, all_channels),
-        convolved, back,
+        home,
     )
     return (output, query_grad, key_grad, value_grad, filter_grad)
 

time: 64.5 us -> 48.5 us (0.75)
  blocking collectives: 17.4 us -> 0 us
  waiting for transfers between devices: 25.1 us -> 27.1 us
    all_to_all x1 -> x0, blocking collectives: 17.4 us -> none  [exchange(): lax.all_to_all(blocks, 'seq', split_axis=0, concat_axis=0, tiled=True)]
    ppermute x1, waiting for transfers between devices: 0.01 us -> 2.83 us  [per_device(): filter_grad = filter_grad + lax.ppermute(lag[step], 'batch', pairs)]
    all_to_all x3 -> x2, waiting for transfers between devices: 25.1 us -> 24.3 us  [exchange(): lax.all_to_all(blocks, 'seq', split_axis=0, concat_axis=0, tiled=True, ax...]
    pallas_call x6 -> x5, Pallas kernels: 7.58 us -> 6.94 us  [call(): pl.pallas_call(kernel, out_shape=out_shape, scratch_shapes=scratch, compi...]
    all_to_all x3 -> x2, starting transfers between devices: 10.9 us -> 11.1 us  [exchange(): lax.all_to_all(blocks, 'seq', split_axis=0, concat_axis=0, tiled=True, ax...]
  transfers between devices with their start and end apart: 4 -> 3, of which waited for: 3 -> 3; matrix products, arithmetic and copies ran while one was open for 1% -> 1% of each run, Pallas kernels for 4% -> 2%
where the time goes in v3:
time: 48.5 us; the launch traced here: 48.2 us
  waiting for transfers between devices  27.1 us (56%)
  starting transfers between devices  12.7 us (26%)
  Pallas kernels  6.94 us (14%)
  between operations  0.78 us (2%)
  other arithmetic  0.64 us (1%)
    all_to_all x2, waiting for transfers between devices, exchange(): lax.all_to_all(blocks, 'seq', split_axis=0, concat_axis=0, tiled=True, ax...  24.3 us
    all_to_all x2, starting transfers between devices, exchange(): lax.all_to_all(blocks, 'seq', split_axis=0, concat_axis=0, tiled=True, ax...  11.1 us
    pallas_call x5, Pallas kernels, call(): pl.pallas_call(kernel, out_shape=out_shape, scratch_shapes=scratch, compi...  6.94 us
    ppermute x1, waiting for transfers between devices, per_device(): filter_grad = filter_grad + lax.ppermute(lag[step], 'batch', pairs)  2.83 us
    ppermute x1, starting transfers between devices, per_device(): filter_grad = filter_grad + lax.ppermute(lag[step], 'batch', pairs)  1.57 us
  transfers between devices with their start and end apart: 3, of which 3 were waited for; matrix products, arithmetic and copies ran while one was open for 1% of the time, Pallas kernels for 2%

profile of v3, /device:TPU:0, one launch (start us, length us, event | category | flops | bytes accessed | tf_op | source)
XLA Modules:
  0.0 48.2 jit_solution(4192591972308613041)
XLA Ops:
  0.6 2.3 %gate.1 = f32[16,2,2,8,256]{4,3,2,1,0:T(8,128)} custom-call(f32[2,256,128]{2,1,0:T(8,128)} %query_ref.1, f32[2,256,128]{2,1,0:T(8,128)} %key_ref.1, f32[2,256,128]{2,1,0:T(8,128)} %value_ref.1, f32[2,256,128]{2,1,0:T(8,128)} %cotangent_ref.1), custom_call_target="tpu_custom_call" | custom-call | flops 201326592 | bytes 262144 | tf_op jit(solution)/shard_map/gate/pallas_call | solution.py:309
  3.0 0.0 copy-start.4
  3.0 0.0 copy-start.5
  3.0 0.0 copy-start.7
  3.0 7.5 %all-to-all-start = ((f32[16,2,2,8,256]{4,3,2,1,0:T(8,128)}), f32[16,2,2,8,256]{4,3,2,1,0:T(8,128)S(1)}, u32[]{:S(2)}, u32[]{:S(2)}) async-start(f32[16,2,2,8,256]{4,3,2,1,0:T(8,128)} %gate.1), calls=%async_computation | async-start | bytes 1048576 | tf_op jit(solution)/shard_map/all_to_all | solution.py:323
  10.5 0.0 copy-done.4
  10.5 0.0 copy-done.5
  10.5 0.0 copy-done.7
  10.6 0.5 %filter.1.filter_ref = f32[64,8,256]{2,1,0:T(8,128)S(1)} custom-call(f32[8,4096]{1,0:T(8,128)S(1)} %copy-done.7, f32[64,256]{1,0:T(8,128)S(1)} %copy-done.5, bf16[768,256]{1,0:T(8,128)(2,1)S(1)} %copy-done.4), custom_call_target="tpu_custom_call" | custom-call | flops 402653184 | bytes 524288 | tf_op jit(solution)/shard_map/filter/pallas_call | solution.py:309
  11.1 14.7 %all-to-all-done.held_ref = f32[16,2,2,8,256]{4,3,2,1,0:T(8,128)S(1)} async-done(((f32[16,2,2,8,256]{4,3,2,1,0:T(8,128)}), f32[16,2,2,8,256]{4,3,2,1,0:T(8,128)S(1)}, u32[]{:S(2)}, u32[]{:S(2)}) %all-to-all-start) | async-done | bytes 524320 | tf_op jit(solution)/shard_map/all_to_all | solution.py:323
  25.8 2.5 %convolve.1 = (f32[16,2,2,8,256]{4,3,2,1,0:T(8,128)}, f32[1,64,8,256]{3,2,1,0:T(8,128)S(1)}, f32[1,64,8,256]{3,2,1,0:T(8,128)S(1)}) custom-call(f32[16,2,2,8,256]{4,3,2,1,0:T(8,128)S(1)} %all-to-all-done.held_ref, f32[64,8,256]{2,1,0:T(8,128)S(1)} %filter.1.filter_ref, f32[64,256]{1,0:T(8,128)S(1)} %copy-done.5, bf16[768,256]{1,0:T(8,128)(2,1)S(1)} %copy-done.4), custom_call_target="tpu_custom_call" | custom-call | flops 1610612736 | bytes 2097152 | tf_op jit(solution)/shard_map/convolve/pallas_call | solution.py:309
  28.3 3.6 %all-to-all-start.1 = ((f32[16,2,2,8,256]{4,3,2,1,0:T(8,128)}), f32[16,2,2,8,256]{4,3,2,1,0:T(8,128)S(1)}, u32[]{:S(2)}, u32[]{:S(2)}) async-start(f32[16,2,2,8,256]{4,3,2,1,0:T(8,128)} %get-tuple-element.12), calls=%async_computation.1 | async-start | bytes 1048576 | tf_op jit(solution)/shard_map/all_to_all | solution.py:323
  31.8 0.0 copy-start.1
  31.8 0.0 copy-start.2
  31.9 0.0 copy-start.3
  31.9 0.5 %lags.1 = f32[2,8,2048]{2,1,0:T(8,128)S(1)} custom-call(f32[1,64,8,256]{3,2,1,0:T(8,128)S(1)} %get-tuple-element.17.mixed_ref, f32[1,64,8,256]{3,2,1,0:T(8,128)S(1)} %get-tuple-element.18.upstream_ref, f32[64,256]{1,0:T(8,128)S(1)} %copy-done.5, bf16[768,256]{1,0:T(8,128)(2,1)S(1)} %copy-done.4), custom_call_target="tpu_custom_call" | custom-call | flops 402653184 | bytes 524288 | tf_op jit(solution)/shard_map/lags/pallas_call | solution.py:309
  32.4 0.0 copy-start
  32.4 1.6 %collective-permute-start = (f32[8,2048]{1,0:T(8,128)S(1)}, f32[8,2048]{1,0:T(8,128)S(1)}, u32[]{:S(2)}, u32[]{:S(2)}) collective-permute-start(f32[8,2048]{1,0:T(8,128)S(1)} %slice_bitcast_fusion), channel_id=1, source_target_pairs={{0,16},{16,0},{1,17},{17,1},{2,18},{18,2},{3,19},{19,3},{4,20},{20... | collective-permute-start | bytes 196616 | tf_op jit(solution)/shard_map/ppermute | solution.py:360
  34.0 2.8 %collective-permute-done = f32[8,2048]{1,0:T(8,128)S(1)} collective-permute-done((f32[8,2048]{1,0:T(8,128)S(1)}, f32[8,2048]{1,0:T(8,128)S(1)}, u32[]{:S(2)}, u32[]{:S(2)}) %collective-permute-start) | collective-permute-done | bytes 65568 | tf_op jit(solution)/shard_map/ppermute | solution.py:360
  36.8 0.6 %fusion = f32[8,2048]{1,0:T(8,128)} fusion(f32[8,2048]{1,0:T(8,128)S(1)} %collective-permute-done, f32[2,8,2048]{2,1,0:T(8,128)S(1)} %lags.1), kind=kLoop, calls=%fused_computation.2 | loop fusion | flops 16384 | bytes 196608 | tf_op jit(solution)/shard_map/add | solution.py:360
  37.5 0.0 copy-start.6
  37.5 9.5 %all-to-all-done.1.home_ref = f32[16,2,2,8,256]{4,3,2,1,0:T(8,128)S(1)} async-done(((f32[16,2,2,8,256]{4,3,2,1,0:T(8,128)}), f32[16,2,2,8,256]{4,3,2,1,0:T(8,128)S(1)}, u32[]{:S(2)}, u32[]{:S(2)}) %all-to-all-start.1) | async-done | bytes 524320 | tf_op jit(solution)/shard_map/all_to_all | solution.py:323
  47.0 0.0 copy-done.1
  47.0 0.0 copy-done.2
  47.0 0.0 copy-done.3
  47.0 0.0 copy-done
  47.0 0.0 copy-done.6
  47.0 1.1 %outputs.1 = (f32[2,256,128]{2,1,0:T(8,128)}, f32[2,256,128]{2,1,0:T(8,128)}, f32[2,256,128]{2,1,0:T(8,128)}, f32[2,256,128]{2,1,0:T(8,128)}) custom-call(f32[2,256,128]{2,1,0:T(8,128)S(1)} %copy-done, f32[2,256,128]{2,1,0:T(8,128)S(1)} %copy-done.1, f32[2,256,128]{2,1,0:T(8,128)S(1)} %copy-done.2, f32[2,256,128]{2,1,0:T(8,128)S(1)} %copy-done.3, ...), custom_call_target="tpu_custom_call" | custom-call | flops 402653184 | bytes 524288 | tf_op jit(solution)/shard_map/outputs/pallas_call | solution.py:309
  (1 shorter events, 0.0 us)
Async XLA Ops:
  3.0 7.6 %copy-start.4 = (bf16[768,256]{1,0:T(8,128)(2,1)S(1)}, bf16[768,256]{1,0:T(8,128)(2,1)}, u32[]{:S(2)}) copy-start(bf16[768,256]{1,0:T(8,128)(2,1)} %constant.5.clone.matrix_ref) | copy-start | bytes 1179652
  3.0 7.6 %copy-start.5 = (f32[64,256]{1,0:T(8,128)S(1)}, f32[64,256]{1,0:T(8,128)}, u32[]{:S(2)}) copy-start(f32[64,256]{1,0:T(8,128)} %constant.4.clone.twist_ref) | copy-start | bytes 196612
  3.0 7.6 %copy-start.7 = (f32[8,4096]{1,0:T(8,128)S(1)}, f32[8,4096]{1,0:T(8,128)}, u32[]{:S(2)}) copy-start(f32[8,4096]{1,0:T(8,128)} %filter_ref.1) | copy-start | bytes 393220
  3.0 22.8 %all-to-all-start = ((f32[16,2,2,8,256]{4,3,2,1,0:T(8,128)}), f32[16,2,2,8,256]{4,3,2,1,0:T(8,128)S(1)}, u32[]{:S(2)}, u32[]{:S(2)}) async-start(f32[16,2,2,8,256]{4,3,2,1,0:T(8,128)} %gate.1), calls=%async_computation | async-start | bytes 1048576 | tf_op jit(solution)/shard_map/all_to_all | solution.py:323
  28.3 18.7 %all-to-all-start.1 = ((f32[16,2,2,8,256]{4,3,2,1,0:T(8,128)}), f32[16,2,2,8,256]{4,3,2,1,0:T(8,128)S(1)}, u32[]{:S(2)}, u32[]{:S(2)}) async-start(f32[16,2,2,8,256]{4,3,2,1,0:T(8,128)} %get-tuple-element.12), calls=%async_computation.1 | async-start | bytes 1048576 | tf_op jit(solution)/shard_map/all_to_all | solution.py:323
  31.8 15.2 %copy-start.1 = (f32[2,256,128]{2,1,0:T(8,128)S(1)}, f32[2,256,128]{2,1,0:T(8,128)}, u32[]{:S(2)}) copy-start(f32[2,256,128]{2,1,0:T(8,128)} %key_ref.1) | copy-start | bytes 786436
  31.8 15.2 %copy-start.2 = (f32[2,256,128]{2,1,0:T(8,128)S(1)}, f32[2,256,128]{2,1,0:T(8,128)}, u32[]{:S(2)}) copy-start(f32[2,256,128]{2,1,0:T(8,128)} %value_ref.1) | copy-start | bytes 786436
  31.9 15.1 %copy-start.3 = (f32[2,256,128]{2,1,0:T(8,128)S(1)}, f32[2,256,128]{2,1,0:T(8,128)}, u32[]{:S(2)}) copy-start(f32[2,256,128]{2,1,0:T(8,128)} %cotangent_ref.1) | copy-start | bytes 786436
  32.4 14.6 %copy-start = (f32[2,256,128]{2,1,0:T(8,128)S(1)}, f32[2,256,128]{2,1,0:T(8,128)}, u32[]{:S(2)}) copy-start(f32[2,256,128]{2,1,0:T(8,128)} %query_ref.1) | copy-start | bytes 786436
  32.4 4.4 %collective-permute-start = (f32[8,2048]{1,0:T(8,128)S(1)}, f32[8,2048]{1,0:T(8,128)S(1)}, u32[]{:S(2)}, u32[]{:S(2)}) collective-permute-start(f32[8,2048]{1,0:T(8,128)S(1)} %slice_bitcast_fusion), channel_id=1, source_target_pairs={{0,16},{16,0},{1,17},{17,1},{2,18},{18,2},{3,19},{19,3},{4,20},{20... | collective-permute-start | bytes 196616 | tf_op jit(solution)/shard_map/ppermute | solution.py:360
  37.5 9.6 %copy-start.6 = (f32[128]{0:T(128)S(1)}, f32[128]{0:T(128)}, u32[]{:S(2)}) copy-start(f32[128]{0:T(128)} %param.12) | copy-start | bytes 1540

commit v4 on v3

--- a/solution.py
+++ b/solution.py
@@ -134,9 +134,8 @@
     )
 
 
-def reversed_order(shards):
-    width = shards.bit_length() - 1
-    return [int(format(place, f"0{width}b")[::-1], 2) if width else 0 for place in range(shards)]
+def spread_order(shards):
+    return [5 * place % shards for place in range(shards)]
 
 
 def gate_kernel(order, query_hbm, key_hbm, value_hbm, cotangent_hbm, sent_ref, held, sems):
@@ -299,7 +298,7 @@
     lanes = 128 if 2 * length // 128 <= 64 else tokens
     count = 2 * length // lanes
     twist, matrix = tables(count, lanes)
-    order = reversed_order(shards)
+    order = spread_order(shards)
     lane_work = 2 * 3 * count * channels * (2 * lanes) ** 2
 
     def of(*shape):

time: 48.5 us -> 48.1 us (level)
  the two profiles are of different devices: /device:TPU:0 before, /device:TPU:1 now
where the time goes in v4:
time: 48.1 us; the launch traced here: 47.7 us
  waiting for transfers between devices  26.2 us (54%)
  starting transfers between devices  13.1 us (27%)
  Pallas kernels  6.94 us (14%)
  between operations  0.76 us (2%)
  other arithmetic  0.64 us (1%)
    all_to_all x2, waiting for transfers between devices, exchange(): lax.all_to_all(blocks, 'seq', split_axis=0, concat_axis=0, tiled=True, ax...  23.8 us
    all_to_all x2, starting transfers between devices, exchange(): lax.all_to_all(blocks, 'seq', split_axis=0, concat_axis=0, tiled=True, ax...  11.8 us
    pallas_call x5, Pallas kernels, call(): pl.pallas_call(kernel, out_shape=out_shape, scratch_shapes=scratch, compi...  6.94 us
    ppermute x1, waiting for transfers between devices, per_device(): filter_grad = filter_grad + lax.ppermute(lag[step], 'batch', pairs)  2.43 us
    ppermute x1, starting transfers between devices, per_device(): filter_grad = filter_grad + lax.ppermute(lag[step], 'batch', pairs)  1.29 us
  transfers between devices with their start and end apart: 3, of which 3 were waited for; matrix products, arithmetic and copies ran while one was open for 1% of the time, Pallas kernels for 2%

profile of v4, /device:TPU:1, one launch (start us, length us, event | category | flops | bytes accessed | tf_op | source)
XLA Modules:
  0.0 47.7 jit_solution(16657921497903564613)
XLA Ops:
  0.6 2.3 %gate.1 = f32[16,2,2,8,256]{4,3,2,1,0:T(8,128)} custom-call(f32[2,256,128]{2,1,0:T(8,128)} %query_ref.1, f32[2,256,128]{2,1,0:T(8,128)} %key_ref.1, f32[2,256,128]{2,1,0:T(8,128)} %value_ref.1, f32[2,256,128]{2,1,0:T(8,128)} %cotangent_ref.1), custom_call_target="tpu_custom_call" | custom-call | flops 201326592 | bytes 262144 | tf_op jit(solution)/shard_map/gate/pallas_call | solution.py:308
  3.0 0.0 copy-start.4
  3.0 0.0 copy-start.5
  3.0 0.0 copy-start.7
  3.0 7.5 %all-to-all-start = ((f32[16,2,2,8,256]{4,3,2,1,0:T(8,128)}), f32[16,2,2,8,256]{4,3,2,1,0:T(8,128)S(1)}, u32[]{:S(2)}, u32[]{:S(2)}) async-start(f32[16,2,2,8,256]{4,3,2,1,0:T(8,128)} %gate.1), calls=%async_computation | async-start | bytes 1048576 | tf_op jit(solution)/shard_map/all_to_all | solution.py:322
  10.5 0.0 copy-done.4
  10.5 0.0 copy-done.5
  10.5 0.0 copy-done.7
  10.5 0.5 %filter.1.filter_ref = f32[64,8,256]{2,1,0:T(8,128)S(1)} custom-call(f32[8,4096]{1,0:T(8,128)S(1)} %copy-done.7, f32[64,256]{1,0:T(8,128)S(1)} %copy-done.5, bf16[768,256]{1,0:T(8,128)(2,1)S(1)} %copy-done.4), custom_call_target="tpu_custom_call" | custom-call | flops 402653184 | bytes 524288 | tf_op jit(solution)/shard_map/filter/pallas_call | solution.py:308
  11.0 14.1 %all-to-all-done.held_ref = f32[16,2,2,8,256]{4,3,2,1,0:T(8,128)S(1)} async-done(((f32[16,2,2,8,256]{4,3,2,1,0:T(8,128)}), f32[16,2,2,8,256]{4,3,2,1,0:T(8,128)S(1)}, u32[]{:S(2)}, u32[]{:S(2)}) %all-to-all-start) | async-done | bytes 524320 | tf_op jit(solution)/shard_map/all_to_all | solution.py:322
  25.1 2.5 %convolve.1 = (f32[16,2,2,8,256]{4,3,2,1,0:T(8,128)}, f32[1,64,8,256]{3,2,1,0:T(8,128)S(1)}, f32[1,64,8,256]{3,2,1,0:T(8,128)S(1)}) custom-call(f32[16,2,2,8,256]{4,3,2,1,0:T(8,128)S(1)} %all-to-all-done.held_ref, f32[64,8,256]{2,1,0:T(8,128)S(1)} %filter.1.filter_ref, f32[64,256]{1,0:T(8,128)S(1)} %copy-done.5, bf16[768,256]{1,0:T(8,128)(2,1)S(1)} %copy-done.4), custom_call_target="tpu_custom_call" | custom-call | flops 1610612736 | bytes 2097152 | tf_op jit(solution)/shard_map/convolve/pallas_call | solution.py:308
  27.6 4.3 %all-to-all-start.1 = ((f32[16,2,2,8,256]{4,3,2,1,0:T(8,128)}), f32[16,2,2,8,256]{4,3,2,1,0:T(8,128)S(1)}, u32[]{:S(2)}, u32[]{:S(2)}) async-start(f32[16,2,2,8,256]{4,3,2,1,0:T(8,128)} %get-tuple-element.12), calls=%async_computation.1 | async-start | bytes 1048576 | tf_op jit(solution)/shard_map/all_to_all | solution.py:322
  31.9 0.0 copy-start.1
  31.9 0.0 copy-start.2
  32.0 0.0 copy-start.3
  32.0 0.5 %lags.1 = f32[2,8,2048]{2,1,0:T(8,128)S(1)} custom-call(f32[1,64,8,256]{3,2,1,0:T(8,128)S(1)} %get-tuple-element.17.mixed_ref, f32[1,64,8,256]{3,2,1,0:T(8,128)S(1)} %get-tuple-element.18.upstream_ref, f32[64,256]{1,0:T(8,128)S(1)} %copy-done.5, bf16[768,256]{1,0:T(8,128)(2,1)S(1)} %copy-done.4), custom_call_target="tpu_custom_call" | custom-call | flops 402653184 | bytes 524288 | tf_op jit(solution)/shard_map/lags/pallas_call | solution.py:308
  32.5 0.0 copy-start
  32.5 1.3 %collective-permute-start = (f32[8,2048]{1,0:T(8,128)S(1)}, f32[8,2048]{1,0:T(8,128)S(1)}, u32[]{:S(2)}, u32[]{:S(2)}) collective-permute-start(f32[8,2048]{1,0:T(8,128)S(1)} %slice_bitcast_fusion), channel_id=1, source_target_pairs={{0,16},{16,0},{1,17},{17,1},{2,18},{18,2},{3,19},{19,3},{4,20},{20... | collective-permute-start | bytes 196616 | tf_op jit(solution)/shard_map/ppermute | solution.py:359
  33.8 2.4 %collective-permute-done = f32[8,2048]{1,0:T(8,128)S(1)} collective-permute-done((f32[8,2048]{1,0:T(8,128)S(1)}, f32[8,2048]{1,0:T(8,128)S(1)}, u32[]{:S(2)}, u32[]{:S(2)}) %collective-permute-start) | collective-permute-done | bytes 65568 | tf_op jit(solution)/shard_map/ppermute | solution.py:359
  36.2 0.6 %fusion = f32[8,2048]{1,0:T(8,128)} fusion(f32[8,2048]{1,0:T(8,128)S(1)} %collective-permute-done, f32[2,8,2048]{2,1,0:T(8,128)S(1)} %lags.1), kind=kLoop, calls=%fused_computation.2 | loop fusion | flops 16384 | bytes 196608 | tf_op jit(solution)/shard_map/add | solution.py:359
  36.9 0.0 copy-start.6
  36.9 9.7 %all-to-all-done.1.home_ref = f32[16,2,2,8,256]{4,3,2,1,0:T(8,128)S(1)} async-done(((f32[16,2,2,8,256]{4,3,2,1,0:T(8,128)}), f32[16,2,2,8,256]{4,3,2,1,0:T(8,128)S(1)}, u32[]{:S(2)}, u32[]{:S(2)}) %all-to-all-start.1) | async-done | bytes 524320 | tf_op jit(solution)/shard_map/all_to_all | solution.py:322
  46.6 0.0 copy-done.1
  46.6 0.0 copy-done.2
  46.6 0.0 copy-done.3
  46.6 0.0 copy-done
  46.6 0.0 copy-done.6
  46.6 1.1 %outputs.1 = (f32[2,256,128]{2,1,0:T(8,128)}, f32[2,256,128]{2,1,0:T(8,128)}, f32[2,256,128]{2,1,0:T(8,128)}, f32[2,256,128]{2,1,0:T(8,128)}) custom-call(f32[2,256,128]{2,1,0:T(8,128)S(1)} %copy-done, f32[2,256,128]{2,1,0:T(8,128)S(1)} %copy-done.1, f32[2,256,128]{2,1,0:T(8,128)S(1)} %copy-done.2, f32[2,256,128]{2,1,0:T(8,128)S(1)} %copy-done.3, ...), custom_call_target="tpu_custom_call" | custom-call | flops 402653184 | bytes 524288 | tf_op jit(solution)/shard_map/outputs/pallas_call | solution.py:308
  (1 shorter events, 0.0 us)
Async XLA Ops:
  3.0 7.5 %copy-start.4 = (bf16[768,256]{1,0:T(8,128)(2,1)S(1)}, bf16[768,256]{1,0:T(8,128)(2,1)}, u32[]{:S(2)}) copy-start(bf16[768,256]{1,0:T(8,128)(2,1)} %constant.5.clone.matrix_ref) | copy-start | bytes 1179652
  3.0 7.5 %copy-start.5 = (f32[64,256]{1,0:T(8,128)S(1)}, f32[64,256]{1,0:T(8,128)}, u32[]{:S(2)}) copy-start(f32[64,256]{1,0:T(8,128)} %constant.4.clone.twist_ref) | copy-start | bytes 196612
  3.0 7.5 %copy-start.7 = (f32[8,4096]{1,0:T(8,128)S(1)}, f32[8,4096]{1,0:T(8,128)}, u32[]{:S(2)}) copy-start(f32[8,4096]{1,0:T(8,128)} %filter_ref.1) | copy-start | bytes 393220
  3.0 22.1 %all-to-all-start = ((f32[16,2,2,8,256]{4,3,2,1,0:T(8,128)}), f32[16,2,2,8,256]{4,3,2,1,0:T(8,128)S(1)}, u32[]{:S(2)}, u32[]{:S(2)}) async-start(f32[16,2,2,8,256]{4,3,2,1,0:T(8,128)} %gate.1), calls=%async_computation | async-start | bytes 1048576 | tf_op jit(solution)/shard_map/all_to_all | solution.py:322
  27.6 19.0 %all-to-all-start.1 = ((f32[16,2,2,8,256]{4,3,2,1,0:T(8,128)}), f32[16,2,2,8,256]{4,3,2,1,0:T(8,128)S(1)}, u32[]{:S(2)}, u32[]{:S(2)}) async-start(f32[16,2,2,8,256]{4,3,2,1,0:T(8,128)} %get-tuple-element.12), calls=%async_computation.1 | async-start | bytes 1048576 | tf_op jit(solution)/shard_map/all_to_all | solution.py:322
  31.9 14.6 %copy-start.1 = (f32[2,256,128]{2,1,0:T(8,128)S(1)}, f32[2,256,128]{2,1,0:T(8,128)}, u32[]{:S(2)}) copy-start(f32[2,256,128]{2,1,0:T(8,128)} %key_ref.1) | copy-start | bytes 786436
  31.9 14.6 %copy-start.2 = (f32[2,256,128]{2,1,0:T(8,128)S(1)}, f32[2,256,128]{2,1,0:T(8,128)}, u32[]{:S(2)}) copy-start(f32[2,256,128]{2,1,0:T(8,128)} %value_ref.1) | copy-start | bytes 786436
  32.0 14.6 %copy-start.3 = (f32[2,256,128]{2,1,0:T(8,128)S(1)}, f32[2,256,128]{2,1,0:T(8,128)}, u32[]{:S(2)}) copy-start(f32[2,256,128]{2,1,0:T(8,128)} %cotangent_ref.1) | copy-start | bytes 786436
  32.5 14.1 %copy-start = (f32[2,256,128]{2,1,0:T(8,128)S(1)}, f32[2,256,128]{2,1,0:T(8,128)}, u32[]{:S(2)}) copy-start(f32[2,256,128]{2,1,0:T(8,128)} %query_ref.1) | copy-start | bytes 786436
  32.5 3.7 %collective-permute-start = (f32[8,2048]{1,0:T(8,128)S(1)}, f32[8,2048]{1,0:T(8,128)S(1)}, u32[]{:S(2)}, u32[]{:S(2)}) collective-permute-start(f32[8,2048]{1,0:T(8,128)S(1)} %slice_bitcast_fusion), channel_id=1, source_target_pairs={{0,16},{16,0},{1,17},{17,1},{2,18},{18,2},{3,19},{19,3},{4,20},{20... | collective-permute-start | bytes 196616 | tf_op jit(solution)/shard_map/ppermute | solution.py:359
  36.9 9.7 %copy-start.6 = (f32[128]{0:T(128)S(1)}, f32[128]{0:T(128)}, u32[]{:S(2)}) copy-start(f32[128]{0:T(128)} %param.12) | copy-start | bytes 1540

commit v5 on v4

--- a/solution.py
+++ b/solution.py
@@ -134,12 +134,14 @@
     )
 
 
-def spread_order(shards):
-    return [5 * place % shards for place in range(shards)]
-
-
-def gate_kernel(order, query_hbm, key_hbm, value_hbm, cotangent_hbm, sent_ref, held, sems):
-    shards, _, batch, channels, tokens = sent_ref.shape
+def near_base(me, shards):
+    return me // (shards // 2) * (shards // 2)
+
+
+def gate_kernel(query_hbm, key_hbm, value_hbm, cotangent_hbm, near_ref, *refs):
+    *far, blocks, held, sems = refs
+    shards, _, batch, channels, tokens = blocks.shape
+    me = lax.axis_index("seq")
     sources = (key_hbm, value_hbm, cotangent_hbm, query_hbm)
 
     def copy(b, i):
@@ -152,10 +154,23 @@
         for b in range(batch):
             copy(b, 2 * kind).wait()
             copy(b, 2 * kind + 1).wait()
-            columns = jnp.transpose(held[2 * kind, b] * held[2 * kind + 1, b])
-            for place, shard in enumerate(order):
-                rows = columns[shard * channels : (shard + 1) * channels]
-                sent_ref[place, kind, b] = rows
+            product = held[2 * kind, b] * held[2 * kind + 1, b]
+            blocks[:, kind, b] = jnp.transpose(product).reshape(shards, channels, tokens)
+    hand_out(blocks, me, near_ref, far)
+
+
+def hand_out(blocks, me, near_ref, far):
+    shards = blocks.shape[0]
+    near_ref[...] = blocks[pl.ds(near_base(me, shards), shards // 2)]
+    for i, ref in enumerate(far):
+        ref[...] = blocks[me ^ (shards // 2 + i)]
+
+
+def take_in(blocks, me, near_ref, far):
+    shards = blocks.shape[0]
+    blocks[pl.ds(near_base(me, shards), shards // 2)] = near_ref[...]
+    for i, ref in enumerate(far):
+        blocks[me ^ (shards // 2 + i)] = ref[...]
 
 
 def transforms(twist_ref, matrix_ref, middle, turned):
@@ -205,23 +220,23 @@
     return forward, inverse
 
 
-def token_blocks(ref, order, kind, lanes, pair, live):
+def token_blocks(ref, kind, lanes, pair, live):
     pieces = ref.shape[4] // lanes
 
     def where(n1):
         at = n1 % pieces * lanes
-        return order.index(n1 // pieces), slice(at, at + lanes)
+        return n1 // pieces, slice(at, at + lanes)
 
     def load(n1):
         if n1 >= live:
             return None
-        place, span = where(n1)
-        return (ref[place, kind, 2 * pair, :, span], ref[place, kind, 2 * pair + 1, :, span])
+        shard, span = where(n1)
+        return (ref[shard, kind, 2 * pair, :, span], ref[shard, kind, 2 * pair + 1, :, span])
 
     def emit(n1, value):
-        place, span = where(n1)
-        ref[place, kind, 2 * pair, :, span] = value[0]
-        ref[place, kind, 2 * pair + 1, :, span] = -value[1]
+        shard, span = where(n1)
+        ref[shard, kind, 2 * pair, :, span] = value[0]
+        ref[shard, kind, 2 * pair + 1, :, span] = -value[1]
 
     return load, emit
 
@@ -239,17 +254,22 @@
     forward(load, spec_ref)
 
 
-def convolve_kernel(
-    order, held_ref, filter_ref, twist_ref, matrix_ref, back_ref, mixed_ref, upstream_ref, middle, turned
-):
+def convolve_kernel(far, filter_ref, twist_ref, matrix_ref, near_ref, *refs):
+    far_refs, refs = refs[:far], refs[far:]
+    near_back, refs = refs[0], refs[1:]
+    far_back, refs = refs[:far], refs[far:]
+    mixed_ref, upstream_ref, held_ref, back_ref, middle, turned = refs
+    me = lax.axis_index("seq")
+    take_in(held_ref, me, near_ref, far_refs)
     count, width = twist_ref.shape
     forward, inverse = transforms(twist_ref, matrix_ref, middle, turned)
     for kind, spec_ref in enumerate((mixed_ref, upstream_ref)):
         for pair in range(spec_ref.shape[0]):
-            load, _ = token_blocks(held_ref, order, kind, width // 2, pair, count // 2)
-            _, emit = token_blocks(back_ref, order, kind, width // 2, pair, count // 2)
+            load, _ = token_blocks(held_ref, kind, width // 2, pair, count // 2)
+            _, emit = token_blocks(back_ref, kind, width // 2, pair, count // 2)
             forward(load, spec_ref.at[pair])
             inverse(filter_ref, spec_ref.at[pair], kind == 1, emit)
+    hand_out(back_ref, me, near_back, far_back)
 
 
 def lag_kernel(scaling, mixed_ref, upstream_ref, twist_ref, matrix_ref, lag_ref, middle, turned):
@@ -271,16 +291,14 @@
         inverse(mixed_ref.at[pair], upstream_ref.at[pair], True, emit)
 
 
-def output_kernel(
-    order, query_ref, key_ref, value_ref, cotangent_ref, skip_ref, home_ref,
-    output_ref, query_grad_ref, key_grad_ref, value_grad_ref,
-):
-    shards, _, batch, _, _ = home_ref.shape
+def output_kernel(query_ref, key_ref, value_ref, cotangent_ref, skip_ref, near_ref, *refs):
+    *far, output_ref, query_grad_ref, key_grad_ref, value_grad_ref, home_ref = refs
+    shards, _, batch, channels, tokens = home_ref.shape
+    take_in(home_ref, lax.axis_index("seq"), near_ref, far)
     skip = skip_ref[...]
 
     def rows(kind, b):
-        blocks = [home_ref[order.index(shard), kind, b] for shard in range(shards)]
-        return jnp.transpose(jnp.concatenate(blocks, axis=0))
+        return jnp.transpose(home_ref[:, kind, b].reshape(shards * channels, tokens))
 
     for b in range(batch):
         query, key, value, cotangent = query_ref[b], key_ref[b], value_ref[b], cotangent_ref[b]
@@ -298,7 +316,7 @@
     lanes = 128 if 2 * length // 128 <= 64 else tokens
     count = 2 * length // lanes
     twist, matrix = tables(count, lanes)
-    order = spread_order(shards)
+    half = shards // 2
     lane_work = 2 * 3 * count * channels * (2 * lanes) ** 2
 
     def of(*shape):
@@ -318,18 +336,28 @@
             **options,
         )(*arrays)
 
-    def exchange(blocks):
-        return lax.all_to_all(
-            blocks, "seq", split_axis=0, concat_axis=0, tiled=True, axis_index_groups=[order]
+    def exchange(near, *far):
+        groups_of = [list(range(first, first + half)) for first in (0, half)]
+        near = lax.all_to_all(
+            near, "seq", split_axis=0, concat_axis=0, tiled=True, axis_index_groups=groups_of
         )
-
-    swap = of(shards, 2, batch, channels, tokens)
+        steps = enumerate(far, half)
+        far = [
+            lax.ppermute(block, "seq", [(source, source ^ step) for source in range(shards)])
+            for step, block in steps
+        ]
+        return near, *far
+
+    block = (2, batch, channels, tokens)
+    moved = (of(half, *block),) + (of(*block),) * half
+    whole = pltpu.VMEM((shards,) + block, jnp.float32)
     spectrum = of(batch // 2, count, channels, 2 * lanes)
     work = [pltpu.VMEM((count, channels, 2 * lanes), jnp.float32)] * 2
     sent = call(
-        functools.partial(gate_kernel, order),
-        "gate", 1, swap,
+        gate_kernel,
+        "gate", 1, moved,
         [
+            whole,
             pltpu.VMEM((4, batch, tokens, all_channels), jnp.float32),
             pltpu.SemaphoreType.DMA((4, batch)),
         ],
@@ -339,15 +367,16 @@
         ),
         in_specs=[pl.BlockSpec(memory_space=pltpu.HBM)] * 4,
     )
-    held = exchange(sent)
+    held = exchange(*sent)
     filter_spec = call(
         filter_kernel, "filter", 2, of(count, channels, 2 * lanes), work, filters, twist, matrix
     )
-    back, mixed_spec, upstream_spec = call(
-        functools.partial(convolve_kernel, order),
-        "convolve", 8, (swap, spectrum, spectrum), work, held, filter_spec, twist, matrix,
-    )
-    home = exchange(back)
+    *back, mixed_spec, upstream_spec = call(
+        functools.partial(convolve_kernel, half),
+        "convolve", 8, moved + (spectrum, spectrum), [whole, whole] + work,
+        filter_spec, twist, matrix, *held,
+    )
+    home = exchange(*back)
     lag = call(
         functools.partial(lag_kernel, 1.0 / (2.0 * length * math.sqrt(length))),
         "lags", 2, of(groups, channels, length // groups), work,
@@ -358,10 +387,10 @@
         pairs = [(source, (source + step) % groups) for source in range(groups)]
         filter_grad = filter_grad + lax.ppermute(lag[step], "batch", pairs)
     output, query_grad, key_grad, value_grad = call(
-        functools.partial(output_kernel, order),
-        "outputs", 2, (of(*query_gate.shape),) * 4, [],
+        output_kernel,
+        "outputs", 2, (of(*query_gate.shape),) * 4, [whole],
         query_gate, key_gate, value_input, cotangent, skip_gain.reshape(1, all_channels),
-        home,
+        *home,
     )
     return (output, query_grad, key_grad, value_grad, filter_grad)
 

time: 48.1 us -> 56.1 us (1.17)
  the two profiles are of different devices: /device:TPU:1 before, /device:TPU:0 now
where the time goes in v5:
time: 56.1 us; the launch traced here: 55.7 us
  starting transfers between devices  39.6 us (71%)
  waiting for transfers between devices  7.65 us (14%)
  Pallas kernels  6.96 us (12%)
  between operations  0.78 us (1%)
  other arithmetic  0.64 us (1%)
    ppermute x16, starting transfers between devices, exchange(): lax.ppermute(block, 'seq', [(source, source ^ step) for source in range(s...  29.1 us
    all_to_all x2, starting transfers between devices, exchange(): lax.all_to_all(near, 'seq', split_axis=0, concat_axis=0, tiled=True, axis...  8.95 us
    ppermute x16, waiting for transfers between devices, exchange(): lax.ppermute(block, 'seq', [(source, source ^ step) for source in range(s...  7.65 us
    pallas_call x5, Pallas kernels, call(): pl.pallas_call(kernel, out_shape=out_shape, scratch_shapes=scratch, compi...  6.96 us
    ppermute x1, starting transfers between devices, per_device(): filter_grad = filter_grad + lax.ppermute(lag[step], 'batch', pairs)  1.56 us
  transfers between devices with their start and end apart: 19, of which 5 were waited for; matrix products, arithmetic and copies ran while one was open for 1% of the time, Pallas kernels for 1%

profile of v5, /device:TPU:0, one launch (start us, length us, event | category | flops | bytes accessed | tf_op | source)
XLA Modules:
  0.0 55.7 jit_solution(11258204982086037097)
XLA Ops:
  0.6 0.0 copy-start.7
  0.6 2.3 %gate.1 = (f32[8,2,2,8,256]{4,3,2,1,0:T(8,128)}, f32[2,2,8,256]{3,2,1,0:T(8,128)S(1)}, f32[2,2,8,256]{3,2,1,0:T(8,128)S(1)}, f32[2,2,8,256]{3,2,1,0:T(8,128)S(1)...) custom-call(f32[2,256,128]{2,1,0:T(8,128)} %query_ref.1, ...), custom_call_target="tpu_custom_call" | custom-call | flops 201326592 | bytes 262144 | tf_op jit(solution)/shard_map/gate/pallas_call | solution.py:326
  2.9 0.0 copy-start.4
  3.0 0.0 copy-start.5
  3.0 5.4 %all-to-all-start = ((f32[8,2,2,8,256]{4,3,2,1,0:T(8,128)}), f32[8,2,2,8,256]{4,3,2,1,0:T(8,128)S(1)}, u32[]{:S(2)}, u32[]{:S(2)}) async-start(f32[8,2,2,8,256]{4,3,2,1,0:T(8,128)} %get-tuple-element.29), calls=%async_computation | async-start | bytes 524288 | tf_op jit(solution)/shard_map/all_to_all | solution.py:341
  8.4 2.6 %collective-permute-start = (f32[2,2,8,256]{3,2,1,0:T(8,128)S(1)}, f32[2,2,8,256]{3,2,1,0:T(8,128)S(1)}, u32[]{:S(2)}, u32[]{:S(2)}) collective-permute-start(f32[2,2,8,256]{3,2,1,0:T(8,128)S(1)} %get-tuple-element.30), channel_id=1, source_target_pairs={{0,8},{1,9},{2,10},{3,11},{4,12},{5,13},{6,14},{7,15},{8,0},{9,1},... | collective-permute-start | bytes 98312 | tf_op jit(solution)/shard_map/ppermute | solution.py:346
  11.0 0.2 collective-permute-start.1
  11.1 3.7 %collective-permute-start.2 = (f32[2,2,8,256]{3,2,1,0:T(8,128)S(1)}, f32[2,2,8,256]{3,2,1,0:T(8,128)S(1)}, u32[]{:S(2)}, u32[]{:S(2)}) collective-permute-start(f32[2,2,8,256]{3,2,1,0:T(8,128)S(1)} %get-tuple-element.32), channel_id=1, source_target_pairs={{0,10},{1,11},{2,8},{3,9},{4,14},{5,15},{6,12},{7,13},{8,2},{9,3},... | collective-permute-start | bytes 98312 | tf_op jit(solution)/shard_map/ppermute | solution.py:346
  14.8 0.3 collective-permute-start.3
  15.1 3.5 %collective-permute-start.4 = (f32[2,2,8,256]{3,2,1,0:T(8,128)S(1)}, f32[2,2,8,256]{3,2,1,0:T(8,128)S(1)}, u32[]{:S(2)}, u32[]{:S(2)}) collective-permute-start(f32[2,2,8,256]{3,2,1,0:T(8,128)S(1)} %get-tuple-element.34), channel_id=1, source_target_pairs={{0,12},{1,13},{2,14},{3,15},{4,8},{5,9},{6,10},{7,11},{8,4},{9,5},... | collective-permute-start | bytes 98312 | tf_op jit(solution)/shard_map/ppermute | solution.py:346
  18.6 0.0 collective-permute-done.refs_0_
  18.6 0.0 collective-permute-start.5
  18.6 0.0 collective-permute-done.1.refs_1_
  18.6 4.2 %collective-permute-start.6 = (f32[2,2,8,256]{3,2,1,0:T(8,128)S(1)}, f32[2,2,8,256]{3,2,1,0:T(8,128)S(1)}, u32[]{:S(2)}, u32[]{:S(2)}) collective-permute-start(f32[2,2,8,256]{3,2,1,0:T(8,128)S(1)} %get-tuple-element.36), channel_id=1, source_target_pairs={{0,14},{1,15},{2,12},{3,13},{4,10},{5,11},{6,8},{7,9},{8,6},{9,7},... | collective-permute-start | bytes 98312 | tf_op jit(solution)/shard_map/ppermute | solution.py:346
  22.8 0.0 collective-permute-done.2.refs_2_
  22.8 0.3 collective-permute-start.7
  23.1 0.0 copy-done.7
  23.1 0.0 copy-done.4
  23.1 0.0 copy-done.5
  23.1 0.5 filter.1.filter_ref
  23.6 0.0 collective-permute-done.3.refs_3_
  23.7 0.0 collective-permute-done.4.refs_4_
  23.7 0.5 collective-permute-done.5.refs_5_
  24.1 1.7 %collective-permute-done.6.refs_6_ = f32[2,2,8,256]{3,2,1,0:T(8,128)S(1)} collective-permute-done((f32[2,2,8,256]{3,2,1,0:T(8,128)S(1)}, f32[2,2,8,256]{3,2,1,0:T(8,128)S(1)}, u32[]{:S(2)}, u32[]{:S(2)}) %collective-permute-start.6) | collective-permute-done | bytes 32800 | tf_op jit(solution)/shard_map/ppermute | solution.py:346
  25.8 3.1 %collective-permute-done.7.refs_7_ = f32[2,2,8,256]{3,2,1,0:T(8,128)S(1)} collective-permute-done((f32[2,2,8,256]{3,2,1,0:T(8,128)S(1)}, f32[2,2,8,256]{3,2,1,0:T(8,128)S(1)}, u32[]{:S(2)}, u32[]{:S(2)}) %collective-permute-start.7) | collective-permute-done | bytes 32800 | tf_op jit(solution)/shard_map/ppermute | solution.py:346
  28.9 0.0 all-to-all-done.near_ref
  28.9 2.5 %convolve.1 = (f32[8,2,2,8,256]{4,3,2,1,0:T(8,128)}, f32[2,2,8,256]{3,2,1,0:T(8,128)S(1)}, f32[2,2,8,256]{3,2,1,0:T(8,128)S(1)}, f32[2,2,8,256]{3,2,1,0:T(8,128)...) custom-call(f32[64,8,256]{2,1,0:T(8,128)S(1)} %filter.1.filter_ref, ...), custom_call_target="tpu_custom_call" | custom-call | flops 1610612736 | bytes 2097152 | tf_op jit(solution)/shard_map/convolve/pallas_call | solution.py:326
  31.3 0.0 copy-start.3
  31.3 0.5 lags.1
  31.9 0.0 copy-start.2
  31.9 1.6 %collective-permute-start.16 = (f32[8,2048]{1,0:T(8,128)S(1)}, f32[8,2048]{1,0:T(8,128)S(1)}, u32[]{:S(2)}, u32[]{:S(2)}) collective-permute-start(f32[8,2048]{1,0:T(8,128)S(1)} %slice_bitcast_fusion), channel_id=1, source_target_pairs={{0,16},{16,0},{1,17},{17,1},{2,18},{18,2},{3,19},{19,3},{4,20},{20... | collective-permute-start | bytes 196616 | tf_op jit(solution)/shard_map/ppermute | solution.py:388
  33.4 0.0 collective-permute-start.8
  33.4 2.3 %collective-permute-start.9 = (f32[2,2,8,256]{3,2,1,0:T(8,128)S(1)}, f32[2,2,8,256]{3,2,1,0:T(8,128)S(1)}, u32[]{:S(2)}, u32[]{:S(2)}) collective-permute-start(f32[2,2,8,256]{3,2,1,0:T(8,128)S(1)} %get-tuple-element.40), channel_id=1, source_target_pairs={{0,9},{1,8},{2,11},{3,10},{4,13},{5,12},{6,15},{7,14},{8,1},{9,0},... | collective-permute-start | bytes 98312 | tf_op jit(solution)/shard_map/ppermute | solution.py:346
  35.8 0.6 %collective-permute-start.10 = (f32[2,2,8,256]{3,2,1,0:T(8,128)S(1)}, f32[2,2,8,256]{3,2,1,0:T(8,128)S(1)}, u32[]{:S(2)}, u32[]{:S(2)}) collective-permute-start(f32[2,2,8,256]{3,2,1,0:T(8,128)S(1)} %get-tuple-element.41), channel_id=1, source_target_pairs={{0,10},{1,11},{2,8},{3,9},{4,14},{5,15},{6,12},{7,13},{8,2},{9,3},... | collective-permute-start | bytes 98312 | tf_op jit(solution)/shard_map/ppermute | solution.py:346
  36.4 0.0 copy-start
  36.4 0.0 copy-start.1
  36.4 3.5 %all-to-all-start.1 = ((f32[8,2,2,8,256]{4,3,2,1,0:T(8,128)}), f32[8,2,2,8,256]{4,3,2,1,0:T(8,128)S(1)}, u32[]{:S(2)}, u32[]{:S(2)}) async-start(f32[8,2,2,8,256]{4,3,2,1,0:T(8,128)} %get-tuple-element.38), calls=%async_computation.1 | async-start | bytes 524288 | tf_op jit(solution)/shard_map/all_to_all | solution.py:341
  39.9 3.4 %collective-permute-start.11 = (f32[2,2,8,256]{3,2,1,0:T(8,128)S(1)}, f32[2,2,8,256]{3,2,1,0:T(8,128)S(1)}, u32[]{:S(2)}, u32[]{:S(2)}) collective-permute-start(f32[2,2,8,256]{3,2,1,0:T(8,128)S(1)} %get-tuple-element.42), channel_id=1, source_target_pairs={{0,11},{1,10},{2,9},{3,8},{4,15},{5,14},{6,13},{7,12},{8,3},{9,2},... | collective-permute-start | bytes 98312 | tf_op jit(solution)/shard_map/ppermute | solution.py:346
  43.4 0.0 collective-permute-done.8.refs_0_
  43.4 1.5 %collective-permute-start.12 = (f32[2,2,8,256]{3,2,1,0:T(8,128)S(1)}, f32[2,2,8,256]{3,2,1,0:T(8,128)S(1)}, u32[]{:S(2)}, u32[]{:S(2)}) collective-permute-start(f32[2,2,8,256]{3,2,1,0:T(8,128)S(1)} %get-tuple-element.43), channel_id=1, source_target_pairs={{0,12},{1,13},{2,14},{3,15},{4,8},{5,9},{6,10},{7,11},{8,4},{9,5},... | collective-permute-start | bytes 98312 | tf_op jit(solution)/shard_map/ppermute | solution.py:346
  44.9 0.0 collective-permute-done.9.refs_1_
  44.9 2.0 %collective-permute-start.13 = (f32[2,2,8,256]{3,2,1,0:T(8,128)S(1)}, f32[2,2,8,256]{3,2,1,0:T(8,128)S(1)}, u32[]{:S(2)}, u32[]{:S(2)}) collective-permute-start(f32[2,2,8,256]{3,2,1,0:T(8,128)S(1)} %get-tuple-element.44), channel_id=1, source_target_pairs={{0,13},{1,12},{2,15},{3,14},{4,9},{5,8},{6,11},{7,10},{8,5},{9,4},... | collective-permute-start | bytes 98312 | tf_op jit(solution)/shard_map/ppermute | solution.py:346
  46.9 0.0 collective-permute-done.10.refs_2_
  46.9 1.5 %collective-permute-start.14 = (f32[2,2,8,256]{3,2,1,0:T(8,128)S(1)}, f32[2,2,8,256]{3,2,1,0:T(8,128)S(1)}, u32[]{:S(2)}, u32[]{:S(2)}) collective-permute-start(f32[2,2,8,256]{3,2,1,0:T(8,128)S(1)} %get-tuple-element.45), channel_id=1, source_target_pairs={{0,14},{1,15},{2,12},{3,13},{4,10},{5,11},{6,8},{7,9},{8,6},{9,7},... | collective-permute-start | bytes 98312 | tf_op jit(solution)/shard_map/ppermute | solution.py:346
  48.4 0.0 collective-permute-done.16
  48.4 3.0 %collective-permute-start.15 = (f32[2,2,8,256]{3,2,1,0:T(8,128)S(1)}, f32[2,2,8,256]{3,2,1,0:T(8,128)S(1)}, u32[]{:S(2)}, u32[]{:S(2)}) collective-permute-start(f32[2,2,8,256]{3,2,1,0:T(8,128)S(1)} %get-tuple-element.46), channel_id=1, source_target_pairs={{0,15},{1,14},{2,13},{3,12},{4,11},{5,10},{6,9},{7,8},{8,7},{9,6},... | collective-permute-start | bytes 98312 | tf_op jit(solution)/shard_map/ppermute | solution.py:346
  51.4 0.6 %fusion = f32[8,2048]{1,0:T(8,128)} fusion(f32[8,2048]{1,0:T(8,128)S(1)} %collective-permute-done.16, f32[2,8,2048]{2,1,0:T(8,128)S(1)} %lags.1), kind=kLoop, calls=%fused_computation.2 | loop fusion | flops 16384 | bytes 196608 | tf_op jit(solution)/shard_map/add | solution.py:388
  52.0 0.0 copy-start.6
  52.0 0.0 collective-permute-done.11.refs_3_
  52.0 0.0 collective-permute-done.12.refs_4_
  52.0 0.0 collective-permute-done.13.refs_5_
  52.0 1.5 %collective-permute-done.14.refs_6_ = f32[2,2,8,256]{3,2,1,0:T(8,128)S(1)} collective-permute-done((f32[2,2,8,256]{3,2,1,0:T(8,128)S(1)}, f32[2,2,8,256]{3,2,1,0:T(8,128)S(1)}, u32[]{:S(2)}, u32[]{:S(2)}) %collective-permute-start.14) | collective-permute-done | bytes 32800 | tf_op jit(solution)/shard_map/ppermute | solution.py:346
  53.5 1.0 %collective-permute-done.15.refs_7_ = f32[2,2,8,256]{3,2,1,0:T(8,128)S(1)} collective-permute-done((f32[2,2,8,256]{3,2,1,0:T(8,128)S(1)}, f32[2,2,8,256]{3,2,1,0:T(8,128)S(1)}, u32[]{:S(2)}, u32[]{:S(2)}) %collective-permute-start.15) | collective-permute-done | bytes 32800 | tf_op jit(solution)/shard_map/ppermute | solution.py:346
  54.4 0.0 all-to-all-done.1.near_ref
  54.4 0.0 copy-done.3
  54.4 0.0 copy-done.2
  54.5 0.0 copy-done
  54.5 0.0 copy-done.1
  54.5 0.0 copy-done.6
  54.5 1.2 %outputs.1 = (f32[2,256,128]{2,1,0:T(8,128)}, f32[2,256,128]{2,1,0:T(8,128)}, f32[2,256,128]{2,1,0:T(8,128)}, f32[2,256,128]{2,1,0:T(8,128)}) custom-call(f32[2,256,128]{2,1,0:T(8,128)S(1)} %copy-done, f32[2,256,128]{2,1,0:T(8,128)S(1)} %copy-done.1, f32[2,256,128]{2,1,0:T(8,128)S(1)} %copy-done.2, f32[2,256,128]{2,1,0:T(8,128)S(1)} %copy-done.3, ...), custom_call_target="tpu_custom_call" | custom-call | flops 402653184 | bytes 524288 | tf_op jit(solution)/shard_map/outputs/pallas_call | solution.py:326
  (1 shorter events, 0.0 us)
Async XLA Ops:
  0.6 22.5 %copy-start.7 = (f32[8,4096]{1,0:T(8,128)S(1)}, f32[8,4096]{1,0:T(8,128)}, u32[]{:S(2)}) copy-start(f32[8,4096]{1,0:T(8,128)} %filter_ref.1) | copy-start | bytes 393220
  2.9 20.2 %copy-start.4 = (bf16[768,256]{1,0:T(8,128)(2,1)S(1)}, bf16[768,256]{1,0:T(8,128)(2,1)}, u32[]{:S(2)}) copy-start(bf16[768,256]{1,0:T(8,128)(2,1)} %constant.5.clone.matrix_ref) | copy-start | bytes 1179652
  3.0 20.2 %copy-start.5 = (f32[64,256]{1,0:T(8,128)S(1)}, f32[64,256]{1,0:T(8,128)}, u32[]{:S(2)}) copy-start(f32[64,256]{1,0:T(8,128)} %constant.4.clone.twist_ref) | copy-start | bytes 196612
  3.0 25.9 %all-to-all-start = ((f32[8,2,2,8,256]{4,3,2,1,0:T(8,128)}), f32[8,2,2,8,256]{4,3,2,1,0:T(8,128)S(1)}, u32[]{:S(2)}, u32[]{:S(2)}) async-start(f32[8,2,2,8,256]{4,3,2,1,0:T(8,128)} %get-tuple-element.29), calls=%async_computation | async-start | bytes 524288 | tf_op jit(solution)/shard_map/all_to_all | solution.py:341
  8.4 10.2 %collective-permute-start = (f32[2,2,8,256]{3,2,1,0:T(8,128)S(1)}, f32[2,2,8,256]{3,2,1,0:T(8,128)S(1)}, u32[]{:S(2)}, u32[]{:S(2)}) collective-permute-start(f32[2,2,8,256]{3,2,1,0:T(8,128)S(1)} %get-tuple-element.30), channel_id=1, source_target_pairs={{0,8},{1,9},{2,10},{3,11},{4,12},{5,13},{6,14},{7,15},{8,0},{9,1},... | collective-permute-start | bytes 98312 | tf_op jit(solution)/shard_map/ppermute | solution.py:346
  11.0 7.7 %collective-permute-start.1 = (f32[2,2,8,256]{3,2,1,0:T(8,128)S(1)}, f32[2,2,8,256]{3,2,1,0:T(8,128)S(1)}, u32[]{:S(2)}, u32[]{:S(2)}) collective-permute-start(f32[2,2,8,256]{3,2,1,0:T(8,128)S(1)} %get-tuple-element.31), channel_id=1, source_target_pairs={{0,9},{1,8},{2,11},{3,10},{4,13},{5,12},{6,15},{7,14},{8,1},{9,0},... | collective-permute-start | bytes 98312 | tf_op jit(solution)/shard_map/ppermute | solution.py:346
  11.1 11.7 %collective-permute-start.2 = (f32[2,2,8,256]{3,2,1,0:T(8,128)S(1)}, f32[2,2,8,256]{3,2,1,0:T(8,128)S(1)}, u32[]{:S(2)}, u32[]{:S(2)}) collective-permute-start(f32[2,2,8,256]{3,2,1,0:T(8,128)S(1)} %get-tuple-element.32), channel_id=1, source_target_pairs={{0,10},{1,11},{2,8},{3,9},{4,14},{5,15},{6,12},{7,13},{8,2},{9,3},... | collective-permute-start | bytes 98312 | tf_op jit(solution)/shard_map/ppermute | solution.py:346
  14.8 8.8 %collective-permute-start.3 = (f32[2,2,8,256]{3,2,1,0:T(8,128)S(1)}, f32[2,2,8,256]{3,2,1,0:T(8,128)S(1)}, u32[]{:S(2)}, u32[]{:S(2)}) collective-permute-start(f32[2,2,8,256]{3,2,1,0:T(8,128)S(1)} %get-tuple-element.33), channel_id=1, source_target_pairs={{0,11},{1,10},{2,9},{3,8},{4,15},{5,14},{6,13},{7,12},{8,3},{9,2},... | collective-permute-start | bytes 98312 | tf_op jit(solution)/shard_map/ppermute | solution.py:346
  15.1 8.6 %collective-permute-start.4 = (f32[2,2,8,256]{3,2,1,0:T(8,128)S(1)}, f32[2,2,8,256]{3,2,1,0:T(8,128)S(1)}, u32[]{:S(2)}, u32[]{:S(2)}) collective-permute-start(f32[2,2,8,256]{3,2,1,0:T(8,128)S(1)} %get-tuple-element.34), channel_id=1, source_target_pairs={{0,12},{1,13},{2,14},{3,15},{4,8},{5,9},{6,10},{7,11},{8,4},{9,5},... | collective-permute-start | bytes 98312 | tf_op jit(solution)/shard_map/ppermute | solution.py:346
  18.6 5.5 %collective-permute-start.5 = (f32[2,2,8,256]{3,2,1,0:T(8,128)S(1)}, f32[2,2,8,256]{3,2,1,0:T(8,128)S(1)}, u32[]{:S(2)}, u32[]{:S(2)}) collective-permute-start(f32[2,2,8,256]{3,2,1,0:T(8,128)S(1)} %get-tuple-element.35), channel_id=1, source_target_pairs={{0,13},{1,12},{2,15},{3,14},{4,9},{5,8},{6,11},{7,10},{8,5},{9,4},... | collective-permute-start | bytes 98312 | tf_op jit(solution)/shard_map/ppermute | solution.py:346
  18.6 7.2 %collective-permute-start.6 = (f32[2,2,8,256]{3,2,1,0:T(8,128)S(1)}, f32[2,2,8,256]{3,2,1,0:T(8,128)S(1)}, u32[]{:S(2)}, u32[]{:S(2)}) collective-permute-start(f32[2,2,8,256]{3,2,1,0:T(8,128)S(1)} %get-tuple-element.36), channel_id=1, source_target_pairs={{0,14},{1,15},{2,12},{3,13},{4,10},{5,11},{6,8},{7,9},{8,6},{9,7},... | collective-permute-start | bytes 98312 | tf_op jit(solution)/shard_map/ppermute | solution.py:346
  22.8 6.0 %collective-permute-start.7 = (f32[2,2,8,256]{3,2,1,0:T(8,128)S(1)}, f32[2,2,8,256]{3,2,1,0:T(8,128)S(1)}, u32[]{:S(2)}, u32[]{:S(2)}) collective-permute-start(f32[2,2,8,256]{3,2,1,0:T(8,128)S(1)} %get-tuple-element.37), channel_id=1, source_target_pairs={{0,15},{1,14},{2,13},{3,12},{4,11},{5,10},{6,9},{7,8},{8,7},{9,6},... | collective-permute-start | bytes 98312 | tf_op jit(solution)/shard_map/ppermute | solution.py:346
  31.3 23.1 %copy-start.3 = (f32[2,256,128]{2,1,0:T(8,128)S(1)}, f32[2,256,128]{2,1,0:T(8,128)}, u32[]{:S(2)}) copy-start(f32[2,256,128]{2,1,0:T(8,128)} %cotangent_ref.1) | copy-start | bytes 786436
  31.9 22.6 %copy-start.2 = (f32[2,256,128]{2,1,0:T(8,128)S(1)}, f32[2,256,128]{2,1,0:T(8,128)}, u32[]{:S(2)}) copy-start(f32[2,256,128]{2,1,0:T(8,128)} %value_ref.1) | copy-start | bytes 786436
  31.9 16.5 %collective-permute-start.16 = (f32[8,2048]{1,0:T(8,128)S(1)}, f32[8,2048]{1,0:T(8,128)S(1)}, u32[]{:S(2)}, u32[]{:S(2)}) collective-permute-start(f32[8,2048]{1,0:T(8,128)S(1)} %slice_bitcast_fusion), channel_id=1, source_target_pairs={{0,16},{16,0},{1,17},{17,1},{2,18},{18,2},{3,19},{19,3},{4,20},{20... | collective-permute-start | bytes 196616 | tf_op jit(solution)/shard_map/ppermute | solution.py:388
  33.4 9.9 %collective-permute-start.8 = (f32[2,2,8,256]{3,2,1,0:T(8,128)S(1)}, f32[2,2,8,256]{3,2,1,0:T(8,128)S(1)}, u32[]{:S(2)}, u32[]{:S(2)}) collective-permute-start(f32[2,2,8,256]{3,2,1,0:T(8,128)S(1)} %get-tuple-element.39), channel_id=1, source_target_pairs={{0,8},{1,9},{2,10},{3,11},{4,12},{5,13},{6,14},{7,15},{8,0},{9,1},... | collective-permute-start | bytes 98312 | tf_op jit(solution)/shard_map/ppermute | solution.py:346
  33.4 11.5 %collective-permute-start.9 = (f32[2,2,8,256]{3,2,1,0:T(8,128)S(1)}, f32[2,2,8,256]{3,2,1,0:T(8,128)S(1)}, u32[]{:S(2)}, u32[]{:S(2)}) collective-permute-start(f32[2,2,8,256]{3,2,1,0:T(8,128)S(1)} %get-tuple-element.40), channel_id=1, source_target_pairs={{0,9},{1,8},{2,11},{3,10},{4,13},{5,12},{6,15},{7,14},{8,1},{9,0},... | collective-permute-start | bytes 98312 | tf_op jit(solution)/shard_map/ppermute | solution.py:346
  35.8 11.1 %collective-permute-start.10 = (f32[2,2,8,256]{3,2,1,0:T(8,128)S(1)}, f32[2,2,8,256]{3,2,1,0:T(8,128)S(1)}, u32[]{:S(2)}, u32[]{:S(2)}) collective-permute-start(f32[2,2,8,256]{3,2,1,0:T(8,128)S(1)} %get-tuple-element.41), channel_id=1, source_target_pairs={{0,10},{1,11},{2,8},{3,9},{4,14},{5,15},{6,12},{7,13},{8,2},{9,3},... | collective-permute-start | bytes 98312 | tf_op jit(solution)/shard_map/ppermute | solution.py:346
  36.4 18.1 %copy-start = (f32[2,256,128]{2,1,0:T(8,128)S(1)}, f32[2,256,128]{2,1,0:T(8,128)}, u32[]{:S(2)}) copy-start(f32[2,256,128]{2,1,0:T(8,128)} %query_ref.1) | copy-start | bytes 786436
  36.4 18.1 %copy-start.1 = (f32[2,256,128]{2,1,0:T(8,128)S(1)}, f32[2,256,128]{2,1,0:T(8,128)}, u32[]{:S(2)}) copy-start(f32[2,256,128]{2,1,0:T(8,128)} %key_ref.1) | copy-start | bytes 786436
  36.4 18.1 %all-to-all-start.1 = ((f32[8,2,2,8,256]{4,3,2,1,0:T(8,128)}), f32[8,2,2,8,256]{4,3,2,1,0:T(8,128)S(1)}, u32[]{:S(2)}, u32[]{:S(2)}) async-start(f32[8,2,2,8,256]{4,3,2,1,0:T(8,128)} %get-tuple-element.38), calls=%async_computation.1 | async-start | bytes 524288 | tf_op jit(solution)/shard_map/all_to_all | solution.py:341
  39.9 12.1 %collective-permute-start.11 = (f32[2,2,8,256]{3,2,1,0:T(8,128)S(1)}, f32[2,2,8,256]{3,2,1,0:T(8,128)S(1)}, u32[]{:S(2)}, u32[]{:S(2)}) collective-permute-start(f32[2,2,8,256]{3,2,1,0:T(8,128)S(1)} %get-tuple-element.42), channel_id=1, source_target_pairs={{0,11},{1,10},{2,9},{3,8},{4,15},{5,14},{6,13},{7,12},{8,3},{9,2},... | collective-permute-start | bytes 98312 | tf_op jit(solution)/shard_map/ppermute | solution.py:346
  43.4 8.7 %collective-permute-start.12 = (f32[2,2,8,256]{3,2,1,0:T(8,128)S(1)}, f32[2,2,8,256]{3,2,1,0:T(8,128)S(1)}, u32[]{:S(2)}, u32[]{:S(2)}) collective-permute-start(f32[2,2,8,256]{3,2,1,0:T(8,128)S(1)} %get-tuple-element.43), channel_id=1, source_target_pairs={{0,12},{1,13},{2,14},{3,15},{4,8},{5,9},{6,10},{7,11},{8,4},{9,5},... | collective-permute-start | bytes 98312 | tf_op jit(solution)/shard_map/ppermute | solution.py:346
  44.9 7.1 %collective-permute-start.13 = (f32[2,2,8,256]{3,2,1,0:T(8,128)S(1)}, f32[2,2,8,256]{3,2,1,0:T(8,128)S(1)}, u32[]{:S(2)}, u32[]{:S(2)}) collective-permute-start(f32[2,2,8,256]{3,2,1,0:T(8,128)S(1)} %get-tuple-element.44), channel_id=1, source_target_pairs={{0,13},{1,12},{2,15},{3,14},{4,9},{5,8},{6,11},{7,10},{8,5},{9,4},... | collective-permute-start | bytes 98312 | tf_op jit(solution)/shard_map/ppermute | solution.py:346
  46.9 6.6 %collective-permute-start.14 = (f32[2,2,8,256]{3,2,1,0:T(8,128)S(1)}, f32[2,2,8,256]{3,2,1,0:T(8,128)S(1)}, u32[]{:S(2)}, u32[]{:S(2)}) collective-permute-start(f32[2,2,8,256]{3,2,1,0:T(8,128)S(1)} %get-tuple-element.45), channel_id=1, source_target_pairs={{0,14},{1,15},{2,12},{3,13},{4,10},{5,11},{6,8},{7,9},{8,6},{9,7},... | collective-permute-start | bytes 98312 | tf_op jit(solution)/shard_map/ppermute | solution.py:346
  48.4 6.0 %collective-permute-start.15 = (f32[2,2,8,256]{3,2,1,0:T(8,128)S(1)}, f32[2,2,8,256]{3,2,1,0:T(8,128)S(1)}, u32[]{:S(2)}, u32[]{:S(2)}) collective-permute-start(f32[2,2,8,256]{3,2,1,0:T(8,128)S(1)} %get-tuple-element.46), channel_id=1, source_target_pairs={{0,15},{1,14},{2,13},{3,12},{4,11},{5,10},{6,9},{7,8},{8,7},{9,6},... | collective-permute-start | bytes 98312 | tf_op jit(solution)/shard_map/ppermute | solution.py:346
  52.0 2.5 %copy-start.6 = (f32[128]{0:T(128)S(1)}, f32[128]{0:T(128)}, u32[]{:S(2)}) copy-start(f32[128]{0:T(128)} %param.12) | copy-start | bytes 1540

commit v6 on v4

--- a/solution.py
+++ b/solution.py
@@ -134,16 +134,23 @@
     )
 
 
-def spread_order(shards):
-    return [5 * place % shards for place in range(shards)]
-
-
-def gate_kernel(order, query_hbm, key_hbm, value_hbm, cotangent_hbm, sent_ref, held, sems):
-    shards, _, batch, channels, tokens = sent_ref.shape
+def block_rows(kind, sequence, piece, batch, pieces, channels):
+    first = ((kind * batch + sequence) * pieces + piece) * channels
+    return slice(first, first + channels)
+
+
+def gate_kernel(batch, query_hbm, key_hbm, value_hbm, cotangent_hbm, sent_hbm, held, sent, sems, out_sems):
+    shards, rows, lanes = sent.shape
+    _, _, tokens, all_channels = held.shape
+    channels, pieces = all_channels // shards, tokens // lanes
     sources = (key_hbm, value_hbm, cotangent_hbm, query_hbm)
 
     def copy(b, i):
         return pltpu.make_async_copy(sources[i].at[b], held.at[i, b], sems.at[i, b])
+
+    def send(kind):
+        span = pl.ds(kind * (rows // 2), rows // 2)
+        return pltpu.make_async_copy(sent.at[:, span], sent_hbm.at[:, span], out_sems.at[kind])
 
     for i in range(4):
         for b in range(batch):
@@ -153,9 +160,13 @@
             copy(b, 2 * kind).wait()
             copy(b, 2 * kind + 1).wait()
             columns = jnp.transpose(held[2 * kind, b] * held[2 * kind + 1, b])
-            for place, shard in enumerate(order):
-                rows = columns[shard * channels : (shard + 1) * channels]
-                sent_ref[place, kind, b] = rows
+            columns = columns.reshape(shards, channels, tokens)
+            for piece in range(pieces):
+                at = block_rows(kind, b, piece, batch, pieces, channels)
+                sent[:, at] = columns[:, :, piece * lanes : (piece + 1) * lanes]
+        send(kind).start()
+    for kind in range(2):
+        send(kind).wait()
 
 
 def transforms(twist_ref, matrix_ref, middle, turned):
@@ -205,23 +216,21 @@
     return forward, inverse
 
 
-def token_blocks(ref, order, kind, lanes, pair, live):
-    pieces = ref.shape[4] // lanes
-
-    def where(n1):
-        at = n1 % pieces * lanes
-        return order.index(n1 // pieces), slice(at, at + lanes)
+def token_blocks(ref, kind, pair, batch, channels, live):
+    pieces = ref.shape[1] // (2 * batch * channels)
+
+    def where(n1, sequence):
+        at = block_rows(kind, 2 * pair + sequence, n1 % pieces, batch, pieces, channels)
+        return n1 // pieces, at
 
     def load(n1):
         if n1 >= live:
             return None
-        place, span = where(n1)
-        return (ref[place, kind, 2 * pair, :, span], ref[place, kind, 2 * pair + 1, :, span])
+        return (ref[where(n1, 0)], ref[where(n1, 1)])
 
     def emit(n1, value):
-        place, span = where(n1)
-        ref[place, kind, 2 * pair, :, span] = value[0]
-        ref[place, kind, 2 * pair + 1, :, span] = -value[1]
+        ref[where(n1, 0)] = value[0]
+        ref[where(n1, 1)] = -value[1]
 
     return load, emit
 
@@ -240,16 +249,31 @@
 
 
 def convolve_kernel(
-    order, held_ref, filter_ref, twist_ref, matrix_ref, back_ref, mixed_ref, upstream_ref, middle, turned
+    held_ref, filter_ref, twist_ref, matrix_ref, back_hbm, mixed_ref, upstream_ref,
+    back, middles, turneds, out_sems,
 ):
-    count, width = twist_ref.shape
-    forward, inverse = transforms(twist_ref, matrix_ref, middle, turned)
-    for kind, spec_ref in enumerate((mixed_ref, upstream_ref)):
-        for pair in range(spec_ref.shape[0]):
-            load, _ = token_blocks(held_ref, order, kind, width // 2, pair, count // 2)
-            _, emit = token_blocks(back_ref, order, kind, width // 2, pair, count // 2)
-            forward(load, spec_ref.at[pair])
-            inverse(filter_ref, spec_ref.at[pair], kind == 1, emit)
+    pairs, count, channels, _ = mixed_ref.shape
+    half = back.shape[1] // 2
+    kinds = (mixed_ref, upstream_ref)
+    scratch = [
+        transforms(twist_ref, matrix_ref, middles.at[kind], turneds.at[kind]) for kind in range(2)
+    ]
+
+    def send(kind):
+        span = pl.ds(kind * half, half)
+        return pltpu.make_async_copy(back.at[:, span], back_hbm.at[:, span], out_sems.at[kind])
+
+    for pair in range(pairs):
+        for kind in range(2):
+            load, _ = token_blocks(held_ref, kind, pair, 2 * pairs, channels, count // 2)
+            scratch[kind][0](load, kinds[kind].at[pair])
+        for kind in range(2):
+            _, emit = token_blocks(back, kind, pair, 2 * pairs, channels, count // 2)
+            scratch[kind][1](filter_ref, kinds[kind].at[pair], kind == 1, emit)
+            if pair == pairs - 1:
+                send(kind).start()
+    for kind in range(2):
+        send(kind).wait()
 
 
 def lag_kernel(scaling, mixed_ref, upstream_ref, twist_ref, matrix_ref, lag_ref, middle, turned):
@@ -272,24 +296,41 @@
 
 
 def output_kernel(
-    order, query_ref, key_ref, value_ref, cotangent_ref, skip_ref, home_ref,
-    output_ref, query_grad_ref, key_grad_ref, value_grad_ref,
+    query_ref, key_ref, value_ref, cotangent_ref, skip_ref, home_ref, *refs
 ):
-    shards, _, batch, _, _ = home_ref.shape
+    *results, ready, out_sems = refs
+    shards, _, lanes = home_ref.shape
+    batch, tokens, all_channels = query_ref.shape
+    channels, pieces = all_channels // shards, tokens // lanes
     skip = skip_ref[...]
 
-    def rows(kind, b):
-        blocks = [home_ref[order.index(shard), kind, b] for shard in range(shards)]
-        return jnp.transpose(jnp.concatenate(blocks, axis=0))
+    def columns(kind, b):
+        parts = [
+            home_ref[:, block_rows(kind, b, piece, batch, pieces, channels)]
+            for piece in range(pieces)
+        ]
+        return jnp.concatenate(
+            [jnp.transpose(part.reshape(all_channels, lanes)) for part in parts], axis=0
+        )
+
+    def finish(i, b):
+        return pltpu.make_async_copy(ready.at[i, b], results[i].at[b], out_sems.at[i, b])
 
     for b in range(batch):
         query, key, value, cotangent = query_ref[b], key_ref[b], value_ref[b], cotangent_ref[b]
-        hidden = rows(0, b) + skip * (key * value)
-        output_ref[b] = query * hidden
-        query_grad_ref[b] = cotangent * hidden
-        mixed_grad = rows(1, b) + skip * (cotangent * query)
-        key_grad_ref[b] = mixed_grad * value
-        value_grad_ref[b] = mixed_grad * key
+        hidden = columns(0, b) + skip * (key * value)
+        ready[0, b] = query * hidden
+        finish(0, b).start()
+        ready[1, b] = cotangent * hidden
+        finish(1, b).start()
+        mixed_grad = columns(1, b) + skip * (cotangent * query)
+        ready[2, b] = mixed_grad * value
+        finish(2, b).start()
+        ready[3, b] = mixed_grad * key
+        finish(3, b).start()
+    for b in range(batch):
+        for i in range(4):
+            finish(i, b).wait()
 
 
 def per_device(query_gate, key_gate, value_input, filters, skip_gain, cotangent, *, shards, groups):
@@ -298,7 +339,6 @@
     lanes = 128 if 2 * length // 128 <= 64 else tokens
     count = 2 * length // lanes
     twist, matrix = tables(count, lanes)
-    order = spread_order(shards)
     lane_work = 2 * 3 * count * channels * (2 * lanes) ** 2
 
     def of(*shape):
@@ -319,33 +359,45 @@
         )(*arrays)
 
     def exchange(blocks):
-        return lax.all_to_all(
-            blocks, "seq", split_axis=0, concat_axis=0, tiled=True, axis_index_groups=[order]
-        )
-
-    swap = of(shards, 2, batch, channels, tokens)
+        return lax.all_to_all(blocks, "seq", split_axis=0, concat_axis=0, tiled=True)
+
+    rows = 2 * batch * channels * tokens // lanes
+    swap = of(shards, rows, lanes)
+    anywhere = pl.BlockSpec(memory_space=pl.ANY)
+    in_vmem = pl.BlockSpec(memory_space=pltpu.VMEM)
     spectrum = of(batch // 2, count, channels, 2 * lanes)
     work = [pltpu.VMEM((count, channels, 2 * lanes), jnp.float32)] * 2
     sent = call(
-        functools.partial(gate_kernel, order),
+        functools.partial(gate_kernel, batch),
         "gate", 1, swap,
         [
             pltpu.VMEM((4, batch, tokens, all_channels), jnp.float32),
+            pltpu.VMEM((shards, rows, lanes), jnp.float32),
             pltpu.SemaphoreType.DMA((4, batch)),
+            pltpu.SemaphoreType.DMA((2,)),
         ],
         *(
             pltpu.with_memory_space_constraint(x, pltpu.HBM)
             for x in (query_gate, key_gate, value_input, cotangent)
         ),
         in_specs=[pl.BlockSpec(memory_space=pltpu.HBM)] * 4,
+        out_specs=anywhere,
     )
     held = exchange(sent)
     filter_spec = call(
         filter_kernel, "filter", 2, of(count, channels, 2 * lanes), work, filters, twist, matrix
     )
     back, mixed_spec, upstream_spec = call(
-        functools.partial(convolve_kernel, order),
-        "convolve", 8, (swap, spectrum, spectrum), work, held, filter_spec, twist, matrix,
+        convolve_kernel,
+        "convolve", 8, (swap, spectrum, spectrum),
+        [
+            pltpu.VMEM((shards, rows, lanes), jnp.float32),
+            pltpu.VMEM((2, count, channels, 2 * lanes), jnp.float32),
+            pltpu.VMEM((2, count, channels, 2 * lanes), jnp.float32),
+            pltpu.SemaphoreType.DMA((2,)),
+        ],
+        held, filter_spec, twist, matrix,
+        out_specs=(anywhere, in_vmem, in_vmem),
     )
     home = exchange(back)
     lag = call(
@@ -358,10 +410,15 @@
         pairs = [(source, (source + step) % groups) for source in range(groups)]
         filter_grad = filter_grad + lax.ppermute(lag[step], "batch", pairs)
     output, query_grad, key_grad, value_grad = call(
-        functools.partial(output_kernel, order),
-        "outputs", 2, (of(*query_gate.shape),) * 4, [],
+        output_kernel,
+        "outputs", 2, (of(*query_gate.shape),) * 4,
+        [
+            pltpu.VMEM((4, batch, tokens, all_channels), jnp.float32),
+            pltpu.SemaphoreType.DMA((4, batch)),
+        ],
         query_gate, key_gate, value_input, cotangent, skip_gain.reshape(1, all_channels),
         home,
+        out_specs=(anywhere,) * 4,
     )
     return (output, query_grad, key_grad, value_grad, filter_grad)
 

time: 48.1 us -> 47.4 us (0.985)
  the two profiles are of different devices: /device:TPU:1 before, /device:TPU:0 now
where the time goes in v6:
time: 47.4 us; the launch traced here: 47 us
  waiting for transfers between devices  25.6 us (54%)
  starting transfers between devices  13.2 us (28%)
  Pallas kernels  6.73 us (14%)
  between operations  0.79 us (2%)
  other arithmetic  0.64 us (1%)
    all_to_all x2, waiting for transfers between devices, exchange(): lax.all_to_all(blocks, 'seq', split_axis=0, concat_axis=0, tiled=True)  22.7 us
    all_to_all x2, starting transfers between devices, exchange(): lax.all_to_all(blocks, 'seq', split_axis=0, concat_axis=0, tiled=True)  11.6 us
    pallas_call x5, Pallas kernels, call(): pl.pallas_call(kernel, out_shape=out_shape, scratch_shapes=scratch, compi...  6.73 us
    ppermute x1, waiting for transfers between devices, per_device(): filter_grad = filter_grad + lax.ppermute(lag[step], 'batch', pairs)  2.93 us
    ppermute x1, starting transfers between devices, per_device(): filter_grad = filter_grad + lax.ppermute(lag[step], 'batch', pairs)  1.56 us
  transfers between devices with their start and end apart: 3, of which 3 were waited for; matrix products, arithmetic and copies ran while one was open for 1% of the time, Pallas kernels for 2%

profile of v6, /device:TPU:0, one launch (start us, length us, event | category | flops | bytes accessed | tf_op | source)
XLA Modules:
  0.0 47.0 jit_solution(17552948737222011949)
XLA Ops:
  0.6 2.3 %gate.1 = f32[16,64,128]{2,1,0:T(8,128)} custom-call(f32[2,256,128]{2,1,0:T(8,128)} %query_ref.1, f32[2,256,128]{2,1,0:T(8,128)} %key_ref.1, f32[2,256,128]{2,1,0:T(8,128)} %value_ref.1, f32[2,256,128]{2,1,0:T(8,128)} %cotangent_ref.1), custom_call_target="tpu_custom_call" | custom-call | flops 201326592 | bytes 262144 | tf_op jit(solution)/shard_map/gate/pallas_call | solution.py:348
  2.9 0.0 copy-start.4
  2.9 0.0 copy-start.5
  2.9 0.0 copy-start.7
  2.9 7.5 %all-to-all-start = ((f32[16,64,128]{2,1,0:T(8,128)}), f32[16,64,128]{2,1,0:T(8,128)S(1)}, u32[]{:S(2)}, u32[]{:S(2)}) async-start(f32[16,64,128]{2,1,0:T(8,128)} %gate.1), calls=%async_computation | async-start | bytes 1048576 | tf_op jit(solution)/shard_map/all_to_all | solution.py:362
  10.5 0.0 copy-done.4
  10.5 0.0 copy-done.5
  10.5 0.0 copy-done.7
  10.5 0.5 %filter.1.filter_ref = f32[64,8,256]{2,1,0:T(8,128)S(1)} custom-call(f32[8,4096]{1,0:T(8,128)S(1)} %copy-done.7, f32[64,256]{1,0:T(8,128)S(1)} %copy-done.5, bf16[768,256]{1,0:T(8,128)(2,1)S(1)} %copy-done.4), custom_call_target="tpu_custom_call" | custom-call | flops 402653184 | bytes 524288 | tf_op jit(solution)/shard_map/filter/pallas_call | solution.py:348
  11.0 13.9 %all-to-all-done.held_ref = f32[16,64,128]{2,1,0:T(8,128)S(1)} async-done(((f32[16,64,128]{2,1,0:T(8,128)}), f32[16,64,128]{2,1,0:T(8,128)S(1)}, u32[]{:S(2)}, u32[]{:S(2)}) %all-to-all-start) | async-done | bytes 524320 | tf_op jit(solution)/shard_map/all_to_all | solution.py:362
  24.9 2.3 %convolve.1 = (f32[16,64,128]{2,1,0:T(8,128)}, f32[1,64,8,256]{3,2,1,0:T(8,128)S(1)}, f32[1,64,8,256]{3,2,1,0:T(8,128)S(1)}) custom-call(f32[16,64,128]{2,1,0:T(8,128)S(1)} %all-to-all-done.held_ref, f32[64,8,256]{2,1,0:T(8,128)S(1)} %filter.1.filter_ref, f32[64,256]{1,0:T(8,128)S(1)} %copy-done.5, bf16[768,256]{1,0:T(8,128)(2,1)S(1)} %copy-done.4), custom_call_target="tpu_custom_call" | custom-call | flops 1610612736 | bytes 2097152 | tf_op jit(solution)/shard_map/convolve/pallas_call | solution.py:348
  27.3 4.1 %all-to-all-start.1 = ((f32[16,64,128]{2,1,0:T(8,128)}), f32[16,64,128]{2,1,0:T(8,128)S(1)}, u32[]{:S(2)}, u32[]{:S(2)}) async-start(f32[16,64,128]{2,1,0:T(8,128)} %get-tuple-element.12), calls=%async_computation.1 | async-start | bytes 1048576 | tf_op jit(solution)/shard_map/all_to_all | solution.py:362
  31.4 0.0 copy-start.1
  31.4 0.0 copy-start.2
  31.4 0.0 copy-start.3
  31.4 0.5 %lags.1 = f32[2,8,2048]{2,1,0:T(8,128)S(1)} custom-call(f32[1,64,8,256]{3,2,1,0:T(8,128)S(1)} %get-tuple-element.17.mixed_ref, f32[1,64,8,256]{3,2,1,0:T(8,128)S(1)} %get-tuple-element.18.upstream_ref, f32[64,256]{1,0:T(8,128)S(1)} %copy-done.5, bf16[768,256]{1,0:T(8,128)(2,1)S(1)} %copy-done.4), custom_call_target="tpu_custom_call" | custom-call | flops 402653184 | bytes 524288 | tf_op jit(solution)/shard_map/lags/pallas_call | solution.py:348
  32.0 0.0 copy-start
  32.0 1.6 %collective-permute-start = (f32[8,2048]{1,0:T(8,128)S(1)}, f32[8,2048]{1,0:T(8,128)S(1)}, u32[]{:S(2)}, u32[]{:S(2)}) collective-permute-start(f32[8,2048]{1,0:T(8,128)S(1)} %slice_bitcast_fusion), channel_id=1, source_target_pairs={{0,16},{16,0},{1,17},{17,1},{2,18},{18,2},{3,19},{19,3},{4,20},{20... | collective-permute-start | bytes 196616 | tf_op jit(solution)/shard_map/ppermute | solution.py:411
  33.5 2.9 %collective-permute-done = f32[8,2048]{1,0:T(8,128)S(1)} collective-permute-done((f32[8,2048]{1,0:T(8,128)S(1)}, f32[8,2048]{1,0:T(8,128)S(1)}, u32[]{:S(2)}, u32[]{:S(2)}) %collective-permute-start) | collective-permute-done | bytes 65568 | tf_op jit(solution)/shard_map/ppermute | solution.py:411
  36.5 0.6 %fusion = f32[8,2048]{1,0:T(8,128)} fusion(f32[8,2048]{1,0:T(8,128)S(1)} %collective-permute-done, f32[2,8,2048]{2,1,0:T(8,128)S(1)} %lags.1), kind=kLoop, calls=%fused_computation.2 | loop fusion | flops 16384 | bytes 196608 | tf_op jit(solution)/shard_map/add | solution.py:411
  37.1 0.0 copy-start.6
  37.1 8.7 %all-to-all-done.1.home_ref = f32[16,64,128]{2,1,0:T(8,128)S(1)} async-done(((f32[16,64,128]{2,1,0:T(8,128)}), f32[16,64,128]{2,1,0:T(8,128)S(1)}, u32[]{:S(2)}, u32[]{:S(2)}) %all-to-all-start.1) | async-done | bytes 524320 | tf_op jit(solution)/shard_map/all_to_all | solution.py:362
  45.9 0.0 copy-done.1
  45.9 0.0 copy-done.2
  45.9 0.0 copy-done.3
  45.9 0.0 copy-done
  45.9 0.0 copy-done.6
  45.9 1.1 %outputs.1 = (f32[2,256,128]{2,1,0:T(8,128)}, f32[2,256,128]{2,1,0:T(8,128)}, f32[2,256,128]{2,1,0:T(8,128)}, f32[2,256,128]{2,1,0:T(8,128)}) custom-call(f32[2,256,128]{2,1,0:T(8,128)S(1)} %copy-done, f32[2,256,128]{2,1,0:T(8,128)S(1)} %copy-done.1, f32[2,256,128]{2,1,0:T(8,128)S(1)} %copy-done.2, f32[2,256,128]{2,1,0:T(8,128)S(1)} %copy-done.3, ...), custom_call_target="tpu_custom_call" | custom-call | flops 402653184 | bytes 524288 | tf_op jit(solution)/shard_map/outputs/pallas_call | solution.py:348
  (1 shorter events, 0.0 us)
Async XLA Ops:
  2.9 7.6 %copy-start.4 = (bf16[768,256]{1,0:T(8,128)(2,1)S(1)}, bf16[768,256]{1,0:T(8,128)(2,1)}, u32[]{:S(2)}) copy-start(bf16[768,256]{1,0:T(8,128)(2,1)} %constant.5.clone.matrix_ref) | copy-start | bytes 1179652
  2.9 7.6 %copy-start.5 = (f32[64,256]{1,0:T(8,128)S(1)}, f32[64,256]{1,0:T(8,128)}, u32[]{:S(2)}) copy-start(f32[64,256]{1,0:T(8,128)} %constant.4.clone.twist_ref) | copy-start | bytes 196612
  2.9 7.6 %copy-start.7 = (f32[8,4096]{1,0:T(8,128)S(1)}, f32[8,4096]{1,0:T(8,128)}, u32[]{:S(2)}) copy-start(f32[8,4096]{1,0:T(8,128)} %filter_ref.1) | copy-start | bytes 393220
  2.9 22.0 %all-to-all-start = ((f32[16,64,128]{2,1,0:T(8,128)}), f32[16,64,128]{2,1,0:T(8,128)S(1)}, u32[]{:S(2)}, u32[]{:S(2)}) async-start(f32[16,64,128]{2,1,0:T(8,128)} %gate.1), calls=%async_computation | async-start | bytes 1048576 | tf_op jit(solution)/shard_map/all_to_all | solution.py:362
  27.3 18.6 %all-to-all-start.1 = ((f32[16,64,128]{2,1,0:T(8,128)}), f32[16,64,128]{2,1,0:T(8,128)S(1)}, u32[]{:S(2)}, u32[]{:S(2)}) async-start(f32[16,64,128]{2,1,0:T(8,128)} %get-tuple-element.12), calls=%async_computation.1 | async-start | bytes 1048576 | tf_op jit(solution)/shard_map/all_to_all | solution.py:362
  31.4 14.5 %copy-start.1 = (f32[2,256,128]{2,1,0:T(8,128)S(1)}, f32[2,256,128]{2,1,0:T(8,128)}, u32[]{:S(2)}) copy-start(f32[2,256,128]{2,1,0:T(8,128)} %key_ref.1) | copy-start | bytes 786436
  31.4 14.5 %copy-start.2 = (f32[2,256,128]{2,1,0:T(8,128)S(1)}, f32[2,256,128]{2,1,0:T(8,128)}, u32[]{:S(2)}) copy-start(f32[2,256,128]{2,1,0:T(8,128)} %value_ref.1) | copy-start | bytes 786436
  31.4 14.5 %copy-start.3 = (f32[2,256,128]{2,1,0:T(8,128)S(1)}, f32[2,256,128]{2,1,0:T(8,128)}, u32[]{:S(2)}) copy-start(f32[2,256,128]{2,1,0:T(8,128)} %cotangent_ref.1) | copy-start | bytes 786436
  32.0 13.9 %copy-start = (f32[2,256,128]{2,1,0:T(8,128)S(1)}, f32[2,256,128]{2,1,0:T(8,128)}, u32[]{:S(2)}) copy-start(f32[2,256,128]{2,1,0:T(8,128)} %query_ref.1) | copy-start | bytes 786436
  32.0 4.5 %collective-permute-start = (f32[8,2048]{1,0:T(8,128)S(1)}, f32[8,2048]{1,0:T(8,128)S(1)}, u32[]{:S(2)}, u32[]{:S(2)}) collective-permute-start(f32[8,2048]{1,0:T(8,128)S(1)} %slice_bitcast_fusion), channel_id=1, source_target_pairs={{0,16},{16,0},{1,17},{17,1},{2,18},{18,2},{3,19},{19,3},{4,20},{20... | collective-permute-start | bytes 196616 | tf_op jit(solution)/shard_map/ppermute | solution.py:411
  37.1 8.8 %copy-start.6 = (f32[128]{0:T(128)S(1)}, f32[128]{0:T(128)}, u32[]{:S(2)}) copy-start(f32[128]{0:T(128)} %param.12) | copy-start | bytes 1540

commit v7 on v2

--- a/solution.py
+++ b/solution.py
@@ -134,22 +134,56 @@
     )
 
 
-def gate_kernel(query_hbm, key_hbm, value_hbm, cotangent_hbm, mixed_ref, upstream_ref, held, sems):
-    shards, batch, channels, tokens = mixed_ref.shape
+def is_low(shards):
+    return lax.axis_index("seq") < shards // 2
+
+
+def block_rows(sequence, piece, pieces, channels, part=None):
+    first = (sequence * pieces + piece) * 2 * channels
+    if part is None:
+        return slice(first, first + 2 * channels)
+    return slice(first + part * channels, first + (part + 1) * channels)
+
+
+def gate_kernel(
+    query_hbm, key_hbm, value_hbm, cotangent_hbm, own_hbm, other_hbm, held, sent, sems, out_sems
+):
+    _, half, _, lanes = sent.shape
+    _, batch, tokens, all_channels = held.shape
+    channels, pieces = all_channels // (2 * half), tokens // lanes
+    low = is_low(2 * half)
     sources = (key_hbm, value_hbm, cotangent_hbm, query_hbm)
 
     def copy(b, i):
         return pltpu.make_async_copy(sources[i].at[b], held.at[i, b], sems.at[i, b])
 
-    for i in range(4):
-        for b in range(batch):
+    def send(kind):
+        return pltpu.make_async_copy(
+            sent.at[kind], (own_hbm, other_hbm)[kind], out_sems.at[kind]
+        )
+
+    def put(kind, b, product):
+        columns = jnp.transpose(product).reshape(2, half, channels, tokens)
+        for piece in range(pieces):
+            for part in range(2):
+                at = block_rows(b, piece, pieces, channels, part)
+                sent[kind, :, at] = columns[part, :, :, piece * lanes : (piece + 1) * lanes]
+
+    for b in range(batch):
+        for i in range(4):
             copy(b, i).start()
-    for kind, sent in enumerate((mixed_ref, upstream_ref)):
-        for b in range(batch):
-            copy(b, 2 * kind).wait()
-            copy(b, 2 * kind + 1).wait()
-            product = held[2 * kind, b] * held[2 * kind + 1, b]
-            sent[:, b] = jnp.transpose(product).reshape(shards, channels, tokens)
+    for b in range(batch):
+        for i in range(4):
+            copy(b, i).wait()
+        mixed, upstream = held[0, b] * held[1, b], held[2, b] * held[3, b]
+        put(0, b, jnp.where(low, mixed, upstream))
+    send(0).start()
+    for b in range(batch):
+        mixed, upstream = held[0, b] * held[1, b], held[2, b] * held[3, b]
+        put(1, b, jnp.where(low, upstream, mixed))
+    send(1).start()
+    send(0).wait()
+    send(1).wait()
 
 
 def transforms(twist_ref, matrix_ref, middle, turned):
@@ -180,125 +214,236 @@
             x = turned[part].reshape(-1, width)
             spec[part] = lane_dft(x, matrix_ref[...]).reshape(-1, channels, width)
 
-    def inverse(left, right, conjugate_left, emit):
+    def inverse(product, emit, kept):
         for part in chunks:
-            lr, li = left[part, :, :lanes], left[part, :, lanes:]
-            rr, ri = right[part, :, :lanes], right[part, :, lanes:]
-            if conjugate_left:
-                re, im = lr * rr + li * ri, li * rr - lr * ri
-            else:
-                re, im = lr * rr - li * ri, -(lr * ri + li * rr)
+            re, im = product(part)
             x = jnp.concatenate([re.reshape(-1, lanes), im.reshape(-1, lanes)], axis=1)
             turned[part] = lane_dft(x, matrix_ref[...]).reshape(-1, channels, width)
 
         def load(k1):
             return twist(k1, (turned[k1, :, :lanes], turned[k1, :, lanes:]))
 
-        across_rows(load, emit, count, count // 2, store, fetch)
+        across_rows(load, emit, count, kept, store, fetch)
 
     return forward, inverse
 
 
-def token_blocks(ref, lanes, pair, live):
-    pieces = ref.shape[3] // lanes
-
-    def where(n1):
-        at = n1 % pieces * lanes
-        return n1 // pieces, slice(at, at + lanes)
+def spectrum_part(ref, part):
+    lanes = ref.shape[-1] // 2
+    return ref[part, :, :lanes], ref[part, :, lanes:]
+
+
+def token_blocks(ref, pair, batch, channels, live):
+    pieces = ref.shape[1] // (2 * batch * channels)
+
+    def where(n1, sequence):
+        return n1 // pieces, block_rows(2 * pair + sequence, n1 % pieces, pieces, channels)
 
     def load(n1):
         if n1 >= live:
             return None
-        shard, span = where(n1)
-        return (ref[shard, 2 * pair, :, span], ref[shard, 2 * pair + 1, :, span])
+        return (ref[where(n1, 0)], ref[where(n1, 1)])
 
     def emit(n1, value):
-        shard, span = where(n1)
-        ref[shard, 2 * pair, :, span] = value[0]
-        ref[shard, 2 * pair + 1, :, span] = -value[1]
+        ref[where(n1, 0)] = value[0]
+        ref[where(n1, 1)] = -value[1]
 
     return load, emit
 
 
-def filter_kernel(filter_ref, twist_ref, matrix_ref, spec_ref, middle, turned):
-    length = filter_ref.shape[1]
+def filter_kernel(
+    shards, own_ref, other_ref, twist_ref, matrix_ref, near_ref, cross_ref, middle, turned
+):
+    length = own_ref.shape[1]
     lanes = twist_ref.shape[1] // 2
+    low = is_low(shards)
+    count = length // lanes
     forward, _ = transforms(twist_ref, matrix_ref, middle, turned)
 
-    def load(n1):
-        if n1 * lanes >= length:
-            return None
-        return (filter_ref[:, n1 * lanes : (n1 + 1) * lanes] * (0.5 / length), None)
-
-    forward(load, spec_ref)
-
-
-def convolve_kernel(
-    conjugate, held_ref, filter_ref, twist_ref, matrix_ref, back_ref, spec_ref, middle, turned
+    def load_half(first):
+        def load(n1):
+            if n1 >= count // 2:
+                return None
+            span = slice(first + n1 * lanes, first + (n1 + 1) * lanes)
+            own, other = own_ref[:, span], other_ref[:, span]
+            taps = jnp.concatenate([jnp.where(low, own, other), jnp.where(low, other, own)], axis=0)
+            return (taps * (1.0 / length), None)
+
+        return load
+
+    forward(load_half(0), near_ref)
+    forward(load_half(length // 2), cross_ref)
+    for k1 in range(count):
+        if k1 % 2 == 0:
+            cross_ref[k1] += near_ref[k1]
+        else:
+            cross_ref[k1] -= near_ref[k1]
+
+
+def near_kernel(
+    shards, own_ref, other_ref, filter_ref, twist_ref, matrix_ref,
+    back_ref, own_spec, other_spec, lag_mine, lag_theirs, middles, turneds,
 ):
-    count, width = twist_ref.shape
+    pairs, count, rows, width = own_spec.shape
+    channels, lanes = rows // 2, width // 2
+    low = is_low(shards)
+    sign = jnp.where(low, 1.0, -1.0)
+    scratch = [transforms(twist_ref, matrix_ref, middles.at[i], turneds.at[i]) for i in range(2)]
+    for pair in range(pairs):
+        own, other = own_spec.at[pair], other_spec.at[pair]
+        load, _ = token_blocks(own_ref, pair, 2 * pairs, channels, count // 2)
+        scratch[0][0](load, own)
+        load, _ = token_blocks(other_ref, pair, 2 * pairs, channels, count // 2)
+        scratch[1][0](load, other)
+
+        def result(part):
+            fr, fi = spectrum_part(filter_ref, part)
+            ar, ai = spectrum_part(own, part)
+            fi = sign * fi
+            return (fr * ar - fi * ai, -(fr * ai + fi * ar))
+
+        def lags(part):
+            ar, ai = spectrum_part(own, part)
+            br, bi = spectrum_part(other, part)
+            return (ar * br + ai * bi, sign * (ai * br - ar * bi))
+
+        def emit_lag(n1, value):
+            first, second = value[0][:channels], value[0][channels:]
+            span = slice(n1 * lanes, (n1 + 1) * lanes)
+            mine, theirs = jnp.where(low, first, second), jnp.where(low, second, first)
+            if pair == 0:
+                lag_mine[:, span] = mine
+                lag_theirs[:, span] = theirs
+            else:
+                lag_mine[:, span] += mine
+                lag_theirs[:, span] += theirs
+
+        _, emit = token_blocks(back_ref, pair, 2 * pairs, channels, count // 2)
+        scratch[0][1](result, emit, count // 2)
+        scratch[1][1](lags, emit_lag, count // 2)
+
+
+def cross_kernel(
+    shards, far_ref, other_spec, near_ref, cross_ref, twist_ref, matrix_ref,
+    back_ref, far_spec, middle, turned,
+):
+    pairs, count, rows, _ = other_spec.shape
+    sign = jnp.where(is_low(shards), -1.0, 1.0)
     forward, inverse = transforms(twist_ref, matrix_ref, middle, turned)
-    for pair in range(spec_ref.shape[0]):
-        load, _ = token_blocks(held_ref, width // 2, pair, count // 2)
-        _, emit = token_blocks(back_ref, width // 2, pair, count // 2)
-        forward(load, spec_ref.at[pair])
-        inverse(filter_ref, spec_ref.at[pair], conjugate, emit)
-
-
-def lag_kernel(scaling, mixed_ref, upstream_ref, twist_ref, matrix_ref, lag_ref, middle, turned):
-    lanes = twist_ref.shape[1] // 2
+    for pair in range(pairs):
+        far, other = far_spec.at[pair], other_spec.at[pair]
+        load, _ = token_blocks(far_ref, pair, 2 * pairs, rows // 2, count // 2)
+        forward(load, far)
+
+        def result(part):
+            nr, ni = spectrum_part(near_ref, part)
+            cr, ci = spectrum_part(cross_ref, part)
+            br, bi = spectrum_part(other, part)
+            gr, gi = spectrum_part(far, part)
+            ni, ci = sign * ni, sign * ci
+            return (
+                nr * br - ni * bi + (cr * gr - ci * gi),
+                -(nr * bi + ni * br + (cr * gi + ci * gr)),
+            )
+
+        _, emit = token_blocks(back_ref, pair, 2 * pairs, rows // 2, count // 2)
+        inverse(result, emit, count // 2)
+
+
+def lag_kernel(
+    shards, scaling, own_spec, far_spec, mine_ref, theirs_ref, twist_ref, matrix_ref,
+    lag_ref, middle, turned,
+):
+    pairs, count, rows, width = own_spec.shape
+    channels, lanes = rows // 2, width // 2
     groups, _, share = lag_ref.shape
+    low = is_low(shards)
+    sign = jnp.where(low, 1.0, -1.0)
     group = lax.axis_index("batch")
     _, inverse = transforms(twist_ref, matrix_ref, middle, turned)
-    for pair in range(mixed_ref.shape[0]):
+    for pair in range(pairs):
+
+        def mine(ref, part):
+            x = jnp.where(low, ref[pair, part, :channels], ref[pair, part, channels:])
+            return x[..., :lanes], x[..., lanes:]
+
+        def lags(part):
+            ar, ai = mine(own_spec, part)
+            gr, gi = mine(far_spec, part)
+            return (ar * gr + ai * gi, sign * (ai * gr - ar * gi))
 
         def emit(n1, value):
-            at = n1 * lanes
+            total = value[0]
+            if n1 >= count // 2:
+                at = (n1 - count // 2) * lanes
+                if pair == 0:
+                    total += mine_ref[:, at : at + lanes] + theirs_ref[:, at : at + lanes]
+            else:
+                at = (n1 + count // 2) * lanes
             slot = lax.rem(at // share - group + groups, groups)
             span = slice(at % share, at % share + lanes)
             if pair == 0:
-                lag_ref[slot, :, span] = value[0] * scaling
+                lag_ref[slot, :, span] = total * scaling
             else:
-                lag_ref[slot, :, span] += value[0] * scaling
-
-        inverse(mixed_ref.at[pair], upstream_ref.at[pair], True, emit)
+                lag_ref[slot, :, span] += total * scaling
+
+        inverse(lags, emit, count)
 
 
 def output_kernel(
-    query_ref, key_ref, value_ref, cotangent_ref, skip_ref, convolved_ref, back_ref,
-    output_ref, query_grad_ref, key_grad_ref, value_grad_ref,
+    query_ref, key_ref, value_ref, cotangent_ref, skip_ref, own_ref, other_ref, *refs
 ):
-    shards, batch, channels, tokens = convolved_ref.shape
+    *results, ready, out_sems = refs
+    half, _, lanes = own_ref.shape
+    batch, tokens, all_channels = query_ref.shape
+    channels, pieces = all_channels // (2 * half), tokens // lanes
+    low = is_low(2 * half)
     skip = skip_ref[...]
 
-    def rows(ref, b):
-        return jnp.transpose(ref[:, b].reshape(shards * channels, tokens))
+    def columns(ref, b):
+        pieces_of = []
+        for piece in range(pieces):
+            parts = [
+                ref[:, block_rows(b, piece, pieces, channels, part)].reshape(half * channels, lanes)
+                for part in range(2)
+            ]
+            pieces_of.append(jnp.transpose(jnp.concatenate(parts, axis=0)))
+        return jnp.concatenate(pieces_of, axis=0)
+
+    def finish(i, b):
+        return pltpu.make_async_copy(ready.at[i, b], results[i].at[b], out_sems.at[i, b])
 
     for b in range(batch):
         query, key, value, cotangent = query_ref[b], key_ref[b], value_ref[b], cotangent_ref[b]
-        hidden = rows(convolved_ref, b) + skip * (key * value)
-        output_ref[b] = query * hidden
-        query_grad_ref[b] = cotangent * hidden
-        mixed_grad = rows(back_ref, b) + skip * (cotangent * query)
-        key_grad_ref[b] = mixed_grad * value
-        value_grad_ref[b] = mixed_grad * key
-
-
-def exchange(blocks):
-    return lax.all_to_all(blocks, "seq", split_axis=0, concat_axis=0, tiled=True)
+        own, other = columns(own_ref, b), columns(other_ref, b)
+        hidden = jnp.where(low, own, other) + skip * (key * value)
+        ready[0, b] = query * hidden
+        finish(0, b).start()
+        ready[1, b] = cotangent * hidden
+        finish(1, b).start()
+        mixed_grad = jnp.where(low, other, own) + skip * (cotangent * query)
+        ready[2, b] = mixed_grad * value
+        finish(2, b).start()
+        ready[3, b] = mixed_grad * key
+        finish(3, b).start()
+    for b in range(batch):
+        for i in range(4):
+            finish(i, b).wait()
 
 
 def per_device(query_gate, key_gate, value_input, filters, skip_gain, cotangent, *, shards, groups):
     batch, tokens, all_channels = query_gate.shape
     channels, length = filters.shape
-    lanes = 128 if 2 * length // 128 <= 64 else tokens
-    count = 2 * length // lanes
+    lanes = 128 if length // 128 <= 64 else tokens
+    count, half, pairs = length // lanes, shards // 2, batch // 2
     twist, matrix = tables(count, lanes)
-
-    lane_work = 2 * 3 * count * channels * (2 * lanes) ** 2
+    lane_work = 2 * 3 * count * 2 * channels * (2 * lanes) ** 2
 
     def of(*shape):
         return jax.ShapeDtypeStruct(shape, jnp.float32)
+
+    def vmem(*shape):
+        return pltpu.VMEM(shape, jnp.float32)
 
     def call(kernel, name, stages, out_shape, scratch, *arrays, **options):
         return pl.pallas_call(
@@ -314,53 +459,78 @@
             **options,
         )(*arrays)
 
-    swap = of(shards, batch, channels, tokens)
-    spectrum = of(batch // 2, count, channels, 2 * lanes)
-    work = [pltpu.VMEM((count, channels, 2 * lanes), jnp.float32)] * 2
-    mixed, upstream = call(
+    def within_half(blocks):
+        members = [list(range(first, first + half)) for first in (0, half)]
+        return lax.all_to_all(
+            blocks, "seq", split_axis=0, concat_axis=0, tiled=True, axis_index_groups=members
+        )
+
+    def swap_halves(x):
+        return lax.ppermute(x, "seq", [(i, (i + half) % shards) for i in range(shards)])
+
+    rows = 2 * batch * channels * tokens // lanes
+    blocks = of(half, rows, lanes)
+    spectra = of(pairs, count, 2 * channels, 2 * lanes)
+    spectrum = of(count, 2 * channels, 2 * lanes)
+    work = [vmem(count, 2 * channels, 2 * lanes)] * 2
+    anywhere = pl.BlockSpec(memory_space=pl.ANY)
+
+    other_filters = swap_halves(filters)
+    own, other = call(
         gate_kernel,
-        "gate", 1,
-        (swap, swap),
+        "gate", 1, (blocks, blocks),
         [
-            pltpu.VMEM((4, batch, tokens, all_channels), jnp.float32),
+            vmem(4, batch, tokens, all_channels),
+            vmem(2, half, rows, lanes),
             pltpu.SemaphoreType.DMA((4, batch)),
+            pltpu.SemaphoreType.DMA((2,)),
         ],
         *(
             pltpu.with_memory_space_constraint(x, pltpu.HBM)
             for x in (query_gate, key_gate, value_input, cotangent)
         ),
         in_specs=[pl.BlockSpec(memory_space=pltpu.HBM)] * 4,
-    )
-    mixed = exchange(mixed)
-    upstream = exchange(upstream)
-    filter_spec = call(
-        filter_kernel, "filter", 2, of(count, channels, 2 * lanes), work, filters, twist, matrix
-    )
-    convolved, mixed_spec = call(
-        functools.partial(convolve_kernel, False),
-        "convolve", 4, (swap, spectrum), work, mixed, filter_spec, twist, matrix,
-    )
-    convolved = exchange(convolved)
-    filter_spec, mixed_spec = lax.optimization_barrier((filter_spec, mixed_spec))
-    back, upstream_spec = call(
-        functools.partial(convolve_kernel, True),
-        "correlate", 4, (swap, spectrum), work, upstream, filter_spec, twist, matrix,
-    )
-    back = exchange(back)
+        out_specs=(anywhere,) * 2,
+    )
+    own = within_half(own)
+    far = swap_halves(own)
+    other = within_half(other)
+    near_filter, cross_filter = call(
+        functools.partial(filter_kernel, shards),
+        "filter", 4, (spectrum, spectrum), work, filters, other_filters, twist, matrix,
+    )
+    own_back, own_spec, other_spec, lag_mine, lag_theirs = call(
+        functools.partial(near_kernel, shards),
+        "near", 8,
+        (blocks, spectra, spectra) + (of(channels, length // 2),) * 2,
+        [vmem(2, count, 2 * channels, 2 * lanes)] * 2,
+        own, other, near_filter, twist, matrix,
+    )
+    own_home = within_half(own_back)
+    lag_theirs = swap_halves(lag_theirs)
+    other_back, far_spec = call(
+        functools.partial(cross_kernel, shards),
+        "cross", 4, (blocks, spectra), work,
+        far, other_spec, near_filter, cross_filter, twist, matrix,
+    )
+    other_home = within_half(other_back)
     lag = call(
-        functools.partial(lag_kernel, 1.0 / (2.0 * length * math.sqrt(length))),
-        "lags", 2, of(groups, channels, length // groups), work,
-        mixed_spec, upstream_spec, twist, matrix,
+        functools.partial(lag_kernel, shards, 1.0 / (length * math.sqrt(length))),
+        "lags", 2, of(groups, channels, length // groups),
+        [vmem(count, channels, 2 * lanes)] * 2,
+        own_spec, far_spec, lag_mine, lag_theirs, twist, matrix,
     )
     filter_grad = lag[0]
     for step in range(1, groups):
-        pairs = [(source, (source + step) % groups) for source in range(groups)]
-        filter_grad = filter_grad + lax.ppermute(lag[step], "batch", pairs)
+        members = [(source, (source + step) % groups) for source in range(groups)]
+        filter_grad = filter_grad + lax.ppermute(lag[step], "batch", members)
     output, query_grad, key_grad, value_grad = call(
         output_kernel,
-        "outputs", 2, (of(*query_gate.shape),) * 4, [],
+        "outputs", 2, (of(*query_gate.shape),) * 4,
+        [vmem(4, batch, tokens, all_channels), pltpu.SemaphoreType.DMA((4, batch))],
         query_gate, key_gate, value_input, cotangent, skip_gain.reshape(1, all_channels),
-        convolved, back,
+        own_home, other_home,
+        out_specs=(anywhere,) * 4,
     )
     return (output, query_grad, key_grad, value_grad, filter_grad)
 

time: 64.5 us -> 62.9 us (0.975)
  starting transfers between devices: 12.4 us -> 27.8 us
  waiting for transfers between devices: 25.1 us -> 12 us
  blocking collectives: 17.4 us -> 11.2 us
  local copies, waits for them, and re-layouts: 0.04 us -> 1.89 us
    all_to_all x3, waiting for transfers between devices: 25.1 us -> 7.47 us  [within_half(): lax.all_to_all(blocks, 'seq', split_axis=0, concat_axis=0, tiled=True, ax...]
    all_to_all x3, starting transfers between devices: 10.9 us -> 19.9 us  [within_half(): lax.all_to_all(blocks, 'seq', split_axis=0, concat_axis=0, tiled=True, ax...]
    ppermute x1 -> x4, starting transfers between devices: 1.56 us -> 7.93 us  [the longest x3 6.37 us: swap_halves(): lax.ppermute(x, 'seq', [(i, (i + half) % shards) for i in range(shards)])]
    all_to_all x1, blocking collectives: 17.4 us -> 11.2 us  [within_half(): lax.all_to_all(blocks, 'seq', split_axis=0, concat_axis=0, tiled=True, ax...]
    ppermute x1 -> x4, waiting for transfers between devices: 0.01 us -> 4.53 us  [the longest x3 4.53 us: swap_halves(): lax.ppermute(x, 'seq', [(i, (i + half) % shards) for i in range(shards)])]
    unnamed x16 -> x20, local copies, waits for them, and re-layouts: 0.04 us -> 1.88 us
  transfers between devices with their start and end apart: 4 -> 7, of which waited for: 3 -> 4; matrix products, arithmetic and copies ran while one was open for 1% -> 1% of each run, Pallas kernels for 4% -> 7%
where the time goes in v7:
time: 62.9 us; the launch traced here: 62.3 us
  starting transfers between devices  27.8 us (44%)
  waiting for transfers between devices  12 us (19%)
  blocking collectives  11.2 us (18%)
  Pallas kernels  8.05 us (13%)
  local copies, waits for them, and re-layouts  1.89 us (3%)
  between operations  0.72 us (1%)
  other arithmetic  0.64 us (1%)
    all_to_all x3, starting transfers between devices, within_half(): lax.all_to_all(blocks, 'seq', split_axis=0, concat_axis=0, tiled=True, ax...  19.9 us
    all_to_all x1, blocking collectives, within_half(): lax.all_to_all(blocks, 'seq', split_axis=0, concat_axis=0, tiled=True, ax...  11.2 us
    pallas_call x6, Pallas kernels, call(): pl.pallas_call(kernel, out_shape=out_shape, scratch_shapes=scratch, compi...  8.05 us
    all_to_all x3, waiting for transfers between devices, within_half(): lax.all_to_all(blocks, 'seq', split_axis=0, concat_axis=0, tiled=True, ax...  7.47 us
    ppermute x3, starting transfers between devices, swap_halves(): lax.ppermute(x, 'seq', [(i, (i + half) % shards) for i in range(shards)])  6.37 us
    ppermute x3, waiting for transfers between devices, swap_halves(): lax.ppermute(x, 'seq', [(i, (i + half) % shards) for i in range(shards)])  4.53 us
    unnamed x20, local copies, waits for them, and re-layouts  1.88 us
    ppermute x1, starting transfers between devices, per_device(): filter_grad = filter_grad + lax.ppermute(lag[step], 'batch', members)  1.55 us
  transfers between devices with their start and end apart: 7, of which 4 were waited for; matrix products, arithmetic and copies ran while one was open for 1% of the time, Pallas kernels for 7%

profile of v7, /device:TPU:0, one launch (start us, length us, event | category | flops | bytes accessed | tf_op | source)
XLA Modules:
  0.0 62.3 jit_solution(10082591083530745053)
XLA Ops:
  0.6 2.3 %gate.1 = (f32[8,64,128]{2,1,0:T(8,128)S(1)}, f32[8,64,128]{2,1,0:T(8,128)}) custom-call(f32[2,256,128]{2,1,0:T(8,128)} %query_ref.1, f32[2,256,128]{2,1,0:T(8,128)} %key_ref.1, f32[2,256,128]{2,1,0:T(8,128)} %value_ref.1, f32[2,256,128]{2,1,0:T(8,128)} %cotangent_ref.1), custom_call_target="tpu_custom_call" | custom-call | flops 201326592 | bytes 262144 | tf_op jit(solution)/shard_map/gate/pallas_call | solution.py:449
  3.0 0.0 copy-start.7
  3.0 11.2 %all_to_all.20.own_ref = f32[8,64,128]{2,1,0:T(8,128)S(1)} all-to-all(f32[8,64,128]{2,1,0:T(8,128)S(1)} %get-tuple-element.20), channel_id=1, replica_groups={{0,1,2,3,4,5,6,7},{8,9,10,11,12,13,14,15},{16,17,18,19,20,21,22,23},{24..., dimensions={0} | all-to-all | bytes 524288 | tf_op jit(solution)/shard_map/all_to_all | solution.py:464
  14.2 0.0 copy-start.4
  14.2 0.0 copy-start.5
  14.2 3.5 %all-to-all-start.1 = ((f32[8,64,128]{2,1,0:T(8,128)}), f32[8,64,128]{2,1,0:T(8,128)S(1)}, u32[]{:S(2)}, u32[]{:S(2)}) async-start(f32[8,64,128]{2,1,0:T(8,128)} %get-tuple-element.21), calls=%async_computation.1 | async-start | bytes 524288 | tf_op jit(solution)/shard_map/all_to_all | solution.py:464
  17.8 0.0 copy-done.7
  17.8 2.7 %collective-permute-start = (f32[8,4096]{1,0:T(8,128)S(1)}, f32[8,4096]{1,0:T(8,128)S(1)}, u32[]{:S(2)}, u32[]{:S(2)}) collective-permute-start(f32[8,4096]{1,0:T(8,128)S(1)} %copy-done.7), channel_id=1, source_target_pairs={{0,8},{1,9},{2,10},{3,11},{4,12},{5,13},{6,14},{7,15},{8,0},{9,1},... | collective-permute-start | bytes 393224 | tf_op jit(solution)/shard_map/ppermute | solution.py:469
  20.4 0.3 collective-permute-start.1
  20.8 4.3 %collective-permute-done.other_ref = f32[8,4096]{1,0:T(8,128)S(1)} collective-permute-done((f32[8,4096]{1,0:T(8,128)S(1)}, f32[8,4096]{1,0:T(8,128)S(1)}, u32[]{:S(2)}, u32[]{:S(2)}) %collective-permute-start) | collective-permute-done | bytes 131104 | tf_op jit(solution)/shard_map/ppermute | solution.py:469
  25.1 0.0 copy-done.4
  25.1 0.0 copy-done.5
  25.1 0.7 %filter.1 = (f32[32,16,256]{2,1,0:T(8,128)S(1)}, f32[32,16,256]{2,1,0:T(8,128)S(1)}) custom-call(f32[8,4096]{1,0:T(8,128)S(1)} %copy-done.7, f32[8,4096]{1,0:T(8,128)S(1)} %collective-permute-done.other_ref, f32[32,256]{1,0:T(8,128)S(1)} %copy-done.5, bf16[768,256]{1,0:T(8,128)(2,1)S(1)} %copy-done.4), custom_call_target="tpu_custom_call" | custom-call | flops 805306368 | bytes 1048576 | tf_op jit(solution)/shard_map/filter/pallas_call | solution.py:449
  25.8 2.1 %all-to-all-done.1.other_ref = f32[8,64,128]{2,1,0:T(8,128)S(1)} async-done(((f32[8,64,128]{2,1,0:T(8,128)}), f32[8,64,128]{2,1,0:T(8,128)S(1)}, u32[]{:S(2)}, u32[]{:S(2)}) %all-to-all-start.1) | async-done | bytes 262176 | tf_op jit(solution)/shard_map/all_to_all | solution.py:464
  27.9 1.9 %near.1 = (f32[8,64,128]{2,1,0:T(8,128)}, f32[1,32,16,256]{3,2,1,0:T(8,128)S(1)}, f32[1,32,16,256]{3,2,1,0:T(8,128)S(1)}, f32[8,2048]{1,0:T(8,128)S(1)}, f32[8,2048]{1,0:T(8,128)S(1)}) custom-call(f32[8,64,128]{2,1,0:T(8,128)S(1)} %all_to_all.20.own_ref, f32[8,64,128]{2,1,0:T(8,128)S(1)} %all-to-all-done.1.other_ref, ...), custom_call_target="tpu_custom_call" | custom-call | flops 1610612736 | bytes 2097152 | tf_op jit(solution)/shard_map/near/pallas_call | solution.py:449
  29.8 0.0 copy-start.8
  29.8 0.8 %copy-done.8 = f32[1,32,16,256]{3,2,1,0:T(8,128)} copy-done((f32[1,32,16,256]{3,2,1,0:T(8,128)}, f32[1,32,16,256]{3,2,1,0:T(8,128)S(1)}, u32[]{:S(2)}) %copy-start.8) | copy-done | bytes 524312
  30.6 9.4 %all-to-all-start.2 = ((f32[8,64,128]{2,1,0:T(8,128)}), f32[8,64,128]{2,1,0:T(8,128)S(1)}, u32[]{:S(2)}, u32[]{:S(2)}) async-start(f32[8,64,128]{2,1,0:T(8,128)} %get-tuple-element.23), calls=%async_computation.2 | async-start | bytes 524288 | tf_op jit(solution)/shard_map/all_to_all | solution.py:464
  40.0 3.4 %collective-permute-start.2 = (f32[8,2048]{1,0:T(8,128)S(1)}, f32[8,2048]{1,0:T(8,128)S(1)}, u32[]{:S(2)}, u32[]{:S(2)}) collective-permute-start(f32[8,2048]{1,0:T(8,128)S(1)} %get-tuple-element.34), channel_id=1, source_target_pairs={{0,8},{1,9},{2,10},{3,11},{4,12},{5,13},{6,14},{7,15},{8,0},{9,1},... | collective-permute-start | bytes 196616 | tf_op jit(solution)/shard_map/ppermute | solution.py:469
  43.3 0.0 collective-permute-done.1.far_ref
  43.3 0.0 copy-start.9
  43.3 1.0 %copy-done.9 = f32[1,32,16,256]{3,2,1,0:T(8,128)S(1)} copy-done((f32[1,32,16,256]{3,2,1,0:T(8,128)S(1)}, f32[1,32,16,256]{3,2,1,0:T(8,128)}, u32[]{:S(2)}) %copy-start.9) | copy-done | bytes 524312
  44.4 1.6 %cross.1 = (f32[8,64,128]{2,1,0:T(8,128)}, f32[1,32,16,256]{3,2,1,0:T(8,128)S(1)}) custom-call(f32[8,64,128]{2,1,0:T(8,128)S(1)} %collective-permute-done.1.far_ref, f32[1,32,16,256]{3,2,1,0:T(8,128)S(1)} %copy-done.9, f32[32,16,256]{2,1,0:T(8,128)S(1)} %get-tuple-element.22.filter_ref.near_ref, f32[32,16,256]{2,1,0:T(8,128)S(1)} %get-tuple-element.25.cross_ref, ...), custom_call_target="tpu_custom_call" | custom-call | flops 805306368 | bytes 1048576 | tf_op jit(solution)/shard_map/cross/pallas_call | solution.py:449
  46.0 0.2 collective-permute-done.2.theirs_ref
  46.2 0.0 copy-start.2
  46.2 0.0 copy-start.3
  46.2 0.3 lags.1
  46.6 1.6 %collective-permute-start.3 = (f32[8,2048]{1,0:T(8,128)S(1)}, f32[8,2048]{1,0:T(8,128)S(1)}, u32[]{:S(2)}, u32[]{:S(2)}) collective-permute-start(f32[8,2048]{1,0:T(8,128)S(1)} %slice_bitcast_fusion), channel_id=1, source_target_pairs={{0,16},{16,0},{1,17},{17,1},{2,18},{18,2},{3,19},{19,3},{4,20},{20... | collective-permute-start | bytes 196616 | tf_op jit(solution)/shard_map/ppermute | solution.py:526
  48.1 0.0 all-to-all-done.2.own_ref
  48.1 0.0 copy-start
  48.1 0.0 copy-start.1
  48.1 6.9 %all-to-all-start.3 = ((f32[8,64,128]{2,1,0:T(8,128)}), f32[8,64,128]{2,1,0:T(8,128)S(1)}, u32[]{:S(2)}, u32[]{:S(2)}) async-start(f32[8,64,128]{2,1,0:T(8,128)} %get-tuple-element.26), calls=%async_computation.3 | async-start | bytes 524288 | tf_op jit(solution)/shard_map/all_to_all | solution.py:464
  55.1 0.0 collective-permute-done.3
  55.1 0.6 %fusion = f32[8,2048]{1,0:T(8,128)} fusion(f32[8,2048]{1,0:T(8,128)S(1)} %collective-permute-done.3, f32[2,8,2048]{2,1,0:T(8,128)S(1)} %lags.1), kind=kLoop, calls=%fused_computation.2 | loop fusion | flops 16384 | bytes 196608 | tf_op jit(solution)/shard_map/add | solution.py:526
  55.7 0.0 copy-start.6
  55.7 5.4 %all-to-all-done.3.other_ref = f32[8,64,128]{2,1,0:T(8,128)S(1)} async-done(((f32[8,64,128]{2,1,0:T(8,128)}), f32[8,64,128]{2,1,0:T(8,128)S(1)}, u32[]{:S(2)}, u32[]{:S(2)}) %all-to-all-start.3) | async-done | bytes 262176 | tf_op jit(solution)/shard_map/all_to_all | solution.py:464
  61.1 0.0 copy-done.2
  61.1 0.0 copy-done.3
  61.1 0.0 copy-done
  61.1 0.0 copy-done.1
  61.1 0.0 copy-done.6
  61.1 1.2 %outputs.1 = (f32[2,256,128]{2,1,0:T(8,128)}, f32[2,256,128]{2,1,0:T(8,128)}, f32[2,256,128]{2,1,0:T(8,128)}, f32[2,256,128]{2,1,0:T(8,128)}) custom-call(f32[2,256,128]{2,1,0:T(8,128)S(1)} %copy-done, f32[2,256,128]{2,1,0:T(8,128)S(1)} %copy-done.1, f32[2,256,128]{2,1,0:T(8,128)S(1)} %copy-done.2, f32[2,256,128]{2,1,0:T(8,128)S(1)} %copy-done.3, ...), custom_call_target="tpu_custom_call" | custom-call | flops 402653184 | bytes 524288 | tf_op jit(solution)/shard_map/outputs/pallas_call | solution.py:449
  (1 shorter events, 0.0 us)
Async XLA Ops:
  3.0 14.8 %copy-start.7 = (f32[8,4096]{1,0:T(8,128)S(1)}, f32[8,4096]{1,0:T(8,128)}, u32[]{:S(2)}) copy-start(f32[8,4096]{1,0:T(8,128)} %own_ref.1) | copy-start | bytes 393220
  14.2 10.8 %copy-start.4 = (bf16[768,256]{1,0:T(8,128)(2,1)S(1)}, bf16[768,256]{1,0:T(8,128)(2,1)}, u32[]{:S(2)}) copy-start(bf16[768,256]{1,0:T(8,128)(2,1)} %constant.5.clone.matrix_ref) | copy-start | bytes 1179652
  14.2 10.8 %copy-start.5 = (f32[32,256]{1,0:T(8,128)S(1)}, f32[32,256]{1,0:T(8,128)}, u32[]{:S(2)}) copy-start(f32[32,256]{1,0:T(8,128)} %constant.4.clone.twist_ref) | copy-start | bytes 98308
  14.2 13.6 %all-to-all-start.1 = ((f32[8,64,128]{2,1,0:T(8,128)}), f32[8,64,128]{2,1,0:T(8,128)S(1)}, u32[]{:S(2)}, u32[]{:S(2)}) async-start(f32[8,64,128]{2,1,0:T(8,128)} %get-tuple-element.21), calls=%async_computation.1 | async-start | bytes 524288 | tf_op jit(solution)/shard_map/all_to_all | solution.py:464
  17.8 7.3 %collective-permute-start = (f32[8,4096]{1,0:T(8,128)S(1)}, f32[8,4096]{1,0:T(8,128)S(1)}, u32[]{:S(2)}, u32[]{:S(2)}) collective-permute-start(f32[8,4096]{1,0:T(8,128)S(1)} %copy-done.7), channel_id=1, source_target_pairs={{0,8},{1,9},{2,10},{3,11},{4,12},{5,13},{6,14},{7,15},{8,0},{9,1},... | collective-permute-start | bytes 393224 | tf_op jit(solution)/shard_map/ppermute | solution.py:469
  20.4 22.9 %collective-permute-start.1 = (f32[8,64,128]{2,1,0:T(8,128)S(1)}, f32[8,64,128]{2,1,0:T(8,128)S(1)}, u32[]{:S(2)}, u32[]{:S(2)}) collective-permute-start(f32[8,64,128]{2,1,0:T(8,128)S(1)} %all_to_all.20.own_ref), channel_id=1, source_target_pairs={{0,8},{1,9},{2,10},{3,11},{4,12},{5,13},{6,14},{7,15},{8,0},{9,1},... | collective-permute-start | bytes 786440 | tf_op jit(solution)/shard_map/ppermute | solution.py:469
  29.8 0.8 %copy-start.8 = (f32[1,32,16,256]{3,2,1,0:T(8,128)}, f32[1,32,16,256]{3,2,1,0:T(8,128)S(1)}, u32[]{:S(2)}) copy-start(f32[1,32,16,256]{3,2,1,0:T(8,128)S(1)} %get-tuple-element.24.other_spec) | copy-start | bytes 1572868
  30.6 17.5 %all-to-all-start.2 = ((f32[8,64,128]{2,1,0:T(8,128)}), f32[8,64,128]{2,1,0:T(8,128)S(1)}, u32[]{:S(2)}, u32[]{:S(2)}) async-start(f32[8,64,128]{2,1,0:T(8,128)} %get-tuple-element.23), calls=%async_computation.2 | async-start | bytes 524288 | tf_op jit(solution)/shard_map/all_to_all | solution.py:464
  40.0 6.2 %collective-permute-start.2 = (f32[8,2048]{1,0:T(8,128)S(1)}, f32[8,2048]{1,0:T(8,128)S(1)}, u32[]{:S(2)}, u32[]{:S(2)}) collective-permute-start(f32[8,2048]{1,0:T(8,128)S(1)} %get-tuple-element.34), channel_id=1, source_target_pairs={{0,8},{1,9},{2,10},{3,11},{4,12},{5,13},{6,14},{7,15},{8,0},{9,1},... | collective-permute-start | bytes 196616 | tf_op jit(solution)/shard_map/ppermute | solution.py:469
  43.3 1.0 %copy-start.9 = (f32[1,32,16,256]{3,2,1,0:T(8,128)S(1)}, f32[1,32,16,256]{3,2,1,0:T(8,128)}, u32[]{:S(2)}) copy-start(f32[1,32,16,256]{3,2,1,0:T(8,128)} %copy-done.8) | copy-start | bytes 1572868
  46.2 14.9 %copy-start.2 = (f32[2,256,128]{2,1,0:T(8,128)S(1)}, f32[2,256,128]{2,1,0:T(8,128)}, u32[]{:S(2)}) copy-start(f32[2,256,128]{2,1,0:T(8,128)} %value_ref.1) | copy-start | bytes 786436
  46.2 14.9 %copy-start.3 = (f32[2,256,128]{2,1,0:T(8,128)S(1)}, f32[2,256,128]{2,1,0:T(8,128)}, u32[]{:S(2)}) copy-start(f32[2,256,128]{2,1,0:T(8,128)} %cotangent_ref.1) | copy-start | bytes 786436
  46.6 8.5 %collective-permute-start.3 = (f32[8,2048]{1,0:T(8,128)S(1)}, f32[8,2048]{1,0:T(8,128)S(1)}, u32[]{:S(2)}, u32[]{:S(2)}) collective-permute-start(f32[8,2048]{1,0:T(8,128)S(1)} %slice_bitcast_fusion), channel_id=1, source_target_pairs={{0,16},{16,0},{1,17},{17,1},{2,18},{18,2},{3,19},{19,3},{4,20},{20... | collective-permute-start | bytes 196616 | tf_op jit(solution)/shard_map/ppermute | solution.py:526
  48.1 13.0 %copy-start = (f32[2,256,128]{2,1,0:T(8,128)S(1)}, f32[2,256,128]{2,1,0:T(8,128)}, u32[]{:S(2)}) copy-start(f32[2,256,128]{2,1,0:T(8,128)} %query_ref.1) | copy-start | bytes 786436
  48.1 13.0 %copy-start.1 = (f32[2,256,128]{2,1,0:T(8,128)S(1)}, f32[2,256,128]{2,1,0:T(8,128)}, u32[]{:S(2)}) copy-start(f32[2,256,128]{2,1,0:T(8,128)} %key_ref.1) | copy-start | bytes 786436
  48.1 13.0 %all-to-all-start.3 = ((f32[8,64,128]{2,1,0:T(8,128)}), f32[8,64,128]{2,1,0:T(8,128)S(1)}, u32[]{:S(2)}, u32[]{:S(2)}) async-start(f32[8,64,128]{2,1,0:T(8,128)} %get-tuple-element.26), calls=%async_computation.3 | async-start | bytes 524288 | tf_op jit(solution)/shard_map/all_to_all | solution.py:464
  55.7 5.4 %copy-start.6 = (f32[128]{0:T(128)S(1)}, f32[128]{0:T(128)}, u32[]{:S(2)}) copy-start(f32[128]{0:T(128)} %param.12) | copy-start | bytes 1540

commit v8 on v7

--- a/solution.py
+++ b/solution.py
@@ -324,12 +324,22 @@
 
 
 def cross_kernel(
-    shards, far_ref, other_spec, near_ref, cross_ref, twist_ref, matrix_ref,
-    back_ref, far_spec, middle, turned,
+    shards, own_back, far_hbm, other_spec, near_ref, cross_ref, twist_ref, matrix_ref,
+    back_hbm, far_spec, far_ref, back, middle, turned, sems,
 ):
     pairs, count, rows, _ = other_spec.shape
+    half, block, _ = back.shape
     sign = jnp.where(is_low(shards), -1.0, 1.0)
     forward, inverse = transforms(twist_ref, matrix_ref, middle, turned)
+    own_copy = pltpu.make_async_copy(own_back, back_hbm.at[:, pl.ds(0, block)], sems.at[half])
+    copies = [
+        pltpu.make_async_copy(far_hbm.at[i], far_ref.at[i], sems.at[i]) for i in range(half)
+    ]
+    for copy in copies:
+        copy.start()
+    own_copy.start()
+    for copy in copies:
+        copy.wait()
     for pair in range(pairs):
         far, other = far_spec.at[pair], other_spec.at[pair]
         load, _ = token_blocks(far_ref, pair, 2 * pairs, rows // 2, count // 2)
@@ -346,8 +356,12 @@
                 -(nr * bi + ni * br + (cr * gi + ci * gr)),
             )
 
-        _, emit = token_blocks(back_ref, pair, 2 * pairs, rows // 2, count // 2)
+        _, emit = token_blocks(back, pair, 2 * pairs, rows // 2, count // 2)
         inverse(result, emit, count // 2)
+    done = pltpu.make_async_copy(back, back_hbm.at[:, pl.ds(block, block)], sems.at[half + 1])
+    done.start()
+    own_copy.wait()
+    done.wait()
 
 
 def lag_kernel(
@@ -391,22 +405,23 @@
 
 
 def output_kernel(
-    query_ref, key_ref, value_ref, cotangent_ref, skip_ref, own_ref, other_ref, *refs
+    query_ref, key_ref, value_ref, cotangent_ref, skip_ref, home_ref, *refs
 ):
     *results, ready, out_sems = refs
-    half, _, lanes = own_ref.shape
+    half, block, lanes = home_ref.shape
     batch, tokens, all_channels = query_ref.shape
     channels, pieces = all_channels // (2 * half), tokens // lanes
     low = is_low(2 * half)
     skip = skip_ref[...]
 
-    def columns(ref, b):
+    def columns(kind, b):
         pieces_of = []
         for piece in range(pieces):
-            parts = [
-                ref[:, block_rows(b, piece, pieces, channels, part)].reshape(half * channels, lanes)
-                for part in range(2)
-            ]
+            parts = []
+            for part in range(2):
+                at = block_rows(b, piece, pieces, channels, part)
+                at = slice(kind * block // 2 + at.start, kind * block // 2 + at.stop)
+                parts.append(home_ref[:, at].reshape(half * channels, lanes))
             pieces_of.append(jnp.transpose(jnp.concatenate(parts, axis=0)))
         return jnp.concatenate(pieces_of, axis=0)
 
@@ -415,7 +430,7 @@
 
     for b in range(batch):
         query, key, value, cotangent = query_ref[b], key_ref[b], value_ref[b], cotangent_ref[b]
-        own, other = columns(own_ref, b), columns(other_ref, b)
+        own, other = columns(0, b), columns(1, b)
         hidden = jnp.where(low, own, other) + skip * (key * value)
         ready[0, b] = query * hidden
         finish(0, b).start()
@@ -437,7 +452,6 @@
     lanes = 128 if length // 128 <= 64 else tokens
     count, half, pairs = length // lanes, shards // 2, batch // 2
     twist, matrix = tables(count, lanes)
-    lane_work = 2 * 3 * count * 2 * channels * (2 * lanes) ** 2
 
     def of(*shape):
         return jax.ShapeDtypeStruct(shape, jnp.float32)
@@ -445,16 +459,13 @@
     def vmem(*shape):
         return pltpu.VMEM(shape, jnp.float32)
 
-    def call(kernel, name, stages, out_shape, scratch, *arrays, **options):
+    def call(kernel, name, out_shape, scratch, *arrays, **options):
         return pl.pallas_call(
             kernel,
             out_shape=out_shape,
             scratch_shapes=scratch,
             compiler_params=pltpu.CompilerParams(vmem_limit_bytes=VMEM_BYTES),
-            cost_estimate=pl.CostEstimate(
-                flops=stages * lane_work, bytes_accessed=stages * 4 * batch * channels * length,
-                transcendentals=0,
-            ),
+            cost_estimate=pl.CostEstimate(flops=1, bytes_accessed=1, transcendentals=0),
             name=name,
             **options,
         )(*arrays)
@@ -474,11 +485,12 @@
     spectrum = of(count, 2 * channels, 2 * lanes)
     work = [vmem(count, 2 * channels, 2 * lanes)] * 2
     anywhere = pl.BlockSpec(memory_space=pl.ANY)
+    in_vmem = pl.BlockSpec(memory_space=pltpu.VMEM)
 
     other_filters = swap_halves(filters)
     own, other = call(
         gate_kernel,
-        "gate", 1, (blocks, blocks),
+        "gate", (blocks, blocks),
         [
             vmem(4, batch, tokens, all_channels),
             vmem(2, half, rows, lanes),
@@ -494,29 +506,33 @@
     )
     own = within_half(own)
     far = swap_halves(own)
-    other = within_half(other)
+    own_filters, other_filters, own = lax.optimization_barrier((filters, other_filters, own))
     near_filter, cross_filter = call(
         functools.partial(filter_kernel, shards),
-        "filter", 4, (spectrum, spectrum), work, filters, other_filters, twist, matrix,
-    )
+        "filter", (spectrum, spectrum), work, own_filters, other_filters, twist, matrix,
+    )
+    near_filter, other = lax.optimization_barrier((near_filter, other))
+    other = within_half(other)
     own_back, own_spec, other_spec, lag_mine, lag_theirs = call(
         functools.partial(near_kernel, shards),
-        "near", 8,
+        "near",
         (blocks, spectra, spectra) + (of(channels, length // 2),) * 2,
         [vmem(2, count, 2 * channels, 2 * lanes)] * 2,
         own, other, near_filter, twist, matrix,
     )
-    own_home = within_half(own_back)
     lag_theirs = swap_halves(lag_theirs)
-    other_back, far_spec = call(
+    back, far_spec = call(
         functools.partial(cross_kernel, shards),
-        "cross", 4, (blocks, spectra), work,
-        far, other_spec, near_filter, cross_filter, twist, matrix,
-    )
-    other_home = within_half(other_back)
+        "cross", (of(half, 2 * rows, lanes), spectra),
+        [vmem(half, rows, lanes)] * 2 + work + [pltpu.SemaphoreType.DMA((half + 2,))],
+        own_back, far, other_spec, near_filter, cross_filter, twist, matrix,
+        in_specs=[anywhere, anywhere] + [in_vmem] * 5,
+        out_specs=(anywhere, in_vmem),
+    )
+    home = within_half(back)
     lag = call(
         functools.partial(lag_kernel, shards, 1.0 / (length * math.sqrt(length))),
-        "lags", 2, of(groups, channels, length // groups),
+        "lags", of(groups, channels, length // groups),
         [vmem(count, channels, 2 * lanes)] * 2,
         own_spec, far_spec, lag_mine, lag_theirs, twist, matrix,
     )
@@ -526,10 +542,10 @@
         filter_grad = filter_grad + lax.ppermute(lag[step], "batch", members)
     output, query_grad, key_grad, value_grad = call(
         output_kernel,
-        "outputs", 2, (of(*query_gate.shape),) * 4,
+        "outputs", (of(*query_gate.shape),) * 4,
         [vmem(4, batch, tokens, all_channels), pltpu.SemaphoreType.DMA((4, batch))],
         query_gate, key_gate, value_input, cotangent, skip_gain.reshape(1, all_channels),
-        own_home, other_home,
+        home,
         out_specs=(anywhere,) * 4,
     )
     return (output, query_grad, key_grad, value_grad, filter_grad)

time: 62.9 us -> 55.8 us (0.89)
  waiting for transfers between devices: 12 us -> 25.5 us
  blocking collectives: 11.2 us -> 0 us
  starting transfers between devices: 27.8 us -> 20.4 us
  local copies, waits for them, and re-layouts: 1.89 us -> 0.05 us
    all_to_all x1 -> x0, blocking collectives: 11.2 us -> none  [within_half(): lax.all_to_all(blocks, 'seq', split_axis=0, concat_axis=0, tiled=True, ax...]
    all_to_all x3, starting transfers between devices: 19.9 us -> 13.7 us  [within_half(): lax.all_to_all(blocks, 'seq', split_axis=0, concat_axis=0, tiled=True, ax...]
    ppermute x3, waiting for transfers between devices: 4.53 us -> 9.85 us  [swap_halves(): lax.ppermute(x, 'seq', [(i, (i + half) % shards) for i in range(shards)])]
    all_to_all x3, waiting for transfers between devices: 7.47 us -> 12.8 us  [within_half(): lax.all_to_all(blocks, 'seq', split_axis=0, concat_axis=0, tiled=True, ax...]
    ppermute x1, waiting for transfers between devices: 0.01 us -> 2.87 us  [per_device(): filter_grad = filter_grad + lax.ppermute(lag[step], 'batch', members)]
    unnamed x20 -> x16, local copies, waits for them, and re-layouts: 1.88 us -> 0.05 us
    ppermute x3, starting transfers between devices: 6.37 us -> 5.12 us  [swap_halves(): lax.ppermute(x, 'seq', [(i, (i + half) % shards) for i in range(shards)])]
  transfers between devices with their start and end apart: 7 -> 7, of which waited for: 4 -> 6; matrix products, arithmetic and copies ran while one was open for 1% -> 1% of each run, Pallas kernels for 7% -> 7%
where the time goes in v8:
time: 55.8 us; the launch traced here: 55.4 us
  waiting for transfers between devices  25.5 us (46%)
  starting transfers between devices  20.4 us (37%)
  Pallas kernels  7.99 us (14%)
  between operations  0.79 us (1%)
  other arithmetic  0.64 us (1%)
    all_to_all x3, starting transfers between devices, within_half(): lax.all_to_all(blocks, 'seq', split_axis=0, concat_axis=0, tiled=True, ax...  13.7 us
    all_to_all x3, waiting for transfers between devices, within_half(): lax.all_to_all(blocks, 'seq', split_axis=0, concat_axis=0, tiled=True, ax...  12.8 us
    ppermute x3, waiting for transfers between devices, swap_halves(): lax.ppermute(x, 'seq', [(i, (i + half) % shards) for i in range(shards)])  9.85 us
    pallas_call x6, Pallas kernels, call(): pl.pallas_call(kernel, out_shape=out_shape, scratch_shapes=scratch, compi...  7.99 us
    ppermute x3, starting transfers between devices, swap_halves(): lax.ppermute(x, 'seq', [(i, (i + half) % shards) for i in range(shards)])  5.12 us
    ppermute x1, waiting for transfers between devices, per_device(): filter_grad = filter_grad + lax.ppermute(lag[step], 'batch', members)  2.87 us
    ppermute x1, starting transfers between devices, per_device(): filter_grad = filter_grad + lax.ppermute(lag[step], 'batch', members)  1.58 us
  transfers between devices with their start and end apart: 7, of which 6 were waited for; matrix products, arithmetic and copies ran while one was open for 1% of the time, Pallas kernels for 7%

profile of v8, /device:TPU:0, one launch (start us, length us, event | category | flops | bytes accessed | tf_op | source)
XLA Modules:
  0.0 55.4 jit_solution(11097257988976223533)
XLA Ops:
  0.6 0.0 copy-start.6
  0.6 2.3 %gate.1 = (f32[8,64,128]{2,1,0:T(8,128)}, f32[8,64,128]{2,1,0:T(8,128)}) custom-call(f32[2,256,128]{2,1,0:T(8,128)} %query_ref.1, f32[2,256,128]{2,1,0:T(8,128)} %key_ref.1, f32[2,256,128]{2,1,0:T(8,128)} %value_ref.1, f32[2,256,128]{2,1,0:T(8,128)} %cotangent_ref.1), custom_call_target="tpu_custom_call" | custom-call | flops 1 | bytes 1 | tf_op jit(solution)/shard_map/gate/pallas_call | solution.py:463
  2.9 0.0 copy-start
  3.0 0.0 copy-start.5
  3.0 5.4 %all-to-all-start = ((f32[8,64,128]{2,1,0:T(8,128)}), f32[8,64,128]{2,1,0:T(8,128)S(1)}, u32[]{:S(2)}, u32[]{:S(2)}) async-start(f32[8,64,128]{2,1,0:T(8,128)} %get-tuple-element.25), calls=%async_computation | async-start | bytes 524288 | tf_op jit(solution)/shard_map/all_to_all | solution.py:475
  8.4 0.0 copy-done.6
  8.4 2.7 %collective-permute-start = (f32[8,4096]{1,0:T(8,128)S(1)}, f32[8,4096]{1,0:T(8,128)S(1)}, u32[]{:S(2)}, u32[]{:S(2)}) collective-permute-start(f32[8,4096]{1,0:T(8,128)S(1)} %copy-done.6), channel_id=1, source_target_pairs={{0,8},{1,9},{2,10},{3,11},{4,12},{5,13},{6,14},{7,15},{8,0},{9,1},... | collective-permute-start | bytes 393224 | tf_op jit(solution)/shard_map/ppermute | solution.py:480
  11.0 4.3 %collective-permute-done.other_ref = f32[8,4096]{1,0:T(8,128)S(1)} collective-permute-done((f32[8,4096]{1,0:T(8,128)S(1)}, f32[8,4096]{1,0:T(8,128)S(1)}, u32[]{:S(2)}, u32[]{:S(2)}) %collective-permute-start) | collective-permute-done | bytes 131104 | tf_op jit(solution)/shard_map/ppermute | solution.py:480
  15.3 1.9 %all-to-all-done.own_ref = f32[8,64,128]{2,1,0:T(8,128)S(1)} async-done(((f32[8,64,128]{2,1,0:T(8,128)}), f32[8,64,128]{2,1,0:T(8,128)S(1)}, u32[]{:S(2)}, u32[]{:S(2)}) %all-to-all-start) | async-done | bytes 262176 | tf_op jit(solution)/shard_map/all_to_all | solution.py:475
  17.2 0.0 copy-done
  17.2 0.0 copy-done.5
  17.2 0.7 %filter.1 = (f32[32,16,256]{2,1,0:T(8,128)S(1)}, f32[32,16,256]{2,1,0:T(8,128)S(1)}) custom-call(f32[8,4096]{1,0:T(8,128)S(1)} %copy-done.6, f32[8,4096]{1,0:T(8,128)S(1)} %collective-permute-done.other_ref, f32[32,256]{1,0:T(8,128)S(1)} %copy-done.5, bf16[768,256]{1,0:T(8,128)(2,1)S(1)} %copy-done), custom_call_target="tpu_custom_call" | custom-call | flops 1 | bytes 1 | tf_op jit(solution)/shard_map/filter/pallas_call | solution.py:463
  17.9 4.8 %all-to-all-start.1 = ((f32[8,64,128]{2,1,0:T(8,128)}), f32[8,64,128]{2,1,0:T(8,128)S(1)}, u32[]{:S(2)}, u32[]{:S(2)}) async-start(f32[8,64,128]{2,1,0:T(8,128)} %get-tuple-element.31), calls=%async_computation.1 | async-start | bytes 524288 | tf_op jit(solution)/shard_map/all_to_all | solution.py:475
  22.8 2.4 %collective-permute-start.1 = (f32[8,64,128]{2,1,0:T(8,128)S(1)}, f32[8,64,128]{2,1,0:T(8,128)S(1)}, u32[]{:S(2)}, u32[]{:S(2)}) collective-permute-start(f32[8,64,128]{2,1,0:T(8,128)S(1)} %all-to-all-done.own_ref), channel_id=1, source_target_pairs={{0,8},{1,9},{2,10},{3,11},{4,12},{5,13},{6,14},{7,15},{8,0},{9,1},... | collective-permute-start | bytes 786440 | tf_op jit(solution)/shard_map/ppermute | solution.py:480
  25.2 7.6 %all-to-all-done.1.other_ref = f32[8,64,128]{2,1,0:T(8,128)S(1)} async-done(((f32[8,64,128]{2,1,0:T(8,128)}), f32[8,64,128]{2,1,0:T(8,128)S(1)}, u32[]{:S(2)}, u32[]{:S(2)}) %all-to-all-start.1) | async-done | bytes 262176 | tf_op jit(solution)/shard_map/all_to_all | solution.py:475
  32.7 1.4 %near.1 = (f32[8,64,128]{2,1,0:T(8,128)S(1)}, f32[1,32,16,256]{3,2,1,0:T(8,128)S(1)}, f32[1,32,16,256]{3,2,1,0:T(8,128)S(1)}, f32[8,2048]{1,0:T(8,128)S(1)}, f32[8,2048]{1,0:T(8,128)S(1)}) custom-call(f32[8,64,128]{2,1,0:T(8,128)S(1)} %all-to-all-done.own_ref, f32[8,64,128]{2,1,0:T(8,128)S(1)} %all-to-all-done.1.other_ref, ...), custom_call_target="tpu_custom_call" | custom-call | flops 1 | bytes 1 | tf_op jit(solution)/shard_map/near/pallas_call | solution.py:463
  34.2 0.1 collective-permute-start.2
  34.3 5.6 %collective-permute-done.1.far_hbm = f32[8,64,128]{2,1,0:T(8,128)S(1)} collective-permute-done((f32[8,64,128]{2,1,0:T(8,128)S(1)}, f32[8,64,128]{2,1,0:T(8,128)S(1)}, u32[]{:S(2)}, u32[]{:S(2)}) %collective-permute-start.1) | collective-permute-done | bytes 262176 | tf_op jit(solution)/shard_map/ppermute | solution.py:480
  39.8 2.0 %cross.1 = (f32[8,128,128]{2,1,0:T(8,128)}, f32[1,32,16,256]{3,2,1,0:T(8,128)S(1)}) custom-call(f32[8,64,128]{2,1,0:T(8,128)S(1)} %get-tuple-element.33.own_back, f32[8,64,128]{2,1,0:T(8,128)S(1)} %collective-permute-done.1.far_hbm, f32[1,32,16,256]{3,2,1,0:T(8,128)S(1)} %get-tuple-element.34.other_spec, ...), custom_call_target="tpu_custom_call" | custom-call | flops 1 | bytes 1 | tf_op jit(solution)/shard_map/cross/pallas_call | solution.py:463
  41.9 3.5 %all-to-all-start.2 = ((f32[8,128,128]{2,1,0:T(8,128)}), f32[8,128,128]{2,1,0:T(8,128)S(1)}, u32[]{:S(2)}, u32[]{:S(2)}) async-start(f32[8,128,128]{2,1,0:T(8,128)} %get-tuple-element.36), calls=%async_computation.2 | async-start | bytes 1048576 | tf_op jit(solution)/shard_map/all_to_all | solution.py:475
  45.4 0.0 collective-permute-done.2.theirs_ref
  45.4 0.0 copy-start.2
  45.4 0.0 copy-start.3
  45.4 0.0 copy-start.4
  45.4 0.3 lags.1
  45.8 0.0 copy-start.1
  45.8 1.6 %collective-permute-start.3 = (f32[8,2048]{1,0:T(8,128)S(1)}, f32[8,2048]{1,0:T(8,128)S(1)}, u32[]{:S(2)}, u32[]{:S(2)}) collective-permute-start(f32[8,2048]{1,0:T(8,128)S(1)} %slice_bitcast_fusion), channel_id=1, source_target_pairs={{0,16},{16,0},{1,17},{17,1},{2,18},{18,2},{3,19},{19,3},{4,20},{20... | collective-permute-start | bytes 196616 | tf_op jit(solution)/shard_map/ppermute | solution.py:542
  47.4 2.9 %collective-permute-done.3 = f32[8,2048]{1,0:T(8,128)S(1)} collective-permute-done((f32[8,2048]{1,0:T(8,128)S(1)}, f32[8,2048]{1,0:T(8,128)S(1)}, u32[]{:S(2)}, u32[]{:S(2)}) %collective-permute-start.3) | collective-permute-done | bytes 65568 | tf_op jit(solution)/shard_map/ppermute | solution.py:542
  50.3 0.6 %fusion = f32[8,2048]{1,0:T(8,128)} fusion(f32[8,2048]{1,0:T(8,128)S(1)} %collective-permute-done.3, f32[2,8,2048]{2,1,0:T(8,128)S(1)} %lags.1), kind=kLoop, calls=%fused_computation.2 | loop fusion | flops 16384 | bytes 196608 | tf_op jit(solution)/shard_map/add | solution.py:542
  50.9 0.0 copy-start.7
  50.9 3.3 %all-to-all-done.2.home_ref = f32[8,128,128]{2,1,0:T(8,128)S(1)} async-done(((f32[8,128,128]{2,1,0:T(8,128)}), f32[8,128,128]{2,1,0:T(8,128)S(1)}, u32[]{:S(2)}, u32[]{:S(2)}) %all-to-all-start.2) | async-done | bytes 524320 | tf_op jit(solution)/shard_map/all_to_all | solution.py:475
  54.2 0.0 copy-done.2
  54.2 0.0 copy-done.3
  54.2 0.0 copy-done.4
  54.2 0.0 copy-done.1
  54.2 0.0 copy-done.7
  54.2 1.2 %outputs.1 = (f32[2,256,128]{2,1,0:T(8,128)}, f32[2,256,128]{2,1,0:T(8,128)}, f32[2,256,128]{2,1,0:T(8,128)}, f32[2,256,128]{2,1,0:T(8,128)}) custom-call(f32[2,256,128]{2,1,0:T(8,128)S(1)} %copy-done.1, f32[2,256,128]{2,1,0:T(8,128)S(1)} %copy-done.2, f32[2,256,128]{2,1,0:T(8,128)S(1)} %copy-done.3, f32[2,256,128]{2,1,0:T(8,128)S(1)} %copy-done.4, ...), custom_call_target="tpu_custom_call" | custom-call | flops 1 | bytes 1 | tf_op jit(solution)/shard_map/outputs/pallas_call | solution.py:463
  (1 shorter events, 0.0 us)
Async XLA Ops:
  0.6 7.7 %copy-start.6 = (f32[8,4096]{1,0:T(8,128)S(1)}, f32[8,4096]{1,0:T(8,128)}, u32[]{:S(2)}) copy-start(f32[8,4096]{1,0:T(8,128)} %own_ref) | copy-start | bytes 393220
  2.9 14.3 %copy-start = (bf16[768,256]{1,0:T(8,128)(2,1)S(1)}, bf16[768,256]{1,0:T(8,128)(2,1)}, u32[]{:S(2)}) copy-start(bf16[768,256]{1,0:T(8,128)(2,1)} %constant.5.clone.matrix_ref) | copy-start | bytes 1179652
  3.0 14.3 %copy-start.5 = (f32[32,256]{1,0:T(8,128)S(1)}, f32[32,256]{1,0:T(8,128)}, u32[]{:S(2)}) copy-start(f32[32,256]{1,0:T(8,128)} %constant.4.clone.twist_ref) | copy-start | bytes 98308
  3.0 14.2 %all-to-all-start = ((f32[8,64,128]{2,1,0:T(8,128)}), f32[8,64,128]{2,1,0:T(8,128)S(1)}, u32[]{:S(2)}, u32[]{:S(2)}) async-start(f32[8,64,128]{2,1,0:T(8,128)} %get-tuple-element.25), calls=%async_computation | async-start | bytes 524288 | tf_op jit(solution)/shard_map/all_to_all | solution.py:475
  8.4 6.9 %collective-permute-start = (f32[8,4096]{1,0:T(8,128)S(1)}, f32[8,4096]{1,0:T(8,128)S(1)}, u32[]{:S(2)}, u32[]{:S(2)}) collective-permute-start(f32[8,4096]{1,0:T(8,128)S(1)} %copy-done.6), channel_id=1, source_target_pairs={{0,8},{1,9},{2,10},{3,11},{4,12},{5,13},{6,14},{7,15},{8,0},{9,1},... | collective-permute-start | bytes 393224 | tf_op jit(solution)/shard_map/ppermute | solution.py:480
  17.9 14.8 %all-to-all-start.1 = ((f32[8,64,128]{2,1,0:T(8,128)}), f32[8,64,128]{2,1,0:T(8,128)S(1)}, u32[]{:S(2)}, u32[]{:S(2)}) async-start(f32[8,64,128]{2,1,0:T(8,128)} %get-tuple-element.31), calls=%async_computation.1 | async-start | bytes 524288 | tf_op jit(solution)/shard_map/all_to_all | solution.py:475
  22.8 17.1 %collective-permute-start.1 = (f32[8,64,128]{2,1,0:T(8,128)S(1)}, f32[8,64,128]{2,1,0:T(8,128)S(1)}, u32[]{:S(2)}, u32[]{:S(2)}) collective-permute-start(f32[8,64,128]{2,1,0:T(8,128)S(1)} %all-to-all-done.own_ref), channel_id=1, source_target_pairs={{0,8},{1,9},{2,10},{3,11},{4,12},{5,13},{6,14},{7,15},{8,0},{9,1},... | collective-permute-start | bytes 786440 | tf_op jit(solution)/shard_map/ppermute | solution.py:480
  34.2 11.2 %collective-permute-start.2 = (f32[8,2048]{1,0:T(8,128)S(1)}, f32[8,2048]{1,0:T(8,128)S(1)}, u32[]{:S(2)}, u32[]{:S(2)}) collective-permute-start(f32[8,2048]{1,0:T(8,128)S(1)} %get-tuple-element.44), channel_id=1, source_target_pairs={{0,8},{1,9},{2,10},{3,11},{4,12},{5,13},{6,14},{7,15},{8,0},{9,1},... | collective-permute-start | bytes 196616 | tf_op jit(solution)/shard_map/ppermute | solution.py:480
  41.9 12.3 %all-to-all-start.2 = ((f32[8,128,128]{2,1,0:T(8,128)}), f32[8,128,128]{2,1,0:T(8,128)S(1)}, u32[]{:S(2)}, u32[]{:S(2)}) async-start(f32[8,128,128]{2,1,0:T(8,128)} %get-tuple-element.36), calls=%async_computation.2 | async-start | bytes 1048576 | tf_op jit(solution)/shard_map/all_to_all | solution.py:475
  45.4 8.8 %copy-start.2 = (f32[2,256,128]{2,1,0:T(8,128)S(1)}, f32[2,256,128]{2,1,0:T(8,128)}, u32[]{:S(2)}) copy-start(f32[2,256,128]{2,1,0:T(8,128)} %key_ref.1) | copy-start | bytes 786436
  45.4 8.7 %copy-start.3 = (f32[2,256,128]{2,1,0:T(8,128)S(1)}, f32[2,256,128]{2,1,0:T(8,128)}, u32[]{:S(2)}) copy-start(f32[2,256,128]{2,1,0:T(8,128)} %value_ref.1) | copy-start | bytes 786436
  45.4 8.7 %copy-start.4 = (f32[2,256,128]{2,1,0:T(8,128)S(1)}, f32[2,256,128]{2,1,0:T(8,128)}, u32[]{:S(2)}) copy-start(f32[2,256,128]{2,1,0:T(8,128)} %cotangent_ref.1) | copy-start | bytes 786436
  45.8 8.4 %copy-start.1 = (f32[2,256,128]{2,1,0:T(8,128)S(1)}, f32[2,256,128]{2,1,0:T(8,128)}, u32[]{:S(2)}) copy-start(f32[2,256,128]{2,1,0:T(8,128)} %query_ref.1) | copy-start | bytes 786436
  45.8 4.5 %collective-permute-start.3 = (f32[8,2048]{1,0:T(8,128)S(1)}, f32[8,2048]{1,0:T(8,128)S(1)}, u32[]{:S(2)}, u32[]{:S(2)}) collective-permute-start(f32[8,2048]{1,0:T(8,128)S(1)} %slice_bitcast_fusion), channel_id=1, source_target_pairs={{0,16},{16,0},{1,17},{17,1},{2,18},{18,2},{3,19},{19,3},{4,20},{20... | collective-permute-start | bytes 196616 | tf_op jit(solution)/shard_map/ppermute | solution.py:542
  50.9 3.3 %copy-start.7 = (f32[128]{0:T(128)S(1)}, f32[128]{0:T(128)}, u32[]{:S(2)}) copy-start(f32[128]{0:T(128)} %param.12) | copy-start | bytes 1540

commit v9 on v7

--- a/solution.py
+++ b/solution.py
@@ -146,9 +146,9 @@
 
 
 def gate_kernel(
-    query_hbm, key_hbm, value_hbm, cotangent_hbm, own_hbm, other_hbm, held, sent, sems, out_sems
+    query_hbm, key_hbm, value_hbm, cotangent_hbm, sent_hbm, held, sent, sems, out_sems
 ):
-    _, half, _, lanes = sent.shape
+    half, block, lanes = sent.shape
     _, batch, tokens, all_channels = held.shape
     channels, pieces = all_channels // (2 * half), tokens // lanes
     low = is_low(2 * half)
@@ -158,16 +158,15 @@
         return pltpu.make_async_copy(sources[i].at[b], held.at[i, b], sems.at[i, b])
 
     def send(kind):
-        return pltpu.make_async_copy(
-            sent.at[kind], (own_hbm, other_hbm)[kind], out_sems.at[kind]
-        )
+        span = pl.ds(kind * (block // 2), block // 2)
+        return pltpu.make_async_copy(sent.at[:, span], sent_hbm.at[:, span], out_sems.at[kind])
 
     def put(kind, b, product):
         columns = jnp.transpose(product).reshape(2, half, channels, tokens)
         for piece in range(pieces):
             for part in range(2):
-                at = block_rows(b, piece, pieces, channels, part)
-                sent[kind, :, at] = columns[part, :, :, piece * lanes : (piece + 1) * lanes]
+                at = block_rows(kind * batch + b, piece, pieces, channels, part)
+                sent[:, at] = columns[part, :, :, piece * lanes : (piece + 1) * lanes]
 
     for b in range(batch):
         for i in range(4):
@@ -233,11 +232,11 @@
     return ref[part, :, :lanes], ref[part, :, lanes:]
 
 
-def token_blocks(ref, pair, batch, channels, live):
-    pieces = ref.shape[1] // (2 * batch * channels)
+def token_blocks(ref, first, sequences, channels, live):
+    pieces = ref.shape[1] // (2 * sequences * channels)
 
     def where(n1, sequence):
-        return n1 // pieces, block_rows(2 * pair + sequence, n1 % pieces, pieces, channels)
+        return n1 // pieces, block_rows(first + sequence, n1 % pieces, pieces, channels)
 
     def load(n1):
         if n1 >= live:
@@ -281,19 +280,20 @@
 
 
 def near_kernel(
-    shards, own_ref, other_ref, filter_ref, twist_ref, matrix_ref,
-    back_ref, own_spec, other_spec, lag_mine, lag_theirs, middles, turneds,
+    shards, held_ref, filter_ref, twist_ref, matrix_ref,
+    back_hbm, own_spec, other_spec, lag_mine, lag_theirs, back, middles, turneds, sem,
 ):
     pairs, count, rows, width = own_spec.shape
-    channels, lanes = rows // 2, width // 2
+    channels, lanes, batch = rows // 2, width // 2, 2 * pairs
     low = is_low(shards)
     sign = jnp.where(low, 1.0, -1.0)
     scratch = [transforms(twist_ref, matrix_ref, middles.at[i], turneds.at[i]) for i in range(2)]
+    done = pltpu.make_async_copy(back, back_hbm, sem)
     for pair in range(pairs):
         own, other = own_spec.at[pair], other_spec.at[pair]
-        load, _ = token_blocks(own_ref, pair, 2 * pairs, channels, count // 2)
+        load, _ = token_blocks(held_ref, 2 * pair, 2 * batch, channels, count // 2)
         scratch[0][0](load, own)
-        load, _ = token_blocks(other_ref, pair, 2 * pairs, channels, count // 2)
+        load, _ = token_blocks(held_ref, batch + 2 * pair, 2 * batch, channels, count // 2)
         scratch[1][0](load, other)
 
         def result(part):
@@ -318,21 +318,32 @@
                 lag_mine[:, span] += mine
                 lag_theirs[:, span] += theirs
 
-        _, emit = token_blocks(back_ref, pair, 2 * pairs, channels, count // 2)
+        _, emit = token_blocks(back, 2 * pair, batch, channels, count // 2)
         scratch[0][1](result, emit, count // 2)
+        if pair == pairs - 1:
+            done.start()
         scratch[1][1](lags, emit_lag, count // 2)
+    done.wait()
 
 
 def cross_kernel(
-    shards, far_ref, other_spec, near_ref, cross_ref, twist_ref, matrix_ref,
-    back_ref, far_spec, middle, turned,
+    shards, far_hbm, other_spec, near_ref, cross_ref, twist_ref, matrix_ref,
+    back_hbm, far_spec, far_ref, back, middle, turned, sems,
 ):
     pairs, count, rows, _ = other_spec.shape
+    half = back.shape[0]
     sign = jnp.where(is_low(shards), -1.0, 1.0)
     forward, inverse = transforms(twist_ref, matrix_ref, middle, turned)
+    copies = [
+        pltpu.make_async_copy(far_hbm.at[i], far_ref.at[i], sems.at[i]) for i in range(half)
+    ]
+    for copy in copies:
+        copy.start()
+    for copy in copies:
+        copy.wait()
     for pair in range(pairs):
         far, other = far_spec.at[pair], other_spec.at[pair]
-        load, _ = token_blocks(far_ref, pair, 2 * pairs, rows // 2, count // 2)
+        load, _ = token_blocks(far_ref, 2 * pair, 2 * pairs, rows // 2, count // 2)
         forward(load, far)
 
         def result(part):
@@ -346,8 +357,11 @@
                 -(nr * bi + ni * br + (cr * gi + ci * gr)),
             )
 
-        _, emit = token_blocks(back_ref, pair, 2 * pairs, rows // 2, count // 2)
+        _, emit = token_blocks(back, 2 * pair, 2 * pairs, rows // 2, count // 2)
         inverse(result, emit, count // 2)
+    done = pltpu.make_async_copy(back, back_hbm, sems.at[half])
+    done.start()
+    done.wait()
 
 
 def lag_kernel(
@@ -403,10 +417,10 @@
     def columns(ref, b):
         pieces_of = []
         for piece in range(pieces):
-            parts = [
-                ref[:, block_rows(b, piece, pieces, channels, part)].reshape(half * channels, lanes)
-                for part in range(2)
-            ]
+            parts = []
+            for part in range(2):
+                at = block_rows(b, piece, pieces, channels, part)
+                parts.append(ref[:, at].reshape(half * channels, lanes))
             pieces_of.append(jnp.transpose(jnp.concatenate(parts, axis=0)))
         return jnp.concatenate(pieces_of, axis=0)
 
@@ -474,14 +488,15 @@
     spectrum = of(count, 2 * channels, 2 * lanes)
     work = [vmem(count, 2 * channels, 2 * lanes)] * 2
     anywhere = pl.BlockSpec(memory_space=pl.ANY)
+    in_vmem = pl.BlockSpec(memory_space=pltpu.VMEM)
 
     other_filters = swap_halves(filters)
-    own, other = call(
+    sent = call(
         gate_kernel,
-        "gate", 1, (blocks, blocks),
+        "gate", 1, of(half, 2 * rows, lanes),
         [
             vmem(4, batch, tokens, all_channels),
-            vmem(2, half, rows, lanes),
+            vmem(half, 2 * rows, lanes),
             pltpu.SemaphoreType.DMA((4, batch)),
             pltpu.SemaphoreType.DMA((2,)),
         ],
@@ -490,11 +505,10 @@
             for x in (query_gate, key_gate, value_input, cotangent)
         ),
         in_specs=[pl.BlockSpec(memory_space=pltpu.HBM)] * 4,
-        out_specs=(anywhere,) * 2,
-    )
-    own = within_half(own)
-    far = swap_halves(own)
-    other = within_half(other)
+        out_specs=anywhere,
+    )
+    held = within_half(sent)
+    far = swap_halves(held[:, :rows])
     near_filter, cross_filter = call(
         functools.partial(filter_kernel, shards),
         "filter", 4, (spectrum, spectrum), work, filters, other_filters, twist, matrix,
@@ -503,15 +517,21 @@
         functools.partial(near_kernel, shards),
         "near", 8,
         (blocks, spectra, spectra) + (of(channels, length // 2),) * 2,
-        [vmem(2, count, 2 * channels, 2 * lanes)] * 2,
-        own, other, near_filter, twist, matrix,
+        [vmem(half, rows, lanes)] + [vmem(2, count, 2 * channels, 2 * lanes)] * 2
+        + [pltpu.SemaphoreType.DMA],
+        held, near_filter, twist, matrix,
+        out_specs=(anywhere,) + (in_vmem,) * 4,
     )
     own_home = within_half(own_back)
+    lag_theirs, _ = lax.optimization_barrier((lag_theirs, far))
     lag_theirs = swap_halves(lag_theirs)
     other_back, far_spec = call(
         functools.partial(cross_kernel, shards),
-        "cross", 4, (blocks, spectra), work,
+        "cross", 4, (blocks, spectra),
+        [vmem(half, rows, lanes)] * 2 + work + [pltpu.SemaphoreType.DMA((half + 1,))],
         far, other_spec, near_filter, cross_filter, twist, matrix,
+        in_specs=[anywhere] + [in_vmem] * 5,
+        out_specs=(anywhere, in_vmem),
     )
     other_home = within_half(other_back)
     lag = call(

time: 62.9 us -> 53.1 us (0.84)
  blocking collectives: 11.2 us -> 0 us
  waiting for transfers between devices: 12 us -> 22.4 us
  starting transfers between devices: 27.8 us -> 18.6 us
    all_to_all x1 -> x0, blocking collectives: 11.2 us -> none  [within_half(): lax.all_to_all(blocks, 'seq', split_axis=0, concat_axis=0, tiled=True, ax...]
    all_to_all x3, waiting for transfers between devices: 7.47 us -> 14.3 us  [within_half(): lax.all_to_all(blocks, 'seq', split_axis=0, concat_axis=0, tiled=True, ax...]
    all_to_all x3, starting transfers between devices: 19.9 us -> 13.7 us  [within_half(): lax.all_to_all(blocks, 'seq', split_axis=0, concat_axis=0, tiled=True, ax...]
    ppermute x3, waiting for transfers between devices: 4.53 us -> 8.06 us  [swap_halves(): lax.ppermute(x, 'seq', [(i, (i + half) % shards) for i in range(shards)])]
    ppermute x3, starting transfers between devices: 6.37 us -> 3.29 us  [swap_halves(): lax.ppermute(x, 'seq', [(i, (i + half) % shards) for i in range(shards)])]
  transfers between devices with their start and end apart: 7 -> 7, of which waited for: 4 -> 4; matrix products, arithmetic and copies ran while one was open for 1% -> 1% of each run, Pallas kernels for 7% -> 9%
where the time goes in v9:
time: 53.1 us; the launch traced here: 52.6 us
  waiting for transfers between devices  22.4 us (42%)
  starting transfers between devices  18.6 us (35%)
  Pallas kernels  8.39 us (16%)
  local copies, waits for them, and re-layouts  1.9 us (4%)
  between operations  0.77 us (1%)
  other arithmetic  0.64 us (1%)
    all_to_all x3, waiting for transfers between devices, within_half(): lax.all_to_all(blocks, 'seq', split_axis=0, concat_axis=0, tiled=True, ax...  14.3 us
    all_to_all x3, starting transfers between devices, within_half(): lax.all_to_all(blocks, 'seq', split_axis=0, concat_axis=0, tiled=True, ax...  13.7 us
    pallas_call x6, Pallas kernels, call(): pl.pallas_call(kernel, out_shape=out_shape, scratch_shapes=scratch, compi...  8.39 us
    ppermute x3, waiting for transfers between devices, swap_halves(): lax.ppermute(x, 'seq', [(i, (i + half) % shards) for i in range(shards)])  8.06 us
    ppermute x3, starting transfers between devices, swap_halves(): lax.ppermute(x, 'seq', [(i, (i + half) % shards) for i in range(shards)])  3.29 us
    unnamed x20, local copies, waits for them, and re-layouts  1.88 us
    ppermute x1, starting transfers between devices, per_device(): filter_grad = filter_grad + lax.ppermute(lag[step], 'batch', members)  1.56 us
  transfers between devices with their start and end apart: 7, of which 4 were waited for; matrix products, arithmetic and copies ran while one was open for 1% of the time, Pallas kernels for 9%

profile of v9, /device:TPU:0, one launch (start us, length us, event | category | flops | bytes accessed | tf_op | source)
XLA Modules:
  0.0 52.6 jit_solution(17967768444801240937)
XLA Ops:
  0.6 2.3 %gate.1 = f32[8,128,128]{2,1,0:T(8,128)} custom-call(f32[2,256,128]{2,1,0:T(8,128)} %query_ref.1, f32[2,256,128]{2,1,0:T(8,128)} %key_ref.1, f32[2,256,128]{2,1,0:T(8,128)} %value_ref.1, f32[2,256,128]{2,1,0:T(8,128)} %cotangent_ref.1), custom_call_target="tpu_custom_call" | custom-call | flops 201326592 | bytes 262144 | tf_op jit(solution)/shard_map/gate/pallas_call | solution.py:463
  2.9 0.0 copy-start.7
  2.9 5.4 %all-to-all-start = ((f32[8,128,128]{2,1,0:T(8,128)}), f32[8,128,128]{2,1,0:T(8,128)S(1)}, u32[]{:S(2)}, u32[]{:S(2)}) async-start(f32[8,128,128]{2,1,0:T(8,128)} %gate.1), calls=%async_computation | async-start | bytes 1048576 | tf_op jit(solution)/shard_map/all_to_all | solution.py:478
  8.3 0.0 copy-done.7
  8.3 0.0 copy-start.4
  8.3 0.0 copy-start.5
  8.3 2.7 %collective-permute-start = (f32[8,4096]{1,0:T(8,128)S(1)}, f32[8,4096]{1,0:T(8,128)S(1)}, u32[]{:S(2)}, u32[]{:S(2)}) collective-permute-start(f32[8,4096]{1,0:T(8,128)S(1)} %copy-done.7), channel_id=1, source_target_pairs={{0,8},{1,9},{2,10},{3,11},{4,12},{5,13},{6,14},{7,15},{8,0},{9,1},... | collective-permute-start | bytes 393224 | tf_op jit(solution)/shard_map/ppermute | solution.py:483
  11.0 9.0 %all-to-all-done.held_ref = f32[8,128,128]{2,1,0:T(8,128)S(1)} async-done(((f32[8,128,128]{2,1,0:T(8,128)}), f32[8,128,128]{2,1,0:T(8,128)S(1)}, u32[]{:S(2)}, u32[]{:S(2)}) %all-to-all-start) | async-done | bytes 524320 | tf_op jit(solution)/shard_map/all_to_all | solution.py:478
  20.0 0.6 %collective-permute-start.1 = (f32[8,64,128]{2,1,0:T(8,128)S(1)}, f32[8,64,128]{2,1,0:T(8,128)S(1)}, u32[]{:S(2)}, u32[]{:S(2)}) collective-permute-start(f32[8,64,128]{2,1,0:T(8,128)S(1)} %slice.12), channel_id=1, source_target_pairs={{0,8},{1,9},{2,10},{3,11},{4,12},{5,13},{6,14},{7,15},{8,0},{9,1},... | collective-permute-start | bytes 786440 | tf_op jit(solution)/shard_map/ppermute | solution.py:483
  20.6 0.0 collective-permute-done.other_ref
  20.6 0.0 copy-done.4
  20.6 0.0 copy-done.5
  20.6 0.7 %filter.1 = (f32[32,16,256]{2,1,0:T(8,128)S(1)}, f32[32,16,256]{2,1,0:T(8,128)S(1)}) custom-call(f32[8,4096]{1,0:T(8,128)S(1)} %copy-done.7, f32[8,4096]{1,0:T(8,128)S(1)} %collective-permute-done.other_ref, f32[32,256]{1,0:T(8,128)S(1)} %copy-done.5, bf16[768,256]{1,0:T(8,128)(2,1)S(1)} %copy-done.4), custom_call_target="tpu_custom_call" | custom-call | flops 805306368 | bytes 1048576 | tf_op jit(solution)/shard_map/filter/pallas_call | solution.py:463
  21.4 1.9 %near.1 = (f32[8,64,128]{2,1,0:T(8,128)}, f32[1,32,16,256]{3,2,1,0:T(8,128)S(1)}, f32[1,32,16,256]{3,2,1,0:T(8,128)S(1)}, f32[8,2048]{1,0:T(8,128)S(1)}, f32[8,2048]{1,0:T(8,128)S(1)}) custom-call(f32[8,128,128]{2,1,0:T(8,128)S(1)} %all-to-all-done.held_ref, f32[32,16,256]{2,1,0:T(8,128)S(1)} %get-tuple-element.19.filter_ref.near_ref, ...), custom_call_target="tpu_custom_call" | custom-call | flops 1610612736 | bytes 2097152 | tf_op jit(solution)/shard_map/near/pallas_call | solution.py:463
  23.3 0.0 copy-start.8
  23.3 0.8 %copy-done.8 = f32[1,32,16,256]{3,2,1,0:T(8,128)} copy-done((f32[1,32,16,256]{3,2,1,0:T(8,128)}, f32[1,32,16,256]{3,2,1,0:T(8,128)S(1)}, u32[]{:S(2)}) %copy-start.8) | copy-done | bytes 524312
  24.1 4.8 %all-to-all-start.1 = ((f32[8,64,128]{2,1,0:T(8,128)}), f32[8,64,128]{2,1,0:T(8,128)S(1)}, u32[]{:S(2)}, u32[]{:S(2)}) async-start(f32[8,64,128]{2,1,0:T(8,128)} %get-tuple-element.20), calls=%async_computation.1 | async-start | bytes 524288 | tf_op jit(solution)/shard_map/all_to_all | solution.py:478
  28.8 5.7 %collective-permute-done.1.far_hbm = f32[8,64,128]{2,1,0:T(8,128)S(1)} collective-permute-done((f32[8,64,128]{2,1,0:T(8,128)S(1)}, f32[8,64,128]{2,1,0:T(8,128)S(1)}, u32[]{:S(2)}, u32[]{:S(2)}) %collective-permute-start.1) | collective-permute-done | bytes 262176 | tf_op jit(solution)/shard_map/ppermute | solution.py:483
  34.5 0.0 collective-permute-start.2
  34.5 0.0 copy-start.9
  34.5 1.0 %copy-done.9 = f32[1,32,16,256]{3,2,1,0:T(8,128)S(1)} copy-done((f32[1,32,16,256]{3,2,1,0:T(8,128)S(1)}, f32[1,32,16,256]{3,2,1,0:T(8,128)}, u32[]{:S(2)}) %copy-start.9) | copy-done | bytes 524312
  35.6 2.0 %cross.1 = (f32[8,64,128]{2,1,0:T(8,128)}, f32[1,32,16,256]{3,2,1,0:T(8,128)S(1)}) custom-call(f32[8,64,128]{2,1,0:T(8,128)S(1)} %collective-permute-done.1.far_hbm, f32[1,32,16,256]{3,2,1,0:T(8,128)S(1)} %copy-done.9, f32[32,16,256]{2,1,0:T(8,128)S(1)} %get-tuple-element.19.filter_ref.near_ref, f32[32,16,256]{2,1,0:T(8,128)S(1)} %get-tuple-element.22.cross_ref, ...), custom_call_target="tpu_custom_call" | custom-call | flops 805306368 | bytes 1048576 | tf_op jit(solution)/shard_map/cross/pallas_call | solution.py:463
  37.5 2.4 %collective-permute-done.2.theirs_ref = f32[8,2048]{1,0:T(8,128)S(1)} collective-permute-done((f32[8,2048]{1,0:T(8,128)S(1)}, f32[8,2048]{1,0:T(8,128)S(1)}, u32[]{:S(2)}, u32[]{:S(2)}) %collective-permute-start.2) | collective-permute-done | bytes 65568 | tf_op jit(solution)/shard_map/ppermute | solution.py:483
  39.9 0.0 copy-start.2
  39.9 0.0 copy-start.3
  39.9 0.3 lags.1
  40.3 1.6 %collective-permute-start.3 = (f32[8,2048]{1,0:T(8,128)S(1)}, f32[8,2048]{1,0:T(8,128)S(1)}, u32[]{:S(2)}, u32[]{:S(2)}) collective-permute-start(f32[8,2048]{1,0:T(8,128)S(1)} %slice_bitcast_fusion), channel_id=1, source_target_pairs={{0,16},{16,0},{1,17},{17,1},{2,18},{18,2},{3,19},{19,3},{4,20},{20... | collective-permute-start | bytes 196616 | tf_op jit(solution)/shard_map/ppermute | solution.py:546
  41.8 0.0 all-to-all-done.1.own_ref
  41.8 0.0 copy-start
  41.8 0.0 copy-start.1
  41.9 3.5 %all-to-all-start.2 = ((f32[8,64,128]{2,1,0:T(8,128)}), f32[8,64,128]{2,1,0:T(8,128)S(1)}, u32[]{:S(2)}, u32[]{:S(2)}) async-start(f32[8,64,128]{2,1,0:T(8,128)} %get-tuple-element.23), calls=%async_computation.2 | async-start | bytes 524288 | tf_op jit(solution)/shard_map/all_to_all | solution.py:478
  45.4 0.0 collective-permute-done.3
  45.4 0.6 %fusion = f32[8,2048]{1,0:T(8,128)} fusion(f32[8,2048]{1,0:T(8,128)S(1)} %collective-permute-done.3, f32[2,8,2048]{2,1,0:T(8,128)S(1)} %lags.1), kind=kLoop, calls=%fused_computation.2 | loop fusion | flops 16384 | bytes 196608 | tf_op jit(solution)/shard_map/add | solution.py:546
  46.1 0.0 copy-start.6
  46.1 5.3 %all-to-all-done.2.other_ref = f32[8,64,128]{2,1,0:T(8,128)S(1)} async-done(((f32[8,64,128]{2,1,0:T(8,128)}), f32[8,64,128]{2,1,0:T(8,128)S(1)}, u32[]{:S(2)}, u32[]{:S(2)}) %all-to-all-start.2) | async-done | bytes 262176 | tf_op jit(solution)/shard_map/all_to_all | solution.py:478
  51.4 0.0 copy-done.2
  51.4 0.0 copy-done.3
  51.4 0.0 copy-done
  51.4 0.0 copy-done.1
  51.4 0.0 copy-done.6
  51.4 1.2 %outputs.1 = (f32[2,256,128]{2,1,0:T(8,128)}, f32[2,256,128]{2,1,0:T(8,128)}, f32[2,256,128]{2,1,0:T(8,128)}, f32[2,256,128]{2,1,0:T(8,128)}) custom-call(f32[2,256,128]{2,1,0:T(8,128)S(1)} %copy-done, f32[2,256,128]{2,1,0:T(8,128)S(1)} %copy-done.1, f32[2,256,128]{2,1,0:T(8,128)S(1)} %copy-done.2, f32[2,256,128]{2,1,0:T(8,128)S(1)} %copy-done.3, ...), custom_call_target="tpu_custom_call" | custom-call | flops 402653184 | bytes 524288 | tf_op jit(solution)/shard_map/outputs/pallas_call | solution.py:463
  (2 shorter events, 0.0 us)
Async XLA Ops:
  2.9 5.4 %copy-start.7 = (f32[8,4096]{1,0:T(8,128)S(1)}, f32[8,4096]{1,0:T(8,128)}, u32[]{:S(2)}) copy-start(f32[8,4096]{1,0:T(8,128)} %own_ref.1) | copy-start | bytes 393220
  2.9 17.1 %all-to-all-start = ((f32[8,128,128]{2,1,0:T(8,128)}), f32[8,128,128]{2,1,0:T(8,128)S(1)}, u32[]{:S(2)}, u32[]{:S(2)}) async-start(f32[8,128,128]{2,1,0:T(8,128)} %gate.1), calls=%async_computation | async-start | bytes 1048576 | tf_op jit(solution)/shard_map/all_to_all | solution.py:478
  8.3 12.3 %copy-start.4 = (bf16[768,256]{1,0:T(8,128)(2,1)S(1)}, bf16[768,256]{1,0:T(8,128)(2,1)}, u32[]{:S(2)}) copy-start(bf16[768,256]{1,0:T(8,128)(2,1)} %constant.5.clone.matrix_ref) | copy-start | bytes 1179652
  8.3 12.3 %copy-start.5 = (f32[32,256]{1,0:T(8,128)S(1)}, f32[32,256]{1,0:T(8,128)}, u32[]{:S(2)}) copy-start(f32[32,256]{1,0:T(8,128)} %constant.4.clone.twist_ref) | copy-start | bytes 98308
  8.3 12.3 %collective-permute-start = (f32[8,4096]{1,0:T(8,128)S(1)}, f32[8,4096]{1,0:T(8,128)S(1)}, u32[]{:S(2)}, u32[]{:S(2)}) collective-permute-start(f32[8,4096]{1,0:T(8,128)S(1)} %copy-done.7), channel_id=1, source_target_pairs={{0,8},{1,9},{2,10},{3,11},{4,12},{5,13},{6,14},{7,15},{8,0},{9,1},... | collective-permute-start | bytes 393224 | tf_op jit(solution)/shard_map/ppermute | solution.py:483
  20.0 14.5 %collective-permute-start.1 = (f32[8,64,128]{2,1,0:T(8,128)S(1)}, f32[8,64,128]{2,1,0:T(8,128)S(1)}, u32[]{:S(2)}, u32[]{:S(2)}) collective-permute-start(f32[8,64,128]{2,1,0:T(8,128)S(1)} %slice.12), channel_id=1, source_target_pairs={{0,8},{1,9},{2,10},{3,11},{4,12},{5,13},{6,14},{7,15},{8,0},{9,1},... | collective-permute-start | bytes 786440 | tf_op jit(solution)/shard_map/ppermute | solution.py:483
  23.3 0.8 %copy-start.8 = (f32[1,32,16,256]{3,2,1,0:T(8,128)}, f32[1,32,16,256]{3,2,1,0:T(8,128)S(1)}, u32[]{:S(2)}) copy-start(f32[1,32,16,256]{3,2,1,0:T(8,128)S(1)} %get-tuple-element.21.other_spec) | copy-start | bytes 1572868
  24.1 17.8 %all-to-all-start.1 = ((f32[8,64,128]{2,1,0:T(8,128)}), f32[8,64,128]{2,1,0:T(8,128)S(1)}, u32[]{:S(2)}, u32[]{:S(2)}) async-start(f32[8,64,128]{2,1,0:T(8,128)} %get-tuple-element.20), calls=%async_computation.1 | async-start | bytes 524288 | tf_op jit(solution)/shard_map/all_to_all | solution.py:478
  34.5 5.4 %collective-permute-start.2 = (f32[8,2048]{1,0:T(8,128)S(1)}, f32[8,2048]{1,0:T(8,128)S(1)}, u32[]{:S(2)}, u32[]{:S(2)}) collective-permute-start(f32[8,2048]{1,0:T(8,128)S(1)} %get-tuple-element.32), channel_id=1, source_target_pairs={{0,8},{1,9},{2,10},{3,11},{4,12},{5,13},{6,14},{7,15},{8,0},{9,1},... | collective-permute-start | bytes 196616 | tf_op jit(solution)/shard_map/ppermute | solution.py:483
  34.5 1.0 %copy-start.9 = (f32[1,32,16,256]{3,2,1,0:T(8,128)S(1)}, f32[1,32,16,256]{3,2,1,0:T(8,128)}, u32[]{:S(2)}) copy-start(f32[1,32,16,256]{3,2,1,0:T(8,128)} %copy-done.8) | copy-start | bytes 1572868
  39.9 11.4 %copy-start.2 = (f32[2,256,128]{2,1,0:T(8,128)S(1)}, f32[2,256,128]{2,1,0:T(8,128)}, u32[]{:S(2)}) copy-start(f32[2,256,128]{2,1,0:T(8,128)} %value_ref.1) | copy-start | bytes 786436
  39.9 11.5 %copy-start.3 = (f32[2,256,128]{2,1,0:T(8,128)S(1)}, f32[2,256,128]{2,1,0:T(8,128)}, u32[]{:S(2)}) copy-start(f32[2,256,128]{2,1,0:T(8,128)} %cotangent_ref.1) | copy-start | bytes 786436
  40.3 5.1 %collective-permute-start.3 = (f32[8,2048]{1,0:T(8,128)S(1)}, f32[8,2048]{1,0:T(8,128)S(1)}, u32[]{:S(2)}, u32[]{:S(2)}) collective-permute-start(f32[8,2048]{1,0:T(8,128)S(1)} %slice_bitcast_fusion), channel_id=1, source_target_pairs={{0,16},{16,0},{1,17},{17,1},{2,18},{18,2},{3,19},{19,3},{4,20},{20... | collective-permute-start | bytes 196616 | tf_op jit(solution)/shard_map/ppermute | solution.py:546
  41.8 9.5 %copy-start = (f32[2,256,128]{2,1,0:T(8,128)S(1)}, f32[2,256,128]{2,1,0:T(8,128)}, u32[]{:S(2)}) copy-start(f32[2,256,128]{2,1,0:T(8,128)} %query_ref.1) | copy-start | bytes 786436
  41.8 9.5 %copy-start.1 = (f32[2,256,128]{2,1,0:T(8,128)S(1)}, f32[2,256,128]{2,1,0:T(8,128)}, u32[]{:S(2)}) copy-start(f32[2,256,128]{2,1,0:T(8,128)} %key_ref.1) | copy-start | bytes 786436
  41.9 9.5 %all-to-all-start.2 = ((f32[8,64,128]{2,1,0:T(8,128)}), f32[8,64,128]{2,1,0:T(8,128)S(1)}, u32[]{:S(2)}, u32[]{:S(2)}) async-start(f32[8,64,128]{2,1,0:T(8,128)} %get-tuple-element.23), calls=%async_computation.2 | async-start | bytes 524288 | tf_op jit(solution)/shard_map/all_to_all | solution.py:478
  46.1 5.4 %copy-start.6 = (f32[128]{0:T(128)S(1)}, f32[128]{0:T(128)}, u32[]{:S(2)}) copy-start(f32[128]{0:T(128)} %param.12) | copy-start | bytes 1540

commit v10 on v6

--- a/solution.py
+++ b/solution.py
@@ -134,36 +134,77 @@
     )
 
 
+def exchange_order(shards):
+    if shards < 8:
+        return list(range(shards))
+    steps = shards // 4
+    uses = np.zeros((shards, shards, 2, steps, 2), np.int32)
+    for a in range(shards):
+        for b in range(shards):
+            (za, ya), (zb, yb) = (a // 4, a // 2 % 2), (b // 4, b // 2 % 2)
+            for z in range(min(za, zb), max(za, zb)):
+                uses[a, b, ya, z, int(za > zb)] = 1
+    uses = uses.reshape(shards, shards, -1)
+    place, shift = np.arange(shards)[:, None], np.arange(1, shards)[None, :]
+
+    def load(order):
+        total = 0
+        for partner in ((place + shift) % shards, place ^ shift):
+            total += uses[order[place], order[partner]].sum(axis=0).max(axis=1).sum()
+        return int(total)
+
+    draw = np.random.RandomState(0)
+    order = 5 * np.arange(shards) % shards
+    least = load(order)
+    for _ in range(24000 // shards):
+        i, j = draw.randint(shards), draw.randint(shards)
+        order[[i, j]] = order[[j, i]]
+        now = load(order)
+        if now <= least:
+            least = now
+        else:
+            order[[i, j]] = order[[j, i]]
+    return [int(shard) for shard in order]
+
+
 def block_rows(kind, sequence, piece, batch, pieces, channels):
     first = ((kind * batch + sequence) * pieces + piece) * channels
     return slice(first, first + channels)
 
 
-def gate_kernel(batch, query_hbm, key_hbm, value_hbm, cotangent_hbm, sent_hbm, held, sent, sems, out_sems):
+def gate_kernel(order, query_hbm, key_hbm, value_hbm, cotangent_hbm, sent_hbm, held, sent, sems, out_sems):
     shards, rows, lanes = sent.shape
-    _, _, tokens, all_channels = held.shape
+    _, batch, tokens, all_channels = held.shape
     channels, pieces = all_channels // shards, tokens // lanes
     sources = (key_hbm, value_hbm, cotangent_hbm, query_hbm)
-
-    def copy(b, i):
-        return pltpu.make_async_copy(sources[i].at[b], held.at[i, b], sems.at[i, b])
+    parts = sems.shape[2]
+
+    def copy(b, i, part):
+        span = pl.ds(part * (tokens // parts), tokens // parts)
+        return pltpu.make_async_copy(
+            sources[i].at[b, span], held.at[i, b, span], sems.at[i, b, part]
+        )
 
     def send(kind):
         span = pl.ds(kind * (rows // 2), rows // 2)
         return pltpu.make_async_copy(sent.at[:, span], sent_hbm.at[:, span], out_sems.at[kind])
 
-    for i in range(4):
-        for b in range(batch):
-            copy(b, i).start()
     for kind in range(2):
         for b in range(batch):
-            copy(b, 2 * kind).wait()
-            copy(b, 2 * kind + 1).wait()
+            for part in range(parts):
+                copy(b, 2 * kind, part).start()
+                copy(b, 2 * kind + 1, part).start()
+    for kind in range(2):
+        for b in range(batch):
+            for part in range(parts):
+                copy(b, 2 * kind, part).wait()
+                copy(b, 2 * kind + 1, part).wait()
             columns = jnp.transpose(held[2 * kind, b] * held[2 * kind + 1, b])
             columns = columns.reshape(shards, channels, tokens)
             for piece in range(pieces):
                 at = block_rows(kind, b, piece, batch, pieces, channels)
-                sent[:, at] = columns[:, :, piece * lanes : (piece + 1) * lanes]
+                for place, shard in enumerate(order):
+                    sent[place, at] = columns[shard, :, piece * lanes : (piece + 1) * lanes]
         send(kind).start()
     for kind in range(2):
         send(kind).wait()
@@ -216,12 +257,12 @@
     return forward, inverse
 
 
-def token_blocks(ref, kind, pair, batch, channels, live):
+def token_blocks(ref, order, kind, pair, batch, channels, live):
     pieces = ref.shape[1] // (2 * batch * channels)
 
     def where(n1, sequence):
         at = block_rows(kind, 2 * pair + sequence, n1 % pieces, batch, pieces, channels)
-        return n1 // pieces, at
+        return order.index(n1 // pieces), at
 
     def load(n1):
         if n1 >= live:
@@ -249,7 +290,7 @@
 
 
 def convolve_kernel(
-    held_ref, filter_ref, twist_ref, matrix_ref, back_hbm, mixed_ref, upstream_ref,
+    order, held_ref, filter_ref, twist_ref, matrix_ref, back_hbm, mixed_ref, upstream_ref,
     back, middles, turneds, out_sems,
 ):
     pairs, count, channels, _ = mixed_ref.shape
@@ -265,10 +306,10 @@
 
     for pair in range(pairs):
         for kind in range(2):
-            load, _ = token_blocks(held_ref, kind, pair, 2 * pairs, channels, count // 2)
+            load, _ = token_blocks(held_ref, order, kind, pair, 2 * pairs, channels, count // 2)
             scratch[kind][0](load, kinds[kind].at[pair])
         for kind in range(2):
-            _, emit = token_blocks(back, kind, pair, 2 * pairs, channels, count // 2)
+            _, emit = token_blocks(back, order, kind, pair, 2 * pairs, channels, count // 2)
             scratch[kind][1](filter_ref, kinds[kind].at[pair], kind == 1, emit)
             if pair == pairs - 1:
                 send(kind).start()
@@ -296,7 +337,7 @@
 
 
 def output_kernel(
-    query_ref, key_ref, value_ref, cotangent_ref, skip_ref, home_ref, *refs
+    order, query_ref, key_ref, value_ref, cotangent_ref, skip_ref, home_ref, *refs
 ):
     *results, ready, out_sems = refs
     shards, _, lanes = home_ref.shape
@@ -305,13 +346,12 @@
     skip = skip_ref[...]
 
     def columns(kind, b):
-        parts = [
-            home_ref[:, block_rows(kind, b, piece, batch, pieces, channels)]
-            for piece in range(pieces)
-        ]
-        return jnp.concatenate(
-            [jnp.transpose(part.reshape(all_channels, lanes)) for part in parts], axis=0
-        )
+        turned = []
+        for piece in range(pieces):
+            at = block_rows(kind, b, piece, batch, pieces, channels)
+            blocks = [home_ref[order.index(shard), at] for shard in range(shards)]
+            turned.append(jnp.transpose(jnp.concatenate(blocks, axis=0)))
+        return jnp.concatenate(turned, axis=0)
 
     def finish(i, b):
         return pltpu.make_async_copy(ready.at[i, b], results[i].at[b], out_sems.at[i, b])
@@ -339,6 +379,7 @@
     lanes = 128 if 2 * length // 128 <= 64 else tokens
     count = 2 * length // lanes
     twist, matrix = tables(count, lanes)
+    order = exchange_order(shards)
     lane_work = 2 * 3 * count * channels * (2 * lanes) ** 2
 
     def of(*shape):
@@ -359,7 +400,9 @@
         )(*arrays)
 
     def exchange(blocks):
-        return lax.all_to_all(blocks, "seq", split_axis=0, concat_axis=0, tiled=True)
+        return lax.all_to_all(
+            blocks, "seq", split_axis=0, concat_axis=0, tiled=True, axis_index_groups=[order]
+        )
 
     rows = 2 * batch * channels * tokens // lanes
     swap = of(shards, rows, lanes)
@@ -368,12 +411,12 @@
     spectrum = of(batch // 2, count, channels, 2 * lanes)
     work = [pltpu.VMEM((count, channels, 2 * lanes), jnp.float32)] * 2
     sent = call(
-        functools.partial(gate_kernel, batch),
+        functools.partial(gate_kernel, order),
         "gate", 1, swap,
         [
             pltpu.VMEM((4, batch, tokens, all_channels), jnp.float32),
             pltpu.VMEM((shards, rows, lanes), jnp.float32),
-            pltpu.SemaphoreType.DMA((4, batch)),
+            pltpu.SemaphoreType.DMA((4, batch, 4)),
             pltpu.SemaphoreType.DMA((2,)),
         ],
         *(
@@ -388,7 +431,7 @@
         filter_kernel, "filter", 2, of(count, channels, 2 * lanes), work, filters, twist, matrix
     )
     back, mixed_spec, upstream_spec = call(
-        convolve_kernel,
+        functools.partial(convolve_kernel, order),
         "convolve", 8, (swap, spectrum, spectrum),
         [
             pltpu.VMEM((shards, rows, lanes), jnp.float32),
@@ -410,7 +453,7 @@
         pairs = [(source, (source + step) % groups) for source in range(groups)]
         filter_grad = filter_grad + lax.ppermute(lag[step], "batch", pairs)
     output, query_grad, key_grad, value_grad = call(
-        output_kernel,
+        functools.partial(output_kernel, order),
         "outputs", 2, (of(*query_gate.shape),) * 4,
         [
             pltpu.VMEM((4, batch, tokens, all_channels), jnp.float32),

time: 47.4 us -> 46.7 us (0.985)
  waiting for transfers between devices: 25.6 us -> 23.6 us
  starting transfers between devices: 13.2 us -> 14.2 us
    all_to_all x2, waiting for transfers between devices: 22.7 us -> 20.9 us  [exchange(): lax.all_to_all(blocks, 'seq', split_axis=0, concat_axis=0, tiled=True, ax...]
    all_to_all x2, starting transfers between devices: 11.6 us -> 12.7 us  [exchange(): lax.all_to_all(blocks, 'seq', split_axis=0, concat_axis=0, tiled=True, ax...]
where the time goes in v10:
time: 46.7 us; the launch traced here: 46.2 us
  waiting for transfers between devices  23.6 us (51%)
  starting transfers between devices  14.2 us (30%)
  Pallas kernels  6.83 us (15%)
  between operations  0.77 us (2%)
  other arithmetic  0.64 us (1%)
    all_to_all x2, waiting for transfers between devices, exchange(): lax.all_to_all(blocks, 'seq', split_axis=0, concat_axis=0, tiled=True, ax...  20.9 us
    all_to_all x2, starting transfers between devices, exchange(): lax.all_to_all(blocks, 'seq', split_axis=0, concat_axis=0, tiled=True, ax...  12.7 us
    pallas_call x5, Pallas kernels, call(): pl.pallas_call(kernel, out_shape=out_shape, scratch_shapes=scratch, compi...  6.83 us
    ppermute x1, waiting for transfers between devices, per_device(): filter_grad = filter_grad + lax.ppermute(lag[step], 'batch', pairs)  2.78 us
    ppermute x1, starting transfers between devices, per_device(): filter_grad = filter_grad + lax.ppermute(lag[step], 'batch', pairs)  1.55 us
  transfers between devices with their start and end apart: 3, of which 3 were waited for; matrix products, arithmetic and copies ran while one was open for 1% of the time, Pallas kernels for 2%

profile of v10, /device:TPU:0, one launch (start us, length us, event | category | flops | bytes accessed | tf_op | source)
XLA Modules:
  0.0 46.2 jit_solution(10689273966114692373)
XLA Ops:
  0.6 2.3 %gate.1 = f32[16,64,128]{2,1,0:T(8,128)} custom-call(f32[2,256,128]{2,1,0:T(8,128)} %query_ref.1, f32[2,256,128]{2,1,0:T(8,128)} %key_ref.1, f32[2,256,128]{2,1,0:T(8,128)} %value_ref.1, f32[2,256,128]{2,1,0:T(8,128)} %cotangent_ref.1), custom_call_target="tpu_custom_call" | custom-call | flops 201326592 | bytes 262144 | tf_op jit(solution)/shard_map/gate/pallas_call | solution.py:389
  3.0 0.0 copy-start.4
  3.0 0.0 copy-start.5
  3.0 0.0 copy-start.7
  3.0 8.0 %all-to-all-start = ((f32[16,64,128]{2,1,0:T(8,128)}), f32[16,64,128]{2,1,0:T(8,128)S(1)}, u32[]{:S(2)}, u32[]{:S(2)}) async-start(f32[16,64,128]{2,1,0:T(8,128)} %gate.1), calls=%async_computation | async-start | bytes 1048576 | tf_op jit(solution)/shard_map/all_to_all | solution.py:403
  11.1 0.0 copy-done.4
  11.1 0.0 copy-done.5
  11.1 0.0 copy-done.7
  11.1 0.5 %filter.1.filter_ref = f32[64,8,256]{2,1,0:T(8,128)S(1)} custom-call(f32[8,4096]{1,0:T(8,128)S(1)} %copy-done.7, f32[64,256]{1,0:T(8,128)S(1)} %copy-done.5, bf16[768,256]{1,0:T(8,128)(2,1)S(1)} %copy-done.4), custom_call_target="tpu_custom_call" | custom-call | flops 402653184 | bytes 524288 | tf_op jit(solution)/shard_map/filter/pallas_call | solution.py:389
  11.6 12.9 %all-to-all-done.held_ref = f32[16,64,128]{2,1,0:T(8,128)S(1)} async-done(((f32[16,64,128]{2,1,0:T(8,128)}), f32[16,64,128]{2,1,0:T(8,128)S(1)}, u32[]{:S(2)}, u32[]{:S(2)}) %all-to-all-start) | async-done | bytes 524320 | tf_op jit(solution)/shard_map/all_to_all | solution.py:403
  24.5 2.3 %convolve.1 = (f32[16,64,128]{2,1,0:T(8,128)}, f32[1,64,8,256]{3,2,1,0:T(8,128)S(1)}, f32[1,64,8,256]{3,2,1,0:T(8,128)S(1)}) custom-call(f32[16,64,128]{2,1,0:T(8,128)S(1)} %all-to-all-done.held_ref, f32[64,8,256]{2,1,0:T(8,128)S(1)} %filter.1.filter_ref, f32[64,256]{1,0:T(8,128)S(1)} %copy-done.5, bf16[768,256]{1,0:T(8,128)(2,1)S(1)} %copy-done.4), custom_call_target="tpu_custom_call" | custom-call | flops 1610612736 | bytes 2097152 | tf_op jit(solution)/shard_map/convolve/pallas_call | solution.py:389
  26.9 4.7 %all-to-all-start.1 = ((f32[16,64,128]{2,1,0:T(8,128)}), f32[16,64,128]{2,1,0:T(8,128)S(1)}, u32[]{:S(2)}, u32[]{:S(2)}) async-start(f32[16,64,128]{2,1,0:T(8,128)} %get-tuple-element.12), calls=%async_computation.1 | async-start | bytes 1048576 | tf_op jit(solution)/shard_map/all_to_all | solution.py:403
  31.5 0.0 copy-start.1
  31.5 0.0 copy-start.2
  31.5 0.0 copy-start.3
  31.6 0.5 %lags.1 = f32[2,8,2048]{2,1,0:T(8,128)S(1)} custom-call(f32[1,64,8,256]{3,2,1,0:T(8,128)S(1)} %get-tuple-element.17.mixed_ref, f32[1,64,8,256]{3,2,1,0:T(8,128)S(1)} %get-tuple-element.18.upstream_ref, f32[64,256]{1,0:T(8,128)S(1)} %copy-done.5, bf16[768,256]{1,0:T(8,128)(2,1)S(1)} %copy-done.4), custom_call_target="tpu_custom_call" | custom-call | flops 402653184 | bytes 524288 | tf_op jit(solution)/shard_map/lags/pallas_call | solution.py:389
  32.1 0.0 copy-start
  32.1 1.6 %collective-permute-start = (f32[8,2048]{1,0:T(8,128)S(1)}, f32[8,2048]{1,0:T(8,128)S(1)}, u32[]{:S(2)}, u32[]{:S(2)}) collective-permute-start(f32[8,2048]{1,0:T(8,128)S(1)} %slice_bitcast_fusion), channel_id=1, source_target_pairs={{0,16},{16,0},{1,17},{17,1},{2,18},{18,2},{3,19},{19,3},{4,20},{20... | collective-permute-start | bytes 196616 | tf_op jit(solution)/shard_map/ppermute | solution.py:454
  33.7 2.8 %collective-permute-done = f32[8,2048]{1,0:T(8,128)S(1)} collective-permute-done((f32[8,2048]{1,0:T(8,128)S(1)}, f32[8,2048]{1,0:T(8,128)S(1)}, u32[]{:S(2)}, u32[]{:S(2)}) %collective-permute-start) | collective-permute-done | bytes 65568 | tf_op jit(solution)/shard_map/ppermute | solution.py:454
  36.4 0.6 %fusion = f32[8,2048]{1,0:T(8,128)} fusion(f32[8,2048]{1,0:T(8,128)S(1)} %collective-permute-done, f32[2,8,2048]{2,1,0:T(8,128)S(1)} %lags.1), kind=kLoop, calls=%fused_computation.2 | loop fusion | flops 16384 | bytes 196608 | tf_op jit(solution)/shard_map/add | solution.py:454
  37.1 0.0 copy-start.6
  37.1 7.9 %all-to-all-done.1.home_ref = f32[16,64,128]{2,1,0:T(8,128)S(1)} async-done(((f32[16,64,128]{2,1,0:T(8,128)}), f32[16,64,128]{2,1,0:T(8,128)S(1)}, u32[]{:S(2)}, u32[]{:S(2)}) %all-to-all-start.1) | async-done | bytes 524320 | tf_op jit(solution)/shard_map/all_to_all | solution.py:403
  45.0 0.0 copy-done.1
  45.0 0.0 copy-done.2
  45.0 0.0 copy-done.3
  45.0 0.0 copy-done
  45.0 0.0 copy-done.6
  45.0 1.1 %outputs.1 = (f32[2,256,128]{2,1,0:T(8,128)}, f32[2,256,128]{2,1,0:T(8,128)}, f32[2,256,128]{2,1,0:T(8,128)}, f32[2,256,128]{2,1,0:T(8,128)}) custom-call(f32[2,256,128]{2,1,0:T(8,128)S(1)} %copy-done, f32[2,256,128]{2,1,0:T(8,128)S(1)} %copy-done.1, f32[2,256,128]{2,1,0:T(8,128)S(1)} %copy-done.2, f32[2,256,128]{2,1,0:T(8,128)S(1)} %copy-done.3, ...), custom_call_target="tpu_custom_call" | custom-call | flops 402653184 | bytes 524288 | tf_op jit(solution)/shard_map/outputs/pallas_call | solution.py:389
  (1 shorter events, 0.0 us)
Async XLA Ops:
  3.0 8.1 %copy-start.4 = (bf16[768,256]{1,0:T(8,128)(2,1)S(1)}, bf16[768,256]{1,0:T(8,128)(2,1)}, u32[]{:S(2)}) copy-start(bf16[768,256]{1,0:T(8,128)(2,1)} %constant.5.clone.matrix_ref) | copy-start | bytes 1179652
  3.0 8.1 %copy-start.5 = (f32[64,256]{1,0:T(8,128)S(1)}, f32[64,256]{1,0:T(8,128)}, u32[]{:S(2)}) copy-start(f32[64,256]{1,0:T(8,128)} %constant.4.clone.twist_ref) | copy-start | bytes 196612
  3.0 8.1 %copy-start.7 = (f32[8,4096]{1,0:T(8,128)S(1)}, f32[8,4096]{1,0:T(8,128)}, u32[]{:S(2)}) copy-start(f32[8,4096]{1,0:T(8,128)} %filter_ref.1) | copy-start | bytes 393220
  3.0 21.5 %all-to-all-start = ((f32[16,64,128]{2,1,0:T(8,128)}), f32[16,64,128]{2,1,0:T(8,128)S(1)}, u32[]{:S(2)}, u32[]{:S(2)}) async-start(f32[16,64,128]{2,1,0:T(8,128)} %gate.1), calls=%async_computation | async-start | bytes 1048576 | tf_op jit(solution)/shard_map/all_to_all | solution.py:403
  26.9 18.1 %all-to-all-start.1 = ((f32[16,64,128]{2,1,0:T(8,128)}), f32[16,64,128]{2,1,0:T(8,128)S(1)}, u32[]{:S(2)}, u32[]{:S(2)}) async-start(f32[16,64,128]{2,1,0:T(8,128)} %get-tuple-element.12), calls=%async_computation.1 | async-start | bytes 1048576 | tf_op jit(solution)/shard_map/all_to_all | solution.py:403
  31.5 13.5 %copy-start.1 = (f32[2,256,128]{2,1,0:T(8,128)S(1)}, f32[2,256,128]{2,1,0:T(8,128)}, u32[]{:S(2)}) copy-start(f32[2,256,128]{2,1,0:T(8,128)} %key_ref.1) | copy-start | bytes 786436
  31.5 13.5 %copy-start.2 = (f32[2,256,128]{2,1,0:T(8,128)S(1)}, f32[2,256,128]{2,1,0:T(8,128)}, u32[]{:S(2)}) copy-start(f32[2,256,128]{2,1,0:T(8,128)} %value_ref.1) | copy-start | bytes 786436
  31.5 13.5 %copy-start.3 = (f32[2,256,128]{2,1,0:T(8,128)S(1)}, f32[2,256,128]{2,1,0:T(8,128)}, u32[]{:S(2)}) copy-start(f32[2,256,128]{2,1,0:T(8,128)} %cotangent_ref.1) | copy-start | bytes 786436
  32.1 12.9 %copy-start = (f32[2,256,128]{2,1,0:T(8,128)S(1)}, f32[2,256,128]{2,1,0:T(8,128)}, u32[]{:S(2)}) copy-start(f32[2,256,128]{2,1,0:T(8,128)} %query_ref.1) | copy-start | bytes 786436
  32.1 4.3 %collective-permute-start = (f32[8,2048]{1,0:T(8,128)S(1)}, f32[8,2048]{1,0:T(8,128)S(1)}, u32[]{:S(2)}, u32[]{:S(2)}) collective-permute-start(f32[8,2048]{1,0:T(8,128)S(1)} %slice_bitcast_fusion), channel_id=1, source_target_pairs={{0,16},{16,0},{1,17},{17,1},{2,18},{18,2},{3,19},{19,3},{4,20},{20... | collective-permute-start | bytes 196616 | tf_op jit(solution)/shard_map/ppermute | solution.py:454
  37.1 7.9 %copy-start.6 = (f32[128]{0:T(128)S(1)}, f32[128]{0:T(128)}, u32[]{:S(2)}) copy-start(f32[128]{0:T(128)} %param.12) | copy-start | bytes 1540

commit v11 on v1

--- a/solution.py
+++ b/solution.py
@@ -1,3 +1,4 @@
+import itertools
 import math
 
 import jax
@@ -313,7 +314,9 @@
 def exchange(blocks):
     shards = len(blocks)
     received = [blocks[0]] + [None] * (shards - 1)
-    for step in range(shards - 1, 0, -1):
+    far, near = range(shards - 1, shards // 2 - 1, -1), range(shards // 2 - 1, 0, -1)
+    steps = [step for both in itertools.zip_longest(far, near) for step in both if step is not None]
+    for step in steps:
         pairs = [(source, source ^ step) for source in range(shards)]
         received[step] = lax.ppermute(blocks[step], "seq", pairs)
     return received

time: 59.9 us -> 59.9 us (level)
  no operation moved by 1% of the time
where the time goes in v11:
time: 59.9 us; the launch traced here: 59.8 us
  starting transfers between devices  43.7 us (73%)
  waiting for transfers between devices  8.72 us (15%)
  Pallas kernels  5.23 us (9%)
  between operations  0.76 us (1%)
  local copies, waits for them, and re-layouts  0.68 us (1%)
  other arithmetic  0.64 us (1%)
    ppermute x30, starting transfers between devices, exchange(): received[step] = lax.ppermute(blocks[step], 'seq', pairs)  42.2 us
    ppermute x30, waiting for transfers between devices, exchange(): received[step] = lax.ppermute(blocks[step], 'seq', pairs)  8.72 us
    pallas_call x1, Pallas kernels, per_device(): pl.pallas_call(body, out_shape=(block,) * shards + (jax.ShapeDtypeStruct(...  2.46 us
    pallas_call x1, Pallas kernels, per_device(): pl.pallas_call(gate_kernel, out_shape=(block,) * shards, in_specs=[pl.Blo...  1.58 us
    ppermute x1, starting transfers between devices, per_device(): filter_grad = filter_grad + lax.ppermute(lag[step], 'batch', pairs)  1.55 us
  transfers between devices with their start and end apart: 31, of which 6 were waited for; matrix products, arithmetic and copies ran while one was open for 0% of the time, Pallas kernels for 2%

profile of v11, /device:TPU:0, one launch (start us, length us, event | category | flops | bytes accessed | tf_op | source)
XLA Modules:
  0.0 59.8 jit_solution(7858771875367915754)
XLA Ops:
  0.6 0.0 copy-start.4
  0.7 0.0 copy-start.6
  0.7 1.6 %gate.1 = (f32[2,2,8,256]{3,2,1,0:T(8,128)S(1)}, f32[2,2,8,256]{3,2,1,0:T(8,128)S(1)}, f32[2,2,8,256]{3,2,1,0:T(8,128)S(1)}, f32[2,2,8,256]{3,2,1,0:T(8,128)S(1)...) custom-call(f32[2,256,128]{2,1,0:T(8,128)} %query_ref.1, ...), custom_call_target="tpu_custom_call" | custom-call | tf_op jit(solution)/shard_map/gate/pallas_call | solution.py:334
  2.3 0.5 collective-permute-start
  2.8 2.6 %collective-permute-start.1 = (f32[2,2,8,256]{3,2,1,0:T(8,128)S(1)}, f32[2,2,8,256]{3,2,1,0:T(8,128)S(1)}, u32[]{:S(2)}, u32[]{:S(2)}) collective-permute-start(f32[2,2,8,256]{3,2,1,0:T(8,128)S(1)} %get-tuple-element.44), channel_id=1, source_target_pairs={{0,2},{1,3},{2,0},{3,1},{4,6},{5,7},{6,4},{7,5},{8,10},{9,11},{10,... | collective-permute-start | bytes 98312 | tf_op jit(solution)/shard_map/ppermute | solution.py:321
  5.4 0.1 collective-permute-start.2
  5.4 1.8 %collective-permute-start.3 = (f32[2,2,8,256]{3,2,1,0:T(8,128)S(1)}, f32[2,2,8,256]{3,2,1,0:T(8,128)S(1)}, u32[]{:S(2)}, u32[]{:S(2)}) collective-permute-start(f32[2,2,8,256]{3,2,1,0:T(8,128)S(1)} %get-tuple-element.46), channel_id=1, source_target_pairs={{0,4},{1,5},{2,6},{3,7},{4,0},{5,1},{6,2},{7,3},{8,12},{9,13},{10,... | collective-permute-start | bytes 98312 | tf_op jit(solution)/shard_map/ppermute | solution.py:321
  7.2 0.0 collective-permute-start.4
  7.2 0.0 collective-permute-done.refs_4_
  7.2 2.6 %collective-permute-start.5 = (f32[2,2,8,256]{3,2,1,0:T(8,128)S(1)}, f32[2,2,8,256]{3,2,1,0:T(8,128)S(1)}, u32[]{:S(2)}, u32[]{:S(2)}) collective-permute-start(f32[2,2,8,256]{3,2,1,0:T(8,128)S(1)} %get-tuple-element.48), channel_id=1, source_target_pairs={{0,6},{1,7},{2,4},{3,5},{4,2},{5,3},{6,0},{7,1},{8,14},{9,15},{10,... | collective-permute-start | bytes 98312 | tf_op jit(solution)/shard_map/ppermute | solution.py:321
  9.9 0.0 collective-permute-done.1.refs_5_
  9.9 0.1 collective-permute-start.6
  10.0 0.0 collective-permute-done.2.refs_6_
  10.0 2.6 %collective-permute-start.7 = (f32[2,2,8,256]{3,2,1,0:T(8,128)S(1)}, f32[2,2,8,256]{3,2,1,0:T(8,128)S(1)}, u32[]{:S(2)}, u32[]{:S(2)}) collective-permute-start(f32[2,2,8,256]{3,2,1,0:T(8,128)S(1)} %get-tuple-element.50), channel_id=1, source_target_pairs={{0,8},{1,9},{2,10},{3,11},{4,12},{5,13},{6,14},{7,15},{8,0},{9,1},... | collective-permute-start | bytes 98312 | tf_op jit(solution)/shard_map/ppermute | solution.py:321
  12.6 0.0 collective-permute-done.3.refs_7_
  12.6 0.3 collective-permute-start.8
  13.0 0.0 collective-permute-done.4.refs_8_
  13.0 3.2 %collective-permute-start.9 = (f32[2,2,8,256]{3,2,1,0:T(8,128)S(1)}, f32[2,2,8,256]{3,2,1,0:T(8,128)S(1)}, u32[]{:S(2)}, u32[]{:S(2)}) collective-permute-start(f32[2,2,8,256]{3,2,1,0:T(8,128)S(1)} %get-tuple-element.52), channel_id=1, source_target_pairs={{0,10},{1,11},{2,8},{3,9},{4,14},{5,15},{6,12},{7,13},{8,2},{9,3},... | collective-permute-start | bytes 98312 | tf_op jit(solution)/shard_map/ppermute | solution.py:321
  16.2 0.0 collective-permute-done.5.refs_9_
  16.2 0.1 collective-permute-start.10
  16.3 0.0 collective-permute-done.6.refs_10_
  16.3 3.5 %collective-permute-start.11 = (f32[2,2,8,256]{3,2,1,0:T(8,128)S(1)}, f32[2,2,8,256]{3,2,1,0:T(8,128)S(1)}, u32[]{:S(2)}, u32[]{:S(2)}) collective-permute-start(f32[2,2,8,256]{3,2,1,0:T(8,128)S(1)} %get-tuple-element.54), channel_id=1, source_target_pairs={{0,12},{1,13},{2,14},{3,15},{4,8},{5,9},{6,10},{7,11},{8,4},{9,5},... | collective-permute-start | bytes 98312 | tf_op jit(solution)/shard_map/ppermute | solution.py:321
  19.9 0.0 collective-permute-done.7.refs_11_
  19.9 0.2 collective-permute-start.12
  20.1 0.0 collective-permute-done.8.refs_12_
  20.1 4.2 %collective-permute-start.13 = (f32[2,2,8,256]{3,2,1,0:T(8,128)S(1)}, f32[2,2,8,256]{3,2,1,0:T(8,128)S(1)}, u32[]{:S(2)}, u32[]{:S(2)}) collective-permute-start(f32[2,2,8,256]{3,2,1,0:T(8,128)S(1)} %get-tuple-element.56), channel_id=1, source_target_pairs={{0,14},{1,15},{2,12},{3,13},{4,10},{5,11},{6,8},{7,9},{8,6},{9,7},... | collective-permute-start | bytes 98312 | tf_op jit(solution)/shard_map/ppermute | solution.py:321
  24.3 0.0 collective-permute-done.9.refs_13_
  24.3 0.1 collective-permute-start.14
  24.4 0.0 collective-permute-done.10.refs_14_
  24.4 0.0 collective-permute-done.11.refs_15_
  24.4 0.7 %collective-permute-done.12.refs_16_ = f32[2,2,8,256]{3,2,1,0:T(8,128)S(1)} collective-permute-done((f32[2,2,8,256]{3,2,1,0:T(8,128)S(1)}, f32[2,2,8,256]{3,2,1,0:T(8,128)S(1)}, u32[]{:S(2)}, u32[]{:S(2)}) %collective-permute-start.12) | collective-permute-done | bytes 32800 | tf_op jit(solution)/shard_map/ppermute | solution.py:321
  25.1 2.0 %collective-permute-done.13.refs_17_ = f32[2,2,8,256]{3,2,1,0:T(8,128)S(1)} collective-permute-done((f32[2,2,8,256]{3,2,1,0:T(8,128)S(1)}, f32[2,2,8,256]{3,2,1,0:T(8,128)S(1)}, u32[]{:S(2)}, u32[]{:S(2)}) %collective-permute-start.13) | collective-permute-done | bytes 32800 | tf_op jit(solution)/shard_map/ppermute | solution.py:321
  27.1 3.2 %collective-permute-done.14.refs_18_ = f32[2,2,8,256]{3,2,1,0:T(8,128)S(1)} collective-permute-done((f32[2,2,8,256]{3,2,1,0:T(8,128)S(1)}, f32[2,2,8,256]{3,2,1,0:T(8,128)S(1)}, u32[]{:S(2)}, u32[]{:S(2)}) %collective-permute-start.14) | collective-permute-done | bytes 32800 | tf_op jit(solution)/shard_map/ppermute | solution.py:321
  30.4 0.0 copy-start
  30.4 0.0 copy-start.1
  30.4 0.0 copy-start.2
  30.4 0.0 copy-start.3
  30.4 2.5 %spectral.1 = (f32[2,2,8,256]{3,2,1,0:T(8,128)S(1)}, f32[2,2,8,256]{3,2,1,0:T(8,128)S(1)}, f32[2,2,8,256]{3,2,1,0:T(8,128)S(1)}, f32[2,2,8,256]{3,2,1,0:T(8,128)...) custom-call(f32[8,4096]{1,0:T(8,128)S(1)} %copy-done.5, ...), custom_call_target="tpu_custom_call" | custom-call | tf_op jit(solution)/shard_map/spectral/pallas_call | solution.py:355
  32.9 0.2 collective-permute-start.15
  33.1 0.5 collective-permute-start.16
  33.6 1.2 %collective-permute-start.17 = (f32[2,2,8,256]{3,2,1,0:T(8,128)S(1)}, f32[2,2,8,256]{3,2,1,0:T(8,128)S(1)}, u32[]{:S(2)}, u32[]{:S(2)}) collective-permute-start(f32[2,2,8,256]{3,2,1,0:T(8,128)S(1)} %get-tuple-element.61), channel_id=1, source_target_pairs={{0,3},{1,2},{2,1},{3,0},{4,7},{5,6},{6,5},{7,4},{8,11},{9,10},{10,... | collective-permute-start | bytes 98312 | tf_op jit(solution)/shard_map/ppermute | solution.py:321
  34.8 0.0 collective-permute-start.18
  34.8 1.8 %collective-permute-start.19 = (f32[2,2,8,256]{3,2,1,0:T(8,128)S(1)}, f32[2,2,8,256]{3,2,1,0:T(8,128)S(1)}, u32[]{:S(2)}, u32[]{:S(2)}) collective-permute-start(f32[2,2,8,256]{3,2,1,0:T(8,128)S(1)} %get-tuple-element.63), channel_id=1, source_target_pairs={{0,5},{1,4},{2,7},{3,6},{4,1},{5,0},{6,3},{7,2},{8,13},{9,12},{10,... | collective-permute-start | bytes 98312 | tf_op jit(solution)/shard_map/ppermute | solution.py:321
  36.6 0.0 collective-permute-done.15.refs_1_
  36.6 0.2 collective-permute-start.20
  36.9 0.4 collective-permute-done.16.refs_2_
  37.3 1.9 %collective-permute-start.21 = (f32[2,2,8,256]{3,2,1,0:T(8,128)S(1)}, f32[2,2,8,256]{3,2,1,0:T(8,128)S(1)}, u32[]{:S(2)}, u32[]{:S(2)}) collective-permute-start(f32[2,2,8,256]{3,2,1,0:T(8,128)S(1)} %get-tuple-element.65), channel_id=1, source_target_pairs={{0,7},{1,6},{2,5},{3,4},{4,3},{5,2},{6,1},{7,0},{8,15},{9,14},{10,... | collective-permute-start | bytes 98312 | tf_op jit(solution)/shard_map/ppermute | solution.py:321
  39.2 0.0 collective-permute-done.17.refs_3_
  39.2 2.7 %collective-permute-start.23 = (f32[2,2,8,256]{3,2,1,0:T(8,128)S(1)}, f32[2,2,8,256]{3,2,1,0:T(8,128)S(1)}, u32[]{:S(2)}, u32[]{:S(2)}) collective-permute-start(f32[2,2,8,256]{3,2,1,0:T(8,128)S(1)} %get-tuple-element.67), channel_id=1, source_target_pairs={{0,9},{1,8},{2,11},{3,10},{4,13},{5,12},{6,15},{7,14},{8,1},{9,0},... | collective-permute-start | bytes 98312 | tf_op jit(solution)/shard_map/ppermute | solution.py:321
  41.9 0.0 collective-permute-done.19.refs_5_
  41.9 0.3 collective-permute-start.24
  42.2 0.0 collective-permute-done.20.refs_6_
  42.2 3.2 %collective-permute-start.25 = (f32[2,2,8,256]{3,2,1,0:T(8,128)S(1)}, f32[2,2,8,256]{3,2,1,0:T(8,128)S(1)}, u32[]{:S(2)}, u32[]{:S(2)}) collective-permute-start(f32[2,2,8,256]{3,2,1,0:T(8,128)S(1)} %get-tuple-element.69), channel_id=1, source_target_pairs={{0,11},{1,10},{2,9},{3,8},{4,15},{5,14},{6,13},{7,12},{8,3},{9,2},... | collective-permute-start | bytes 98312 | tf_op jit(solution)/shard_map/ppermute | solution.py:321
  45.4 1.6 %collective-permute-start.30 = (f32[8,2048]{1,0:T(8,128)S(1)}, f32[8,2048]{1,0:T(8,128)S(1)}, u32[]{:S(2)}, u32[]{:S(2)}) collective-permute-start(f32[8,2048]{1,0:T(8,128)S(1)} %slice_bitcast_fusion), channel_id=1, source_target_pairs={{0,16},{16,0},{1,17},{17,1},{2,18},{18,2},{3,19},{19,3},{4,20},{20... | collective-permute-start | bytes 196616 | tf_op jit(solution)/shard_map/ppermute | solution.py:367
  47.0 0.6 %collective-permute-start.26 = (f32[2,2,8,256]{3,2,1,0:T(8,128)S(1)}, f32[2,2,8,256]{3,2,1,0:T(8,128)S(1)}, u32[]{:S(2)}, u32[]{:S(2)}) collective-permute-start(f32[2,2,8,256]{3,2,1,0:T(8,128)S(1)} %get-tuple-element.70), channel_id=1, source_target_pairs={{0,12},{1,13},{2,14},{3,15},{4,8},{5,9},{6,10},{7,11},{8,4},{9,5},... | collective-permute-start | bytes 98312 | tf_op jit(solution)/shard_map/ppermute | solution.py:321
  47.6 2.7 %collective-permute-start.27 = (f32[2,2,8,256]{3,2,1,0:T(8,128)S(1)}, f32[2,2,8,256]{3,2,1,0:T(8,128)S(1)}, u32[]{:S(2)}, u32[]{:S(2)}) collective-permute-start(f32[2,2,8,256]{3,2,1,0:T(8,128)S(1)} %get-tuple-element.71), channel_id=1, source_target_pairs={{0,13},{1,12},{2,15},{3,14},{4,9},{5,8},{6,11},{7,10},{8,5},{9,4},... | collective-permute-start | bytes 98312 | tf_op jit(solution)/shard_map/ppermute | solution.py:321
  50.3 0.8 %collective-permute-start.28 = (f32[2,2,8,256]{3,2,1,0:T(8,128)S(1)}, f32[2,2,8,256]{3,2,1,0:T(8,128)S(1)}, u32[]{:S(2)}, u32[]{:S(2)}) collective-permute-start(f32[2,2,8,256]{3,2,1,0:T(8,128)S(1)} %get-tuple-element.72), channel_id=1, source_target_pairs={{0,14},{1,15},{2,12},{3,13},{4,10},{5,11},{6,8},{7,9},{8,6},{9,7},... | collective-permute-start | bytes 98312 | tf_op jit(solution)/shard_map/ppermute | solution.py:321
  51.2 0.0 collective-permute-done.25.refs_11_
  51.2 3.8 %collective-permute-start.29 = (f32[2,2,8,256]{3,2,1,0:T(8,128)S(1)}, f32[2,2,8,256]{3,2,1,0:T(8,128)S(1)}, u32[]{:S(2)}, u32[]{:S(2)}) collective-permute-start(f32[2,2,8,256]{3,2,1,0:T(8,128)S(1)} %get-tuple-element.73), channel_id=1, source_target_pairs={{0,15},{1,14},{2,13},{3,12},{4,11},{5,10},{6,9},{7,8},{8,7},{9,6},... | collective-permute-start | bytes 98312 | tf_op jit(solution)/shard_map/ppermute | solution.py:321
  55.0 2.0 %collective-permute-done.28.refs_14_ = f32[2,2,8,256]{3,2,1,0:T(8,128)S(1)} collective-permute-done((f32[2,2,8,256]{3,2,1,0:T(8,128)S(1)}, f32[2,2,8,256]{3,2,1,0:T(8,128)S(1)}, u32[]{:S(2)}, u32[]{:S(2)}) %collective-permute-start.28) | collective-permute-done | bytes 32800 | tf_op jit(solution)/shard_map/ppermute | solution.py:321
  57.0 0.3 collective-permute-done.29.refs_15_
  57.3 0.6 %copy-done.7 = f32[128]{0:T(128)S(1)} copy-done((f32[128]{0:T(128)S(1)}, f32[128]{0:T(128)}, u32[]{:S(2)}) %copy-start.7) | copy-done | bytes 536
  57.9 1.2 %outputs.1 = (f32[2,256,128]{2,1,0:T(8,128)}, f32[2,256,128]{2,1,0:T(8,128)}, f32[2,256,128]{2,1,0:T(8,128)}, f32[2,256,128]{2,1,0:T(8,128)}) custom-call(f32[2,256,128]{2,1,0:T(8,128)S(1)} %copy-done, f32[2,256,128]{2,1,0:T(8,128)S(1)} %copy-done.1, f32[2,256,128]{2,1,0:T(8,128)S(1)} %copy-done.2, f32[2,256,128]{2,1,0:T(8,128)S(1)} %copy-done.3, ...), custom_call_target="tpu_custom_call" | custom-call | tf_op jit(solution)/shard_map/outputs/pallas_call | solution.py:369
  59.1 0.6 %bitcast_add_fusion = f32[8,2048]{1,0:T(8,128)} fusion(f32[8,2048]{1,0:T(8,128)S(1)} %collective-permute-done.30, f32[2,8,2048]{2,1,0:T(8,128)S(1)} %get-tuple-element.78), kind=kLoop, calls=%fused_computation | loop fusion | flops 16384 | bytes 196608 | tf_op jit(solution)/shard_map/add | solution.py:367
  (19 shorter events, 0.0 us)
Async XLA Ops:
  0.6 29.7 %copy-start.4 = (bf16[768,256]{1,0:T(8,128)(2,1)S(1)}, bf16[768,256]{1,0:T(8,128)(2,1)}, u32[]{:S(2)}) copy-start(bf16[768,256]{1,0:T(8,128)(2,1)} %constant.5.clone.refs_2_) | copy-start | bytes 1179652
  0.6 29.7 %copy-start.5 = (f32[8,4096]{1,0:T(8,128)S(1)}, f32[8,4096]{1,0:T(8,128)}, u32[]{:S(2)}) copy-start(f32[8,4096]{1,0:T(8,128)} %refs_0_.1) | copy-start | bytes 393220
  0.7 29.7 %copy-start.6 = (f32[64,256]{1,0:T(8,128)S(1)}, f32[64,256]{1,0:T(8,128)}, u32[]{:S(2)}) copy-start(f32[64,256]{1,0:T(8,128)} %constant.4.clone.refs_1_) | copy-start | bytes 196612
  2.3 5.0 %collective-permute-start = (f32[2,2,8,256]{3,2,1,0:T(8,128)S(1)}, f32[2,2,8,256]{3,2,1,0:T(8,128)S(1)}, u32[]{:S(2)}, u32[]{:S(2)}) collective-permute-start(f32[2,2,8,256]{3,2,1,0:T(8,128)S(1)} %get-tuple-element.43), channel_id=1, source_target_pairs={{0,1},{1,0},{2,3},{3,2},{4,5},{5,4},{6,7},{7,6},{8,9},{9,8},{10,11... | collective-permute-start | bytes 98312 | tf_op jit(solution)/shard_map/ppermute | solution.py:321
  2.8 7.1 %collective-permute-start.1 = (f32[2,2,8,256]{3,2,1,0:T(8,128)S(1)}, f32[2,2,8,256]{3,2,1,0:T(8,128)S(1)}, u32[]{:S(2)}, u32[]{:S(2)}) collective-permute-start(f32[2,2,8,256]{3,2,1,0:T(8,128)S(1)} %get-tuple-element.44), channel_id=1, source_target_pairs={{0,2},{1,3},{2,0},{3,1},{4,6},{5,7},{6,4},{7,5},{8,10},{9,11},{10,... | collective-permute-start | bytes 98312 | tf_op jit(solution)/shard_map/ppermute | solution.py:321
  5.4 4.6 %collective-permute-start.2 = (f32[2,2,8,256]{3,2,1,0:T(8,128)S(1)}, f32[2,2,8,256]{3,2,1,0:T(8,128)S(1)}, u32[]{:S(2)}, u32[]{:S(2)}) collective-permute-start(f32[2,2,8,256]{3,2,1,0:T(8,128)S(1)} %get-tuple-element.45), channel_id=1, source_target_pairs={{0,3},{1,2},{2,1},{3,0},{4,7},{5,6},{6,5},{7,4},{8,11},{9,10},{10,... | collective-permute-start | bytes 98312 | tf_op jit(solution)/shard_map/ppermute | solution.py:321
  5.4 7.2 %collective-permute-start.3 = (f32[2,2,8,256]{3,2,1,0:T(8,128)S(1)}, f32[2,2,8,256]{3,2,1,0:T(8,128)S(1)}, u32[]{:S(2)}, u32[]{:S(2)}) collective-permute-start(f32[2,2,8,256]{3,2,1,0:T(8,128)S(1)} %get-tuple-element.46), channel_id=1, source_target_pairs={{0,4},{1,5},{2,6},{3,7},{4,0},{5,1},{6,2},{7,3},{8,12},{9,13},{10,... | collective-permute-start | bytes 98312 | tf_op jit(solution)/shard_map/ppermute | solution.py:321
  7.2 5.7 %collective-permute-start.4 = (f32[2,2,8,256]{3,2,1,0:T(8,128)S(1)}, f32[2,2,8,256]{3,2,1,0:T(8,128)S(1)}, u32[]{:S(2)}, u32[]{:S(2)}) collective-permute-start(f32[2,2,8,256]{3,2,1,0:T(8,128)S(1)} %get-tuple-element.47), channel_id=1, source_target_pairs={{0,5},{1,4},{2,7},{3,6},{4,1},{5,0},{6,3},{7,2},{8,13},{9,12},{10,... | collective-permute-start | bytes 98312 | tf_op jit(solution)/shard_map/ppermute | solution.py:321
  7.2 9.0 %collective-permute-start.5 = (f32[2,2,8,256]{3,2,1,0:T(8,128)S(1)}, f32[2,2,8,256]{3,2,1,0:T(8,128)S(1)}, u32[]{:S(2)}, u32[]{:S(2)}) collective-permute-start(f32[2,2,8,256]{3,2,1,0:T(8,128)S(1)} %get-tuple-element.48), channel_id=1, source_target_pairs={{0,6},{1,7},{2,4},{3,5},{4,2},{5,3},{6,0},{7,1},{8,14},{9,15},{10,... | collective-permute-start | bytes 98312 | tf_op jit(solution)/shard_map/ppermute | solution.py:321
  9.9 6.4 %collective-permute-start.6 = (f32[2,2,8,256]{3,2,1,0:T(8,128)S(1)}, f32[2,2,8,256]{3,2,1,0:T(8,128)S(1)}, u32[]{:S(2)}, u32[]{:S(2)}) collective-permute-start(f32[2,2,8,256]{3,2,1,0:T(8,128)S(1)} %get-tuple-element.49), channel_id=1, source_target_pairs={{0,7},{1,6},{2,5},{3,4},{4,3},{5,2},{6,1},{7,0},{8,15},{9,14},{10,... | collective-permute-start | bytes 98312 | tf_op jit(solution)/shard_map/ppermute | solution.py:321
  10.0 9.9 %collective-permute-start.7 = (f32[2,2,8,256]{3,2,1,0:T(8,128)S(1)}, f32[2,2,8,256]{3,2,1,0:T(8,128)S(1)}, u32[]{:S(2)}, u32[]{:S(2)}) collective-permute-start(f32[2,2,8,256]{3,2,1,0:T(8,128)S(1)} %get-tuple-element.50), channel_id=1, source_target_pairs={{0,8},{1,9},{2,10},{3,11},{4,12},{5,13},{6,14},{7,15},{8,0},{9,1},... | collective-permute-start | bytes 98312 | tf_op jit(solution)/shard_map/ppermute | solution.py:321
  12.6 7.4 %collective-permute-start.8 = (f32[2,2,8,256]{3,2,1,0:T(8,128)S(1)}, f32[2,2,8,256]{3,2,1,0:T(8,128)S(1)}, u32[]{:S(2)}, u32[]{:S(2)}) collective-permute-start(f32[2,2,8,256]{3,2,1,0:T(8,128)S(1)} %get-tuple-element.51), channel_id=1, source_target_pairs={{0,9},{1,8},{2,11},{3,10},{4,13},{5,12},{6,15},{7,14},{8,1},{9,0},... | collective-permute-start | bytes 98312 | tf_op jit(solution)/shard_map/ppermute | solution.py:321
  13.0 11.3 %collective-permute-start.9 = (f32[2,2,8,256]{3,2,1,0:T(8,128)S(1)}, f32[2,2,8,256]{3,2,1,0:T(8,128)S(1)}, u32[]{:S(2)}, u32[]{:S(2)}) collective-permute-start(f32[2,2,8,256]{3,2,1,0:T(8,128)S(1)} %get-tuple-element.52), channel_id=1, source_target_pairs={{0,10},{1,11},{2,8},{3,9},{4,14},{5,15},{6,12},{7,13},{8,2},{9,3},... | collective-permute-start | bytes 98312 | tf_op jit(solution)/shard_map/ppermute | solution.py:321
  16.2 8.2 %collective-permute-start.10 = (f32[2,2,8,256]{3,2,1,0:T(8,128)S(1)}, f32[2,2,8,256]{3,2,1,0:T(8,128)S(1)}, u32[]{:S(2)}, u32[]{:S(2)}) collective-permute-start(f32[2,2,8,256]{3,2,1,0:T(8,128)S(1)} %get-tuple-element.53), channel_id=1, source_target_pairs={{0,11},{1,10},{2,9},{3,8},{4,15},{5,14},{6,13},{7,12},{8,3},{9,2},... | collective-permute-start | bytes 98312 | tf_op jit(solution)/shard_map/ppermute | solution.py:321
  16.3 8.1 %collective-permute-start.11 = (f32[2,2,8,256]{3,2,1,0:T(8,128)S(1)}, f32[2,2,8,256]{3,2,1,0:T(8,128)S(1)}, u32[]{:S(2)}, u32[]{:S(2)}) collective-permute-start(f32[2,2,8,256]{3,2,1,0:T(8,128)S(1)} %get-tuple-element.54), channel_id=1, source_target_pairs={{0,12},{1,13},{2,14},{3,15},{4,8},{5,9},{6,10},{7,11},{8,4},{9,5},... | collective-permute-start | bytes 98312 | tf_op jit(solution)/shard_map/ppermute | solution.py:321
  19.9 5.3 %collective-permute-start.12 = (f32[2,2,8,256]{3,2,1,0:T(8,128)S(1)}, f32[2,2,8,256]{3,2,1,0:T(8,128)S(1)}, u32[]{:S(2)}, u32[]{:S(2)}) collective-permute-start(f32[2,2,8,256]{3,2,1,0:T(8,128)S(1)} %get-tuple-element.55), channel_id=1, source_target_pairs={{0,13},{1,12},{2,15},{3,14},{4,9},{5,8},{6,11},{7,10},{8,5},{9,4},... | collective-permute-start | bytes 98312 | tf_op jit(solution)/shard_map/ppermute | solution.py:321
  20.1 7.0 %collective-permute-start.13 = (f32[2,2,8,256]{3,2,1,0:T(8,128)S(1)}, f32[2,2,8,256]{3,2,1,0:T(8,128)S(1)}, u32[]{:S(2)}, u32[]{:S(2)}) collective-permute-start(f32[2,2,8,256]{3,2,1,0:T(8,128)S(1)} %get-tuple-element.56), channel_id=1, source_target_pairs={{0,14},{1,15},{2,12},{3,13},{4,10},{5,11},{6,8},{7,9},{8,6},{9,7},... | collective-permute-start | bytes 98312 | tf_op jit(solution)/shard_map/ppermute | solution.py:321
  24.3 6.0 %collective-permute-start.14 = (f32[2,2,8,256]{3,2,1,0:T(8,128)S(1)}, f32[2,2,8,256]{3,2,1,0:T(8,128)S(1)}, u32[]{:S(2)}, u32[]{:S(2)}) collective-permute-start(f32[2,2,8,256]{3,2,1,0:T(8,128)S(1)} %get-tuple-element.57), channel_id=1, source_target_pairs={{0,15},{1,14},{2,13},{3,12},{4,11},{5,10},{6,9},{7,8},{8,7},{9,6},... | collective-permute-start | bytes 98312 | tf_op jit(solution)/shard_map/ppermute | solution.py:321
  30.4 26.9 %copy-start = (f32[2,256,128]{2,1,0:T(8,128)S(1)}, f32[2,256,128]{2,1,0:T(8,128)}, u32[]{:S(2)}) copy-start(f32[2,256,128]{2,1,0:T(8,128)} %query_ref.1) | copy-start | bytes 786436
  30.4 26.9 %copy-start.1 = (f32[2,256,128]{2,1,0:T(8,128)S(1)}, f32[2,256,128]{2,1,0:T(8,128)}, u32[]{:S(2)}) copy-start(f32[2,256,128]{2,1,0:T(8,128)} %key_ref.1) | copy-start | bytes 786436
  30.4 26.9 %copy-start.2 = (f32[2,256,128]{2,1,0:T(8,128)S(1)}, f32[2,256,128]{2,1,0:T(8,128)}, u32[]{:S(2)}) copy-start(f32[2,256,128]{2,1,0:T(8,128)} %value_ref.1) | copy-start | bytes 786436
  30.4 26.9 %copy-start.3 = (f32[2,256,128]{2,1,0:T(8,128)S(1)}, f32[2,256,128]{2,1,0:T(8,128)}, u32[]{:S(2)}) copy-start(f32[2,256,128]{2,1,0:T(8,128)} %cotangent_ref.1) | copy-start | bytes 786436
  32.9 3.7 %collective-permute-start.15 = (f32[2,2,8,256]{3,2,1,0:T(8,128)S(1)}, f32[2,2,8,256]{3,2,1,0:T(8,128)S(1)}, u32[]{:S(2)}, u32[]{:S(2)}) collective-permute-start(f32[2,2,8,256]{3,2,1,0:T(8,128)S(1)} %get-tuple-element.59), channel_id=1, source_target_pairs={{0,1},{1,0},{2,3},{3,2},{4,5},{5,4},{6,7},{7,6},{8,9},{9,8},{10,11... | collective-permute-start | bytes 98312 | tf_op jit(solution)/shard_map/ppermute | solution.py:321
  33.1 4.2 %collective-permute-start.16 = (f32[2,2,8,256]{3,2,1,0:T(8,128)S(1)}, f32[2,2,8,256]{3,2,1,0:T(8,128)S(1)}, u32[]{:S(2)}, u32[]{:S(2)}) collective-permute-start(f32[2,2,8,256]{3,2,1,0:T(8,128)S(1)} %get-tuple-element.60), channel_id=1, source_target_pairs={{0,2},{1,3},{2,0},{3,1},{4,6},{5,7},{6,4},{7,5},{8,10},{9,11},{10,... | collective-permute-start | bytes 98312 | tf_op jit(solution)/shard_map/ppermute | solution.py:321
  33.6 5.6 %collective-permute-start.17 = (f32[2,2,8,256]{3,2,1,0:T(8,128)S(1)}, f32[2,2,8,256]{3,2,1,0:T(8,128)S(1)}, u32[]{:S(2)}, u32[]{:S(2)}) collective-permute-start(f32[2,2,8,256]{3,2,1,0:T(8,128)S(1)} %get-tuple-element.61), channel_id=1, source_target_pairs={{0,3},{1,2},{2,1},{3,0},{4,7},{5,6},{6,5},{7,4},{8,11},{9,10},{10,... | collective-permute-start | bytes 98312 | tf_op jit(solution)/shard_map/ppermute | solution.py:321
  34.8 4.4 %collective-permute-start.18 = (f32[2,2,8,256]{3,2,1,0:T(8,128)S(1)}, f32[2,2,8,256]{3,2,1,0:T(8,128)S(1)}, u32[]{:S(2)}, u32[]{:S(2)}) collective-permute-start(f32[2,2,8,256]{3,2,1,0:T(8,128)S(1)} %get-tuple-element.62), channel_id=1, source_target_pairs={{0,4},{1,5},{2,6},{3,7},{4,0},{5,1},{6,2},{7,3},{8,12},{9,13},{10,... | collective-permute-start | bytes 98312 | tf_op jit(solution)/shard_map/ppermute | solution.py:321
  34.8 7.1 %collective-permute-start.19 = (f32[2,2,8,256]{3,2,1,0:T(8,128)S(1)}, f32[2,2,8,256]{3,2,1,0:T(8,128)S(1)}, u32[]{:S(2)}, u32[]{:S(2)}) collective-permute-start(f32[2,2,8,256]{3,2,1,0:T(8,128)S(1)} %get-tuple-element.63), channel_id=1, source_target_pairs={{0,5},{1,4},{2,7},{3,6},{4,1},{5,0},{6,3},{7,2},{8,13},{9,12},{10,... | collective-permute-start | bytes 98312 | tf_op jit(solution)/shard_map/ppermute | solution.py:321
  36.6 5.6 %collective-permute-start.20 = (f32[2,2,8,256]{3,2,1,0:T(8,128)S(1)}, f32[2,2,8,256]{3,2,1,0:T(8,128)S(1)}, u32[]{:S(2)}, u32[]{:S(2)}) collective-permute-start(f32[2,2,8,256]{3,2,1,0:T(8,128)S(1)} %get-tuple-element.64), channel_id=1, source_target_pairs={{0,6},{1,7},{2,4},{3,5},{4,2},{5,3},{6,0},{7,1},{8,14},{9,15},{10,... | collective-permute-start | bytes 98312 | tf_op jit(solution)/shard_map/ppermute | solution.py:321
  37.3 8.1 %collective-permute-start.21 = (f32[2,2,8,256]{3,2,1,0:T(8,128)S(1)}, f32[2,2,8,256]{3,2,1,0:T(8,128)S(1)}, u32[]{:S(2)}, u32[]{:S(2)}) collective-permute-start(f32[2,2,8,256]{3,2,1,0:T(8,128)S(1)} %get-tuple-element.65), channel_id=1, source_target_pairs={{0,7},{1,6},{2,5},{3,4},{4,3},{5,2},{6,1},{7,0},{8,15},{9,14},{10,... | collective-permute-start | bytes 98312 | tf_op jit(solution)/shard_map/ppermute | solution.py:321
  39.2 7.8 %collective-permute-start.22 = (f32[2,2,8,256]{3,2,1,0:T(8,128)S(1)}, f32[2,2,8,256]{3,2,1,0:T(8,128)S(1)}, u32[]{:S(2)}, u32[]{:S(2)}) collective-permute-start(f32[2,2,8,256]{3,2,1,0:T(8,128)S(1)} %get-tuple-element.66), channel_id=1, source_target_pairs={{0,8},{1,9},{2,10},{3,11},{4,12},{5,13},{6,14},{7,15},{8,0},{9,1},... | collective-permute-start | bytes 98312 | tf_op jit(solution)/shard_map/ppermute | solution.py:321
  39.2 8.4 %collective-permute-start.23 = (f32[2,2,8,256]{3,2,1,0:T(8,128)S(1)}, f32[2,2,8,256]{3,2,1,0:T(8,128)S(1)}, u32[]{:S(2)}, u32[]{:S(2)}) collective-permute-start(f32[2,2,8,256]{3,2,1,0:T(8,128)S(1)} %get-tuple-element.67), channel_id=1, source_target_pairs={{0,9},{1,8},{2,11},{3,10},{4,13},{5,12},{6,15},{7,14},{8,1},{9,0},... | collective-permute-start | bytes 98312 | tf_op jit(solution)/shard_map/ppermute | solution.py:321
  41.9 8.4 %collective-permute-start.24 = (f32[2,2,8,256]{3,2,1,0:T(8,128)S(1)}, f32[2,2,8,256]{3,2,1,0:T(8,128)S(1)}, u32[]{:S(2)}, u32[]{:S(2)}) collective-permute-start(f32[2,2,8,256]{3,2,1,0:T(8,128)S(1)} %get-tuple-element.68), channel_id=1, source_target_pairs={{0,10},{1,11},{2,8},{3,9},{4,14},{5,15},{6,12},{7,13},{8,2},{9,3},... | collective-permute-start | bytes 98312 | tf_op jit(solution)/shard_map/ppermute | solution.py:321
  42.2 8.9 %collective-permute-start.25 = (f32[2,2,8,256]{3,2,1,0:T(8,128)S(1)}, f32[2,2,8,256]{3,2,1,0:T(8,128)S(1)}, u32[]{:S(2)}, u32[]{:S(2)}) collective-permute-start(f32[2,2,8,256]{3,2,1,0:T(8,128)S(1)} %get-tuple-element.69), channel_id=1, source_target_pairs={{0,11},{1,10},{2,9},{3,8},{4,15},{5,14},{6,13},{7,12},{8,3},{9,2},... | collective-permute-start | bytes 98312 | tf_op jit(solution)/shard_map/ppermute | solution.py:321
  45.4 13.7 %collective-permute-start.30 = (f32[8,2048]{1,0:T(8,128)S(1)}, f32[8,2048]{1,0:T(8,128)S(1)}, u32[]{:S(2)}, u32[]{:S(2)}) collective-permute-start(f32[8,2048]{1,0:T(8,128)S(1)} %slice_bitcast_fusion), channel_id=1, source_target_pairs={{0,16},{16,0},{1,17},{17,1},{2,18},{18,2},{3,19},{19,3},{4,20},{20... | collective-permute-start | bytes 196616 | tf_op jit(solution)/shard_map/ppermute | solution.py:367
  47.0 8.0 %collective-permute-start.26 = (f32[2,2,8,256]{3,2,1,0:T(8,128)S(1)}, f32[2,2,8,256]{3,2,1,0:T(8,128)S(1)}, u32[]{:S(2)}, u32[]{:S(2)}) collective-permute-start(f32[2,2,8,256]{3,2,1,0:T(8,128)S(1)} %get-tuple-element.70), channel_id=1, source_target_pairs={{0,12},{1,13},{2,14},{3,15},{4,8},{5,9},{6,10},{7,11},{8,4},{9,5},... | collective-permute-start | bytes 98312 | tf_op jit(solution)/shard_map/ppermute | solution.py:321
  47.6 7.4 %collective-permute-start.27 = (f32[2,2,8,256]{3,2,1,0:T(8,128)S(1)}, f32[2,2,8,256]{3,2,1,0:T(8,128)S(1)}, u32[]{:S(2)}, u32[]{:S(2)}) collective-permute-start(f32[2,2,8,256]{3,2,1,0:T(8,128)S(1)} %get-tuple-element.71), channel_id=1, source_target_pairs={{0,13},{1,12},{2,15},{3,14},{4,9},{5,8},{6,11},{7,10},{8,5},{9,4},... | collective-permute-start | bytes 98312 | tf_op jit(solution)/shard_map/ppermute | solution.py:321
  50.3 6.7 %collective-permute-start.28 = (f32[2,2,8,256]{3,2,1,0:T(8,128)S(1)}, f32[2,2,8,256]{3,2,1,0:T(8,128)S(1)}, u32[]{:S(2)}, u32[]{:S(2)}) collective-permute-start(f32[2,2,8,256]{3,2,1,0:T(8,128)S(1)} %get-tuple-element.72), channel_id=1, source_target_pairs={{0,14},{1,15},{2,12},{3,13},{4,10},{5,11},{6,8},{7,9},{8,6},{9,7},... | collective-permute-start | bytes 98312 | tf_op jit(solution)/shard_map/ppermute | solution.py:321
  51.2 6.1 %collective-permute-start.29 = (f32[2,2,8,256]{3,2,1,0:T(8,128)S(1)}, f32[2,2,8,256]{3,2,1,0:T(8,128)S(1)}, u32[]{:S(2)}, u32[]{:S(2)}) collective-permute-start(f32[2,2,8,256]{3,2,1,0:T(8,128)S(1)} %get-tuple-element.73), channel_id=1, source_target_pairs={{0,15},{1,14},{2,13},{3,12},{4,11},{5,10},{6,9},{7,8},{8,7},{9,6},... | collective-permute-start | bytes 98312 | tf_op jit(solution)/shard_map/ppermute | solution.py:321
  57.3 0.7 %copy-start.7 = (f32[128]{0:T(128)S(1)}, f32[128]{0:T(128)}, u32[]{:S(2)}) copy-start(f32[128]{0:T(128)} %param.12) | copy-start | bytes 1540

commit v12 on v1

--- a/solution.py
+++ b/solution.py
@@ -1,3 +1,4 @@
+import itertools
 import math
 
 import jax
@@ -152,8 +153,8 @@
             copy(b, 2 * kind + 1).wait()
             product = held[2 * kind, b] * held[2 * kind + 1, b]
             turned[:, kind, b] = jnp.transpose(product).reshape(shards, channels, tokens)
-    for step in range(shards):
-        sent[step][...] = turned[me ^ step]
+    for ref, step in zip(sent, exchange_steps(shards)):
+        ref[...] = turned[me ^ step]
 
 
 def spectral_kernel(
@@ -171,8 +172,8 @@
     groups = lag_ref.shape[0]
     group = lax.axis_index("batch")
     me = lax.axis_index("seq")
-    for step in range(shards):
-        held_ref[me ^ step] = received[step][...]
+    for ref, step in zip(received, exchange_steps(shards)):
+        held_ref[me ^ step] = ref[...]
 
     def store(b, p, value):
         first, _ = factors_of(count)
@@ -285,15 +286,15 @@
         forward(load_kind(1), upstream_spec)
         inverse(correlate, emit_kind(1))
         inverse(lags, emit_lag)
-    for step in range(shards):
-        returned[step][...] = back_ref[me ^ step]
+    for ref, step in zip(returned, exchange_steps(shards)):
+        ref[...] = back_ref[me ^ step]
 
 
 def output_kernel(query_ref, key_ref, value_ref, cotangent_ref, skip_ref, *refs):
     *home, output_ref, query_grad_ref, key_grad_ref, value_grad_ref, turned = refs
     _, batch, channels, tokens = home[0].shape
     me = lax.axis_index("seq")
-    for step, block in enumerate(home):
+    for block, step in zip(home, exchange_steps(len(home))):
         turned[me ^ step] = block[...]
     skip = skip_ref[...]
 
@@ -310,12 +311,18 @@
         value_grad_ref[b] = mixed_grad * key
 
 
+def exchange_steps(shards):
+    far, near = range(shards - 1, shards // 2 - 1, -1), range(shards // 2 - 1, 0, -1)
+    both = itertools.zip_longest(far, near)
+    return [0] + [step for pair in both for step in pair if step is not None]
+
+
 def exchange(blocks):
     shards = len(blocks)
-    received = [blocks[0]] + [None] * (shards - 1)
-    for step in range(shards - 1, 0, -1):
+    received = []
+    for block, step in zip(blocks, exchange_steps(shards)):
         pairs = [(source, source ^ step) for source in range(shards)]
-        received[step] = lax.ppermute(blocks[step], "seq", pairs)
+        received.append(lax.ppermute(block, "seq", pairs) if step else block)
     return received
 
 

time: 59.9 us -> 58.2 us (0.972)
  waiting for transfers between devices: 8.72 us -> 7.34 us
    ppermute x30, waiting for transfers between devices: 8.72 us -> 7.34 us  [exchange(): received.append(lax.ppermute(block, 'seq', pairs) if step else block)]
  transfers between devices with their start and end apart: 31 -> 31, of which waited for: 6 -> 7; matrix products, arithmetic and copies ran while one was open for 0% -> 0% of each run, Pallas kernels for 2% -> 2%
where the time goes in v12:
time: 58.2 us; the launch traced here: 58 us
  starting transfers between devices  43.4 us (75%)
  waiting for transfers between devices  7.34 us (13%)
  Pallas kernels  5.23 us (9%)
  between operations  0.76 us (1%)
  local copies, waits for them, and re-layouts  0.68 us (1%)
  other arithmetic  0.64 us (1%)
    ppermute x30, starting transfers between devices, exchange(): received.append(lax.ppermute(block, 'seq', pairs) if step else block)  41.8 us
    ppermute x30, waiting for transfers between devices, exchange(): received.append(lax.ppermute(block, 'seq', pairs) if step else block)  7.34 us
    pallas_call x1, Pallas kernels, per_device(): pl.pallas_call(body, out_shape=(block,) * shards + (jax.ShapeDtypeStruct(...  2.46 us
    pallas_call x1, Pallas kernels, per_device(): pl.pallas_call(gate_kernel, out_shape=(block,) * shards, in_specs=[pl.Blo...  1.58 us
    ppermute x1, starting transfers between devices, per_device(): filter_grad = filter_grad + lax.ppermute(lag[step], 'batch', pairs)  1.56 us
    pallas_call x1, Pallas kernels, per_device(): pl.pallas_call(output_kernel, out_shape=(token_out,) * 4, scratch_shapes=...  1.19 us
  transfers between devices with their start and end apart: 31, of which 7 were waited for; matrix products, arithmetic and copies ran while one was open for 0% of the time, Pallas kernels for 2%

profile of v12, /device:TPU:0, one launch (start us, length us, event | category | flops | bytes accessed | tf_op | source)
XLA Modules:
  0.0 58.0 jit_solution(7043874650362089109)
XLA Ops:
  0.6 0.0 copy-start.4
  0.7 0.0 copy-start.6
  0.7 1.6 %gate.1 = (f32[2,2,8,256]{3,2,1,0:T(8,128)S(1)}, f32[2,2,8,256]{3,2,1,0:T(8,128)S(1)}, f32[2,2,8,256]{3,2,1,0:T(8,128)S(1)}, f32[2,2,8,256]{3,2,1,0:T(8,128)S(1)...) custom-call(f32[2,256,128]{2,1,0:T(8,128)} %query_ref.1, ...), custom_call_target="tpu_custom_call" | custom-call | tf_op jit(solution)/shard_map/gate/pallas_call | solution.py:338
  2.3 5.5 %collective-permute-start = (f32[2,2,8,256]{3,2,1,0:T(8,128)S(1)}, f32[2,2,8,256]{3,2,1,0:T(8,128)S(1)}, u32[]{:S(2)}, u32[]{:S(2)}) collective-permute-start(f32[2,2,8,256]{3,2,1,0:T(8,128)S(1)} %get-tuple-element.43), channel_id=1, source_target_pairs={{0,15},{1,14},{2,13},{3,12},{4,11},{5,10},{6,9},{7,8},{8,7},{9,6},... | collective-permute-start | bytes 98312 | tf_op jit(solution)/shard_map/ppermute | solution.py:325
  7.8 0.0 collective-permute-start.1
  7.8 2.1 %collective-permute-start.2 = (f32[2,2,8,256]{3,2,1,0:T(8,128)S(1)}, f32[2,2,8,256]{3,2,1,0:T(8,128)S(1)}, u32[]{:S(2)}, u32[]{:S(2)}) collective-permute-start(f32[2,2,8,256]{3,2,1,0:T(8,128)S(1)} %get-tuple-element.45), channel_id=1, source_target_pairs={{0,14},{1,15},{2,12},{3,13},{4,10},{5,11},{6,8},{7,9},{8,6},{9,7},... | collective-permute-start | bytes 98312 | tf_op jit(solution)/shard_map/ppermute | solution.py:325
  9.8 1.1 %collective-permute-start.3 = (f32[2,2,8,256]{3,2,1,0:T(8,128)S(1)}, f32[2,2,8,256]{3,2,1,0:T(8,128)S(1)}, u32[]{:S(2)}, u32[]{:S(2)}) collective-permute-start(f32[2,2,8,256]{3,2,1,0:T(8,128)S(1)} %get-tuple-element.46), channel_id=1, source_target_pairs={{0,6},{1,7},{2,4},{3,5},{4,2},{5,3},{6,0},{7,1},{8,14},{9,15},{10,... | collective-permute-start | bytes 98312 | tf_op jit(solution)/shard_map/ppermute | solution.py:325
  11.0 1.7 %collective-permute-start.4 = (f32[2,2,8,256]{3,2,1,0:T(8,128)S(1)}, f32[2,2,8,256]{3,2,1,0:T(8,128)S(1)}, u32[]{:S(2)}, u32[]{:S(2)}) collective-permute-start(f32[2,2,8,256]{3,2,1,0:T(8,128)S(1)} %get-tuple-element.47), channel_id=1, source_target_pairs={{0,13},{1,12},{2,15},{3,14},{4,9},{5,8},{6,11},{7,10},{8,5},{9,4},... | collective-permute-start | bytes 98312 | tf_op jit(solution)/shard_map/ppermute | solution.py:325
  12.7 0.0 collective-permute-done.refs_4_
  12.7 0.7 %collective-permute-start.5 = (f32[2,2,8,256]{3,2,1,0:T(8,128)S(1)}, f32[2,2,8,256]{3,2,1,0:T(8,128)S(1)}, u32[]{:S(2)}, u32[]{:S(2)}) collective-permute-start(f32[2,2,8,256]{3,2,1,0:T(8,128)S(1)} %get-tuple-element.48), channel_id=1, source_target_pairs={{0,5},{1,4},{2,7},{3,6},{4,1},{5,0},{6,3},{7,2},{8,13},{9,12},{10,... | collective-permute-start | bytes 98312 | tf_op jit(solution)/shard_map/ppermute | solution.py:325
  13.4 0.0 collective-permute-done.1.refs_5_
  13.4 1.1 %collective-permute-start.6 = (f32[2,2,8,256]{3,2,1,0:T(8,128)S(1)}, f32[2,2,8,256]{3,2,1,0:T(8,128)S(1)}, u32[]{:S(2)}, u32[]{:S(2)}) collective-permute-start(f32[2,2,8,256]{3,2,1,0:T(8,128)S(1)} %get-tuple-element.49), channel_id=1, source_target_pairs={{0,12},{1,13},{2,14},{3,15},{4,8},{5,9},{6,10},{7,11},{8,4},{9,5},... | collective-permute-start | bytes 98312 | tf_op jit(solution)/shard_map/ppermute | solution.py:325
  14.5 0.0 collective-permute-done.2.refs_6_
  14.5 1.2 %collective-permute-start.7 = (f32[2,2,8,256]{3,2,1,0:T(8,128)S(1)}, f32[2,2,8,256]{3,2,1,0:T(8,128)S(1)}, u32[]{:S(2)}, u32[]{:S(2)}) collective-permute-start(f32[2,2,8,256]{3,2,1,0:T(8,128)S(1)} %get-tuple-element.50), channel_id=1, source_target_pairs={{0,4},{1,5},{2,6},{3,7},{4,0},{5,1},{6,2},{7,3},{8,12},{9,13},{10,... | collective-permute-start | bytes 98312 | tf_op jit(solution)/shard_map/ppermute | solution.py:325
  15.7 0.0 collective-permute-done.3.refs_7_
  15.7 2.8 %collective-permute-start.8 = (f32[2,2,8,256]{3,2,1,0:T(8,128)S(1)}, f32[2,2,8,256]{3,2,1,0:T(8,128)S(1)}, u32[]{:S(2)}, u32[]{:S(2)}) collective-permute-start(f32[2,2,8,256]{3,2,1,0:T(8,128)S(1)} %get-tuple-element.51), channel_id=1, source_target_pairs={{0,11},{1,10},{2,9},{3,8},{4,15},{5,14},{6,13},{7,12},{8,3},{9,2},... | collective-permute-start | bytes 98312 | tf_op jit(solution)/shard_map/ppermute | solution.py:325
  18.4 0.0 collective-permute-done.4.refs_8_
  18.4 0.5 collective-permute-start.9
  19.0 0.0 collective-permute-done.5.refs_9_
  19.0 1.8 %collective-permute-start.10 = (f32[2,2,8,256]{3,2,1,0:T(8,128)S(1)}, f32[2,2,8,256]{3,2,1,0:T(8,128)S(1)}, u32[]{:S(2)}, u32[]{:S(2)}) collective-permute-start(f32[2,2,8,256]{3,2,1,0:T(8,128)S(1)} %get-tuple-element.53), channel_id=1, source_target_pairs={{0,10},{1,11},{2,8},{3,9},{4,14},{5,15},{6,12},{7,13},{8,2},{9,3},... | collective-permute-start | bytes 98312 | tf_op jit(solution)/shard_map/ppermute | solution.py:325
  20.7 0.0 collective-permute-done.6.refs_10_
  20.7 0.5 collective-permute-start.11
  21.3 1.2 %collective-permute-start.12 = (f32[2,2,8,256]{3,2,1,0:T(8,128)S(1)}, f32[2,2,8,256]{3,2,1,0:T(8,128)S(1)}, u32[]{:S(2)}, u32[]{:S(2)}) collective-permute-start(f32[2,2,8,256]{3,2,1,0:T(8,128)S(1)} %get-tuple-element.55), channel_id=1, source_target_pairs={{0,9},{1,8},{2,11},{3,10},{4,13},{5,12},{6,15},{7,14},{8,1},{9,0},... | collective-permute-start | bytes 98312 | tf_op jit(solution)/shard_map/ppermute | solution.py:325
  22.5 0.0 collective-permute-done.8.refs_12_
  22.5 1.0 %collective-permute-start.13 = (f32[2,2,8,256]{3,2,1,0:T(8,128)S(1)}, f32[2,2,8,256]{3,2,1,0:T(8,128)S(1)}, u32[]{:S(2)}, u32[]{:S(2)}) collective-permute-start(f32[2,2,8,256]{3,2,1,0:T(8,128)S(1)} %get-tuple-element.56), channel_id=1, source_target_pairs={{0,1},{1,0},{2,3},{3,2},{4,5},{5,4},{6,7},{7,6},{8,9},{9,8},{10,11... | collective-permute-start | bytes 98312 | tf_op jit(solution)/shard_map/ppermute | solution.py:325
  23.5 0.0 collective-permute-done.9.refs_13_
  23.5 0.8 %collective-permute-start.14 = (f32[2,2,8,256]{3,2,1,0:T(8,128)S(1)}, f32[2,2,8,256]{3,2,1,0:T(8,128)S(1)}, u32[]{:S(2)}, u32[]{:S(2)}) collective-permute-start(f32[2,2,8,256]{3,2,1,0:T(8,128)S(1)} %get-tuple-element.57), channel_id=1, source_target_pairs={{0,8},{1,9},{2,10},{3,11},{4,12},{5,13},{6,14},{7,15},{8,0},{9,1},... | collective-permute-start | bytes 98312 | tf_op jit(solution)/shard_map/ppermute | solution.py:325
  24.3 0.6 collective-permute-done.10.refs_14_
  24.9 0.1 collective-permute-done.11.refs_15_
  25.0 1.7 %collective-permute-done.12.refs_16_ = f32[2,2,8,256]{3,2,1,0:T(8,128)S(1)} collective-permute-done((f32[2,2,8,256]{3,2,1,0:T(8,128)S(1)}, f32[2,2,8,256]{3,2,1,0:T(8,128)S(1)}, u32[]{:S(2)}, u32[]{:S(2)}) %collective-permute-start.12) | collective-permute-done | bytes 32800 | tf_op jit(solution)/shard_map/ppermute | solution.py:325
  26.7 0.0 collective-permute-done.13.refs_17_
  26.7 1.8 %collective-permute-done.14.refs_18_ = f32[2,2,8,256]{3,2,1,0:T(8,128)S(1)} collective-permute-done((f32[2,2,8,256]{3,2,1,0:T(8,128)S(1)}, f32[2,2,8,256]{3,2,1,0:T(8,128)S(1)}, u32[]{:S(2)}, u32[]{:S(2)}) %collective-permute-start.14) | collective-permute-done | bytes 32800 | tf_op jit(solution)/shard_map/ppermute | solution.py:325
  28.5 0.0 copy-start
  28.5 0.0 copy-start.1
  28.5 0.0 copy-start.2
  28.5 0.0 copy-start.3
  28.6 2.5 %spectral.1 = (f32[2,2,8,256]{3,2,1,0:T(8,128)S(1)}, f32[2,2,8,256]{3,2,1,0:T(8,128)S(1)}, f32[2,2,8,256]{3,2,1,0:T(8,128)S(1)}, f32[2,2,8,256]{3,2,1,0:T(8,128)...) custom-call(f32[8,4096]{1,0:T(8,128)S(1)} %copy-done.5, ...), custom_call_target="tpu_custom_call" | custom-call | tf_op jit(solution)/shard_map/spectral/pallas_call | solution.py:359
  31.0 2.4 %collective-permute-start.15 = (f32[2,2,8,256]{3,2,1,0:T(8,128)S(1)}, f32[2,2,8,256]{3,2,1,0:T(8,128)S(1)}, u32[]{:S(2)}, u32[]{:S(2)}) collective-permute-start(f32[2,2,8,256]{3,2,1,0:T(8,128)S(1)} %get-tuple-element.59), channel_id=1, source_target_pairs={{0,15},{1,14},{2,13},{3,12},{4,11},{5,10},{6,9},{7,8},{8,7},{9,6},... | collective-permute-start | bytes 98312 | tf_op jit(solution)/shard_map/ppermute | solution.py:325
  33.4 0.0 collective-permute-start.16
  33.4 3.3 %collective-permute-start.17 = (f32[2,2,8,256]{3,2,1,0:T(8,128)S(1)}, f32[2,2,8,256]{3,2,1,0:T(8,128)S(1)}, u32[]{:S(2)}, u32[]{:S(2)}) collective-permute-start(f32[2,2,8,256]{3,2,1,0:T(8,128)S(1)} %get-tuple-element.61), channel_id=1, source_target_pairs={{0,14},{1,15},{2,12},{3,13},{4,10},{5,11},{6,8},{7,9},{8,6},{9,7},... | collective-permute-start | bytes 98312 | tf_op jit(solution)/shard_map/ppermute | solution.py:325
  36.7 0.9 %collective-permute-start.18 = (f32[2,2,8,256]{3,2,1,0:T(8,128)S(1)}, f32[2,2,8,256]{3,2,1,0:T(8,128)S(1)}, u32[]{:S(2)}, u32[]{:S(2)}) collective-permute-start(f32[2,2,8,256]{3,2,1,0:T(8,128)S(1)} %get-tuple-element.62), channel_id=1, source_target_pairs={{0,6},{1,7},{2,4},{3,5},{4,2},{5,3},{6,0},{7,1},{8,14},{9,15},{10,... | collective-permute-start | bytes 98312 | tf_op jit(solution)/shard_map/ppermute | solution.py:325
  37.6 0.8 %collective-permute-start.19 = (f32[2,2,8,256]{3,2,1,0:T(8,128)S(1)}, f32[2,2,8,256]{3,2,1,0:T(8,128)S(1)}, u32[]{:S(2)}, u32[]{:S(2)}) collective-permute-start(f32[2,2,8,256]{3,2,1,0:T(8,128)S(1)} %get-tuple-element.63), channel_id=1, source_target_pairs={{0,13},{1,12},{2,15},{3,14},{4,9},{5,8},{6,11},{7,10},{8,5},{9,4},... | collective-permute-start | bytes 98312 | tf_op jit(solution)/shard_map/ppermute | solution.py:325
  38.4 0.0 collective-permute-done.15.refs_1_
  38.4 0.6 %collective-permute-start.20 = (f32[2,2,8,256]{3,2,1,0:T(8,128)S(1)}, f32[2,2,8,256]{3,2,1,0:T(8,128)S(1)}, u32[]{:S(2)}, u32[]{:S(2)}) collective-permute-start(f32[2,2,8,256]{3,2,1,0:T(8,128)S(1)} %get-tuple-element.64), channel_id=1, source_target_pairs={{0,5},{1,4},{2,7},{3,6},{4,1},{5,0},{6,3},{7,2},{8,13},{9,12},{10,... | collective-permute-start | bytes 98312 | tf_op jit(solution)/shard_map/ppermute | solution.py:325
  39.0 2.3 %collective-permute-start.21 = (f32[2,2,8,256]{3,2,1,0:T(8,128)S(1)}, f32[2,2,8,256]{3,2,1,0:T(8,128)S(1)}, u32[]{:S(2)}, u32[]{:S(2)}) collective-permute-start(f32[2,2,8,256]{3,2,1,0:T(8,128)S(1)} %get-tuple-element.65), channel_id=1, source_target_pairs={{0,12},{1,13},{2,14},{3,15},{4,8},{5,9},{6,10},{7,11},{8,4},{9,5},... | collective-permute-start | bytes 98312 | tf_op jit(solution)/shard_map/ppermute | solution.py:325
  41.3 0.0 collective-permute-done.17.refs_3_
  41.3 0.9 %collective-permute-start.22 = (f32[2,2,8,256]{3,2,1,0:T(8,128)S(1)}, f32[2,2,8,256]{3,2,1,0:T(8,128)S(1)}, u32[]{:S(2)}, u32[]{:S(2)}) collective-permute-start(f32[2,2,8,256]{3,2,1,0:T(8,128)S(1)} %get-tuple-element.66), channel_id=1, source_target_pairs={{0,4},{1,5},{2,6},{3,7},{4,0},{5,1},{6,2},{7,3},{8,12},{9,13},{10,... | collective-permute-start | bytes 98312 | tf_op jit(solution)/shard_map/ppermute | solution.py:325
  42.2 0.0 collective-permute-done.18.refs_4_
  42.2 1.6 %collective-permute-start.23 = (f32[2,2,8,256]{3,2,1,0:T(8,128)S(1)}, f32[2,2,8,256]{3,2,1,0:T(8,128)S(1)}, u32[]{:S(2)}, u32[]{:S(2)}) collective-permute-start(f32[2,2,8,256]{3,2,1,0:T(8,128)S(1)} %get-tuple-element.67), channel_id=1, source_target_pairs={{0,11},{1,10},{2,9},{3,8},{4,15},{5,14},{6,13},{7,12},{8,3},{9,2},... | collective-permute-start | bytes 98312 | tf_op jit(solution)/shard_map/ppermute | solution.py:325
  43.9 0.7 %collective-permute-start.24 = (f32[2,2,8,256]{3,2,1,0:T(8,128)S(1)}, f32[2,2,8,256]{3,2,1,0:T(8,128)S(1)}, u32[]{:S(2)}, u32[]{:S(2)}) collective-permute-start(f32[2,2,8,256]{3,2,1,0:T(8,128)S(1)} %get-tuple-element.68), channel_id=1, source_target_pairs={{0,3},{1,2},{2,1},{3,0},{4,7},{5,6},{6,5},{7,4},{8,11},{9,10},{10,... | collective-permute-start | bytes 98312 | tf_op jit(solution)/shard_map/ppermute | solution.py:325
  44.6 2.6 %collective-permute-start.25 = (f32[2,2,8,256]{3,2,1,0:T(8,128)S(1)}, f32[2,2,8,256]{3,2,1,0:T(8,128)S(1)}, u32[]{:S(2)}, u32[]{:S(2)}) collective-permute-start(f32[2,2,8,256]{3,2,1,0:T(8,128)S(1)} %get-tuple-element.69), channel_id=1, source_target_pairs={{0,10},{1,11},{2,8},{3,9},{4,14},{5,15},{6,12},{7,13},{8,2},{9,3},... | collective-permute-start | bytes 98312 | tf_op jit(solution)/shard_map/ppermute | solution.py:325
  47.2 1.6 %collective-permute-start.30 = (f32[8,2048]{1,0:T(8,128)S(1)}, f32[8,2048]{1,0:T(8,128)S(1)}, u32[]{:S(2)}, u32[]{:S(2)}) collective-permute-start(f32[8,2048]{1,0:T(8,128)S(1)} %slice_bitcast_fusion), channel_id=1, source_target_pairs={{0,16},{16,0},{1,17},{17,1},{2,18},{18,2},{3,19},{19,3},{4,20},{20... | collective-permute-start | bytes 196616 | tf_op jit(solution)/shard_map/ppermute | solution.py:371
  48.8 0.6 %collective-permute-start.26 = (f32[2,2,8,256]{3,2,1,0:T(8,128)S(1)}, f32[2,2,8,256]{3,2,1,0:T(8,128)S(1)}, u32[]{:S(2)}, u32[]{:S(2)}) collective-permute-start(f32[2,2,8,256]{3,2,1,0:T(8,128)S(1)} %get-tuple-element.70), channel_id=1, source_target_pairs={{0,2},{1,3},{2,0},{3,1},{4,6},{5,7},{6,4},{7,5},{8,10},{9,11},{10,... | collective-permute-start | bytes 98312 | tf_op jit(solution)/shard_map/ppermute | solution.py:325
  49.4 1.3 %collective-permute-start.28 = (f32[2,2,8,256]{3,2,1,0:T(8,128)S(1)}, f32[2,2,8,256]{3,2,1,0:T(8,128)S(1)}, u32[]{:S(2)}, u32[]{:S(2)}) collective-permute-start(f32[2,2,8,256]{3,2,1,0:T(8,128)S(1)} %get-tuple-element.72), channel_id=1, source_target_pairs={{0,1},{1,0},{2,3},{3,2},{4,5},{5,4},{6,7},{7,6},{8,9},{9,8},{10,11... | collective-permute-start | bytes 98312 | tf_op jit(solution)/shard_map/ppermute | solution.py:325
  50.7 0.0 collective-permute-done.25.refs_11_
  50.7 1.7 %collective-permute-start.29 = (f32[2,2,8,256]{3,2,1,0:T(8,128)S(1)}, f32[2,2,8,256]{3,2,1,0:T(8,128)S(1)}, u32[]{:S(2)}, u32[]{:S(2)}) collective-permute-start(f32[2,2,8,256]{3,2,1,0:T(8,128)S(1)} %get-tuple-element.73), channel_id=1, source_target_pairs={{0,8},{1,9},{2,10},{3,11},{4,12},{5,13},{6,14},{7,15},{8,0},{9,1},... | collective-permute-start | bytes 98312 | tf_op jit(solution)/shard_map/ppermute | solution.py:325
  52.5 0.2 collective-permute-done.26.refs_12_
  52.7 1.1 %collective-permute-done.27.refs_13_ = f32[2,2,8,256]{3,2,1,0:T(8,128)S(1)} collective-permute-done((f32[2,2,8,256]{3,2,1,0:T(8,128)S(1)}, f32[2,2,8,256]{3,2,1,0:T(8,128)S(1)}, u32[]{:S(2)}, u32[]{:S(2)}) %collective-permute-start.27) | collective-permute-done | bytes 32800 | tf_op jit(solution)/shard_map/ppermute | solution.py:325
  53.8 0.0 collective-permute-done.28.refs_14_
  53.8 1.7 %collective-permute-done.29.refs_15_ = f32[2,2,8,256]{3,2,1,0:T(8,128)S(1)} collective-permute-done((f32[2,2,8,256]{3,2,1,0:T(8,128)S(1)}, f32[2,2,8,256]{3,2,1,0:T(8,128)S(1)}, u32[]{:S(2)}, u32[]{:S(2)}) %collective-permute-start.29) | collective-permute-done | bytes 32800 | tf_op jit(solution)/shard_map/ppermute | solution.py:325
  55.6 0.6 %copy-done.7 = f32[128]{0:T(128)S(1)} copy-done((f32[128]{0:T(128)S(1)}, f32[128]{0:T(128)}, u32[]{:S(2)}) %copy-start.7) | copy-done | bytes 536
  56.2 1.2 %outputs.1 = (f32[2,256,128]{2,1,0:T(8,128)}, f32[2,256,128]{2,1,0:T(8,128)}, f32[2,256,128]{2,1,0:T(8,128)}, f32[2,256,128]{2,1,0:T(8,128)}) custom-call(f32[2,256,128]{2,1,0:T(8,128)S(1)} %copy-done, f32[2,256,128]{2,1,0:T(8,128)S(1)} %copy-done.1, f32[2,256,128]{2,1,0:T(8,128)S(1)} %copy-done.2, f32[2,256,128]{2,1,0:T(8,128)S(1)} %copy-done.3, ...), custom_call_target="tpu_custom_call" | custom-call | tf_op jit(solution)/shard_map/outputs/pallas_call | solution.py:373
  57.4 0.0 collective-permute-done.30
  57.4 0.6 %bitcast_add_fusion = f32[8,2048]{1,0:T(8,128)} fusion(f32[8,2048]{1,0:T(8,128)S(1)} %collective-permute-done.30, f32[2,8,2048]{2,1,0:T(8,128)S(1)} %get-tuple-element.78), kind=kLoop, calls=%fused_computation | loop fusion | flops 16384 | bytes 196608 | tf_op jit(solution)/shard_map/add | solution.py:371
  (19 shorter events, 0.0 us)
Async XLA Ops:
  0.6 27.9 %copy-start.4 = (bf16[768,256]{1,0:T(8,128)(2,1)S(1)}, bf16[768,256]{1,0:T(8,128)(2,1)}, u32[]{:S(2)}) copy-start(bf16[768,256]{1,0:T(8,128)(2,1)} %constant.5.clone.refs_2_) | copy-start | bytes 1179652
  0.6 27.9 %copy-start.5 = (f32[8,4096]{1,0:T(8,128)S(1)}, f32[8,4096]{1,0:T(8,128)}, u32[]{:S(2)}) copy-start(f32[8,4096]{1,0:T(8,128)} %refs_0_.1) | copy-start | bytes 393220
  0.7 27.9 %copy-start.6 = (f32[64,256]{1,0:T(8,128)S(1)}, f32[64,256]{1,0:T(8,128)}, u32[]{:S(2)}) copy-start(f32[64,256]{1,0:T(8,128)} %constant.4.clone.refs_1_) | copy-start | bytes 196612
  2.3 10.5 %collective-permute-start = (f32[2,2,8,256]{3,2,1,0:T(8,128)S(1)}, f32[2,2,8,256]{3,2,1,0:T(8,128)S(1)}, u32[]{:S(2)}, u32[]{:S(2)}) collective-permute-start(f32[2,2,8,256]{3,2,1,0:T(8,128)S(1)} %get-tuple-element.43), channel_id=1, source_target_pairs={{0,15},{1,14},{2,13},{3,12},{4,11},{5,10},{6,9},{7,8},{8,7},{9,6},... | collective-permute-start | bytes 98312 | tf_op jit(solution)/shard_map/ppermute | solution.py:325
  7.8 5.6 %collective-permute-start.1 = (f32[2,2,8,256]{3,2,1,0:T(8,128)S(1)}, f32[2,2,8,256]{3,2,1,0:T(8,128)S(1)}, u32[]{:S(2)}, u32[]{:S(2)}) collective-permute-start(f32[2,2,8,256]{3,2,1,0:T(8,128)S(1)} %get-tuple-element.44), channel_id=1, source_target_pairs={{0,7},{1,6},{2,5},{3,4},{4,3},{5,2},{6,1},{7,0},{8,15},{9,14},{10,... | collective-permute-start | bytes 98312 | tf_op jit(solution)/shard_map/ppermute | solution.py:325
  7.8 6.7 %collective-permute-start.2 = (f32[2,2,8,256]{3,2,1,0:T(8,128)S(1)}, f32[2,2,8,256]{3,2,1,0:T(8,128)S(1)}, u32[]{:S(2)}, u32[]{:S(2)}) collective-permute-start(f32[2,2,8,256]{3,2,1,0:T(8,128)S(1)} %get-tuple-element.45), channel_id=1, source_target_pairs={{0,14},{1,15},{2,12},{3,13},{4,10},{5,11},{6,8},{7,9},{8,6},{9,7},... | collective-permute-start | bytes 98312 | tf_op jit(solution)/shard_map/ppermute | solution.py:325
  9.8 5.8 %collective-permute-start.3 = (f32[2,2,8,256]{3,2,1,0:T(8,128)S(1)}, f32[2,2,8,256]{3,2,1,0:T(8,128)S(1)}, u32[]{:S(2)}, u32[]{:S(2)}) collective-permute-start(f32[2,2,8,256]{3,2,1,0:T(8,128)S(1)} %get-tuple-element.46), channel_id=1, source_target_pairs={{0,6},{1,7},{2,4},{3,5},{4,2},{5,3},{6,0},{7,1},{8,14},{9,15},{10,... | collective-permute-start | bytes 98312 | tf_op jit(solution)/shard_map/ppermute | solution.py:325
  11.0 7.5 %collective-permute-start.4 = (f32[2,2,8,256]{3,2,1,0:T(8,128)S(1)}, f32[2,2,8,256]{3,2,1,0:T(8,128)S(1)}, u32[]{:S(2)}, u32[]{:S(2)}) collective-permute-start(f32[2,2,8,256]{3,2,1,0:T(8,128)S(1)} %get-tuple-element.47), channel_id=1, source_target_pairs={{0,13},{1,12},{2,15},{3,14},{4,9},{5,8},{6,11},{7,10},{8,5},{9,4},... | collective-permute-start | bytes 98312 | tf_op jit(solution)/shard_map/ppermute | solution.py:325
  12.7 6.3 %collective-permute-start.5 = (f32[2,2,8,256]{3,2,1,0:T(8,128)S(1)}, f32[2,2,8,256]{3,2,1,0:T(8,128)S(1)}, u32[]{:S(2)}, u32[]{:S(2)}) collective-permute-start(f32[2,2,8,256]{3,2,1,0:T(8,128)S(1)} %get-tuple-element.48), channel_id=1, source_target_pairs={{0,5},{1,4},{2,7},{3,6},{4,1},{5,0},{6,3},{7,2},{8,13},{9,12},{10,... | collective-permute-start | bytes 98312 | tf_op jit(solution)/shard_map/ppermute | solution.py:325
  13.4 7.3 %collective-permute-start.6 = (f32[2,2,8,256]{3,2,1,0:T(8,128)S(1)}, f32[2,2,8,256]{3,2,1,0:T(8,128)S(1)}, u32[]{:S(2)}, u32[]{:S(2)}) collective-permute-start(f32[2,2,8,256]{3,2,1,0:T(8,128)S(1)} %get-tuple-element.49), channel_id=1, source_target_pairs={{0,12},{1,13},{2,14},{3,15},{4,8},{5,9},{6,10},{7,11},{8,4},{9,5},... | collective-permute-start | bytes 98312 | tf_op jit(solution)/shard_map/ppermute | solution.py:325
  14.5 6.8 %collective-permute-start.7 = (f32[2,2,8,256]{3,2,1,0:T(8,128)S(1)}, f32[2,2,8,256]{3,2,1,0:T(8,128)S(1)}, u32[]{:S(2)}, u32[]{:S(2)}) collective-permute-start(f32[2,2,8,256]{3,2,1,0:T(8,128)S(1)} %get-tuple-element.50), channel_id=1, source_target_pairs={{0,4},{1,5},{2,6},{3,7},{4,0},{5,1},{6,2},{7,3},{8,12},{9,13},{10,... | collective-permute-start | bytes 98312 | tf_op jit(solution)/shard_map/ppermute | solution.py:325
  15.7 6.8 %collective-permute-start.8 = (f32[2,2,8,256]{3,2,1,0:T(8,128)S(1)}, f32[2,2,8,256]{3,2,1,0:T(8,128)S(1)}, u32[]{:S(2)}, u32[]{:S(2)}) collective-permute-start(f32[2,2,8,256]{3,2,1,0:T(8,128)S(1)} %get-tuple-element.51), channel_id=1, source_target_pairs={{0,11},{1,10},{2,9},{3,8},{4,15},{5,14},{6,13},{7,12},{8,3},{9,2},... | collective-permute-start | bytes 98312 | tf_op jit(solution)/shard_map/ppermute | solution.py:325
  18.4 5.1 %collective-permute-start.9 = (f32[2,2,8,256]{3,2,1,0:T(8,128)S(1)}, f32[2,2,8,256]{3,2,1,0:T(8,128)S(1)}, u32[]{:S(2)}, u32[]{:S(2)}) collective-permute-start(f32[2,2,8,256]{3,2,1,0:T(8,128)S(1)} %get-tuple-element.52), channel_id=1, source_target_pairs={{0,3},{1,2},{2,1},{3,0},{4,7},{5,6},{6,5},{7,4},{8,11},{9,10},{10,... | collective-permute-start | bytes 98312 | tf_op jit(solution)/shard_map/ppermute | solution.py:325
  19.0 5.9 %collective-permute-start.10 = (f32[2,2,8,256]{3,2,1,0:T(8,128)S(1)}, f32[2,2,8,256]{3,2,1,0:T(8,128)S(1)}, u32[]{:S(2)}, u32[]{:S(2)}) collective-permute-start(f32[2,2,8,256]{3,2,1,0:T(8,128)S(1)} %get-tuple-element.53), channel_id=1, source_target_pairs={{0,10},{1,11},{2,8},{3,9},{4,14},{5,15},{6,12},{7,13},{8,2},{9,3},... | collective-permute-start | bytes 98312 | tf_op jit(solution)/shard_map/ppermute | solution.py:325
  20.7 4.3 %collective-permute-start.11 = (f32[2,2,8,256]{3,2,1,0:T(8,128)S(1)}, f32[2,2,8,256]{3,2,1,0:T(8,128)S(1)}, u32[]{:S(2)}, u32[]{:S(2)}) collective-permute-start(f32[2,2,8,256]{3,2,1,0:T(8,128)S(1)} %get-tuple-element.54), channel_id=1, source_target_pairs={{0,2},{1,3},{2,0},{3,1},{4,6},{5,7},{6,4},{7,5},{8,10},{9,11},{10,... | collective-permute-start | bytes 98312 | tf_op jit(solution)/shard_map/ppermute | solution.py:325
  21.3 5.4 %collective-permute-start.12 = (f32[2,2,8,256]{3,2,1,0:T(8,128)S(1)}, f32[2,2,8,256]{3,2,1,0:T(8,128)S(1)}, u32[]{:S(2)}, u32[]{:S(2)}) collective-permute-start(f32[2,2,8,256]{3,2,1,0:T(8,128)S(1)} %get-tuple-element.55), channel_id=1, source_target_pairs={{0,9},{1,8},{2,11},{3,10},{4,13},{5,12},{6,15},{7,14},{8,1},{9,0},... | collective-permute-start | bytes 98312 | tf_op jit(solution)/shard_map/ppermute | solution.py:325
  22.5 4.2 %collective-permute-start.13 = (f32[2,2,8,256]{3,2,1,0:T(8,128)S(1)}, f32[2,2,8,256]{3,2,1,0:T(8,128)S(1)}, u32[]{:S(2)}, u32[]{:S(2)}) collective-permute-start(f32[2,2,8,256]{3,2,1,0:T(8,128)S(1)} %get-tuple-element.56), channel_id=1, source_target_pairs={{0,1},{1,0},{2,3},{3,2},{4,5},{5,4},{6,7},{7,6},{8,9},{9,8},{10,11... | collective-permute-start | bytes 98312 | tf_op jit(solution)/shard_map/ppermute | solution.py:325
  23.5 5.0 %collective-permute-start.14 = (f32[2,2,8,256]{3,2,1,0:T(8,128)S(1)}, f32[2,2,8,256]{3,2,1,0:T(8,128)S(1)}, u32[]{:S(2)}, u32[]{:S(2)}) collective-permute-start(f32[2,2,8,256]{3,2,1,0:T(8,128)S(1)} %get-tuple-element.57), channel_id=1, source_target_pairs={{0,8},{1,9},{2,10},{3,11},{4,12},{5,13},{6,14},{7,15},{8,0},{9,1},... | collective-permute-start | bytes 98312 | tf_op jit(solution)/shard_map/ppermute | solution.py:325
  28.5 27.0 %copy-start = (f32[2,256,128]{2,1,0:T(8,128)S(1)}, f32[2,256,128]{2,1,0:T(8,128)}, u32[]{:S(2)}) copy-start(f32[2,256,128]{2,1,0:T(8,128)} %query_ref.1) | copy-start | bytes 786436
  28.5 27.0 %copy-start.1 = (f32[2,256,128]{2,1,0:T(8,128)S(1)}, f32[2,256,128]{2,1,0:T(8,128)}, u32[]{:S(2)}) copy-start(f32[2,256,128]{2,1,0:T(8,128)} %key_ref.1) | copy-start | bytes 786436
  28.5 27.0 %copy-start.2 = (f32[2,256,128]{2,1,0:T(8,128)S(1)}, f32[2,256,128]{2,1,0:T(8,128)}, u32[]{:S(2)}) copy-start(f32[2,256,128]{2,1,0:T(8,128)} %value_ref.1) | copy-start | bytes 786436
  28.5 27.0 %copy-start.3 = (f32[2,256,128]{2,1,0:T(8,128)S(1)}, f32[2,256,128]{2,1,0:T(8,128)}, u32[]{:S(2)}) copy-start(f32[2,256,128]{2,1,0:T(8,128)} %cotangent_ref.1) | copy-start | bytes 786436
  31.0 7.4 %collective-permute-start.15 = (f32[2,2,8,256]{3,2,1,0:T(8,128)S(1)}, f32[2,2,8,256]{3,2,1,0:T(8,128)S(1)}, u32[]{:S(2)}, u32[]{:S(2)}) collective-permute-start(f32[2,2,8,256]{3,2,1,0:T(8,128)S(1)} %get-tuple-element.59), channel_id=1, source_target_pairs={{0,15},{1,14},{2,13},{3,12},{4,11},{5,10},{6,9},{7,8},{8,7},{9,6},... | collective-permute-start | bytes 98312 | tf_op jit(solution)/shard_map/ppermute | solution.py:325
  33.4 5.6 %collective-permute-start.16 = (f32[2,2,8,256]{3,2,1,0:T(8,128)S(1)}, f32[2,2,8,256]{3,2,1,0:T(8,128)S(1)}, u32[]{:S(2)}, u32[]{:S(2)}) collective-permute-start(f32[2,2,8,256]{3,2,1,0:T(8,128)S(1)} %get-tuple-element.60), channel_id=1, source_target_pairs={{0,7},{1,6},{2,5},{3,4},{4,3},{5,2},{6,1},{7,0},{8,15},{9,14},{10,... | collective-permute-start | bytes 98312 | tf_op jit(solution)/shard_map/ppermute | solution.py:325
  33.4 7.9 %collective-permute-start.17 = (f32[2,2,8,256]{3,2,1,0:T(8,128)S(1)}, f32[2,2,8,256]{3,2,1,0:T(8,128)S(1)}, u32[]{:S(2)}, u32[]{:S(2)}) collective-permute-start(f32[2,2,8,256]{3,2,1,0:T(8,128)S(1)} %get-tuple-element.61), channel_id=1, source_target_pairs={{0,14},{1,15},{2,12},{3,13},{4,10},{5,11},{6,8},{7,9},{8,6},{9,7},... | collective-permute-start | bytes 98312 | tf_op jit(solution)/shard_map/ppermute | solution.py:325
  36.7 5.5 %collective-permute-start.18 = (f32[2,2,8,256]{3,2,1,0:T(8,128)S(1)}, f32[2,2,8,256]{3,2,1,0:T(8,128)S(1)}, u32[]{:S(2)}, u32[]{:S(2)}) collective-permute-start(f32[2,2,8,256]{3,2,1,0:T(8,128)S(1)} %get-tuple-element.62), channel_id=1, source_target_pairs={{0,6},{1,7},{2,4},{3,5},{4,2},{5,3},{6,0},{7,1},{8,14},{9,15},{10,... | collective-permute-start | bytes 98312 | tf_op jit(solution)/shard_map/ppermute | solution.py:325
  37.6 6.3 %collective-permute-start.19 = (f32[2,2,8,256]{3,2,1,0:T(8,128)S(1)}, f32[2,2,8,256]{3,2,1,0:T(8,128)S(1)}, u32[]{:S(2)}, u32[]{:S(2)}) collective-permute-start(f32[2,2,8,256]{3,2,1,0:T(8,128)S(1)} %get-tuple-element.63), channel_id=1, source_target_pairs={{0,13},{1,12},{2,15},{3,14},{4,9},{5,8},{6,11},{7,10},{8,5},{9,4},... | collective-permute-start | bytes 98312 | tf_op jit(solution)/shard_map/ppermute | solution.py:325
  38.4 6.2 %collective-permute-start.20 = (f32[2,2,8,256]{3,2,1,0:T(8,128)S(1)}, f32[2,2,8,256]{3,2,1,0:T(8,128)S(1)}, u32[]{:S(2)}, u32[]{:S(2)}) collective-permute-start(f32[2,2,8,256]{3,2,1,0:T(8,128)S(1)} %get-tuple-element.64), channel_id=1, source_target_pairs={{0,5},{1,4},{2,7},{3,6},{4,1},{5,0},{6,3},{7,2},{8,13},{9,12},{10,... | collective-permute-start | bytes 98312 | tf_op jit(solution)/shard_map/ppermute | solution.py:325
  39.0 8.2 %collective-permute-start.21 = (f32[2,2,8,256]{3,2,1,0:T(8,128)S(1)}, f32[2,2,8,256]{3,2,1,0:T(8,128)S(1)}, u32[]{:S(2)}, u32[]{:S(2)}) collective-permute-start(f32[2,2,8,256]{3,2,1,0:T(8,128)S(1)} %get-tuple-element.65), channel_id=1, source_target_pairs={{0,12},{1,13},{2,14},{3,15},{4,8},{5,9},{6,10},{7,11},{8,4},{9,5},... | collective-permute-start | bytes 98312 | tf_op jit(solution)/shard_map/ppermute | solution.py:325
  41.3 7.4 %collective-permute-start.22 = (f32[2,2,8,256]{3,2,1,0:T(8,128)S(1)}, f32[2,2,8,256]{3,2,1,0:T(8,128)S(1)}, u32[]{:S(2)}, u32[]{:S(2)}) collective-permute-start(f32[2,2,8,256]{3,2,1,0:T(8,128)S(1)} %get-tuple-element.66), channel_id=1, source_target_pairs={{0,4},{1,5},{2,6},{3,7},{4,0},{5,1},{6,2},{7,3},{8,12},{9,13},{10,... | collective-permute-start | bytes 98312 | tf_op jit(solution)/shard_map/ppermute | solution.py:325
  42.2 7.2 %collective-permute-start.23 = (f32[2,2,8,256]{3,2,1,0:T(8,128)S(1)}, f32[2,2,8,256]{3,2,1,0:T(8,128)S(1)}, u32[]{:S(2)}, u32[]{:S(2)}) collective-permute-start(f32[2,2,8,256]{3,2,1,0:T(8,128)S(1)} %get-tuple-element.67), channel_id=1, source_target_pairs={{0,11},{1,10},{2,9},{3,8},{4,15},{5,14},{6,13},{7,12},{8,3},{9,2},... | collective-permute-start | bytes 98312 | tf_op jit(solution)/shard_map/ppermute | solution.py:325
  43.9 5.6 %collective-permute-start.24 = (f32[2,2,8,256]{3,2,1,0:T(8,128)S(1)}, f32[2,2,8,256]{3,2,1,0:T(8,128)S(1)}, u32[]{:S(2)}, u32[]{:S(2)}) collective-permute-start(f32[2,2,8,256]{3,2,1,0:T(8,128)S(1)} %get-tuple-element.68), channel_id=1, source_target_pairs={{0,3},{1,2},{2,1},{3,0},{4,7},{5,6},{6,5},{7,4},{8,11},{9,10},{10,... | collective-permute-start | bytes 98312 | tf_op jit(solution)/shard_map/ppermute | solution.py:325
  44.6 6.1 %collective-permute-start.25 = (f32[2,2,8,256]{3,2,1,0:T(8,128)S(1)}, f32[2,2,8,256]{3,2,1,0:T(8,128)S(1)}, u32[]{:S(2)}, u32[]{:S(2)}) collective-permute-start(f32[2,2,8,256]{3,2,1,0:T(8,128)S(1)} %get-tuple-element.69), channel_id=1, source_target_pairs={{0,10},{1,11},{2,8},{3,9},{4,14},{5,15},{6,12},{7,13},{8,2},{9,3},... | collective-permute-start | bytes 98312 | tf_op jit(solution)/shard_map/ppermute | solution.py:325
  47.2 10.2 %collective-permute-start.30 = (f32[8,2048]{1,0:T(8,128)S(1)}, f32[8,2048]{1,0:T(8,128)S(1)}, u32[]{:S(2)}, u32[]{:S(2)}) collective-permute-start(f32[8,2048]{1,0:T(8,128)S(1)} %slice_bitcast_fusion), channel_id=1, source_target_pairs={{0,16},{16,0},{1,17},{17,1},{2,18},{18,2},{3,19},{19,3},{4,20},{20... | collective-permute-start | bytes 196616 | tf_op jit(solution)/shard_map/ppermute | solution.py:371
  48.8 3.9 %collective-permute-start.26 = (f32[2,2,8,256]{3,2,1,0:T(8,128)S(1)}, f32[2,2,8,256]{3,2,1,0:T(8,128)S(1)}, u32[]{:S(2)}, u32[]{:S(2)}) collective-permute-start(f32[2,2,8,256]{3,2,1,0:T(8,128)S(1)} %get-tuple-element.70), channel_id=1, source_target_pairs={{0,2},{1,3},{2,0},{3,1},{4,6},{5,7},{6,4},{7,5},{8,10},{9,11},{10,... | collective-permute-start | bytes 98312 | tf_op jit(solution)/shard_map/ppermute | solution.py:325
  49.4 4.4 %collective-permute-start.27 = (f32[2,2,8,256]{3,2,1,0:T(8,128)S(1)}, f32[2,2,8,256]{3,2,1,0:T(8,128)S(1)}, u32[]{:S(2)}, u32[]{:S(2)}) collective-permute-start(f32[2,2,8,256]{3,2,1,0:T(8,128)S(1)} %get-tuple-element.71), channel_id=1, source_target_pairs={{0,9},{1,8},{2,11},{3,10},{4,13},{5,12},{6,15},{7,14},{8,1},{9,0},... | collective-permute-start | bytes 98312 | tf_op jit(solution)/shard_map/ppermute | solution.py:325
  49.4 4.4 %collective-permute-start.28 = (f32[2,2,8,256]{3,2,1,0:T(8,128)S(1)}, f32[2,2,8,256]{3,2,1,0:T(8,128)S(1)}, u32[]{:S(2)}, u32[]{:S(2)}) collective-permute-start(f32[2,2,8,256]{3,2,1,0:T(8,128)S(1)} %get-tuple-element.72), channel_id=1, source_target_pairs={{0,1},{1,0},{2,3},{3,2},{4,5},{5,4},{6,7},{7,6},{8,9},{9,8},{10,11... | collective-permute-start | bytes 98312 | tf_op jit(solution)/shard_map/ppermute | solution.py:325
  50.7 4.8 %collective-permute-start.29 = (f32[2,2,8,256]{3,2,1,0:T(8,128)S(1)}, f32[2,2,8,256]{3,2,1,0:T(8,128)S(1)}, u32[]{:S(2)}, u32[]{:S(2)}) collective-permute-start(f32[2,2,8,256]{3,2,1,0:T(8,128)S(1)} %get-tuple-element.73), channel_id=1, source_target_pairs={{0,8},{1,9},{2,10},{3,11},{4,12},{5,13},{6,14},{7,15},{8,0},{9,1},... | collective-permute-start | bytes 98312 | tf_op jit(solution)/shard_map/ppermute | solution.py:325
  55.5 0.7 %copy-start.7 = (f32[128]{0:T(128)S(1)}, f32[128]{0:T(128)}, u32[]{:S(2)}) copy-start(f32[128]{0:T(128)} %param.12) | copy-start | bytes 1540

commit v13 on v10

--- a/solution.py
+++ b/solution.py
@@ -177,37 +177,31 @@
     _, batch, tokens, all_channels = held.shape
     channels, pieces = all_channels // shards, tokens // lanes
     sources = (key_hbm, value_hbm, cotangent_hbm, query_hbm)
-    parts = sems.shape[2]
-
-    def copy(b, i, part):
-        span = pl.ds(part * (tokens // parts), tokens // parts)
-        return pltpu.make_async_copy(
-            sources[i].at[b, span], held.at[i, b, span], sems.at[i, b, part]
-        )
-
-    def send(kind):
-        span = pl.ds(kind * (rows // 2), rows // 2)
-        return pltpu.make_async_copy(sent.at[:, span], sent_hbm.at[:, span], out_sems.at[kind])
-
-    for kind in range(2):
-        for b in range(batch):
-            for part in range(parts):
-                copy(b, 2 * kind, part).start()
-                copy(b, 2 * kind + 1, part).start()
-    for kind in range(2):
-        for b in range(batch):
-            for part in range(parts):
-                copy(b, 2 * kind, part).wait()
-                copy(b, 2 * kind + 1, part).wait()
-            columns = jnp.transpose(held[2 * kind, b] * held[2 * kind + 1, b])
-            columns = columns.reshape(shards, channels, tokens)
-            for piece in range(pieces):
-                at = block_rows(kind, b, piece, batch, pieces, channels)
-                for place, shard in enumerate(order):
-                    sent[place, at] = columns[shard, :, piece * lanes : (piece + 1) * lanes]
-        send(kind).start()
-    for kind in range(2):
-        send(kind).wait()
+
+    def copy(b, i):
+        return pltpu.make_async_copy(sources[i].at[b], held.at[i, b], sems.at[i, b])
+
+    def send(kind, b):
+        first = block_rows(kind, b, 0, batch, pieces, channels).start
+        span = pl.ds(first, pieces * channels)
+        return pltpu.make_async_copy(sent.at[:, span], sent_hbm.at[:, span], out_sems.at[kind, b])
+
+    parts = [(kind, b) for kind in range(2) for b in range(batch)]
+    for kind, b in parts:
+        copy(b, 2 * kind).start()
+        copy(b, 2 * kind + 1).start()
+    for kind, b in parts:
+        copy(b, 2 * kind).wait()
+        copy(b, 2 * kind + 1).wait()
+        columns = jnp.transpose(held[2 * kind, b] * held[2 * kind + 1, b])
+        columns = columns.reshape(shards, channels, tokens)
+        for piece in range(pieces):
+            at = block_rows(kind, b, piece, batch, pieces, channels)
+            for place, shard in enumerate(order):
+                sent[place, at] = columns[shard, :, piece * lanes : (piece + 1) * lanes]
+        send(kind, b).start()
+    for kind, b in parts:
+        send(kind, b).wait()
 
 
 def transforms(twist_ref, matrix_ref, middle, turned):
@@ -300,9 +294,24 @@
         transforms(twist_ref, matrix_ref, middles.at[kind], turneds.at[kind]) for kind in range(2)
     ]
 
-    def send(kind):
+    def send(kind, place):
         span = pl.ds(kind * half, half)
-        return pltpu.make_async_copy(back.at[:, span], back_hbm.at[:, span], out_sems.at[kind])
+        return pltpu.make_async_copy(
+            back.at[place, span], back_hbm.at[place, span], out_sems.at[kind, place]
+        )
+
+    def sending(kind, emit):
+        pieces = count // 2 // len(order)
+        left = [pieces] * len(order)
+
+        def emit_and_send(n1, value):
+            emit(n1, value)
+            shard = n1 // pieces
+            left[shard] -= 1
+            if left[shard] == 0:
+                send(kind, order.index(shard)).start()
+
+        return emit_and_send
 
     for pair in range(pairs):
         for kind in range(2):
@@ -310,11 +319,12 @@
             scratch[kind][0](load, kinds[kind].at[pair])
         for kind in range(2):
             _, emit = token_blocks(back, order, kind, pair, 2 * pairs, channels, count // 2)
+            if pair == pairs - 1:
+                emit = sending(kind, emit)
             scratch[kind][1](filter_ref, kinds[kind].at[pair], kind == 1, emit)
-            if pair == pairs - 1:
-                send(kind).start()
     for kind in range(2):
-        send(kind).wait()
+        for place in range(len(order)):
+            send(kind, place).wait()
 
 
 def lag_kernel(scaling, mixed_ref, upstream_ref, twist_ref, matrix_ref, lag_ref, middle, turned):
@@ -416,8 +426,8 @@
         [
             pltpu.VMEM((4, batch, tokens, all_channels), jnp.float32),
             pltpu.VMEM((shards, rows, lanes), jnp.float32),
-            pltpu.SemaphoreType.DMA((4, batch, 4)),
-            pltpu.SemaphoreType.DMA((2,)),
+            pltpu.SemaphoreType.DMA((4, batch)),
+            pltpu.SemaphoreType.DMA((2, batch)),
         ],
         *(
             pltpu.with_memory_space_constraint(x, pltpu.HBM)
@@ -437,7 +447,7 @@
             pltpu.VMEM((shards, rows, lanes), jnp.float32),
             pltpu.VMEM((2, count, channels, 2 * lanes), jnp.float32),
             pltpu.VMEM((2, count, channels, 2 * lanes), jnp.float32),
-            pltpu.SemaphoreType.DMA((2,)),
+            pltpu.SemaphoreType.DMA((2, shards)),
         ],
         held, filter_spec, twist, matrix,
         out_specs=(anywhere, in_vmem, in_vmem),

time: 46.7 us -> 46.7 us (level)
  no operation moved by 1% of the time
where the time goes in v13:
time: 46.7 us; the launch traced here: 46.3 us
  waiting for transfers between devices  23.6 us (51%)
  starting transfers between devices  14.2 us (30%)
  Pallas kernels  6.94 us (15%)
  between operations  0.77 us (2%)
  other arithmetic  0.64 us (1%)
    all_to_all x2, waiting for transfers between devices, exchange(): lax.all_to_all(blocks, 'seq', split_axis=0, concat_axis=0, tiled=True, ax...  20.9 us
    all_to_all x2, starting transfers between devices, exchange(): lax.all_to_all(blocks, 'seq', split_axis=0, concat_axis=0, tiled=True, ax...  12.7 us
    pallas_call x5, Pallas kernels, call(): pl.pallas_call(kernel, out_shape=out_shape, scratch_shapes=scratch, compi...  6.94 us
    ppermute x1, waiting for transfers between devices, per_device(): filter_grad = filter_grad + lax.ppermute(lag[step], 'batch', pairs)  2.78 us
    ppermute x1, starting transfers between devices, per_device(): filter_grad = filter_grad + lax.ppermute(lag[step], 'batch', pairs)  1.55 us
  transfers between devices with their start and end apart: 3, of which 3 were waited for; matrix products, arithmetic and copies ran while one was open for 1% of the time, Pallas kernels for 2%

profile of v13, /device:TPU:0, one launch (start us, length us, event | category | flops | bytes accessed | tf_op | source)
XLA Modules:
  0.0 46.3 jit_solution(670611151187197908)
XLA Ops:
  0.6 2.2 %gate.1 = f32[16,64,128]{2,1,0:T(8,128)} custom-call(f32[2,256,128]{2,1,0:T(8,128)} %query_ref.1, f32[2,256,128]{2,1,0:T(8,128)} %key_ref.1, f32[2,256,128]{2,1,0:T(8,128)} %value_ref.1, f32[2,256,128]{2,1,0:T(8,128)} %cotangent_ref.1), custom_call_target="tpu_custom_call" | custom-call | flops 201326592 | bytes 262144 | tf_op jit(solution)/shard_map/gate/pallas_call | solution.py:399
  2.8 0.0 copy-start.4
  2.9 0.0 copy-start.5
  2.9 0.0 copy-start.7
  2.9 8.0 %all-to-all-start = ((f32[16,64,128]{2,1,0:T(8,128)}), f32[16,64,128]{2,1,0:T(8,128)S(1)}, u32[]{:S(2)}, u32[]{:S(2)}) async-start(f32[16,64,128]{2,1,0:T(8,128)} %gate.1), calls=%async_computation | async-start | bytes 1048576 | tf_op jit(solution)/shard_map/all_to_all | solution.py:413
  10.9 0.0 copy-done.4
  10.9 0.0 copy-done.5
  10.9 0.0 copy-done.7
  10.9 0.5 %filter.1.filter_ref = f32[64,8,256]{2,1,0:T(8,128)S(1)} custom-call(f32[8,4096]{1,0:T(8,128)S(1)} %copy-done.7, f32[64,256]{1,0:T(8,128)S(1)} %copy-done.5, bf16[768,256]{1,0:T(8,128)(2,1)S(1)} %copy-done.4), custom_call_target="tpu_custom_call" | custom-call | flops 402653184 | bytes 524288 | tf_op jit(solution)/shard_map/filter/pallas_call | solution.py:399
  11.4 12.9 %all-to-all-done.held_ref = f32[16,64,128]{2,1,0:T(8,128)S(1)} async-done(((f32[16,64,128]{2,1,0:T(8,128)}), f32[16,64,128]{2,1,0:T(8,128)S(1)}, u32[]{:S(2)}, u32[]{:S(2)}) %all-to-all-start) | async-done | bytes 524320 | tf_op jit(solution)/shard_map/all_to_all | solution.py:413
  24.4 2.6 %convolve.1 = (f32[16,64,128]{2,1,0:T(8,128)}, f32[1,64,8,256]{3,2,1,0:T(8,128)S(1)}, f32[1,64,8,256]{3,2,1,0:T(8,128)S(1)}) custom-call(f32[16,64,128]{2,1,0:T(8,128)S(1)} %all-to-all-done.held_ref, f32[64,8,256]{2,1,0:T(8,128)S(1)} %filter.1.filter_ref, f32[64,256]{1,0:T(8,128)S(1)} %copy-done.5, bf16[768,256]{1,0:T(8,128)(2,1)S(1)} %copy-done.4), custom_call_target="tpu_custom_call" | custom-call | flops 1610612736 | bytes 2097152 | tf_op jit(solution)/shard_map/convolve/pallas_call | solution.py:399
  27.0 4.7 %all-to-all-start.1 = ((f32[16,64,128]{2,1,0:T(8,128)}), f32[16,64,128]{2,1,0:T(8,128)S(1)}, u32[]{:S(2)}, u32[]{:S(2)}) async-start(f32[16,64,128]{2,1,0:T(8,128)} %get-tuple-element.12), calls=%async_computation.1 | async-start | bytes 1048576 | tf_op jit(solution)/shard_map/all_to_all | solution.py:413
  31.6 0.0 copy-start.1
  31.6 0.0 copy-start.2
  31.7 0.0 copy-start.3
  31.7 0.5 %lags.1 = f32[2,8,2048]{2,1,0:T(8,128)S(1)} custom-call(f32[1,64,8,256]{3,2,1,0:T(8,128)S(1)} %get-tuple-element.17.mixed_ref, f32[1,64,8,256]{3,2,1,0:T(8,128)S(1)} %get-tuple-element.18.upstream_ref, f32[64,256]{1,0:T(8,128)S(1)} %copy-done.5, bf16[768,256]{1,0:T(8,128)(2,1)S(1)} %copy-done.4), custom_call_target="tpu_custom_call" | custom-call | flops 402653184 | bytes 524288 | tf_op jit(solution)/shard_map/lags/pallas_call | solution.py:399
  32.2 0.0 copy-start
  32.2 1.6 %collective-permute-start = (f32[8,2048]{1,0:T(8,128)S(1)}, f32[8,2048]{1,0:T(8,128)S(1)}, u32[]{:S(2)}, u32[]{:S(2)}) collective-permute-start(f32[8,2048]{1,0:T(8,128)S(1)} %slice_bitcast_fusion), channel_id=1, source_target_pairs={{0,16},{16,0},{1,17},{17,1},{2,18},{18,2},{3,19},{19,3},{4,20},{20... | collective-permute-start | bytes 196616 | tf_op jit(solution)/shard_map/ppermute | solution.py:464
  33.8 2.8 %collective-permute-done = f32[8,2048]{1,0:T(8,128)S(1)} collective-permute-done((f32[8,2048]{1,0:T(8,128)S(1)}, f32[8,2048]{1,0:T(8,128)S(1)}, u32[]{:S(2)}, u32[]{:S(2)}) %collective-permute-start) | collective-permute-done | bytes 65568 | tf_op jit(solution)/shard_map/ppermute | solution.py:464
  36.6 0.6 %fusion = f32[8,2048]{1,0:T(8,128)} fusion(f32[8,2048]{1,0:T(8,128)S(1)} %collective-permute-done, f32[2,8,2048]{2,1,0:T(8,128)S(1)} %lags.1), kind=kLoop, calls=%fused_computation.2 | loop fusion | flops 16384 | bytes 196608 | tf_op jit(solution)/shard_map/add | solution.py:464
  37.2 0.0 copy-start.6
  37.2 7.9 %all-to-all-done.1.home_ref = f32[16,64,128]{2,1,0:T(8,128)S(1)} async-done(((f32[16,64,128]{2,1,0:T(8,128)}), f32[16,64,128]{2,1,0:T(8,128)S(1)}, u32[]{:S(2)}, u32[]{:S(2)}) %all-to-all-start.1) | async-done | bytes 524320 | tf_op jit(solution)/shard_map/all_to_all | solution.py:413
  45.1 0.0 copy-done.1
  45.1 0.0 copy-done.2
  45.1 0.0 copy-done.3
  45.1 0.0 copy-done
  45.1 0.0 copy-done.6
  45.1 1.1 %outputs.1 = (f32[2,256,128]{2,1,0:T(8,128)}, f32[2,256,128]{2,1,0:T(8,128)}, f32[2,256,128]{2,1,0:T(8,128)}, f32[2,256,128]{2,1,0:T(8,128)}) custom-call(f32[2,256,128]{2,1,0:T(8,128)S(1)} %copy-done, f32[2,256,128]{2,1,0:T(8,128)S(1)} %copy-done.1, f32[2,256,128]{2,1,0:T(8,128)S(1)} %copy-done.2, f32[2,256,128]{2,1,0:T(8,128)S(1)} %copy-done.3, ...), custom_call_target="tpu_custom_call" | custom-call | flops 402653184 | bytes 524288 | tf_op jit(solution)/shard_map/outputs/pallas_call | solution.py:399
  (1 shorter events, 0.0 us)
Async XLA Ops:
  2.8 8.1 %copy-start.4 = (bf16[768,256]{1,0:T(8,128)(2,1)S(1)}, bf16[768,256]{1,0:T(8,128)(2,1)}, u32[]{:S(2)}) copy-start(bf16[768,256]{1,0:T(8,128)(2,1)} %constant.5.clone.matrix_ref) | copy-start | bytes 1179652
  2.9 8.1 %copy-start.5 = (f32[64,256]{1,0:T(8,128)S(1)}, f32[64,256]{1,0:T(8,128)}, u32[]{:S(2)}) copy-start(f32[64,256]{1,0:T(8,128)} %constant.4.clone.twist_ref) | copy-start | bytes 196612
  2.9 8.1 %copy-start.7 = (f32[8,4096]{1,0:T(8,128)S(1)}, f32[8,4096]{1,0:T(8,128)}, u32[]{:S(2)}) copy-start(f32[8,4096]{1,0:T(8,128)} %filter_ref.1) | copy-start | bytes 393220
  2.9 21.5 %all-to-all-start = ((f32[16,64,128]{2,1,0:T(8,128)}), f32[16,64,128]{2,1,0:T(8,128)S(1)}, u32[]{:S(2)}, u32[]{:S(2)}) async-start(f32[16,64,128]{2,1,0:T(8,128)} %gate.1), calls=%async_computation | async-start | bytes 1048576 | tf_op jit(solution)/shard_map/all_to_all | solution.py:413
  27.0 18.1 %all-to-all-start.1 = ((f32[16,64,128]{2,1,0:T(8,128)}), f32[16,64,128]{2,1,0:T(8,128)S(1)}, u32[]{:S(2)}, u32[]{:S(2)}) async-start(f32[16,64,128]{2,1,0:T(8,128)} %get-tuple-element.12), calls=%async_computation.1 | async-start | bytes 1048576 | tf_op jit(solution)/shard_map/all_to_all | solution.py:413
  31.6 13.5 %copy-start.1 = (f32[2,256,128]{2,1,0:T(8,128)S(1)}, f32[2,256,128]{2,1,0:T(8,128)}, u32[]{:S(2)}) copy-start(f32[2,256,128]{2,1,0:T(8,128)} %key_ref.1) | copy-start | bytes 786436
  31.6 13.5 %copy-start.2 = (f32[2,256,128]{2,1,0:T(8,128)S(1)}, f32[2,256,128]{2,1,0:T(8,128)}, u32[]{:S(2)}) copy-start(f32[2,256,128]{2,1,0:T(8,128)} %value_ref.1) | copy-start | bytes 786436
  31.7 13.5 %copy-start.3 = (f32[2,256,128]{2,1,0:T(8,128)S(1)}, f32[2,256,128]{2,1,0:T(8,128)}, u32[]{:S(2)}) copy-start(f32[2,256,128]{2,1,0:T(8,128)} %cotangent_ref.1) | copy-start | bytes 786436
  32.2 12.9 %copy-start = (f32[2,256,128]{2,1,0:T(8,128)S(1)}, f32[2,256,128]{2,1,0:T(8,128)}, u32[]{:S(2)}) copy-start(f32[2,256,128]{2,1,0:T(8,128)} %query_ref.1) | copy-start | bytes 786436
  32.2 4.3 %collective-permute-start = (f32[8,2048]{1,0:T(8,128)S(1)}, f32[8,2048]{1,0:T(8,128)S(1)}, u32[]{:S(2)}, u32[]{:S(2)}) collective-permute-start(f32[8,2048]{1,0:T(8,128)S(1)} %slice_bitcast_fusion), channel_id=1, source_target_pairs={{0,16},{16,0},{1,17},{17,1},{2,18},{18,2},{3,19},{19,3},{4,20},{20... | collective-permute-start | bytes 196616 | tf_op jit(solution)/shard_map/ppermute | solution.py:464
  37.2 7.9 %copy-start.6 = (f32[128]{0:T(128)S(1)}, f32[128]{0:T(128)}, u32[]{:S(2)}) copy-start(f32[128]{0:T(128)} %param.12) | copy-start | bytes 1540

commit v14 on v13

--- a/solution.py
+++ b/solution.py
@@ -11,7 +11,7 @@
 from jax.sharding import PartitionSpec as P
 
 VMEM_BYTES = 48 * 1024 * 1024
-ROW_CHUNK = 128
+ROW_CHUNK = 512
 
 
 def add(a, b):
@@ -294,24 +294,9 @@
         transforms(twist_ref, matrix_ref, middles.at[kind], turneds.at[kind]) for kind in range(2)
     ]
 
-    def send(kind, place):
+    def send(kind):
         span = pl.ds(kind * half, half)
-        return pltpu.make_async_copy(
-            back.at[place, span], back_hbm.at[place, span], out_sems.at[kind, place]
-        )
-
-    def sending(kind, emit):
-        pieces = count // 2 // len(order)
-        left = [pieces] * len(order)
-
-        def emit_and_send(n1, value):
-            emit(n1, value)
-            shard = n1 // pieces
-            left[shard] -= 1
-            if left[shard] == 0:
-                send(kind, order.index(shard)).start()
-
-        return emit_and_send
+        return pltpu.make_async_copy(back.at[:, span], back_hbm.at[:, span], out_sems.at[kind])
 
     for pair in range(pairs):
         for kind in range(2):
@@ -319,12 +304,11 @@
             scratch[kind][0](load, kinds[kind].at[pair])
         for kind in range(2):
             _, emit = token_blocks(back, order, kind, pair, 2 * pairs, channels, count // 2)
+            scratch[kind][1](filter_ref, kinds[kind].at[pair], kind == 1, emit)
             if pair == pairs - 1:
-                emit = sending(kind, emit)
-            scratch[kind][1](filter_ref, kinds[kind].at[pair], kind == 1, emit)
+                send(kind).start()
     for kind in range(2):
-        for place in range(len(order)):
-            send(kind, place).wait()
+        send(kind).wait()
 
 
 def lag_kernel(scaling, mixed_ref, upstream_ref, twist_ref, matrix_ref, lag_ref, middle, turned):
@@ -447,7 +431,7 @@
             pltpu.VMEM((shards, rows, lanes), jnp.float32),
             pltpu.VMEM((2, count, channels, 2 * lanes), jnp.float32),
             pltpu.VMEM((2, count, channels, 2 * lanes), jnp.float32),
-            pltpu.SemaphoreType.DMA((2, shards)),
+            pltpu.SemaphoreType.DMA((2,)),
         ],
         held, filter_spec, twist, matrix,
         out_specs=(anywhere, in_vmem, in_vmem),

time: 46.7 us -> 46.6 us (level)
  no operation moved by 1% of the time
where the time goes in v14:
time: 46.6 us; the launch traced here: 46.1 us
  waiting for transfers between devices  23.7 us (51%)
  starting transfers between devices  14.2 us (30%)
  Pallas kernels  6.76 us (15%)
  between operations  0.77 us (2%)
  other arithmetic  0.64 us (1%)
    all_to_all x2, waiting for transfers between devices, exchange(): lax.all_to_all(blocks, 'seq', split_axis=0, concat_axis=0, tiled=True, ax...  20.9 us
    all_to_all x2, starting transfers between devices, exchange(): lax.all_to_all(blocks, 'seq', split_axis=0, concat_axis=0, tiled=True, ax...  12.7 us
    pallas_call x5, Pallas kernels, call(): pl.pallas_call(kernel, out_shape=out_shape, scratch_shapes=scratch, compi...  6.76 us
    ppermute x1, waiting for transfers between devices, per_device(): filter_grad = filter_grad + lax.ppermute(lag[step], 'batch', pairs)  2.77 us
    ppermute x1, starting transfers between devices, per_device(): filter_grad = filter_grad + lax.ppermute(lag[step], 'batch', pairs)  1.56 us
  transfers between devices with their start and end apart: 3, of which 3 were waited for; matrix products, arithmetic and copies ran while one was open for 1% of the time, Pallas kernels for 2%

profile of v14, /device:TPU:0, one launch (start us, length us, event | category | flops | bytes accessed | tf_op | source)
XLA Modules:
  0.0 46.1 jit_solution(16659582692774668287)
XLA Ops:
  0.6 2.2 %gate.1 = f32[16,64,128]{2,1,0:T(8,128)} custom-call(f32[2,256,128]{2,1,0:T(8,128)} %query_ref.1, f32[2,256,128]{2,1,0:T(8,128)} %key_ref.1, f32[2,256,128]{2,1,0:T(8,128)} %value_ref.1, f32[2,256,128]{2,1,0:T(8,128)} %cotangent_ref.1), custom_call_target="tpu_custom_call" | custom-call | flops 201326592 | bytes 262144 | tf_op jit(solution)/shard_map/gate/pallas_call | solution.py:383
  2.8 0.0 copy-start.4
  2.9 0.0 copy-start.5
  2.9 0.0 copy-start.7
  2.9 8.0 %all-to-all-start = ((f32[16,64,128]{2,1,0:T(8,128)}), f32[16,64,128]{2,1,0:T(8,128)S(1)}, u32[]{:S(2)}, u32[]{:S(2)}) async-start(f32[16,64,128]{2,1,0:T(8,128)} %gate.1), calls=%async_computation | async-start | bytes 1048576 | tf_op jit(solution)/shard_map/all_to_all | solution.py:397
  10.9 0.0 copy-done.4
  10.9 0.0 copy-done.5
  10.9 0.0 copy-done.7
  10.9 0.5 %filter.1.filter_ref = f32[64,8,256]{2,1,0:T(8,128)S(1)} custom-call(f32[8,4096]{1,0:T(8,128)S(1)} %copy-done.7, f32[64,256]{1,0:T(8,128)S(1)} %copy-done.5, bf16[768,256]{1,0:T(8,128)(2,1)S(1)} %copy-done.4), custom_call_target="tpu_custom_call" | custom-call | flops 402653184 | bytes 524288 | tf_op jit(solution)/shard_map/filter/pallas_call | solution.py:383
  11.4 13.0 %all-to-all-done.held_ref = f32[16,64,128]{2,1,0:T(8,128)S(1)} async-done(((f32[16,64,128]{2,1,0:T(8,128)}), f32[16,64,128]{2,1,0:T(8,128)S(1)}, u32[]{:S(2)}, u32[]{:S(2)}) %all-to-all-start) | async-done | bytes 524320 | tf_op jit(solution)/shard_map/all_to_all | solution.py:397
  24.4 2.4 %convolve.1 = (f32[16,64,128]{2,1,0:T(8,128)}, f32[1,64,8,256]{3,2,1,0:T(8,128)S(1)}, f32[1,64,8,256]{3,2,1,0:T(8,128)S(1)}) custom-call(f32[16,64,128]{2,1,0:T(8,128)S(1)} %all-to-all-done.held_ref, f32[64,8,256]{2,1,0:T(8,128)S(1)} %filter.1.filter_ref, f32[64,256]{1,0:T(8,128)S(1)} %copy-done.5, bf16[768,256]{1,0:T(8,128)(2,1)S(1)} %copy-done.4), custom_call_target="tpu_custom_call" | custom-call | flops 1610612736 | bytes 2097152 | tf_op jit(solution)/shard_map/convolve/pallas_call | solution.py:383
  26.8 4.7 %all-to-all-start.1 = ((f32[16,64,128]{2,1,0:T(8,128)}), f32[16,64,128]{2,1,0:T(8,128)S(1)}, u32[]{:S(2)}, u32[]{:S(2)}) async-start(f32[16,64,128]{2,1,0:T(8,128)} %get-tuple-element.12), calls=%async_computation.1 | async-start | bytes 1048576 | tf_op jit(solution)/shard_map/all_to_all | solution.py:397
  31.5 0.0 copy-start.1
  31.5 0.0 copy-start.2
  31.5 0.0 copy-start.3
  31.5 0.5 %lags.1 = f32[2,8,2048]{2,1,0:T(8,128)S(1)} custom-call(f32[1,64,8,256]{3,2,1,0:T(8,128)S(1)} %get-tuple-element.17.mixed_ref, f32[1,64,8,256]{3,2,1,0:T(8,128)S(1)} %get-tuple-element.18.upstream_ref, f32[64,256]{1,0:T(8,128)S(1)} %copy-done.5, bf16[768,256]{1,0:T(8,128)(2,1)S(1)} %copy-done.4), custom_call_target="tpu_custom_call" | custom-call | flops 402653184 | bytes 524288 | tf_op jit(solution)/shard_map/lags/pallas_call | solution.py:383
  32.0 0.0 copy-start
  32.1 1.6 %collective-permute-start = (f32[8,2048]{1,0:T(8,128)S(1)}, f32[8,2048]{1,0:T(8,128)S(1)}, u32[]{:S(2)}, u32[]{:S(2)}) collective-permute-start(f32[8,2048]{1,0:T(8,128)S(1)} %slice_bitcast_fusion), channel_id=1, source_target_pairs={{0,16},{16,0},{1,17},{17,1},{2,18},{18,2},{3,19},{19,3},{4,20},{20... | collective-permute-start | bytes 196616 | tf_op jit(solution)/shard_map/ppermute | solution.py:448
  33.6 2.8 %collective-permute-done = f32[8,2048]{1,0:T(8,128)S(1)} collective-permute-done((f32[8,2048]{1,0:T(8,128)S(1)}, f32[8,2048]{1,0:T(8,128)S(1)}, u32[]{:S(2)}, u32[]{:S(2)}) %collective-permute-start) | collective-permute-done | bytes 65568 | tf_op jit(solution)/shard_map/ppermute | solution.py:448
  36.4 0.6 %fusion = f32[8,2048]{1,0:T(8,128)} fusion(f32[8,2048]{1,0:T(8,128)S(1)} %collective-permute-done, f32[2,8,2048]{2,1,0:T(8,128)S(1)} %lags.1), kind=kLoop, calls=%fused_computation.2 | loop fusion | flops 16384 | bytes 196608 | tf_op jit(solution)/shard_map/add | solution.py:448
  37.0 0.0 copy-start.6
  37.0 7.9 %all-to-all-done.1.home_ref = f32[16,64,128]{2,1,0:T(8,128)S(1)} async-done(((f32[16,64,128]{2,1,0:T(8,128)}), f32[16,64,128]{2,1,0:T(8,128)S(1)}, u32[]{:S(2)}, u32[]{:S(2)}) %all-to-all-start.1) | async-done | bytes 524320 | tf_op jit(solution)/shard_map/all_to_all | solution.py:397
  45.0 0.0 copy-done.1
  45.0 0.0 copy-done.2
  45.0 0.0 copy-done.3
  45.0 0.0 copy-done
  45.0 0.0 copy-done.6
  45.0 1.1 %outputs.1 = (f32[2,256,128]{2,1,0:T(8,128)}, f32[2,256,128]{2,1,0:T(8,128)}, f32[2,256,128]{2,1,0:T(8,128)}, f32[2,256,128]{2,1,0:T(8,128)}) custom-call(f32[2,256,128]{2,1,0:T(8,128)S(1)} %copy-done, f32[2,256,128]{2,1,0:T(8,128)S(1)} %copy-done.1, f32[2,256,128]{2,1,0:T(8,128)S(1)} %copy-done.2, f32[2,256,128]{2,1,0:T(8,128)S(1)} %copy-done.3, ...), custom_call_target="tpu_custom_call" | custom-call | flops 402653184 | bytes 524288 | tf_op jit(solution)/shard_map/outputs/pallas_call | solution.py:383
  (1 shorter events, 0.0 us)
Async XLA Ops:
  2.8 8.1 %copy-start.4 = (bf16[768,256]{1,0:T(8,128)(2,1)S(1)}, bf16[768,256]{1,0:T(8,128)(2,1)}, u32[]{:S(2)}) copy-start(bf16[768,256]{1,0:T(8,128)(2,1)} %constant.5.clone.matrix_ref) | copy-start | bytes 1179652
  2.9 8.1 %copy-start.5 = (f32[64,256]{1,0:T(8,128)S(1)}, f32[64,256]{1,0:T(8,128)}, u32[]{:S(2)}) copy-start(f32[64,256]{1,0:T(8,128)} %constant.4.clone.twist_ref) | copy-start | bytes 196612
  2.9 8.1 %copy-start.7 = (f32[8,4096]{1,0:T(8,128)S(1)}, f32[8,4096]{1,0:T(8,128)}, u32[]{:S(2)}) copy-start(f32[8,4096]{1,0:T(8,128)} %filter_ref.1) | copy-start | bytes 393220
  2.9 21.5 %all-to-all-start = ((f32[16,64,128]{2,1,0:T(8,128)}), f32[16,64,128]{2,1,0:T(8,128)S(1)}, u32[]{:S(2)}, u32[]{:S(2)}) async-start(f32[16,64,128]{2,1,0:T(8,128)} %gate.1), calls=%async_computation | async-start | bytes 1048576 | tf_op jit(solution)/shard_map/all_to_all | solution.py:397
  26.8 18.1 %all-to-all-start.1 = ((f32[16,64,128]{2,1,0:T(8,128)}), f32[16,64,128]{2,1,0:T(8,128)S(1)}, u32[]{:S(2)}, u32[]{:S(2)}) async-start(f32[16,64,128]{2,1,0:T(8,128)} %get-tuple-element.12), calls=%async_computation.1 | async-start | bytes 1048576 | tf_op jit(solution)/shard_map/all_to_all | solution.py:397
  31.5 13.5 %copy-start.1 = (f32[2,256,128]{2,1,0:T(8,128)S(1)}, f32[2,256,128]{2,1,0:T(8,128)}, u32[]{:S(2)}) copy-start(f32[2,256,128]{2,1,0:T(8,128)} %key_ref.1) | copy-start | bytes 786436
  31.5 13.5 %copy-start.2 = (f32[2,256,128]{2,1,0:T(8,128)S(1)}, f32[2,256,128]{2,1,0:T(8,128)}, u32[]{:S(2)}) copy-start(f32[2,256,128]{2,1,0:T(8,128)} %value_ref.1) | copy-start | bytes 786436
  31.5 13.5 %copy-start.3 = (f32[2,256,128]{2,1,0:T(8,128)S(1)}, f32[2,256,128]{2,1,0:T(8,128)}, u32[]{:S(2)}) copy-start(f32[2,256,128]{2,1,0:T(8,128)} %cotangent_ref.1) | copy-start | bytes 786436
  32.0 12.9 %copy-start = (f32[2,256,128]{2,1,0:T(8,128)S(1)}, f32[2,256,128]{2,1,0:T(8,128)}, u32[]{:S(2)}) copy-start(f32[2,256,128]{2,1,0:T(8,128)} %query_ref.1) | copy-start | bytes 786436
  32.1 4.3 %collective-permute-start = (f32[8,2048]{1,0:T(8,128)S(1)}, f32[8,2048]{1,0:T(8,128)S(1)}, u32[]{:S(2)}, u32[]{:S(2)}) collective-permute-start(f32[8,2048]{1,0:T(8,128)S(1)} %slice_bitcast_fusion), channel_id=1, source_target_pairs={{0,16},{16,0},{1,17},{17,1},{2,18},{18,2},{3,19},{19,3},{4,20},{20... | collective-permute-start | bytes 196616 | tf_op jit(solution)/shard_map/ppermute | solution.py:448
  37.0 8.0 %copy-start.6 = (f32[128]{0:T(128)S(1)}, f32[128]{0:T(128)}, u32[]{:S(2)}) copy-start(f32[128]{0:T(128)} %param.12) | copy-start | bytes 1540

commit v15 on v14

--- a/solution.py
+++ b/solution.py
@@ -11,7 +11,7 @@
 from jax.sharding import PartitionSpec as P
 
 VMEM_BYTES = 48 * 1024 * 1024
-ROW_CHUNK = 512
+ROW_CHUNK = 128
 
 
 def add(a, b):
@@ -112,11 +112,12 @@
                 emit(k1, value)
 
 
-def tables(count, lanes):
+def tables(count, channels, lanes):
     k1 = np.arange(count)[:, None]
     n2 = np.arange(lanes)[None, :]
     phase = -2.0 * np.pi * ((k1 * n2) % (count * lanes)) / (count * lanes)
     twist = np.concatenate([np.cos(phase), np.sin(phase)], axis=1).astype(np.float32)
+    twist = np.repeat(twist[:, None], channels, axis=1)
     j = np.arange(lanes)
     phase = -2.0 * np.pi * ((j[:, None] * j[None, :]) % lanes) / lanes
     c, s = np.cos(phase), np.sin(phase)
@@ -220,7 +221,7 @@
         return (middle[b * first + p, :, :lanes], middle[b * first + p, :, lanes:])
 
     def twist(k1, value):
-        c, s = twist_ref[k1 : k1 + 1, :lanes], twist_ref[k1 : k1 + 1, lanes:]
+        c, s = twist_ref[k1, :, :lanes], twist_ref[k1, :, lanes:]
         return (value[0] * c - value[1] * s, value[0] * s + value[1] * c)
 
     def place(k1, value):
@@ -272,7 +273,7 @@
 
 def filter_kernel(filter_ref, twist_ref, matrix_ref, spec_ref, middle, turned):
     length = filter_ref.shape[1]
-    lanes = twist_ref.shape[1] // 2
+    lanes = twist_ref.shape[2] // 2
     forward, _ = transforms(twist_ref, matrix_ref, middle, turned)
 
     def load(n1):
@@ -312,7 +313,7 @@
 
 
 def lag_kernel(scaling, mixed_ref, upstream_ref, twist_ref, matrix_ref, lag_ref, middle, turned):
-    lanes = twist_ref.shape[1] // 2
+    lanes = twist_ref.shape[2] // 2
     groups, _, share = lag_ref.shape
     group = lax.axis_index("batch")
     _, inverse = transforms(twist_ref, matrix_ref, middle, turned)
@@ -372,7 +373,7 @@
     channels, length = filters.shape
     lanes = 128 if 2 * length // 128 <= 64 else tokens
     count = 2 * length // lanes
-    twist, matrix = tables(count, lanes)
+    twist, matrix = tables(count, channels, lanes)
     order = exchange_order(shards)
     lane_work = 2 * 3 * count * channels * (2 * lanes) ** 2
 

time: 46.6 us -> 46.4 us (level)
  no operation moved by 1% of the time
where the time goes in v15:
time: 46.4 us; the launch traced here: 46 us
  waiting for transfers between devices  23.6 us (51%)
  starting transfers between devices  14.2 us (31%)
  Pallas kernels  6.67 us (14%)
  between operations  0.77 us (2%)
  other arithmetic  0.64 us (1%)
    all_to_all x2, waiting for transfers between devices, exchange(): lax.all_to_all(blocks, 'seq', split_axis=0, concat_axis=0, tiled=True, ax...  20.9 us
    all_to_all x2, starting transfers between devices, exchange(): lax.all_to_all(blocks, 'seq', split_axis=0, concat_axis=0, tiled=True, ax...  12.7 us
    pallas_call x5, Pallas kernels, call(): pl.pallas_call(kernel, out_shape=out_shape, scratch_shapes=scratch, compi...  6.67 us
    ppermute x1, waiting for transfers between devices, per_device(): filter_grad = filter_grad + lax.ppermute(lag[step], 'batch', pairs)  2.78 us
    ppermute x1, starting transfers between devices, per_device(): filter_grad = filter_grad + lax.ppermute(lag[step], 'batch', pairs)  1.55 us
  transfers between devices with their start and end apart: 3, of which 3 were waited for; matrix products, arithmetic and copies ran while one was open for 1% of the time, Pallas kernels for 2%

profile of v15, /device:TPU:0, one launch (start us, length us, event | category | flops | bytes accessed | tf_op | source)
XLA Modules:
  0.0 46.0 jit_solution(13804142319775965000)
XLA Ops:
  0.6 2.2 %gate.1 = f32[16,64,128]{2,1,0:T(8,128)} custom-call(f32[2,256,128]{2,1,0:T(8,128)} %query_ref.1, f32[2,256,128]{2,1,0:T(8,128)} %key_ref.1, f32[2,256,128]{2,1,0:T(8,128)} %value_ref.1, f32[2,256,128]{2,1,0:T(8,128)} %cotangent_ref.1), custom_call_target="tpu_custom_call" | custom-call | flops 201326592 | bytes 262144 | tf_op jit(solution)/shard_map/gate/pallas_call | solution.py:384
  2.8 0.0 copy-start
  2.9 0.0 copy-start.1
  2.9 0.0 copy-start.6
  2.9 8.0 %all-to-all-start = ((f32[16,64,128]{2,1,0:T(8,128)}), f32[16,64,128]{2,1,0:T(8,128)S(1)}, u32[]{:S(2)}, u32[]{:S(2)}) async-start(f32[16,64,128]{2,1,0:T(8,128)} %gate.1), calls=%async_computation | async-start | bytes 1048576 | tf_op jit(solution)/shard_map/all_to_all | solution.py:398
  10.9 0.0 copy-done
  10.9 0.0 copy-done.1
  10.9 0.0 copy-done.6
  10.9 0.5 %filter.1.filter_ref = f32[64,8,256]{2,1,0:T(8,128)S(1)} custom-call(f32[8,4096]{1,0:T(8,128)S(1)} %copy-done.6, f32[64,8,256]{2,1,0:T(8,128)S(1)} %copy-done, bf16[768,256]{1,0:T(8,128)(2,1)S(1)} %copy-done.1), custom_call_target="tpu_custom_call" | custom-call | flops 402653184 | bytes 524288 | tf_op jit(solution)/shard_map/filter/pallas_call | solution.py:384
  11.4 12.9 %all-to-all-done.held_ref = f32[16,64,128]{2,1,0:T(8,128)S(1)} async-done(((f32[16,64,128]{2,1,0:T(8,128)}), f32[16,64,128]{2,1,0:T(8,128)S(1)}, u32[]{:S(2)}, u32[]{:S(2)}) %all-to-all-start) | async-done | bytes 524320 | tf_op jit(solution)/shard_map/all_to_all | solution.py:398
  24.4 2.3 %convolve.1 = (f32[16,64,128]{2,1,0:T(8,128)}, f32[1,64,8,256]{3,2,1,0:T(8,128)S(1)}, f32[1,64,8,256]{3,2,1,0:T(8,128)S(1)}) custom-call(f32[16,64,128]{2,1,0:T(8,128)S(1)} %all-to-all-done.held_ref, f32[64,8,256]{2,1,0:T(8,128)S(1)} %filter.1.filter_ref, f32[64,8,256]{2,1,0:T(8,128)S(1)} %copy-done, bf16[768,256]{1,0:T(8,128)(2,1)S(1)} %copy-done.1), custom_call_target="tpu_custom_call" | custom-call | flops 1610612736 | bytes 2097152 | tf_op jit(solution)/shard_map/convolve/pallas_call | solution.py:384
  26.7 4.7 %all-to-all-start.1 = ((f32[16,64,128]{2,1,0:T(8,128)}), f32[16,64,128]{2,1,0:T(8,128)S(1)}, u32[]{:S(2)}, u32[]{:S(2)}) async-start(f32[16,64,128]{2,1,0:T(8,128)} %get-tuple-element.12), calls=%async_computation.1 | async-start | bytes 1048576 | tf_op jit(solution)/shard_map/all_to_all | solution.py:398
  31.4 0.0 copy-start.3
  31.4 0.0 copy-start.4
  31.4 0.0 copy-start.5
  31.4 0.5 %lags.1 = f32[2,8,2048]{2,1,0:T(8,128)S(1)} custom-call(f32[1,64,8,256]{3,2,1,0:T(8,128)S(1)} %get-tuple-element.17.mixed_ref, f32[1,64,8,256]{3,2,1,0:T(8,128)S(1)} %get-tuple-element.18.upstream_ref, f32[64,8,256]{2,1,0:T(8,128)S(1)} %copy-done, bf16[768,256]{1,0:T(8,128)(2,1)S(1)} %copy-done.1), custom_call_target="tpu_custom_call" | custom-call | flops 402653184 | bytes 524288 | tf_op jit(solution)/shard_map/lags/pallas_call | solution.py:384
  31.9 0.0 copy-start.2
  32.0 1.6 %collective-permute-start = (f32[8,2048]{1,0:T(8,128)S(1)}, f32[8,2048]{1,0:T(8,128)S(1)}, u32[]{:S(2)}, u32[]{:S(2)}) collective-permute-start(f32[8,2048]{1,0:T(8,128)S(1)} %slice_bitcast_fusion), channel_id=1, source_target_pairs={{0,16},{16,0},{1,17},{17,1},{2,18},{18,2},{3,19},{19,3},{4,20},{20... | collective-permute-start | bytes 196616 | tf_op jit(solution)/shard_map/ppermute | solution.py:449
  33.5 2.8 %collective-permute-done = f32[8,2048]{1,0:T(8,128)S(1)} collective-permute-done((f32[8,2048]{1,0:T(8,128)S(1)}, f32[8,2048]{1,0:T(8,128)S(1)}, u32[]{:S(2)}, u32[]{:S(2)}) %collective-permute-start) | collective-permute-done | bytes 65568 | tf_op jit(solution)/shard_map/ppermute | solution.py:449
  36.3 0.6 %fusion = f32[8,2048]{1,0:T(8,128)} fusion(f32[8,2048]{1,0:T(8,128)S(1)} %collective-permute-done, f32[2,8,2048]{2,1,0:T(8,128)S(1)} %lags.1), kind=kLoop, calls=%fused_computation.2 | loop fusion | flops 16384 | bytes 196608 | tf_op jit(solution)/shard_map/add | solution.py:449
  36.9 0.0 copy-start.7
  36.9 7.9 %all-to-all-done.1.home_ref = f32[16,64,128]{2,1,0:T(8,128)S(1)} async-done(((f32[16,64,128]{2,1,0:T(8,128)}), f32[16,64,128]{2,1,0:T(8,128)S(1)}, u32[]{:S(2)}, u32[]{:S(2)}) %all-to-all-start.1) | async-done | bytes 524320 | tf_op jit(solution)/shard_map/all_to_all | solution.py:398
  44.8 0.0 copy-done.3
  44.9 0.0 copy-done.4
  44.9 0.0 copy-done.5
  44.9 0.0 copy-done.2
  44.9 0.0 copy-done.7
  44.9 1.1 %outputs.1 = (f32[2,256,128]{2,1,0:T(8,128)}, f32[2,256,128]{2,1,0:T(8,128)}, f32[2,256,128]{2,1,0:T(8,128)}, f32[2,256,128]{2,1,0:T(8,128)}) custom-call(f32[2,256,128]{2,1,0:T(8,128)S(1)} %copy-done.2, f32[2,256,128]{2,1,0:T(8,128)S(1)} %copy-done.3, f32[2,256,128]{2,1,0:T(8,128)S(1)} %copy-done.4, f32[2,256,128]{2,1,0:T(8,128)S(1)} %copy-done.5, ...), custom_call_target="tpu_custom_call" | custom-call | flops 402653184 | bytes 524288 | tf_op jit(solution)/shard_map/outputs/pallas_call | solution.py:384
  (1 shorter events, 0.0 us)
Async XLA Ops:
  2.8 8.1 %copy-start = (f32[64,8,256]{2,1,0:T(8,128)S(1)}, f32[64,8,256]{2,1,0:T(8,128)}, u32[]{:S(2)}) copy-start(f32[64,8,256]{2,1,0:T(8,128)} %constant.4.clone.twist_ref) | copy-start | bytes 1572868
  2.9 8.1 %copy-start.1 = (bf16[768,256]{1,0:T(8,128)(2,1)S(1)}, bf16[768,256]{1,0:T(8,128)(2,1)}, u32[]{:S(2)}) copy-start(bf16[768,256]{1,0:T(8,128)(2,1)} %constant.5.clone.matrix_ref) | copy-start | bytes 1179652
  2.9 8.1 %copy-start.6 = (f32[8,4096]{1,0:T(8,128)S(1)}, f32[8,4096]{1,0:T(8,128)}, u32[]{:S(2)}) copy-start(f32[8,4096]{1,0:T(8,128)} %filter_ref.1) | copy-start | bytes 393220
  2.9 21.5 %all-to-all-start = ((f32[16,64,128]{2,1,0:T(8,128)}), f32[16,64,128]{2,1,0:T(8,128)S(1)}, u32[]{:S(2)}, u32[]{:S(2)}) async-start(f32[16,64,128]{2,1,0:T(8,128)} %gate.1), calls=%async_computation | async-start | bytes 1048576 | tf_op jit(solution)/shard_map/all_to_all | solution.py:398
  26.7 18.1 %all-to-all-start.1 = ((f32[16,64,128]{2,1,0:T(8,128)}), f32[16,64,128]{2,1,0:T(8,128)S(1)}, u32[]{:S(2)}, u32[]{:S(2)}) async-start(f32[16,64,128]{2,1,0:T(8,128)} %get-tuple-element.12), calls=%async_computation.1 | async-start | bytes 1048576 | tf_op jit(solution)/shard_map/all_to_all | solution.py:398
  31.4 13.5 %copy-start.3 = (f32[2,256,128]{2,1,0:T(8,128)S(1)}, f32[2,256,128]{2,1,0:T(8,128)}, u32[]{:S(2)}) copy-start(f32[2,256,128]{2,1,0:T(8,128)} %key_ref.1) | copy-start | bytes 786436
  31.4 13.5 %copy-start.4 = (f32[2,256,128]{2,1,0:T(8,128)S(1)}, f32[2,256,128]{2,1,0:T(8,128)}, u32[]{:S(2)}) copy-start(f32[2,256,128]{2,1,0:T(8,128)} %value_ref.1) | copy-start | bytes 786436
  31.4 13.5 %copy-start.5 = (f32[2,256,128]{2,1,0:T(8,128)S(1)}, f32[2,256,128]{2,1,0:T(8,128)}, u32[]{:S(2)}) copy-start(f32[2,256,128]{2,1,0:T(8,128)} %cotangent_ref.1) | copy-start | bytes 786436
  31.9 12.9 %copy-start.2 = (f32[2,256,128]{2,1,0:T(8,128)S(1)}, f32[2,256,128]{2,1,0:T(8,128)}, u32[]{:S(2)}) copy-start(f32[2,256,128]{2,1,0:T(8,128)} %query_ref.1) | copy-start | bytes 786436
  32.0 4.3 %collective-permute-start = (f32[8,2048]{1,0:T(8,128)S(1)}, f32[8,2048]{1,0:T(8,128)S(1)}, u32[]{:S(2)}, u32[]{:S(2)}) collective-permute-start(f32[8,2048]{1,0:T(8,128)S(1)} %slice_bitcast_fusion), channel_id=1, source_target_pairs={{0,16},{16,0},{1,17},{17,1},{2,18},{18,2},{3,19},{19,3},{4,20},{20... | collective-permute-start | bytes 196616 | tf_op jit(solution)/shard_map/ppermute | solution.py:449
  36.9 7.9 %copy-start.7 = (f32[128]{0:T(128)S(1)}, f32[128]{0:T(128)}, u32[]{:S(2)}) copy-start(f32[128]{0:T(128)} %param.12) | copy-start | bytes 1540

commit v16 on v14

--- a/solution.py
+++ b/solution.py
@@ -11,7 +11,7 @@
 from jax.sharding import PartitionSpec as P
 
 VMEM_BYTES = 48 * 1024 * 1024
-ROW_CHUNK = 512
+ROW_CHUNK = 256
 
 
 def add(a, b):
@@ -370,8 +370,7 @@
 def per_device(query_gate, key_gate, value_input, filters, skip_gain, cotangent, *, shards, groups):
     batch, tokens, all_channels = query_gate.shape
     channels, length = filters.shape
-    lanes = 128 if 2 * length // 128 <= 64 else tokens
-    count = 2 * length // lanes
+    lanes, count = tokens, 2 * shards
     twist, matrix = tables(count, lanes)
     order = exchange_order(shards)
     lane_work = 2 * 3 * count * channels * (2 * lanes) ** 2

time: 46.6 us -> 48.3 us (1.036)
  local copies, waits for them, and re-layouts: 0.05 us -> 2.92 us
  waiting for transfers between devices: 23.7 us -> 21.1 us
  Pallas kernels: 6.76 us -> 8.21 us
    unnamed x16 -> x24, local copies, waits for them, and re-layouts: 0.05 us -> 2.91 us
    all_to_all x2, waiting for transfers between devices: 20.9 us -> 18.4 us  [exchange(): lax.all_to_all(blocks, 'seq', split_axis=0, concat_axis=0, tiled=True, ax...]
    pallas_call x5, Pallas kernels: 6.76 us -> 8.21 us  [call(): pl.pallas_call(kernel, out_shape=out_shape, scratch_shapes=scratch, compi...]
  transfers between devices with their start and end apart: 3 -> 3, of which waited for: 3 -> 3; matrix products, arithmetic and copies ran while one was open for 1% -> 1% of each run, Pallas kernels for 2% -> 3%
where the time goes in v16:
time: 48.3 us; the launch traced here: 47.8 us
  waiting for transfers between devices  21.1 us (44%)
  starting transfers between devices  14.1 us (29%)
  Pallas kernels  8.21 us (17%)
  local copies, waits for them, and re-layouts  2.92 us (6%)
  between operations  0.77 us (2%)
  other arithmetic  0.64 us (1%)
    all_to_all x2, waiting for transfers between devices, exchange(): lax.all_to_all(blocks, 'seq', split_axis=0, concat_axis=0, tiled=True, ax...  18.4 us
    all_to_all x2, starting transfers between devices, exchange(): lax.all_to_all(blocks, 'seq', split_axis=0, concat_axis=0, tiled=True, ax...  12.6 us
    pallas_call x5, Pallas kernels, call(): pl.pallas_call(kernel, out_shape=out_shape, scratch_shapes=scratch, compi...  8.21 us
    unnamed x24, local copies, waits for them, and re-layouts  2.91 us
    ppermute x1, waiting for transfers between devices, per_device(): filter_grad = filter_grad + lax.ppermute(lag[step], 'batch', pairs)  2.77 us
    ppermute x1, starting transfers between devices, per_device(): filter_grad = filter_grad + lax.ppermute(lag[step], 'batch', pairs)  1.56 us
  transfers between devices with their start and end apart: 3, of which 3 were waited for; matrix products, arithmetic and copies ran while one was open for 1% of the time, Pallas kernels for 3%

profile of v16, /device:TPU:0, one launch (start us, length us, event | category | flops | bytes accessed | tf_op | source)
XLA Modules:
  0.0 47.8 jit_solution(6354701402503947984)
XLA Ops:
  0.6 0.0 copy-start.6
  0.6 0.0 copy-start.7
  0.7 0.0 copy-start.4
  0.7 2.3 %gate.1 = f32[16,32,256]{2,1,0:T(8,128)} custom-call(f32[2,256,128]{2,1,0:T(8,128)} %query_ref.1, f32[2,256,128]{2,1,0:T(8,128)} %key_ref.1, f32[2,256,128]{2,1,0:T(8,128)} %value_ref.1, f32[2,256,128]{2,1,0:T(8,128)} %cotangent_ref.1), custom_call_target="tpu_custom_call" | custom-call | flops 402653184 | bytes 262144 | tf_op jit(solution)/shard_map/gate/pallas_call | solution.py:382
  3.0 7.9 %all-to-all-start = ((f32[16,32,256]{2,1,0:T(8,128)}), f32[16,32,256]{2,1,0:T(8,128)S(1)}, u32[]{:S(2)}, u32[]{:S(2)}) async-start(f32[16,32,256]{2,1,0:T(8,128)} %gate.1), calls=%async_computation | async-start | bytes 1048576 | tf_op jit(solution)/shard_map/all_to_all | solution.py:396
  10.9 0.0 copy-done.6
  10.9 0.0 copy-done.7
  10.9 0.0 copy-done.4
  10.9 0.7 %filter.1.filter_ref = f32[32,8,512]{2,1,0:T(8,128)S(1)} custom-call(f32[8,4096]{1,0:T(8,128)S(1)} %copy-done.4, f32[32,512]{1,0:T(8,128)S(1)} %copy-done.7, bf16[1536,512]{1,0:T(8,128)(2,1)S(1)} %copy-done.6), custom_call_target="tpu_custom_call" | custom-call | flops 805306368 | bytes 524288 | tf_op jit(solution)/shard_map/filter/pallas_call | solution.py:382
  11.7 12.7 %all-to-all-done.held_ref = f32[16,32,256]{2,1,0:T(8,128)S(1)} async-done(((f32[16,32,256]{2,1,0:T(8,128)}), f32[16,32,256]{2,1,0:T(8,128)S(1)}, u32[]{:S(2)}, u32[]{:S(2)}) %all-to-all-start) | async-done | bytes 524320 | tf_op jit(solution)/shard_map/all_to_all | solution.py:396
  24.4 3.3 %convolve.1 = (f32[16,32,256]{2,1,0:T(8,128)}, f32[1,32,8,512]{3,2,1,0:T(8,128)S(1)}, f32[1,32,8,512]{3,2,1,0:T(8,128)S(1)}) custom-call(f32[16,32,256]{2,1,0:T(8,128)S(1)} %all-to-all-done.held_ref, f32[32,8,512]{2,1,0:T(8,128)S(1)} %filter.1.filter_ref, f32[32,512]{1,0:T(8,128)S(1)} %copy-done.7, bf16[1536,512]{1,0:T(8,128)(2,1)S(1)} %copy-done.6), custom_call_target="tpu_custom_call" | custom-call | flops 3221225472 | bytes 2097152 | tf_op jit(solution)/shard_map/convolve/pallas_call | solution.py:382
  27.7 0.0 copy-start.8
  27.7 0.8 %copy-done.8 = f32[1,32,8,512]{3,2,1,0:T(8,128)} copy-done((f32[1,32,8,512]{3,2,1,0:T(8,128)}, f32[1,32,8,512]{3,2,1,0:T(8,128)S(1)}, u32[]{:S(2)}) %copy-start.8) | copy-done | bytes 524312
  28.5 0.0 copy-start.10
  28.5 4.7 %all-to-all-start.1 = ((f32[16,32,256]{2,1,0:T(8,128)}), f32[16,32,256]{2,1,0:T(8,128)S(1)}, u32[]{:S(2)}, u32[]{:S(2)}) async-start(f32[16,32,256]{2,1,0:T(8,128)} %get-tuple-element.12), calls=%async_computation.1 | async-start | bytes 1048576 | tf_op jit(solution)/shard_map/all_to_all | solution.py:396
  33.2 0.0 copy-done.10
  33.2 0.0 copy-start.9
  33.2 1.0 %copy-done.9 = f32[1,32,8,512]{3,2,1,0:T(8,128)S(1)} copy-done((f32[1,32,8,512]{3,2,1,0:T(8,128)S(1)}, f32[1,32,8,512]{3,2,1,0:T(8,128)}, u32[]{:S(2)}) %copy-start.9) | copy-done | bytes 524312
  34.2 0.0 copy-start.11
  34.2 1.0 %copy-done.11 = f32[1,32,8,512]{3,2,1,0:T(8,128)S(1)} copy-done((f32[1,32,8,512]{3,2,1,0:T(8,128)S(1)}, f32[1,32,8,512]{3,2,1,0:T(8,128)}, u32[]{:S(2)}) %copy-start.11) | copy-done | bytes 524312
  35.2 0.0 copy-start
  35.2 0.0 copy-start.1
  35.2 0.0 copy-start.2
  35.2 0.0 copy-start.3
  35.3 0.0 copy-start.5
  35.3 0.7 %lags.1 = f32[2,8,2048]{2,1,0:T(8,128)S(1)} custom-call(f32[1,32,8,512]{3,2,1,0:T(8,128)S(1)} %copy-done.9, f32[1,32,8,512]{3,2,1,0:T(8,128)S(1)} %copy-done.11, f32[32,512]{1,0:T(8,128)S(1)} %copy-done.7, bf16[1536,512]{1,0:T(8,128)(2,1)S(1)} %copy-done.6), custom_call_target="tpu_custom_call" | custom-call | flops 805306368 | bytes 524288 | tf_op jit(solution)/shard_map/lags/pallas_call | solution.py:382
  36.0 1.6 %collective-permute-start = (f32[8,2048]{1,0:T(8,128)S(1)}, f32[8,2048]{1,0:T(8,128)S(1)}, u32[]{:S(2)}, u32[]{:S(2)}) collective-permute-start(f32[8,2048]{1,0:T(8,128)S(1)} %slice_bitcast_fusion), channel_id=1, source_target_pairs={{0,16},{16,0},{1,17},{17,1},{2,18},{18,2},{3,19},{19,3},{4,20},{20... | collective-permute-start | bytes 196616 | tf_op jit(solution)/shard_map/ppermute | solution.py:447
  37.6 2.8 %collective-permute-done = f32[8,2048]{1,0:T(8,128)S(1)} collective-permute-done((f32[8,2048]{1,0:T(8,128)S(1)}, f32[8,2048]{1,0:T(8,128)S(1)}, u32[]{:S(2)}, u32[]{:S(2)}) %collective-permute-start) | collective-permute-done | bytes 65568 | tf_op jit(solution)/shard_map/ppermute | solution.py:447
  40.3 0.6 %fusion = f32[8,2048]{1,0:T(8,128)} fusion(f32[8,2048]{1,0:T(8,128)S(1)} %collective-permute-done, f32[2,8,2048]{2,1,0:T(8,128)S(1)} %lags.1), kind=kLoop, calls=%fused_computation.2 | loop fusion | flops 16384 | bytes 196608 | tf_op jit(solution)/shard_map/add | solution.py:447
  41.0 5.7 %all-to-all-done.1.home_ref = f32[16,32,256]{2,1,0:T(8,128)S(1)} async-done(((f32[16,32,256]{2,1,0:T(8,128)}), f32[16,32,256]{2,1,0:T(8,128)S(1)}, u32[]{:S(2)}, u32[]{:S(2)}) %all-to-all-start.1) | async-done | bytes 524320 | tf_op jit(solution)/shard_map/all_to_all | solution.py:396
  46.6 0.0 copy-done
  46.6 0.0 copy-done.1
  46.6 0.0 copy-done.2
  46.6 0.0 copy-done.3
  46.6 0.0 copy-done.5
  46.7 1.1 %outputs.1 = (f32[2,256,128]{2,1,0:T(8,128)}, f32[2,256,128]{2,1,0:T(8,128)}, f32[2,256,128]{2,1,0:T(8,128)}, f32[2,256,128]{2,1,0:T(8,128)}) custom-call(f32[2,256,128]{2,1,0:T(8,128)S(1)} %copy-done, f32[2,256,128]{2,1,0:T(8,128)S(1)} %copy-done.1, f32[2,256,128]{2,1,0:T(8,128)S(1)} %copy-done.2, f32[2,256,128]{2,1,0:T(8,128)S(1)} %copy-done.3, ...), custom_call_target="tpu_custom_call" | custom-call | flops 805306368 | bytes 524288 | tf_op jit(solution)/shard_map/outputs/pallas_call | solution.py:382
  (1 shorter events, 0.0 us)
Async XLA Ops:
  0.6 10.3 %copy-start.6 = (bf16[1536,512]{1,0:T(8,128)(2,1)S(1)}, bf16[1536,512]{1,0:T(8,128)(2,1)}, u32[]{:S(2)}) copy-start(bf16[1536,512]{1,0:T(8,128)(2,1)} %constant.5.clone.matrix_ref) | copy-start | bytes 4718596
  0.6 10.3 %copy-start.7 = (f32[32,512]{1,0:T(8,128)S(1)}, f32[32,512]{1,0:T(8,128)}, u32[]{:S(2)}) copy-start(f32[32,512]{1,0:T(8,128)} %constant.4.clone.twist_ref) | copy-start | bytes 196612
  0.7 10.3 %copy-start.4 = (f32[8,4096]{1,0:T(8,128)S(1)}, f32[8,4096]{1,0:T(8,128)}, u32[]{:S(2)}) copy-start(f32[8,4096]{1,0:T(8,128)} %filter_ref.1) | copy-start | bytes 393220
  3.0 21.4 %all-to-all-start = ((f32[16,32,256]{2,1,0:T(8,128)}), f32[16,32,256]{2,1,0:T(8,128)S(1)}, u32[]{:S(2)}, u32[]{:S(2)}) async-start(f32[16,32,256]{2,1,0:T(8,128)} %gate.1), calls=%async_computation | async-start | bytes 1048576 | tf_op jit(solution)/shard_map/all_to_all | solution.py:396
  27.7 0.8 %copy-start.8 = (f32[1,32,8,512]{3,2,1,0:T(8,128)}, f32[1,32,8,512]{3,2,1,0:T(8,128)S(1)}, u32[]{:S(2)}) copy-start(f32[1,32,8,512]{3,2,1,0:T(8,128)S(1)} %get-tuple-element.17.mixed_ref) | copy-start | bytes 1572868
  28.5 4.7 %copy-start.10 = (f32[1,32,8,512]{3,2,1,0:T(8,128)}, f32[1,32,8,512]{3,2,1,0:T(8,128)S(1)}, u32[]{:S(2)}) copy-start(f32[1,32,8,512]{3,2,1,0:T(8,128)S(1)} %get-tuple-element.18.upstream_ref) | copy-start | bytes 1572868
  28.5 18.1 %all-to-all-start.1 = ((f32[16,32,256]{2,1,0:T(8,128)}), f32[16,32,256]{2,1,0:T(8,128)S(1)}, u32[]{:S(2)}, u32[]{:S(2)}) async-start(f32[16,32,256]{2,1,0:T(8,128)} %get-tuple-element.12), calls=%async_computation.1 | async-start | bytes 1048576 | tf_op jit(solution)/shard_map/all_to_all | solution.py:396
  33.2 1.0 %copy-start.9 = (f32[1,32,8,512]{3,2,1,0:T(8,128)S(1)}, f32[1,32,8,512]{3,2,1,0:T(8,128)}, u32[]{:S(2)}) copy-start(f32[1,32,8,512]{3,2,1,0:T(8,128)} %copy-done.8) | copy-start | bytes 1572868
  34.2 1.0 %copy-start.11 = (f32[1,32,8,512]{3,2,1,0:T(8,128)S(1)}, f32[1,32,8,512]{3,2,1,0:T(8,128)}, u32[]{:S(2)}) copy-start(f32[1,32,8,512]{3,2,1,0:T(8,128)} %copy-done.10) | copy-start | bytes 1572868
  35.2 11.4 %copy-start = (f32[2,256,128]{2,1,0:T(8,128)S(1)}, f32[2,256,128]{2,1,0:T(8,128)}, u32[]{:S(2)}) copy-start(f32[2,256,128]{2,1,0:T(8,128)} %query_ref.1) | copy-start | bytes 786436
  35.2 11.4 %copy-start.1 = (f32[2,256,128]{2,1,0:T(8,128)S(1)}, f32[2,256,128]{2,1,0:T(8,128)}, u32[]{:S(2)}) copy-start(f32[2,256,128]{2,1,0:T(8,128)} %key_ref.1) | copy-start | bytes 786436
  35.2 11.4 %copy-start.2 = (f32[2,256,128]{2,1,0:T(8,128)S(1)}, f32[2,256,128]{2,1,0:T(8,128)}, u32[]{:S(2)}) copy-start(f32[2,256,128]{2,1,0:T(8,128)} %value_ref.1) | copy-start | bytes 786436
  35.2 11.4 %copy-start.3 = (f32[2,256,128]{2,1,0:T(8,128)S(1)}, f32[2,256,128]{2,1,0:T(8,128)}, u32[]{:S(2)}) copy-start(f32[2,256,128]{2,1,0:T(8,128)} %cotangent_ref.1) | copy-start | bytes 786436
  35.3 11.4 %copy-start.5 = (f32[128]{0:T(128)S(1)}, f32[128]{0:T(128)}, u32[]{:S(2)}) copy-start(f32[128]{0:T(128)} %param.12) | copy-start | bytes 1540
  36.0 4.3 %collective-permute-start = (f32[8,2048]{1,0:T(8,128)S(1)}, f32[8,2048]{1,0:T(8,128)S(1)}, u32[]{:S(2)}, u32[]{:S(2)}) collective-permute-start(f32[8,2048]{1,0:T(8,128)S(1)} %slice_bitcast_fusion), channel_id=1, source_target_pairs={{0,16},{16,0},{1,17},{17,1},{2,18},{18,2},{3,19},{19,3},{4,20},{20... | collective-permute-start | bytes 196616 | tf_op jit(solution)/shard_map/ppermute | solution.py:447

commit v17 on v14

--- a/solution.py
+++ b/solution.py
@@ -11,7 +11,7 @@
 from jax.sharding import PartitionSpec as P
 
 VMEM_BYTES = 48 * 1024 * 1024
-ROW_CHUNK = 512
+ROW_CHUNK = 128
 
 
 def add(a, b):
@@ -98,20 +98,6 @@
     return (size // first, first)
 
 
-def across_rows(load, emit, count, kept, store, fetch):
-    first, second = factors_of(count)
-    for b in range(second):
-        values = small_dft([load(second * a + b) for a in range(first)])
-        for p, value in enumerate(values):
-            store(b, p, turn(value, b * p, count))
-    for p in range(first):
-        values = small_dft([fetch(b, p) for b in range(second)])
-        for q, value in enumerate(values):
-            k1 = p + first * q
-            if k1 < kept:
-                emit(k1, value)
-
-
 def tables(count, lanes):
     k1 = np.arange(count)[:, None]
     n2 = np.arange(lanes)[None, :]
@@ -207,33 +193,42 @@
 def transforms(twist_ref, matrix_ref, middle, turned):
     count, channels, width = turned.shape
     lanes = width // 2
-    first, _ = factors_of(count)
-    per_chunk = ROW_CHUNK // channels
-    chunks = [slice(at, min(at + per_chunk, count)) for at in range(0, count, per_chunk)]
-
-    def store(b, p, value):
+    first, second = factors_of(count)
+    in_chunk = max(1, ROW_CHUNK // channels // second)
+    chunks = [range(p, min(p + in_chunk, first)) for p in range(0, first, in_chunk)]
+
+    def store(row, value):
         re, im = value
-        middle[b * first + p, :, :lanes] = jnp.zeros_like(im) if re is None else re
-        middle[b * first + p, :, lanes:] = jnp.zeros_like(re) if im is None else im
-
-    def fetch(b, p):
-        return (middle[b * first + p, :, :lanes], middle[b * first + p, :, lanes:])
+        middle[row, :, :lanes] = jnp.zeros_like(im) if re is None else re
+        middle[row, :, lanes:] = jnp.zeros_like(re) if im is None else im
+
+    def fetch(row):
+        return (middle[row, :, :lanes], middle[row, :, lanes:])
 
     def twist(k1, value):
         c, s = twist_ref[k1 : k1 + 1, :lanes], twist_ref[k1 : k1 + 1, lanes:]
         return (value[0] * c - value[1] * s, value[0] * s + value[1] * c)
 
-    def place(k1, value):
-        turned[k1, :, :lanes], turned[k1, :, lanes:] = twist(k1, value)
+    def places(chunk):
+        return slice(chunk[0] * second, (chunk[-1] + 1) * second)
 
     def forward(load, spec):
-        across_rows(load, place, count, count, store, fetch)
-        for part in chunks:
-            x = turned[part].reshape(-1, width)
-            spec[part] = lane_dft(x, matrix_ref[...]).reshape(-1, channels, width)
+        for b in range(second):
+            values = small_dft([load(second * a + b) for a in range(first)])
+            for p, value in enumerate(values):
+                store(b * first + p, turn(value, b * p, count))
+        for chunk in chunks:
+            for p in chunk:
+                values = small_dft([fetch(b * first + p) for b in range(second)])
+                for q, value in enumerate(values):
+                    place = p * second + q
+                    turned[place, :, :lanes], turned[place, :, lanes:] = twist(p + first * q, value)
+            x = turned[places(chunk)].reshape(-1, width)
+            spec[places(chunk)] = lane_dft(x, matrix_ref[...]).reshape(-1, channels, width)
 
     def inverse(left, right, conjugate_left, emit):
-        for part in chunks:
+        def along_lanes(chunk):
+            part = places(chunk)
             lr, li = left[part, :, :lanes], left[part, :, lanes:]
             rr, ri = right[part, :, :lanes], right[part, :, lanes:]
             if conjugate_left:
@@ -243,10 +238,27 @@
             x = jnp.concatenate([re.reshape(-1, lanes), im.reshape(-1, lanes)], axis=1)
             turned[part] = lane_dft(x, matrix_ref[...]).reshape(-1, channels, width)
 
-        def load(k1):
-            return twist(k1, (turned[k1, :, :lanes], turned[k1, :, lanes:]))
-
-        across_rows(load, emit, count, count // 2, store, fetch)
+        def along_rows(chunk):
+            for p in chunk:
+                values = []
+                for q in range(second):
+                    place = p * second + q
+                    value = (turned[place, :, :lanes], turned[place, :, lanes:])
+                    values.append(twist(p + first * q, value))
+                for r, value in enumerate(small_dft(values)):
+                    store(p * second + r, turn(value, p * r, count))
+
+        along_lanes(chunks[0])
+        for before, chunk in zip(chunks, chunks[1:]):
+            along_lanes(chunk)
+            along_rows(before)
+        along_rows(chunks[-1])
+        for r in range(second):
+            values = small_dft([fetch(p * second + r) for p in range(first)])
+            for t, value in enumerate(values):
+                n1 = r + second * t
+                if n1 < count // 2:
+                    emit(n1, value)
 
     return forward, inverse
 

time: 46.6 us -> 46.4 us (level)
  no operation moved by 1% of the time
where the time goes in v17:
time: 46.4 us; the launch traced here: 46 us
  waiting for transfers between devices  23.7 us (51%)
  starting transfers between devices  14.2 us (31%)
  Pallas kernels  6.55 us (14%)
  between operations  0.76 us (2%)
  other arithmetic  0.64 us (1%)
    all_to_all x2, waiting for transfers between devices, exchange(): lax.all_to_all(blocks, 'seq', split_axis=0, concat_axis=0, tiled=True, ax...  20.9 us
    all_to_all x2, starting transfers between devices, exchange(): lax.all_to_all(blocks, 'seq', split_axis=0, concat_axis=0, tiled=True, ax...  12.7 us
    pallas_call x5, Pallas kernels, call(): pl.pallas_call(kernel, out_shape=out_shape, scratch_shapes=scratch, compi...  6.55 us
    ppermute x1, waiting for transfers between devices, per_device(): filter_grad = filter_grad + lax.ppermute(lag[step], 'batch', pairs)  2.78 us
    ppermute x1, starting transfers between devices, per_device(): filter_grad = filter_grad + lax.ppermute(lag[step], 'batch', pairs)  1.55 us
  transfers between devices with their start and end apart: 3, of which 3 were waited for; matrix products, arithmetic and copies ran while one was open for 1% of the time, Pallas kernels for 2%

profile of v17, /device:TPU:0, one launch (start us, length us, event | category | flops | bytes accessed | tf_op | source)
XLA Modules:
  0.0 46.0 jit_solution(12783451876303452310)
XLA Ops:
  0.6 2.2 %gate.1 = f32[16,64,128]{2,1,0:T(8,128)} custom-call(f32[2,256,128]{2,1,0:T(8,128)} %query_ref.1, f32[2,256,128]{2,1,0:T(8,128)} %key_ref.1, f32[2,256,128]{2,1,0:T(8,128)} %value_ref.1, f32[2,256,128]{2,1,0:T(8,128)} %cotangent_ref.1), custom_call_target="tpu_custom_call" | custom-call | flops 201326592 | bytes 262144 | tf_op jit(solution)/shard_map/gate/pallas_call | solution.py:395
  2.8 0.0 copy-start.4
  2.9 0.0 copy-start.5
  2.9 0.0 copy-start.7
  2.9 8.0 %all-to-all-start = ((f32[16,64,128]{2,1,0:T(8,128)}), f32[16,64,128]{2,1,0:T(8,128)S(1)}, u32[]{:S(2)}, u32[]{:S(2)}) async-start(f32[16,64,128]{2,1,0:T(8,128)} %gate.1), calls=%async_computation | async-start | bytes 1048576 | tf_op jit(solution)/shard_map/all_to_all | solution.py:409
  10.9 0.0 copy-done.4
  10.9 0.0 copy-done.5
  10.9 0.0 copy-done.7
  10.9 0.5 %filter.1.filter_ref = f32[64,8,256]{2,1,0:T(8,128)S(1)} custom-call(f32[8,4096]{1,0:T(8,128)S(1)} %copy-done.7, f32[64,256]{1,0:T(8,128)S(1)} %copy-done.5, bf16[768,256]{1,0:T(8,128)(2,1)S(1)} %copy-done.4), custom_call_target="tpu_custom_call" | custom-call | flops 402653184 | bytes 524288 | tf_op jit(solution)/shard_map/filter/pallas_call | solution.py:395
  11.4 13.0 %all-to-all-done.held_ref = f32[16,64,128]{2,1,0:T(8,128)S(1)} async-done(((f32[16,64,128]{2,1,0:T(8,128)}), f32[16,64,128]{2,1,0:T(8,128)S(1)}, u32[]{:S(2)}, u32[]{:S(2)}) %all-to-all-start) | async-done | bytes 524320 | tf_op jit(solution)/shard_map/all_to_all | solution.py:409
  24.4 2.3 %convolve.1 = (f32[16,64,128]{2,1,0:T(8,128)}, f32[1,64,8,256]{3,2,1,0:T(8,128)S(1)}, f32[1,64,8,256]{3,2,1,0:T(8,128)S(1)}) custom-call(f32[16,64,128]{2,1,0:T(8,128)S(1)} %all-to-all-done.held_ref, f32[64,8,256]{2,1,0:T(8,128)S(1)} %filter.1.filter_ref, f32[64,256]{1,0:T(8,128)S(1)} %copy-done.5, bf16[768,256]{1,0:T(8,128)(2,1)S(1)} %copy-done.4), custom_call_target="tpu_custom_call" | custom-call | flops 1610612736 | bytes 2097152 | tf_op jit(solution)/shard_map/convolve/pallas_call | solution.py:395
  26.7 4.7 %all-to-all-start.1 = ((f32[16,64,128]{2,1,0:T(8,128)}), f32[16,64,128]{2,1,0:T(8,128)S(1)}, u32[]{:S(2)}, u32[]{:S(2)}) async-start(f32[16,64,128]{2,1,0:T(8,128)} %get-tuple-element.12), calls=%async_computation.1 | async-start | bytes 1048576 | tf_op jit(solution)/shard_map/all_to_all | solution.py:409
  31.3 0.0 copy-start.1
  31.3 0.0 copy-start.2
  31.3 0.0 copy-start.3
  31.3 0.5 %lags.1 = f32[2,8,2048]{2,1,0:T(8,128)S(1)} custom-call(f32[1,64,8,256]{3,2,1,0:T(8,128)S(1)} %get-tuple-element.17.mixed_ref, f32[1,64,8,256]{3,2,1,0:T(8,128)S(1)} %get-tuple-element.18.upstream_ref, f32[64,256]{1,0:T(8,128)S(1)} %copy-done.5, bf16[768,256]{1,0:T(8,128)(2,1)S(1)} %copy-done.4), custom_call_target="tpu_custom_call" | custom-call | flops 402653184 | bytes 524288 | tf_op jit(solution)/shard_map/lags/pallas_call | solution.py:395
  31.8 0.0 copy-start
  31.9 1.6 %collective-permute-start = (f32[8,2048]{1,0:T(8,128)S(1)}, f32[8,2048]{1,0:T(8,128)S(1)}, u32[]{:S(2)}, u32[]{:S(2)}) collective-permute-start(f32[8,2048]{1,0:T(8,128)S(1)} %slice_bitcast_fusion), channel_id=1, source_target_pairs={{0,16},{16,0},{1,17},{17,1},{2,18},{18,2},{3,19},{19,3},{4,20},{20... | collective-permute-start | bytes 196616 | tf_op jit(solution)/shard_map/ppermute | solution.py:460
  33.4 2.8 %collective-permute-done = f32[8,2048]{1,0:T(8,128)S(1)} collective-permute-done((f32[8,2048]{1,0:T(8,128)S(1)}, f32[8,2048]{1,0:T(8,128)S(1)}, u32[]{:S(2)}, u32[]{:S(2)}) %collective-permute-start) | collective-permute-done | bytes 65568 | tf_op jit(solution)/shard_map/ppermute | solution.py:460
  36.2 0.6 %fusion = f32[8,2048]{1,0:T(8,128)} fusion(f32[8,2048]{1,0:T(8,128)S(1)} %collective-permute-done, f32[2,8,2048]{2,1,0:T(8,128)S(1)} %lags.1), kind=kLoop, calls=%fused_computation.2 | loop fusion | flops 16384 | bytes 196608 | tf_op jit(solution)/shard_map/add | solution.py:460
  36.8 0.0 copy-start.6
  36.8 8.0 %all-to-all-done.1.home_ref = f32[16,64,128]{2,1,0:T(8,128)S(1)} async-done(((f32[16,64,128]{2,1,0:T(8,128)}), f32[16,64,128]{2,1,0:T(8,128)S(1)}, u32[]{:S(2)}, u32[]{:S(2)}) %all-to-all-start.1) | async-done | bytes 524320 | tf_op jit(solution)/shard_map/all_to_all | solution.py:409
  44.8 0.0 copy-done.1
  44.8 0.0 copy-done.2
  44.8 0.0 copy-done.3
  44.8 0.0 copy-done
  44.8 0.0 copy-done.6
  44.8 1.1 %outputs.1 = (f32[2,256,128]{2,1,0:T(8,128)}, f32[2,256,128]{2,1,0:T(8,128)}, f32[2,256,128]{2,1,0:T(8,128)}, f32[2,256,128]{2,1,0:T(8,128)}) custom-call(f32[2,256,128]{2,1,0:T(8,128)S(1)} %copy-done, f32[2,256,128]{2,1,0:T(8,128)S(1)} %copy-done.1, f32[2,256,128]{2,1,0:T(8,128)S(1)} %copy-done.2, f32[2,256,128]{2,1,0:T(8,128)S(1)} %copy-done.3, ...), custom_call_target="tpu_custom_call" | custom-call | flops 402653184 | bytes 524288 | tf_op jit(solution)/shard_map/outputs/pallas_call | solution.py:395
  (1 shorter events, 0.0 us)
Async XLA Ops:
  2.8 8.1 %copy-start.4 = (bf16[768,256]{1,0:T(8,128)(2,1)S(1)}, bf16[768,256]{1,0:T(8,128)(2,1)}, u32[]{:S(2)}) copy-start(bf16[768,256]{1,0:T(8,128)(2,1)} %constant.5.clone.matrix_ref) | copy-start | bytes 1179652
  2.9 8.1 %copy-start.5 = (f32[64,256]{1,0:T(8,128)S(1)}, f32[64,256]{1,0:T(8,128)}, u32[]{:S(2)}) copy-start(f32[64,256]{1,0:T(8,128)} %constant.4.clone.twist_ref) | copy-start | bytes 196612
  2.9 8.1 %copy-start.7 = (f32[8,4096]{1,0:T(8,128)S(1)}, f32[8,4096]{1,0:T(8,128)}, u32[]{:S(2)}) copy-start(f32[8,4096]{1,0:T(8,128)} %filter_ref.1) | copy-start | bytes 393220
  2.9 21.5 %all-to-all-start = ((f32[16,64,128]{2,1,0:T(8,128)}), f32[16,64,128]{2,1,0:T(8,128)S(1)}, u32[]{:S(2)}, u32[]{:S(2)}) async-start(f32[16,64,128]{2,1,0:T(8,128)} %gate.1), calls=%async_computation | async-start | bytes 1048576 | tf_op jit(solution)/shard_map/all_to_all | solution.py:409
  26.7 18.1 %all-to-all-start.1 = ((f32[16,64,128]{2,1,0:T(8,128)}), f32[16,64,128]{2,1,0:T(8,128)S(1)}, u32[]{:S(2)}, u32[]{:S(2)}) async-start(f32[16,64,128]{2,1,0:T(8,128)} %get-tuple-element.12), calls=%async_computation.1 | async-start | bytes 1048576 | tf_op jit(solution)/shard_map/all_to_all | solution.py:409
  31.3 13.5 %copy-start.1 = (f32[2,256,128]{2,1,0:T(8,128)S(1)}, f32[2,256,128]{2,1,0:T(8,128)}, u32[]{:S(2)}) copy-start(f32[2,256,128]{2,1,0:T(8,128)} %key_ref.1) | copy-start | bytes 786436
  31.3 13.5 %copy-start.2 = (f32[2,256,128]{2,1,0:T(8,128)S(1)}, f32[2,256,128]{2,1,0:T(8,128)}, u32[]{:S(2)}) copy-start(f32[2,256,128]{2,1,0:T(8,128)} %value_ref.1) | copy-start | bytes 786436
  31.3 13.5 %copy-start.3 = (f32[2,256,128]{2,1,0:T(8,128)S(1)}, f32[2,256,128]{2,1,0:T(8,128)}, u32[]{:S(2)}) copy-start(f32[2,256,128]{2,1,0:T(8,128)} %cotangent_ref.1) | copy-start | bytes 786436
  31.8 13.0 %copy-start = (f32[2,256,128]{2,1,0:T(8,128)S(1)}, f32[2,256,128]{2,1,0:T(8,128)}, u32[]{:S(2)}) copy-start(f32[2,256,128]{2,1,0:T(8,128)} %query_ref.1) | copy-start | bytes 786436
  31.9 4.3 %collective-permute-start = (f32[8,2048]{1,0:T(8,128)S(1)}, f32[8,2048]{1,0:T(8,128)S(1)}, u32[]{:S(2)}, u32[]{:S(2)}) collective-permute-start(f32[8,2048]{1,0:T(8,128)S(1)} %slice_bitcast_fusion), channel_id=1, source_target_pairs={{0,16},{16,0},{1,17},{17,1},{2,18},{18,2},{3,19},{19,3},{4,20},{20... | collective-permute-start | bytes 196616 | tf_op jit(solution)/shard_map/ppermute | solution.py:460
  36.8 8.0 %copy-start.6 = (f32[128]{0:T(128)S(1)}, f32[128]{0:T(128)}, u32[]{:S(2)}) copy-start(f32[128]{0:T(128)} %param.12) | copy-start | bytes 1540

commit v18 on v17

--- a/solution.py
+++ b/solution.py
@@ -306,9 +306,14 @@
         transforms(twist_ref, matrix_ref, middles.at[kind], turneds.at[kind]) for kind in range(2)
     ]
 
-    def send(kind):
-        span = pl.ds(kind * half, half)
-        return pltpu.make_async_copy(back.at[:, span], back_hbm.at[:, span], out_sems.at[kind])
+    copies = out_sems.shape[1]
+    share = back.shape[0] // copies
+
+    def send(kind, i):
+        blocks, span = pl.ds(i * share, share), pl.ds(kind * half, half)
+        return pltpu.make_async_copy(
+            back.at[blocks, span], back_hbm.at[blocks, span], out_sems.at[kind, i]
+        )
 
     for pair in range(pairs):
         for kind in range(2):
@@ -318,9 +323,11 @@
             _, emit = token_blocks(back, order, kind, pair, 2 * pairs, channels, count // 2)
             scratch[kind][1](filter_ref, kinds[kind].at[pair], kind == 1, emit)
             if pair == pairs - 1:
-                send(kind).start()
+                for i in range(copies):
+                    send(kind, i).start()
     for kind in range(2):
-        send(kind).wait()
+        for i in range(copies):
+            send(kind, i).wait()
 
 
 def lag_kernel(scaling, mixed_ref, upstream_ref, twist_ref, matrix_ref, lag_ref, middle, turned):
@@ -443,7 +450,7 @@
             pltpu.VMEM((shards, rows, lanes), jnp.float32),
             pltpu.VMEM((2, count, channels, 2 * lanes), jnp.float32),
             pltpu.VMEM((2, count, channels, 2 * lanes), jnp.float32),
-            pltpu.SemaphoreType.DMA((2,)),
+            pltpu.SemaphoreType.DMA((2, math.gcd(shards, 8))),
         ],
         held, filter_spec, twist, matrix,
         out_specs=(anywhere, in_vmem, in_vmem),

time: 46.4 us -> 46.5 us (level)
  no operation moved by 1% of the time
where the time goes in v18:
time: 46.5 us; the launch traced here: 46.1 us
  waiting for transfers between devices  23.7 us (51%)
  starting transfers between devices  14.2 us (31%)
  Pallas kernels  6.67 us (14%)
  between operations  0.76 us (2%)
  other arithmetic  0.64 us (1%)
    all_to_all x2, waiting for transfers between devices, exchange(): lax.all_to_all(blocks, 'seq', split_axis=0, concat_axis=0, tiled=True, ax...  20.9 us
    all_to_all x2, starting transfers between devices, exchange(): lax.all_to_all(blocks, 'seq', split_axis=0, concat_axis=0, tiled=True, ax...  12.7 us
    pallas_call x5, Pallas kernels, call(): pl.pallas_call(kernel, out_shape=out_shape, scratch_shapes=scratch, compi...  6.67 us
    ppermute x1, waiting for transfers between devices, per_device(): filter_grad = filter_grad + lax.ppermute(lag[step], 'batch', pairs)  2.77 us
    ppermute x1, starting transfers between devices, per_device(): filter_grad = filter_grad + lax.ppermute(lag[step], 'batch', pairs)  1.56 us
  transfers between devices with their start and end apart: 3, of which 3 were waited for; matrix products, arithmetic and copies ran while one was open for 1% of the time, Pallas kernels for 2%

profile of v18, /device:TPU:0, one launch (start us, length us, event | category | flops | bytes accessed | tf_op | source)
XLA Modules:
  0.0 46.1 jit_solution(4782211922174106369)
XLA Ops:
  0.6 2.2 %gate.1 = f32[16,64,128]{2,1,0:T(8,128)} custom-call(f32[2,256,128]{2,1,0:T(8,128)} %query_ref.1, f32[2,256,128]{2,1,0:T(8,128)} %key_ref.1, f32[2,256,128]{2,1,0:T(8,128)} %value_ref.1, f32[2,256,128]{2,1,0:T(8,128)} %cotangent_ref.1), custom_call_target="tpu_custom_call" | custom-call | flops 201326592 | bytes 262144 | tf_op jit(solution)/shard_map/gate/pallas_call | solution.py:402
  2.8 0.0 copy-start.4
  2.9 0.0 copy-start.5
  2.9 0.0 copy-start.7
  2.9 8.0 %all-to-all-start = ((f32[16,64,128]{2,1,0:T(8,128)}), f32[16,64,128]{2,1,0:T(8,128)S(1)}, u32[]{:S(2)}, u32[]{:S(2)}) async-start(f32[16,64,128]{2,1,0:T(8,128)} %gate.1), calls=%async_computation | async-start | bytes 1048576 | tf_op jit(solution)/shard_map/all_to_all | solution.py:416
  10.9 0.0 copy-done.4
  10.9 0.0 copy-done.5
  10.9 0.0 copy-done.7
  10.9 0.5 %filter.1.filter_ref = f32[64,8,256]{2,1,0:T(8,128)S(1)} custom-call(f32[8,4096]{1,0:T(8,128)S(1)} %copy-done.7, f32[64,256]{1,0:T(8,128)S(1)} %copy-done.5, bf16[768,256]{1,0:T(8,128)(2,1)S(1)} %copy-done.4), custom_call_target="tpu_custom_call" | custom-call | flops 402653184 | bytes 524288 | tf_op jit(solution)/shard_map/filter/pallas_call | solution.py:402
  11.4 13.0 %all-to-all-done.held_ref = f32[16,64,128]{2,1,0:T(8,128)S(1)} async-done(((f32[16,64,128]{2,1,0:T(8,128)}), f32[16,64,128]{2,1,0:T(8,128)S(1)}, u32[]{:S(2)}, u32[]{:S(2)}) %all-to-all-start) | async-done | bytes 524320 | tf_op jit(solution)/shard_map/all_to_all | solution.py:416
  24.4 2.4 %convolve.1 = (f32[16,64,128]{2,1,0:T(8,128)}, f32[1,64,8,256]{3,2,1,0:T(8,128)S(1)}, f32[1,64,8,256]{3,2,1,0:T(8,128)S(1)}) custom-call(f32[16,64,128]{2,1,0:T(8,128)S(1)} %all-to-all-done.held_ref, f32[64,8,256]{2,1,0:T(8,128)S(1)} %filter.1.filter_ref, f32[64,256]{1,0:T(8,128)S(1)} %copy-done.5, bf16[768,256]{1,0:T(8,128)(2,1)S(1)} %copy-done.4), custom_call_target="tpu_custom_call" | custom-call | flops 1610612736 | bytes 2097152 | tf_op jit(solution)/shard_map/convolve/pallas_call | solution.py:402
  26.8 4.7 %all-to-all-start.1 = ((f32[16,64,128]{2,1,0:T(8,128)}), f32[16,64,128]{2,1,0:T(8,128)S(1)}, u32[]{:S(2)}, u32[]{:S(2)}) async-start(f32[16,64,128]{2,1,0:T(8,128)} %get-tuple-element.12), calls=%async_computation.1 | async-start | bytes 1048576 | tf_op jit(solution)/shard_map/all_to_all | solution.py:416
  31.4 0.0 copy-start.1
  31.4 0.0 copy-start.2
  31.5 0.0 copy-start.3
  31.5 0.5 %lags.1 = f32[2,8,2048]{2,1,0:T(8,128)S(1)} custom-call(f32[1,64,8,256]{3,2,1,0:T(8,128)S(1)} %get-tuple-element.17.mixed_ref, f32[1,64,8,256]{3,2,1,0:T(8,128)S(1)} %get-tuple-element.18.upstream_ref, f32[64,256]{1,0:T(8,128)S(1)} %copy-done.5, bf16[768,256]{1,0:T(8,128)(2,1)S(1)} %copy-done.4), custom_call_target="tpu_custom_call" | custom-call | flops 402653184 | bytes 524288 | tf_op jit(solution)/shard_map/lags/pallas_call | solution.py:402
  31.9 0.0 copy-start
  32.0 1.6 %collective-permute-start = (f32[8,2048]{1,0:T(8,128)S(1)}, f32[8,2048]{1,0:T(8,128)S(1)}, u32[]{:S(2)}, u32[]{:S(2)}) collective-permute-start(f32[8,2048]{1,0:T(8,128)S(1)} %slice_bitcast_fusion), channel_id=1, source_target_pairs={{0,16},{16,0},{1,17},{17,1},{2,18},{18,2},{3,19},{19,3},{4,20},{20... | collective-permute-start | bytes 196616 | tf_op jit(solution)/shard_map/ppermute | solution.py:467
  33.5 2.8 %collective-permute-done = f32[8,2048]{1,0:T(8,128)S(1)} collective-permute-done((f32[8,2048]{1,0:T(8,128)S(1)}, f32[8,2048]{1,0:T(8,128)S(1)}, u32[]{:S(2)}, u32[]{:S(2)}) %collective-permute-start) | collective-permute-done | bytes 65568 | tf_op jit(solution)/shard_map/ppermute | solution.py:467
  36.3 0.6 %fusion = f32[8,2048]{1,0:T(8,128)} fusion(f32[8,2048]{1,0:T(8,128)S(1)} %collective-permute-done, f32[2,8,2048]{2,1,0:T(8,128)S(1)} %lags.1), kind=kLoop, calls=%fused_computation.2 | loop fusion | flops 16384 | bytes 196608 | tf_op jit(solution)/shard_map/add | solution.py:467
  36.9 0.0 copy-start.6
  36.9 8.0 %all-to-all-done.1.home_ref = f32[16,64,128]{2,1,0:T(8,128)S(1)} async-done(((f32[16,64,128]{2,1,0:T(8,128)}), f32[16,64,128]{2,1,0:T(8,128)S(1)}, u32[]{:S(2)}, u32[]{:S(2)}) %all-to-all-start.1) | async-done | bytes 524320 | tf_op jit(solution)/shard_map/all_to_all | solution.py:416
  44.9 0.0 copy-done.1
  44.9 0.0 copy-done.2
  44.9 0.0 copy-done.3
  44.9 0.0 copy-done
  44.9 0.0 copy-done.6
  44.9 1.1 %outputs.1 = (f32[2,256,128]{2,1,0:T(8,128)}, f32[2,256,128]{2,1,0:T(8,128)}, f32[2,256,128]{2,1,0:T(8,128)}, f32[2,256,128]{2,1,0:T(8,128)}) custom-call(f32[2,256,128]{2,1,0:T(8,128)S(1)} %copy-done, f32[2,256,128]{2,1,0:T(8,128)S(1)} %copy-done.1, f32[2,256,128]{2,1,0:T(8,128)S(1)} %copy-done.2, f32[2,256,128]{2,1,0:T(8,128)S(1)} %copy-done.3, ...), custom_call_target="tpu_custom_call" | custom-call | flops 402653184 | bytes 524288 | tf_op jit(solution)/shard_map/outputs/pallas_call | solution.py:402
  (1 shorter events, 0.0 us)
Async XLA Ops:
  2.8 8.1 %copy-start.4 = (bf16[768,256]{1,0:T(8,128)(2,1)S(1)}, bf16[768,256]{1,0:T(8,128)(2,1)}, u32[]{:S(2)}) copy-start(bf16[768,256]{1,0:T(8,128)(2,1)} %constant.5.clone.matrix_ref) | copy-start | bytes 1179652
  2.9 8.1 %copy-start.5 = (f32[64,256]{1,0:T(8,128)S(1)}, f32[64,256]{1,0:T(8,128)}, u32[]{:S(2)}) copy-start(f32[64,256]{1,0:T(8,128)} %constant.4.clone.twist_ref) | copy-start | bytes 196612
  2.9 8.1 %copy-start.7 = (f32[8,4096]{1,0:T(8,128)S(1)}, f32[8,4096]{1,0:T(8,128)}, u32[]{:S(2)}) copy-start(f32[8,4096]{1,0:T(8,128)} %filter_ref.1) | copy-start | bytes 393220
  2.9 21.5 %all-to-all-start = ((f32[16,64,128]{2,1,0:T(8,128)}), f32[16,64,128]{2,1,0:T(8,128)S(1)}, u32[]{:S(2)}, u32[]{:S(2)}) async-start(f32[16,64,128]{2,1,0:T(8,128)} %gate.1), calls=%async_computation | async-start | bytes 1048576 | tf_op jit(solution)/shard_map/all_to_all | solution.py:416
  26.8 18.1 %all-to-all-start.1 = ((f32[16,64,128]{2,1,0:T(8,128)}), f32[16,64,128]{2,1,0:T(8,128)S(1)}, u32[]{:S(2)}, u32[]{:S(2)}) async-start(f32[16,64,128]{2,1,0:T(8,128)} %get-tuple-element.12), calls=%async_computation.1 | async-start | bytes 1048576 | tf_op jit(solution)/shard_map/all_to_all | solution.py:416
  31.4 13.5 %copy-start.1 = (f32[2,256,128]{2,1,0:T(8,128)S(1)}, f32[2,256,128]{2,1,0:T(8,128)}, u32[]{:S(2)}) copy-start(f32[2,256,128]{2,1,0:T(8,128)} %key_ref.1) | copy-start | bytes 786436
  31.4 13.5 %copy-start.2 = (f32[2,256,128]{2,1,0:T(8,128)S(1)}, f32[2,256,128]{2,1,0:T(8,128)}, u32[]{:S(2)}) copy-start(f32[2,256,128]{2,1,0:T(8,128)} %value_ref.1) | copy-start | bytes 786436
  31.5 13.5 %copy-start.3 = (f32[2,256,128]{2,1,0:T(8,128)S(1)}, f32[2,256,128]{2,1,0:T(8,128)}, u32[]{:S(2)}) copy-start(f32[2,256,128]{2,1,0:T(8,128)} %cotangent_ref.1) | copy-start | bytes 786436
  31.9 13.0 %copy-start = (f32[2,256,128]{2,1,0:T(8,128)S(1)}, f32[2,256,128]{2,1,0:T(8,128)}, u32[]{:S(2)}) copy-start(f32[2,256,128]{2,1,0:T(8,128)} %query_ref.1) | copy-start | bytes 786436
  32.0 4.3 %collective-permute-start = (f32[8,2048]{1,0:T(8,128)S(1)}, f32[8,2048]{1,0:T(8,128)S(1)}, u32[]{:S(2)}, u32[]{:S(2)}) collective-permute-start(f32[8,2048]{1,0:T(8,128)S(1)} %slice_bitcast_fusion), channel_id=1, source_target_pairs={{0,16},{16,0},{1,17},{17,1},{2,18},{18,2},{3,19},{19,3},{4,20},{20... | collective-permute-start | bytes 196616 | tf_op jit(solution)/shard_map/ppermute | solution.py:467
  36.9 8.0 %copy-start.6 = (f32[128]{0:T(128)S(1)}, f32[128]{0:T(128)}, u32[]{:S(2)}) copy-start(f32[128]{0:T(128)} %param.12) | copy-start | bytes 1540

commit v19 on v17

--- a/solution.py
+++ b/solution.py
@@ -1,4 +1,5 @@
 import functools
+import itertools
 import math
 
 import jax
@@ -217,6 +218,7 @@
             values = small_dft([load(second * a + b) for a in range(first)])
             for p, value in enumerate(values):
                 store(b * first + p, turn(value, b * p, count))
+            yield
         for chunk in chunks:
             for p in chunk:
                 values = small_dft([fetch(b * first + p) for b in range(second)])
@@ -225,6 +227,7 @@
                     turned[place, :, :lanes], turned[place, :, lanes:] = twist(p + first * q, value)
             x = turned[places(chunk)].reshape(-1, width)
             spec[places(chunk)] = lane_dft(x, matrix_ref[...]).reshape(-1, channels, width)
+            yield
 
     def inverse(left, right, conjugate_left, emit):
         def along_lanes(chunk):
@@ -249,18 +252,28 @@
                     store(p * second + r, turn(value, p * r, count))
 
         along_lanes(chunks[0])
+        yield
         for before, chunk in zip(chunks, chunks[1:]):
             along_lanes(chunk)
+            yield
             along_rows(before)
+            yield
         along_rows(chunks[-1])
+        yield
         for r in range(second):
             values = small_dft([fetch(p * second + r) for p in range(first)])
             for t, value in enumerate(values):
                 n1 = r + second * t
                 if n1 < count // 2:
                     emit(n1, value)
+            yield
 
     return forward, inverse
+
+
+def in_turn(*streams):
+    for _ in itertools.zip_longest(*streams):
+        pass
 
 
 def token_blocks(ref, order, kind, pair, batch, channels, live):
@@ -292,7 +305,7 @@
             return None
         return (filter_ref[:, n1 * lanes : (n1 + 1) * lanes] * (0.5 / length), None)
 
-    forward(load, spec_ref)
+    in_turn(forward(load, spec_ref))
 
 
 def convolve_kernel(
@@ -311,14 +324,21 @@
         return pltpu.make_async_copy(back.at[:, span], back_hbm.at[:, span], out_sems.at[kind])
 
     for pair in range(pairs):
-        for kind in range(2):
+
+        def forward(kind):
             load, _ = token_blocks(held_ref, order, kind, pair, 2 * pairs, channels, count // 2)
-            scratch[kind][0](load, kinds[kind].at[pair])
-        for kind in range(2):
+            return scratch[kind][0](load, kinds[kind].at[pair])
+
+        def inverse(kind):
             _, emit = token_blocks(back, order, kind, pair, 2 * pairs, channels, count // 2)
-            scratch[kind][1](filter_ref, kinds[kind].at[pair], kind == 1, emit)
-            if pair == pairs - 1:
-                send(kind).start()
+            return scratch[kind][1](filter_ref, kinds[kind].at[pair], kind == 1, emit)
+
+        in_turn(forward(0))
+        in_turn(inverse(0), forward(1))
+        if pair == pairs - 1:
+            send(0).start()
+        in_turn(inverse(1))
+    send(1).start()
     for kind in range(2):
         send(kind).wait()
 
@@ -339,7 +359,7 @@
             else:
                 lag_ref[slot, :, span] += value[0] * scaling
 
-        inverse(mixed_ref.at[pair], upstream_ref.at[pair], True, emit)
+        in_turn(inverse(mixed_ref.at[pair], upstream_ref.at[pair], True, emit))
 
 
 def output_kernel(

time: 46.4 us -> 46.5 us (level)
  no operation moved by 1% of the time
where the time goes in v19:
time: 46.5 us; the launch traced here: 46.1 us
  waiting for transfers between devices  23.7 us (51%)
  starting transfers between devices  14.2 us (31%)
  Pallas kernels  6.65 us (14%)
  between operations  0.76 us (2%)
  other arithmetic  0.64 us (1%)
    all_to_all x2, waiting for transfers between devices, exchange(): lax.all_to_all(blocks, 'seq', split_axis=0, concat_axis=0, tiled=True, ax...  20.9 us
    all_to_all x2, starting transfers between devices, exchange(): lax.all_to_all(blocks, 'seq', split_axis=0, concat_axis=0, tiled=True, ax...  12.7 us
    pallas_call x5, Pallas kernels, call(): pl.pallas_call(kernel, out_shape=out_shape, scratch_shapes=scratch, compi...  6.65 us
    ppermute x1, waiting for transfers between devices, per_device(): filter_grad = filter_grad + lax.ppermute(lag[step], 'batch', pairs)  2.78 us
    ppermute x1, starting transfers between devices, per_device(): filter_grad = filter_grad + lax.ppermute(lag[step], 'batch', pairs)  1.55 us
  transfers between devices with their start and end apart: 3, of which 3 were waited for; matrix products, arithmetic and copies ran while one was open for 1% of the time, Pallas kernels for 2%

profile of v19, /device:TPU:0, one launch (start us, length us, event | category | flops | bytes accessed | tf_op | source)
XLA Modules:
  0.0 46.1 jit_solution(1313185102797679707)
XLA Ops:
  0.6 2.2 %gate.1 = f32[16,64,128]{2,1,0:T(8,128)} custom-call(f32[2,256,128]{2,1,0:T(8,128)} %query_ref.1, f32[2,256,128]{2,1,0:T(8,128)} %key_ref.1, f32[2,256,128]{2,1,0:T(8,128)} %value_ref.1, f32[2,256,128]{2,1,0:T(8,128)} %cotangent_ref.1), custom_call_target="tpu_custom_call" | custom-call | flops 201326592 | bytes 262144 | tf_op jit(solution)/shard_map/gate/pallas_call | solution.py:415
  2.8 0.0 copy-start.4
  2.9 0.0 copy-start.5
  2.9 0.0 copy-start.7
  2.9 8.0 %all-to-all-start = ((f32[16,64,128]{2,1,0:T(8,128)}), f32[16,64,128]{2,1,0:T(8,128)S(1)}, u32[]{:S(2)}, u32[]{:S(2)}) async-start(f32[16,64,128]{2,1,0:T(8,128)} %gate.1), calls=%async_computation | async-start | bytes 1048576 | tf_op jit(solution)/shard_map/all_to_all | solution.py:429
  10.9 0.0 copy-done.4
  10.9 0.0 copy-done.5
  10.9 0.0 copy-done.7
  10.9 0.5 %filter.1.filter_ref = f32[64,8,256]{2,1,0:T(8,128)S(1)} custom-call(f32[8,4096]{1,0:T(8,128)S(1)} %copy-done.7, f32[64,256]{1,0:T(8,128)S(1)} %copy-done.5, bf16[768,256]{1,0:T(8,128)(2,1)S(1)} %copy-done.4), custom_call_target="tpu_custom_call" | custom-call | flops 402653184 | bytes 524288 | tf_op jit(solution)/shard_map/filter/pallas_call | solution.py:415
  11.4 13.0 %all-to-all-done.held_ref = f32[16,64,128]{2,1,0:T(8,128)S(1)} async-done(((f32[16,64,128]{2,1,0:T(8,128)}), f32[16,64,128]{2,1,0:T(8,128)S(1)}, u32[]{:S(2)}, u32[]{:S(2)}) %all-to-all-start) | async-done | bytes 524320 | tf_op jit(solution)/shard_map/all_to_all | solution.py:429
  24.4 2.4 %convolve.1 = (f32[16,64,128]{2,1,0:T(8,128)}, f32[1,64,8,256]{3,2,1,0:T(8,128)S(1)}, f32[1,64,8,256]{3,2,1,0:T(8,128)S(1)}) custom-call(f32[16,64,128]{2,1,0:T(8,128)S(1)} %all-to-all-done.held_ref, f32[64,8,256]{2,1,0:T(8,128)S(1)} %filter.1.filter_ref, f32[64,256]{1,0:T(8,128)S(1)} %copy-done.5, bf16[768,256]{1,0:T(8,128)(2,1)S(1)} %copy-done.4), custom_call_target="tpu_custom_call" | custom-call | flops 1610612736 | bytes 2097152 | tf_op jit(solution)/shard_map/convolve/pallas_call | solution.py:415
  26.8 4.7 %all-to-all-start.1 = ((f32[16,64,128]{2,1,0:T(8,128)}), f32[16,64,128]{2,1,0:T(8,128)S(1)}, u32[]{:S(2)}, u32[]{:S(2)}) async-start(f32[16,64,128]{2,1,0:T(8,128)} %get-tuple-element.12), calls=%async_computation.1 | async-start | bytes 1048576 | tf_op jit(solution)/shard_map/all_to_all | solution.py:429
  31.4 0.0 copy-start.1
  31.4 0.0 copy-start.2
  31.4 0.0 copy-start.3
  31.5 0.5 %lags.1 = f32[2,8,2048]{2,1,0:T(8,128)S(1)} custom-call(f32[1,64,8,256]{3,2,1,0:T(8,128)S(1)} %get-tuple-element.17.mixed_ref, f32[1,64,8,256]{3,2,1,0:T(8,128)S(1)} %get-tuple-element.18.upstream_ref, f32[64,256]{1,0:T(8,128)S(1)} %copy-done.5, bf16[768,256]{1,0:T(8,128)(2,1)S(1)} %copy-done.4), custom_call_target="tpu_custom_call" | custom-call | flops 402653184 | bytes 524288 | tf_op jit(solution)/shard_map/lags/pallas_call | solution.py:415
  31.9 0.0 copy-start
  32.0 1.6 %collective-permute-start = (f32[8,2048]{1,0:T(8,128)S(1)}, f32[8,2048]{1,0:T(8,128)S(1)}, u32[]{:S(2)}, u32[]{:S(2)}) collective-permute-start(f32[8,2048]{1,0:T(8,128)S(1)} %slice_bitcast_fusion), channel_id=1, source_target_pairs={{0,16},{16,0},{1,17},{17,1},{2,18},{18,2},{3,19},{19,3},{4,20},{20... | collective-permute-start | bytes 196616 | tf_op jit(solution)/shard_map/ppermute | solution.py:480
  33.5 2.8 %collective-permute-done = f32[8,2048]{1,0:T(8,128)S(1)} collective-permute-done((f32[8,2048]{1,0:T(8,128)S(1)}, f32[8,2048]{1,0:T(8,128)S(1)}, u32[]{:S(2)}, u32[]{:S(2)}) %collective-permute-start) | collective-permute-done | bytes 65568 | tf_op jit(solution)/shard_map/ppermute | solution.py:480
  36.3 0.6 %fusion = f32[8,2048]{1,0:T(8,128)} fusion(f32[8,2048]{1,0:T(8,128)S(1)} %collective-permute-done, f32[2,8,2048]{2,1,0:T(8,128)S(1)} %lags.1), kind=kLoop, calls=%fused_computation.2 | loop fusion | flops 16384 | bytes 196608 | tf_op jit(solution)/shard_map/add | solution.py:480
  36.9 0.0 copy-start.6
  36.9 8.0 %all-to-all-done.1.home_ref = f32[16,64,128]{2,1,0:T(8,128)S(1)} async-done(((f32[16,64,128]{2,1,0:T(8,128)}), f32[16,64,128]{2,1,0:T(8,128)S(1)}, u32[]{:S(2)}, u32[]{:S(2)}) %all-to-all-start.1) | async-done | bytes 524320 | tf_op jit(solution)/shard_map/all_to_all | solution.py:429
  44.9 0.0 copy-done.1
  44.9 0.0 copy-done.2
  44.9 0.0 copy-done.3
  44.9 0.0 copy-done
  44.9 0.0 copy-done.6
  44.9 1.1 %outputs.1 = (f32[2,256,128]{2,1,0:T(8,128)}, f32[2,256,128]{2,1,0:T(8,128)}, f32[2,256,128]{2,1,0:T(8,128)}, f32[2,256,128]{2,1,0:T(8,128)}) custom-call(f32[2,256,128]{2,1,0:T(8,128)S(1)} %copy-done, f32[2,256,128]{2,1,0:T(8,128)S(1)} %copy-done.1, f32[2,256,128]{2,1,0:T(8,128)S(1)} %copy-done.2, f32[2,256,128]{2,1,0:T(8,128)S(1)} %copy-done.3, ...), custom_call_target="tpu_custom_call" | custom-call | flops 402653184 | bytes 524288 | tf_op jit(solution)/shard_map/outputs/pallas_call | solution.py:415
  (1 shorter events, 0.0 us)
Async XLA Ops:
  2.8 8.1 %copy-start.4 = (bf16[768,256]{1,0:T(8,128)(2,1)S(1)}, bf16[768,256]{1,0:T(8,128)(2,1)}, u32[]{:S(2)}) copy-start(bf16[768,256]{1,0:T(8,128)(2,1)} %constant.5.clone.matrix_ref) | copy-start | bytes 1179652
  2.9 8.1 %copy-start.5 = (f32[64,256]{1,0:T(8,128)S(1)}, f32[64,256]{1,0:T(8,128)}, u32[]{:S(2)}) copy-start(f32[64,256]{1,0:T(8,128)} %constant.4.clone.twist_ref) | copy-start | bytes 196612
  2.9 8.1 %copy-start.7 = (f32[8,4096]{1,0:T(8,128)S(1)}, f32[8,4096]{1,0:T(8,128)}, u32[]{:S(2)}) copy-start(f32[8,4096]{1,0:T(8,128)} %filter_ref.1) | copy-start | bytes 393220
  2.9 21.5 %all-to-all-start = ((f32[16,64,128]{2,1,0:T(8,128)}), f32[16,64,128]{2,1,0:T(8,128)S(1)}, u32[]{:S(2)}, u32[]{:S(2)}) async-start(f32[16,64,128]{2,1,0:T(8,128)} %gate.1), calls=%async_computation | async-start | bytes 1048576 | tf_op jit(solution)/shard_map/all_to_all | solution.py:429
  26.8 18.1 %all-to-all-start.1 = ((f32[16,64,128]{2,1,0:T(8,128)}), f32[16,64,128]{2,1,0:T(8,128)S(1)}, u32[]{:S(2)}, u32[]{:S(2)}) async-start(f32[16,64,128]{2,1,0:T(8,128)} %get-tuple-element.12), calls=%async_computation.1 | async-start | bytes 1048576 | tf_op jit(solution)/shard_map/all_to_all | solution.py:429
  31.4 13.5 %copy-start.1 = (f32[2,256,128]{2,1,0:T(8,128)S(1)}, f32[2,256,128]{2,1,0:T(8,128)}, u32[]{:S(2)}) copy-start(f32[2,256,128]{2,1,0:T(8,128)} %key_ref.1) | copy-start | bytes 786436
  31.4 13.5 %copy-start.2 = (f32[2,256,128]{2,1,0:T(8,128)S(1)}, f32[2,256,128]{2,1,0:T(8,128)}, u32[]{:S(2)}) copy-start(f32[2,256,128]{2,1,0:T(8,128)} %value_ref.1) | copy-start | bytes 786436
  31.4 13.5 %copy-start.3 = (f32[2,256,128]{2,1,0:T(8,128)S(1)}, f32[2,256,128]{2,1,0:T(8,128)}, u32[]{:S(2)}) copy-start(f32[2,256,128]{2,1,0:T(8,128)} %cotangent_ref.1) | copy-start | bytes 786436
  31.9 13.0 %copy-start = (f32[2,256,128]{2,1,0:T(8,128)S(1)}, f32[2,256,128]{2,1,0:T(8,128)}, u32[]{:S(2)}) copy-start(f32[2,256,128]{2,1,0:T(8,128)} %query_ref.1) | copy-start | bytes 786436
  32.0 4.3 %collective-permute-start = (f32[8,2048]{1,0:T(8,128)S(1)}, f32[8,2048]{1,0:T(8,128)S(1)}, u32[]{:S(2)}, u32[]{:S(2)}) collective-permute-start(f32[8,2048]{1,0:T(8,128)S(1)} %slice_bitcast_fusion), channel_id=1, source_target_pairs={{0,16},{16,0},{1,17},{17,1},{2,18},{18,2},{3,19},{19,3},{4,20},{20... | collective-permute-start | bytes 196616 | tf_op jit(solution)/shard_map/ppermute | solution.py:480
  36.9 8.0 %copy-start.6 = (f32[128]{0:T(128)S(1)}, f32[128]{0:T(128)}, u32[]{:S(2)}) copy-start(f32[128]{0:T(128)} %param.12) | copy-start | bytes 1540

commit v20 on v17

--- a/solution.py
+++ b/solution.py
@@ -154,7 +154,7 @@
 
 
 def block_rows(kind, sequence, piece, batch, pieces, channels):
-    first = ((kind * batch + sequence) * pieces + piece) * channels
+    first = ((kind * pieces + piece) * batch + sequence) * channels
     return slice(first, first + channels)
 
 
@@ -167,10 +167,9 @@
     def copy(b, i):
         return pltpu.make_async_copy(sources[i].at[b], held.at[i, b], sems.at[i, b])
 
-    def send(kind, b):
-        first = block_rows(kind, b, 0, batch, pieces, channels).start
-        span = pl.ds(first, pieces * channels)
-        return pltpu.make_async_copy(sent.at[:, span], sent_hbm.at[:, span], out_sems.at[kind, b])
+    def send(kind):
+        span = pl.ds(kind * (rows // 2), rows // 2)
+        return pltpu.make_async_copy(sent.at[:, span], sent_hbm.at[:, span], out_sems.at[kind])
 
     parts = [(kind, b) for kind in range(2) for b in range(batch)]
     for kind, b in parts:
@@ -185,9 +184,10 @@
             at = block_rows(kind, b, piece, batch, pieces, channels)
             for place, shard in enumerate(order):
                 sent[place, at] = columns[shard, :, piece * lanes : (piece + 1) * lanes]
-        send(kind, b).start()
-    for kind, b in parts:
-        send(kind, b).wait()
+        if b == batch - 1:
+            send(kind).start()
+    for kind in range(2):
+        send(kind).wait()
 
 
 def transforms(twist_ref, matrix_ref, middle, turned):
@@ -226,7 +226,7 @@
             x = turned[places(chunk)].reshape(-1, width)
             spec[places(chunk)] = lane_dft(x, matrix_ref[...]).reshape(-1, channels, width)
 
-    def inverse(left, right, conjugate_left, emit):
+    def inverse(left, right, conjugate_left, emit, pieces=1):
         def along_lanes(chunk):
             part = places(chunk)
             lr, li = left[part, :, :lanes], left[part, :, lanes:]
@@ -253,7 +253,7 @@
             along_lanes(chunk)
             along_rows(before)
         along_rows(chunks[-1])
-        for r in range(second):
+        for r in sorted(range(second), key=lambda r: r % pieces):
             values = small_dft([fetch(p * second + r) for p in range(first)])
             for t, value in enumerate(values):
                 n1 = r + second * t
@@ -306,9 +306,25 @@
         transforms(twist_ref, matrix_ref, middles.at[kind], turneds.at[kind]) for kind in range(2)
     ]
 
-    def send(kind):
-        span = pl.ds(kind * half, half)
-        return pltpu.make_async_copy(back.at[:, span], back_hbm.at[:, span], out_sems.at[kind])
+    pieces = count // 2 // len(order)
+    share = half // pieces
+
+    def send(kind, piece):
+        span = pl.ds(kind * half + piece * share, share)
+        return pltpu.make_async_copy(
+            back.at[:, span], back_hbm.at[:, span], out_sems.at[kind, piece]
+        )
+
+    def sending(kind, emit):
+        left = [len(order)] * pieces
+
+        def emit_and_send(n1, value):
+            emit(n1, value)
+            left[n1 % pieces] -= 1
+            if left[n1 % pieces] == 0:
+                send(kind, n1 % pieces).start()
+
+        return emit_and_send
 
     for pair in range(pairs):
         for kind in range(2):
@@ -316,11 +332,12 @@
             scratch[kind][0](load, kinds[kind].at[pair])
         for kind in range(2):
             _, emit = token_blocks(back, order, kind, pair, 2 * pairs, channels, count // 2)
-            scratch[kind][1](filter_ref, kinds[kind].at[pair], kind == 1, emit)
             if pair == pairs - 1:
-                send(kind).start()
+                emit = sending(kind, emit)
+            scratch[kind][1](filter_ref, kinds[kind].at[pair], kind == 1, emit, pieces)
     for kind in range(2):
-        send(kind).wait()
+        for piece in range(pieces):
+            send(kind, piece).wait()
 
 
 def lag_kernel(scaling, mixed_ref, upstream_ref, twist_ref, matrix_ref, lag_ref, middle, turned):
@@ -423,7 +440,7 @@
             pltpu.VMEM((4, batch, tokens, all_channels), jnp.float32),
             pltpu.VMEM((shards, rows, lanes), jnp.float32),
             pltpu.SemaphoreType.DMA((4, batch)),
-            pltpu.SemaphoreType.DMA((2, batch)),
+            pltpu.SemaphoreType.DMA((2,)),
         ],
         *(
             pltpu.with_memory_space_constraint(x, pltpu.HBM)
@@ -443,7 +460,7 @@
             pltpu.VMEM((shards, rows, lanes), jnp.float32),
             pltpu.VMEM((2, count, channels, 2 * lanes), jnp.float32),
             pltpu.VMEM((2, count, channels, 2 * lanes), jnp.float32),
-            pltpu.SemaphoreType.DMA((2,)),
+            pltpu.SemaphoreType.DMA((2, tokens // lanes)),
         ],
         held, filter_spec, twist, matrix,
         out_specs=(anywhere, in_vmem, in_vmem),

time: 46.4 us -> 46.4 us (level)
  no operation moved by 1% of the time
where the time goes in v20:
time: 46.4 us; the launch traced here: 46 us
  waiting for transfers between devices  23.7 us (51%)
  starting transfers between devices  14.3 us (31%)
  Pallas kernels  6.56 us (14%)
  between operations  0.76 us (2%)
  other arithmetic  0.64 us (1%)
    all_to_all x2, waiting for transfers between devices, exchange(): lax.all_to_all(blocks, 'seq', split_axis=0, concat_axis=0, tiled=True, ax...  20.9 us
    all_to_all x2, starting transfers between devices, exchange(): lax.all_to_all(blocks, 'seq', split_axis=0, concat_axis=0, tiled=True, ax...  12.7 us
    pallas_call x5, Pallas kernels, call(): pl.pallas_call(kernel, out_shape=out_shape, scratch_shapes=scratch, compi...  6.56 us
    ppermute x1, waiting for transfers between devices, per_device(): filter_grad = filter_grad + lax.ppermute(lag[step], 'batch', pairs)  2.78 us
    ppermute x1, starting transfers between devices, per_device(): filter_grad = filter_grad + lax.ppermute(lag[step], 'batch', pairs)  1.55 us
  transfers between devices with their start and end apart: 3, of which 3 were waited for; matrix products, arithmetic and copies ran while one was open for 1% of the time, Pallas kernels for 2%

profile of v20, /device:TPU:0, one launch (start us, length us, event | category | flops | bytes accessed | tf_op | source)
XLA Modules:
  0.0 46.0 jit_solution(17504934215083026712)
XLA Ops:
  0.6 2.2 %gate.1 = f32[16,64,128]{2,1,0:T(8,128)} custom-call(f32[2,256,128]{2,1,0:T(8,128)} %query_ref.1, f32[2,256,128]{2,1,0:T(8,128)} %key_ref.1, f32[2,256,128]{2,1,0:T(8,128)} %value_ref.1, f32[2,256,128]{2,1,0:T(8,128)} %cotangent_ref.1), custom_call_target="tpu_custom_call" | custom-call | flops 201326592 | bytes 262144 | tf_op jit(solution)/shard_map/gate/pallas_call | solution.py:412
  2.9 0.0 copy-start.4
  2.9 0.0 copy-start.5
  2.9 0.0 copy-start.7
  2.9 8.0 %all-to-all-start = ((f32[16,64,128]{2,1,0:T(8,128)}), f32[16,64,128]{2,1,0:T(8,128)S(1)}, u32[]{:S(2)}, u32[]{:S(2)}) async-start(f32[16,64,128]{2,1,0:T(8,128)} %gate.1), calls=%async_computation | async-start | bytes 1048576 | tf_op jit(solution)/shard_map/all_to_all | solution.py:426
  10.9 0.0 copy-done.4
  10.9 0.0 copy-done.5
  10.9 0.0 copy-done.7
  11.0 0.5 %filter.1.filter_ref = f32[64,8,256]{2,1,0:T(8,128)S(1)} custom-call(f32[8,4096]{1,0:T(8,128)S(1)} %copy-done.7, f32[64,256]{1,0:T(8,128)S(1)} %copy-done.5, bf16[768,256]{1,0:T(8,128)(2,1)S(1)} %copy-done.4), custom_call_target="tpu_custom_call" | custom-call | flops 402653184 | bytes 524288 | tf_op jit(solution)/shard_map/filter/pallas_call | solution.py:412
  11.4 13.0 %all-to-all-done.held_ref = f32[16,64,128]{2,1,0:T(8,128)S(1)} async-done(((f32[16,64,128]{2,1,0:T(8,128)}), f32[16,64,128]{2,1,0:T(8,128)S(1)}, u32[]{:S(2)}, u32[]{:S(2)}) %all-to-all-start) | async-done | bytes 524320 | tf_op jit(solution)/shard_map/all_to_all | solution.py:426
  24.4 2.3 %convolve.1 = (f32[16,64,128]{2,1,0:T(8,128)}, f32[1,64,8,256]{3,2,1,0:T(8,128)S(1)}, f32[1,64,8,256]{3,2,1,0:T(8,128)S(1)}) custom-call(f32[16,64,128]{2,1,0:T(8,128)S(1)} %all-to-all-done.held_ref, f32[64,8,256]{2,1,0:T(8,128)S(1)} %filter.1.filter_ref, f32[64,256]{1,0:T(8,128)S(1)} %copy-done.5, bf16[768,256]{1,0:T(8,128)(2,1)S(1)} %copy-done.4), custom_call_target="tpu_custom_call" | custom-call | flops 1610612736 | bytes 2097152 | tf_op jit(solution)/shard_map/convolve/pallas_call | solution.py:412
  26.7 4.7 %all-to-all-start.1 = ((f32[16,64,128]{2,1,0:T(8,128)}), f32[16,64,128]{2,1,0:T(8,128)S(1)}, u32[]{:S(2)}, u32[]{:S(2)}) async-start(f32[16,64,128]{2,1,0:T(8,128)} %get-tuple-element.12), calls=%async_computation.1 | async-start | bytes 1048576 | tf_op jit(solution)/shard_map/all_to_all | solution.py:426
  31.3 0.0 copy-start.1
  31.3 0.0 copy-start.2
  31.4 0.0 copy-start.3
  31.4 0.5 %lags.1 = f32[2,8,2048]{2,1,0:T(8,128)S(1)} custom-call(f32[1,64,8,256]{3,2,1,0:T(8,128)S(1)} %get-tuple-element.17.mixed_ref, f32[1,64,8,256]{3,2,1,0:T(8,128)S(1)} %get-tuple-element.18.upstream_ref, f32[64,256]{1,0:T(8,128)S(1)} %copy-done.5, bf16[768,256]{1,0:T(8,128)(2,1)S(1)} %copy-done.4), custom_call_target="tpu_custom_call" | custom-call | flops 402653184 | bytes 524288 | tf_op jit(solution)/shard_map/lags/pallas_call | solution.py:412
  31.8 0.0 copy-start
  31.9 1.6 %collective-permute-start = (f32[8,2048]{1,0:T(8,128)S(1)}, f32[8,2048]{1,0:T(8,128)S(1)}, u32[]{:S(2)}, u32[]{:S(2)}) collective-permute-start(f32[8,2048]{1,0:T(8,128)S(1)} %slice_bitcast_fusion), channel_id=1, source_target_pairs={{0,16},{16,0},{1,17},{17,1},{2,18},{18,2},{3,19},{19,3},{4,20},{20... | collective-permute-start | bytes 196616 | tf_op jit(solution)/shard_map/ppermute | solution.py:477
  33.4 2.8 %collective-permute-done = f32[8,2048]{1,0:T(8,128)S(1)} collective-permute-done((f32[8,2048]{1,0:T(8,128)S(1)}, f32[8,2048]{1,0:T(8,128)S(1)}, u32[]{:S(2)}, u32[]{:S(2)}) %collective-permute-start) | collective-permute-done | bytes 65568 | tf_op jit(solution)/shard_map/ppermute | solution.py:477
  36.2 0.6 %fusion = f32[8,2048]{1,0:T(8,128)} fusion(f32[8,2048]{1,0:T(8,128)S(1)} %collective-permute-done, f32[2,8,2048]{2,1,0:T(8,128)S(1)} %lags.1), kind=kLoop, calls=%fused_computation.2 | loop fusion | flops 16384 | bytes 196608 | tf_op jit(solution)/shard_map/add | solution.py:477
  36.8 0.0 copy-start.6
  36.8 8.0 %all-to-all-done.1.home_ref = f32[16,64,128]{2,1,0:T(8,128)S(1)} async-done(((f32[16,64,128]{2,1,0:T(8,128)}), f32[16,64,128]{2,1,0:T(8,128)S(1)}, u32[]{:S(2)}, u32[]{:S(2)}) %all-to-all-start.1) | async-done | bytes 524320 | tf_op jit(solution)/shard_map/all_to_all | solution.py:426
  44.8 0.0 copy-done.1
  44.8 0.0 copy-done.2
  44.8 0.0 copy-done.3
  44.8 0.0 copy-done
  44.8 0.0 copy-done.6
  44.8 1.1 %outputs.1 = (f32[2,256,128]{2,1,0:T(8,128)}, f32[2,256,128]{2,1,0:T(8,128)}, f32[2,256,128]{2,1,0:T(8,128)}, f32[2,256,128]{2,1,0:T(8,128)}) custom-call(f32[2,256,128]{2,1,0:T(8,128)S(1)} %copy-done, f32[2,256,128]{2,1,0:T(8,128)S(1)} %copy-done.1, f32[2,256,128]{2,1,0:T(8,128)S(1)} %copy-done.2, f32[2,256,128]{2,1,0:T(8,128)S(1)} %copy-done.3, ...), custom_call_target="tpu_custom_call" | custom-call | flops 402653184 | bytes 524288 | tf_op jit(solution)/shard_map/outputs/pallas_call | solution.py:412
  (1 shorter events, 0.0 us)
Async XLA Ops:
  2.9 8.1 %copy-start.4 = (bf16[768,256]{1,0:T(8,128)(2,1)S(1)}, bf16[768,256]{1,0:T(8,128)(2,1)}, u32[]{:S(2)}) copy-start(bf16[768,256]{1,0:T(8,128)(2,1)} %constant.5.clone.matrix_ref) | copy-start | bytes 1179652
  2.9 8.1 %copy-start.5 = (f32[64,256]{1,0:T(8,128)S(1)}, f32[64,256]{1,0:T(8,128)}, u32[]{:S(2)}) copy-start(f32[64,256]{1,0:T(8,128)} %constant.4.clone.twist_ref) | copy-start | bytes 196612
  2.9 8.1 %copy-start.7 = (f32[8,4096]{1,0:T(8,128)S(1)}, f32[8,4096]{1,0:T(8,128)}, u32[]{:S(2)}) copy-start(f32[8,4096]{1,0:T(8,128)} %filter_ref.1) | copy-start | bytes 393220
  2.9 21.5 %all-to-all-start = ((f32[16,64,128]{2,1,0:T(8,128)}), f32[16,64,128]{2,1,0:T(8,128)S(1)}, u32[]{:S(2)}, u32[]{:S(2)}) async-start(f32[16,64,128]{2,1,0:T(8,128)} %gate.1), calls=%async_computation | async-start | bytes 1048576 | tf_op jit(solution)/shard_map/all_to_all | solution.py:426
  26.7 18.1 %all-to-all-start.1 = ((f32[16,64,128]{2,1,0:T(8,128)}), f32[16,64,128]{2,1,0:T(8,128)S(1)}, u32[]{:S(2)}, u32[]{:S(2)}) async-start(f32[16,64,128]{2,1,0:T(8,128)} %get-tuple-element.12), calls=%async_computation.1 | async-start | bytes 1048576 | tf_op jit(solution)/shard_map/all_to_all | solution.py:426
  31.3 13.5 %copy-start.1 = (f32[2,256,128]{2,1,0:T(8,128)S(1)}, f32[2,256,128]{2,1,0:T(8,128)}, u32[]{:S(2)}) copy-start(f32[2,256,128]{2,1,0:T(8,128)} %key_ref.1) | copy-start | bytes 786436
  31.3 13.5 %copy-start.2 = (f32[2,256,128]{2,1,0:T(8,128)S(1)}, f32[2,256,128]{2,1,0:T(8,128)}, u32[]{:S(2)}) copy-start(f32[2,256,128]{2,1,0:T(8,128)} %value_ref.1) | copy-start | bytes 786436
  31.4 13.5 %copy-start.3 = (f32[2,256,128]{2,1,0:T(8,128)S(1)}, f32[2,256,128]{2,1,0:T(8,128)}, u32[]{:S(2)}) copy-start(f32[2,256,128]{2,1,0:T(8,128)} %cotangent_ref.1) | copy-start | bytes 786436
  31.8 13.0 %copy-start = (f32[2,256,128]{2,1,0:T(8,128)S(1)}, f32[2,256,128]{2,1,0:T(8,128)}, u32[]{:S(2)}) copy-start(f32[2,256,128]{2,1,0:T(8,128)} %query_ref.1) | copy-start | bytes 786436
  31.9 4.3 %collective-permute-start = (f32[8,2048]{1,0:T(8,128)S(1)}, f32[8,2048]{1,0:T(8,128)S(1)}, u32[]{:S(2)}, u32[]{:S(2)}) collective-permute-start(f32[8,2048]{1,0:T(8,128)S(1)} %slice_bitcast_fusion), channel_id=1, source_target_pairs={{0,16},{16,0},{1,17},{17,1},{2,18},{18,2},{3,19},{19,3},{4,20},{20... | collective-permute-start | bytes 196616 | tf_op jit(solution)/shard_map/ppermute | solution.py:477
  36.8 8.0 %copy-start.6 = (f32[128]{0:T(128)S(1)}, f32[128]{0:T(128)}, u32[]{:S(2)}) copy-start(f32[128]{0:T(128)} %param.12) | copy-start | bytes 1540

commit v21 on v17

--- a/solution.py
+++ b/solution.py
@@ -109,15 +109,18 @@
     matrix = np.block([[c, s], [-s, c]]).astype(np.float32)
     high = matrix.astype(ml_dtypes.bfloat16)
     low = (matrix - high.astype(np.float32)).astype(ml_dtypes.bfloat16)
-    return twist, np.concatenate([high, high, low], axis=0)
+    return twist, np.concatenate([high, low], axis=0)
 
 
 def lane_dft(x, matrix):
     high = x.astype(jnp.bfloat16)
     low = (x - high.astype(jnp.float32)).astype(jnp.bfloat16)
-    return jnp.dot(
-        jnp.concatenate([high, low, high], axis=1), matrix, preferred_element_type=jnp.float32
-    )
+    width = x.shape[1]
+
+    def times(part, rows):
+        return jnp.dot(part, rows, preferred_element_type=jnp.float32)
+
+    return times(high, matrix[:width]) + times(high, matrix[width:]) + times(low, matrix[:width])
 
 
 def exchange_order(shards):

time: 46.4 us -> 46.4 us (level)
  no operation moved by 1% of the time
where the time goes in v21:
time: 46.4 us; the launch traced here: 46 us
  waiting for transfers between devices  23.7 us (51%)
  starting transfers between devices  14.2 us (31%)
  Pallas kernels  6.59 us (14%)
  between operations  0.77 us (2%)
  other arithmetic  0.64 us (1%)
    all_to_all x2, waiting for transfers between devices, exchange(): lax.all_to_all(blocks, 'seq', split_axis=0, concat_axis=0, tiled=True, ax...  20.9 us
    all_to_all x2, starting transfers between devices, exchange(): lax.all_to_all(blocks, 'seq', split_axis=0, concat_axis=0, tiled=True, ax...  12.7 us
    pallas_call x5, Pallas kernels, call(): pl.pallas_call(kernel, out_shape=out_shape, scratch_shapes=scratch, compi...  6.59 us
    ppermute x1, waiting for transfers between devices, per_device(): filter_grad = filter_grad + lax.ppermute(lag[step], 'batch', pairs)  2.78 us
    ppermute x1, starting transfers between devices, per_device(): filter_grad = filter_grad + lax.ppermute(lag[step], 'batch', pairs)  1.55 us
  transfers between devices with their start and end apart: 3, of which 3 were waited for; matrix products, arithmetic and copies ran while one was open for 1% of the time, Pallas kernels for 2%

profile of v21, /device:TPU:0, one launch (start us, length us, event | category | flops | bytes accessed | tf_op | source)
XLA Modules:
  0.0 46.0 jit_solution(4493884136643529446)
XLA Ops:
  0.6 2.2 %gate.1 = f32[16,64,128]{2,1,0:T(8,128)} custom-call(f32[2,256,128]{2,1,0:T(8,128)} %query_ref.1, f32[2,256,128]{2,1,0:T(8,128)} %key_ref.1, f32[2,256,128]{2,1,0:T(8,128)} %value_ref.1, f32[2,256,128]{2,1,0:T(8,128)} %cotangent_ref.1), custom_call_target="tpu_custom_call" | custom-call | flops 201326592 | bytes 262144 | tf_op jit(solution)/shard_map/gate/pallas_call | solution.py:398
  2.8 0.0 copy-start.4
  2.9 0.0 copy-start.5
  2.9 0.0 copy-start.7
  2.9 8.0 %all-to-all-start = ((f32[16,64,128]{2,1,0:T(8,128)}), f32[16,64,128]{2,1,0:T(8,128)S(1)}, u32[]{:S(2)}, u32[]{:S(2)}) async-start(f32[16,64,128]{2,1,0:T(8,128)} %gate.1), calls=%async_computation | async-start | bytes 1048576 | tf_op jit(solution)/shard_map/all_to_all | solution.py:412
  10.9 0.0 copy-done.4
  10.9 0.0 copy-done.5
  10.9 0.0 copy-done.7
  10.9 0.5 %filter.1.filter_ref = f32[64,8,256]{2,1,0:T(8,128)S(1)} custom-call(f32[8,4096]{1,0:T(8,128)S(1)} %copy-done.7, f32[64,256]{1,0:T(8,128)S(1)} %copy-done.5, bf16[512,256]{1,0:T(8,128)(2,1)S(1)} %copy-done.4), custom_call_target="tpu_custom_call" | custom-call | flops 402653184 | bytes 524288 | tf_op jit(solution)/shard_map/filter/pallas_call | solution.py:398
  11.4 13.0 %all-to-all-done.held_ref = f32[16,64,128]{2,1,0:T(8,128)S(1)} async-done(((f32[16,64,128]{2,1,0:T(8,128)}), f32[16,64,128]{2,1,0:T(8,128)S(1)}, u32[]{:S(2)}, u32[]{:S(2)}) %all-to-all-start) | async-done | bytes 524320 | tf_op jit(solution)/shard_map/all_to_all | solution.py:412
  24.4 2.3 %convolve.1 = (f32[16,64,128]{2,1,0:T(8,128)}, f32[1,64,8,256]{3,2,1,0:T(8,128)S(1)}, f32[1,64,8,256]{3,2,1,0:T(8,128)S(1)}) custom-call(f32[16,64,128]{2,1,0:T(8,128)S(1)} %all-to-all-done.held_ref, f32[64,8,256]{2,1,0:T(8,128)S(1)} %filter.1.filter_ref, f32[64,256]{1,0:T(8,128)S(1)} %copy-done.5, bf16[512,256]{1,0:T(8,128)(2,1)S(1)} %copy-done.4), custom_call_target="tpu_custom_call" | custom-call | flops 1610612736 | bytes 2097152 | tf_op jit(solution)/shard_map/convolve/pallas_call | solution.py:398
  26.7 4.7 %all-to-all-start.1 = ((f32[16,64,128]{2,1,0:T(8,128)}), f32[16,64,128]{2,1,0:T(8,128)S(1)}, u32[]{:S(2)}, u32[]{:S(2)}) async-start(f32[16,64,128]{2,1,0:T(8,128)} %get-tuple-element.12), calls=%async_computation.1 | async-start | bytes 1048576 | tf_op jit(solution)/shard_map/all_to_all | solution.py:412
  31.4 0.0 copy-start.1
  31.4 0.0 copy-start.2
  31.4 0.0 copy-start.3
  31.4 0.5 %lags.1 = f32[2,8,2048]{2,1,0:T(8,128)S(1)} custom-call(f32[1,64,8,256]{3,2,1,0:T(8,128)S(1)} %get-tuple-element.17.mixed_ref, f32[1,64,8,256]{3,2,1,0:T(8,128)S(1)} %get-tuple-element.18.upstream_ref, f32[64,256]{1,0:T(8,128)S(1)} %copy-done.5, bf16[512,256]{1,0:T(8,128)(2,1)S(1)} %copy-done.4), custom_call_target="tpu_custom_call" | custom-call | flops 402653184 | bytes 524288 | tf_op jit(solution)/shard_map/lags/pallas_call | solution.py:398
  31.9 0.0 copy-start
  31.9 1.5 %collective-permute-start = (f32[8,2048]{1,0:T(8,128)S(1)}, f32[8,2048]{1,0:T(8,128)S(1)}, u32[]{:S(2)}, u32[]{:S(2)}) collective-permute-start(f32[8,2048]{1,0:T(8,128)S(1)} %slice_bitcast_fusion), channel_id=1, source_target_pairs={{0,16},{16,0},{1,17},{17,1},{2,18},{18,2},{3,19},{19,3},{4,20},{20... | collective-permute-start | bytes 196616 | tf_op jit(solution)/shard_map/ppermute | solution.py:463
  33.4 2.8 %collective-permute-done = f32[8,2048]{1,0:T(8,128)S(1)} collective-permute-done((f32[8,2048]{1,0:T(8,128)S(1)}, f32[8,2048]{1,0:T(8,128)S(1)}, u32[]{:S(2)}, u32[]{:S(2)}) %collective-permute-start) | collective-permute-done | bytes 65568 | tf_op jit(solution)/shard_map/ppermute | solution.py:463
  36.2 0.6 %fusion = f32[8,2048]{1,0:T(8,128)} fusion(f32[8,2048]{1,0:T(8,128)S(1)} %collective-permute-done, f32[2,8,2048]{2,1,0:T(8,128)S(1)} %lags.1), kind=kLoop, calls=%fused_computation.2 | loop fusion | flops 16384 | bytes 196608 | tf_op jit(solution)/shard_map/add | solution.py:463
  36.9 0.0 copy-start.6
  36.9 8.0 %all-to-all-done.1.home_ref = f32[16,64,128]{2,1,0:T(8,128)S(1)} async-done(((f32[16,64,128]{2,1,0:T(8,128)}), f32[16,64,128]{2,1,0:T(8,128)S(1)}, u32[]{:S(2)}, u32[]{:S(2)}) %all-to-all-start.1) | async-done | bytes 524320 | tf_op jit(solution)/shard_map/all_to_all | solution.py:412
  44.8 0.0 copy-done.1
  44.8 0.0 copy-done.2
  44.8 0.0 copy-done.3
  44.8 0.0 copy-done
  44.8 0.0 copy-done.6
  44.9 1.1 %outputs.1 = (f32[2,256,128]{2,1,0:T(8,128)}, f32[2,256,128]{2,1,0:T(8,128)}, f32[2,256,128]{2,1,0:T(8,128)}, f32[2,256,128]{2,1,0:T(8,128)}) custom-call(f32[2,256,128]{2,1,0:T(8,128)S(1)} %copy-done, f32[2,256,128]{2,1,0:T(8,128)S(1)} %copy-done.1, f32[2,256,128]{2,1,0:T(8,128)S(1)} %copy-done.2, f32[2,256,128]{2,1,0:T(8,128)S(1)} %copy-done.3, ...), custom_call_target="tpu_custom_call" | custom-call | flops 402653184 | bytes 524288 | tf_op jit(solution)/shard_map/outputs/pallas_call | solution.py:398
  (1 shorter events, 0.0 us)
Async XLA Ops:
  2.8 8.1 %copy-start.4 = (bf16[512,256]{1,0:T(8,128)(2,1)S(1)}, bf16[512,256]{1,0:T(8,128)(2,1)}, u32[]{:S(2)}) copy-start(bf16[512,256]{1,0:T(8,128)(2,1)} %constant.5.clone.matrix_ref) | copy-start | bytes 786436
  2.9 8.1 %copy-start.5 = (f32[64,256]{1,0:T(8,128)S(1)}, f32[64,256]{1,0:T(8,128)}, u32[]{:S(2)}) copy-start(f32[64,256]{1,0:T(8,128)} %constant.4.clone.twist_ref) | copy-start | bytes 196612
  2.9 8.1 %copy-start.7 = (f32[8,4096]{1,0:T(8,128)S(1)}, f32[8,4096]{1,0:T(8,128)}, u32[]{:S(2)}) copy-start(f32[8,4096]{1,0:T(8,128)} %filter_ref.1) | copy-start | bytes 393220
  2.9 21.5 %all-to-all-start = ((f32[16,64,128]{2,1,0:T(8,128)}), f32[16,64,128]{2,1,0:T(8,128)S(1)}, u32[]{:S(2)}, u32[]{:S(2)}) async-start(f32[16,64,128]{2,1,0:T(8,128)} %gate.1), calls=%async_computation | async-start | bytes 1048576 | tf_op jit(solution)/shard_map/all_to_all | solution.py:412
  26.7 18.1 %all-to-all-start.1 = ((f32[16,64,128]{2,1,0:T(8,128)}), f32[16,64,128]{2,1,0:T(8,128)S(1)}, u32[]{:S(2)}, u32[]{:S(2)}) async-start(f32[16,64,128]{2,1,0:T(8,128)} %get-tuple-element.12), calls=%async_computation.1 | async-start | bytes 1048576 | tf_op jit(solution)/shard_map/all_to_all | solution.py:412
  31.4 13.5 %copy-start.1 = (f32[2,256,128]{2,1,0:T(8,128)S(1)}, f32[2,256,128]{2,1,0:T(8,128)}, u32[]{:S(2)}) copy-start(f32[2,256,128]{2,1,0:T(8,128)} %key_ref.1) | copy-start | bytes 786436
  31.4 13.5 %copy-start.2 = (f32[2,256,128]{2,1,0:T(8,128)S(1)}, f32[2,256,128]{2,1,0:T(8,128)}, u32[]{:S(2)}) copy-start(f32[2,256,128]{2,1,0:T(8,128)} %value_ref.1) | copy-start | bytes 786436
  31.4 13.5 %copy-start.3 = (f32[2,256,128]{2,1,0:T(8,128)S(1)}, f32[2,256,128]{2,1,0:T(8,128)}, u32[]{:S(2)}) copy-start(f32[2,256,128]{2,1,0:T(8,128)} %cotangent_ref.1) | copy-start | bytes 786436
  31.9 13.0 %copy-start = (f32[2,256,128]{2,1,0:T(8,128)S(1)}, f32[2,256,128]{2,1,0:T(8,128)}, u32[]{:S(2)}) copy-start(f32[2,256,128]{2,1,0:T(8,128)} %query_ref.1) | copy-start | bytes 786436
  31.9 4.3 %collective-permute-start = (f32[8,2048]{1,0:T(8,128)S(1)}, f32[8,2048]{1,0:T(8,128)S(1)}, u32[]{:S(2)}, u32[]{:S(2)}) collective-permute-start(f32[8,2048]{1,0:T(8,128)S(1)} %slice_bitcast_fusion), channel_id=1, source_target_pairs={{0,16},{16,0},{1,17},{17,1},{2,18},{18,2},{3,19},{19,3},{4,20},{20... | collective-permute-start | bytes 196616 | tf_op jit(solution)/shard_map/ppermute | solution.py:463
  36.9 8.0 %copy-start.6 = (f32[128]{0:T(128)S(1)}, f32[128]{0:T(128)}, u32[]{:S(2)}) copy-start(f32[128]{0:T(128)} %param.12) | copy-start | bytes 1540

commit v22 on v17

--- a/solution.py
+++ b/solution.py
@@ -11,7 +11,7 @@
 from jax.sharding import PartitionSpec as P
 
 VMEM_BYTES = 48 * 1024 * 1024
-ROW_CHUNK = 128
+ROW_CHUNK = 64
 
 
 def add(a, b):

time: 46.4 us -> 47.2 us (1.017)
  Pallas kernels: 6.55 us -> 7.85 us
    pallas_call x5, Pallas kernels: 6.55 us -> 7.85 us  [call(): pl.pallas_call(kernel, out_shape=out_shape, scratch_shapes=scratch, compi...]
  transfers between devices with their start and end apart: 3 -> 3, of which waited for: 3 -> 3; matrix products, arithmetic and copies ran while one was open for 1% -> 1% of each run, Pallas kernels for 2% -> 3%
where the time goes in v22:
time: 47.2 us; the launch traced here: 46.8 us
  waiting for transfers between devices  23.3 us (49%)
  starting transfers between devices  14.2 us (30%)
  Pallas kernels  7.85 us (17%)
  between operations  0.76 us (2%)
  other arithmetic  0.64 us (1%)
    all_to_all x2, waiting for transfers between devices, exchange(): lax.all_to_all(blocks, 'seq', split_axis=0, concat_axis=0, tiled=True, ax...  20.5 us
    all_to_all x2, starting transfers between devices, exchange(): lax.all_to_all(blocks, 'seq', split_axis=0, concat_axis=0, tiled=True, ax...  12.7 us
    pallas_call x5, Pallas kernels, call(): pl.pallas_call(kernel, out_shape=out_shape, scratch_shapes=scratch, compi...  7.85 us
    ppermute x1, waiting for transfers between devices, per_device(): filter_grad = filter_grad + lax.ppermute(lag[step], 'batch', pairs)  2.78 us
    ppermute x1, starting transfers between devices, per_device(): filter_grad = filter_grad + lax.ppermute(lag[step], 'batch', pairs)  1.55 us
  transfers between devices with their start and end apart: 3, of which 3 were waited for; matrix products, arithmetic and copies ran while one was open for 1% of the time, Pallas kernels for 3%

profile of v22, /device:TPU:0, one launch (start us, length us, event | category | flops | bytes accessed | tf_op | source)
XLA Modules:
  0.0 46.8 jit_solution(17641693983489530116)
XLA Ops:
  0.6 2.2 %gate.1 = f32[16,64,128]{2,1,0:T(8,128)} custom-call(f32[2,256,128]{2,1,0:T(8,128)} %query_ref.1, f32[2,256,128]{2,1,0:T(8,128)} %key_ref.1, f32[2,256,128]{2,1,0:T(8,128)} %value_ref.1, f32[2,256,128]{2,1,0:T(8,128)} %cotangent_ref.1), custom_call_target="tpu_custom_call" | custom-call | flops 201326592 | bytes 262144 | tf_op jit(solution)/shard_map/gate/pallas_call | solution.py:395
  2.8 0.0 copy-start.4
  2.9 0.0 copy-start.5
  2.9 0.0 copy-start.7
  2.9 8.0 %all-to-all-start = ((f32[16,64,128]{2,1,0:T(8,128)}), f32[16,64,128]{2,1,0:T(8,128)S(1)}, u32[]{:S(2)}, u32[]{:S(2)}) async-start(f32[16,64,128]{2,1,0:T(8,128)} %gate.1), calls=%async_computation | async-start | bytes 1048576 | tf_op jit(solution)/shard_map/all_to_all | solution.py:409
  10.9 0.0 copy-done.4
  10.9 0.0 copy-done.5
  10.9 0.0 copy-done.7
  10.9 0.7 %filter.1.filter_ref = f32[64,8,256]{2,1,0:T(8,128)S(1)} custom-call(f32[8,4096]{1,0:T(8,128)S(1)} %copy-done.7, f32[64,256]{1,0:T(8,128)S(1)} %copy-done.5, bf16[768,256]{1,0:T(8,128)(2,1)S(1)} %copy-done.4), custom_call_target="tpu_custom_call" | custom-call | flops 402653184 | bytes 524288 | tf_op jit(solution)/shard_map/filter/pallas_call | solution.py:395
  11.6 12.8 %all-to-all-done.held_ref = f32[16,64,128]{2,1,0:T(8,128)S(1)} async-done(((f32[16,64,128]{2,1,0:T(8,128)}), f32[16,64,128]{2,1,0:T(8,128)S(1)}, u32[]{:S(2)}, u32[]{:S(2)}) %all-to-all-start) | async-done | bytes 524320 | tf_op jit(solution)/shard_map/all_to_all | solution.py:409
  24.4 3.1 %convolve.1 = (f32[16,64,128]{2,1,0:T(8,128)}, f32[1,64,8,256]{3,2,1,0:T(8,128)S(1)}, f32[1,64,8,256]{3,2,1,0:T(8,128)S(1)}) custom-call(f32[16,64,128]{2,1,0:T(8,128)S(1)} %all-to-all-done.held_ref, f32[64,8,256]{2,1,0:T(8,128)S(1)} %filter.1.filter_ref, f32[64,256]{1,0:T(8,128)S(1)} %copy-done.5, bf16[768,256]{1,0:T(8,128)(2,1)S(1)} %copy-done.4), custom_call_target="tpu_custom_call" | custom-call | flops 1610612736 | bytes 2097152 | tf_op jit(solution)/shard_map/convolve/pallas_call | solution.py:395
  27.5 4.7 %all-to-all-start.1 = ((f32[16,64,128]{2,1,0:T(8,128)}), f32[16,64,128]{2,1,0:T(8,128)S(1)}, u32[]{:S(2)}, u32[]{:S(2)}) async-start(f32[16,64,128]{2,1,0:T(8,128)} %get-tuple-element.12), calls=%async_computation.1 | async-start | bytes 1048576 | tf_op jit(solution)/shard_map/all_to_all | solution.py:409
  32.2 0.0 copy-start.1
  32.2 0.0 copy-start.2
  32.2 0.0 copy-start.3
  32.2 0.7 %lags.1 = f32[2,8,2048]{2,1,0:T(8,128)S(1)} custom-call(f32[1,64,8,256]{3,2,1,0:T(8,128)S(1)} %get-tuple-element.17.mixed_ref, f32[1,64,8,256]{3,2,1,0:T(8,128)S(1)} %get-tuple-element.18.upstream_ref, f32[64,256]{1,0:T(8,128)S(1)} %copy-done.5, bf16[768,256]{1,0:T(8,128)(2,1)S(1)} %copy-done.4), custom_call_target="tpu_custom_call" | custom-call | flops 402653184 | bytes 524288 | tf_op jit(solution)/shard_map/lags/pallas_call | solution.py:395
  32.9 0.0 copy-start
  33.0 1.6 %collective-permute-start = (f32[8,2048]{1,0:T(8,128)S(1)}, f32[8,2048]{1,0:T(8,128)S(1)}, u32[]{:S(2)}, u32[]{:S(2)}) collective-permute-start(f32[8,2048]{1,0:T(8,128)S(1)} %slice_bitcast_fusion), channel_id=1, source_target_pairs={{0,16},{16,0},{1,17},{17,1},{2,18},{18,2},{3,19},{19,3},{4,20},{20... | collective-permute-start | bytes 196616 | tf_op jit(solution)/shard_map/ppermute | solution.py:460
  34.5 2.8 %collective-permute-done = f32[8,2048]{1,0:T(8,128)S(1)} collective-permute-done((f32[8,2048]{1,0:T(8,128)S(1)}, f32[8,2048]{1,0:T(8,128)S(1)}, u32[]{:S(2)}, u32[]{:S(2)}) %collective-permute-start) | collective-permute-done | bytes 65568 | tf_op jit(solution)/shard_map/ppermute | solution.py:460
  37.3 0.6 %fusion = f32[8,2048]{1,0:T(8,128)} fusion(f32[8,2048]{1,0:T(8,128)S(1)} %collective-permute-done, f32[2,8,2048]{2,1,0:T(8,128)S(1)} %lags.1), kind=kLoop, calls=%fused_computation.2 | loop fusion | flops 16384 | bytes 196608 | tf_op jit(solution)/shard_map/add | solution.py:460
  37.9 0.0 copy-start.6
  37.9 7.7 %all-to-all-done.1.home_ref = f32[16,64,128]{2,1,0:T(8,128)S(1)} async-done(((f32[16,64,128]{2,1,0:T(8,128)}), f32[16,64,128]{2,1,0:T(8,128)S(1)}, u32[]{:S(2)}, u32[]{:S(2)}) %all-to-all-start.1) | async-done | bytes 524320 | tf_op jit(solution)/shard_map/all_to_all | solution.py:409
  45.7 0.0 copy-done.1
  45.7 0.0 copy-done.2
  45.7 0.0 copy-done.3
  45.7 0.0 copy-done
  45.7 0.0 copy-done.6
  45.7 1.1 %outputs.1 = (f32[2,256,128]{2,1,0:T(8,128)}, f32[2,256,128]{2,1,0:T(8,128)}, f32[2,256,128]{2,1,0:T(8,128)}, f32[2,256,128]{2,1,0:T(8,128)}) custom-call(f32[2,256,128]{2,1,0:T(8,128)S(1)} %copy-done, f32[2,256,128]{2,1,0:T(8,128)S(1)} %copy-done.1, f32[2,256,128]{2,1,0:T(8,128)S(1)} %copy-done.2, f32[2,256,128]{2,1,0:T(8,128)S(1)} %copy-done.3, ...), custom_call_target="tpu_custom_call" | custom-call | flops 402653184 | bytes 524288 | tf_op jit(solution)/shard_map/outputs/pallas_call | solution.py:395
  (1 shorter events, 0.0 us)
Async XLA Ops:
  2.8 8.1 %copy-start.4 = (bf16[768,256]{1,0:T(8,128)(2,1)S(1)}, bf16[768,256]{1,0:T(8,128)(2,1)}, u32[]{:S(2)}) copy-start(bf16[768,256]{1,0:T(8,128)(2,1)} %constant.5.clone.matrix_ref) | copy-start | bytes 1179652
  2.9 8.1 %copy-start.5 = (f32[64,256]{1,0:T(8,128)S(1)}, f32[64,256]{1,0:T(8,128)}, u32[]{:S(2)}) copy-start(f32[64,256]{1,0:T(8,128)} %constant.4.clone.twist_ref) | copy-start | bytes 196612
  2.9 8.1 %copy-start.7 = (f32[8,4096]{1,0:T(8,128)S(1)}, f32[8,4096]{1,0:T(8,128)}, u32[]{:S(2)}) copy-start(f32[8,4096]{1,0:T(8,128)} %filter_ref.1) | copy-start | bytes 393220
  2.9 21.5 %all-to-all-start = ((f32[16,64,128]{2,1,0:T(8,128)}), f32[16,64,128]{2,1,0:T(8,128)S(1)}, u32[]{:S(2)}, u32[]{:S(2)}) async-start(f32[16,64,128]{2,1,0:T(8,128)} %gate.1), calls=%async_computation | async-start | bytes 1048576 | tf_op jit(solution)/shard_map/all_to_all | solution.py:409
  27.5 18.1 %all-to-all-start.1 = ((f32[16,64,128]{2,1,0:T(8,128)}), f32[16,64,128]{2,1,0:T(8,128)S(1)}, u32[]{:S(2)}, u32[]{:S(2)}) async-start(f32[16,64,128]{2,1,0:T(8,128)} %get-tuple-element.12), calls=%async_computation.1 | async-start | bytes 1048576 | tf_op jit(solution)/shard_map/all_to_all | solution.py:409
  32.2 13.5 %copy-start.1 = (f32[2,256,128]{2,1,0:T(8,128)S(1)}, f32[2,256,128]{2,1,0:T(8,128)}, u32[]{:S(2)}) copy-start(f32[2,256,128]{2,1,0:T(8,128)} %key_ref.1) | copy-start | bytes 786436
  32.2 13.5 %copy-start.2 = (f32[2,256,128]{2,1,0:T(8,128)S(1)}, f32[2,256,128]{2,1,0:T(8,128)}, u32[]{:S(2)}) copy-start(f32[2,256,128]{2,1,0:T(8,128)} %value_ref.1) | copy-start | bytes 786436
  32.2 13.5 %copy-start.3 = (f32[2,256,128]{2,1,0:T(8,128)S(1)}, f32[2,256,128]{2,1,0:T(8,128)}, u32[]{:S(2)}) copy-start(f32[2,256,128]{2,1,0:T(8,128)} %cotangent_ref.1) | copy-start | bytes 786436
  32.9 12.7 %copy-start = (f32[2,256,128]{2,1,0:T(8,128)S(1)}, f32[2,256,128]{2,1,0:T(8,128)}, u32[]{:S(2)}) copy-start(f32[2,256,128]{2,1,0:T(8,128)} %query_ref.1) | copy-start | bytes 786436
  33.0 4.3 %collective-permute-start = (f32[8,2048]{1,0:T(8,128)S(1)}, f32[8,2048]{1,0:T(8,128)S(1)}, u32[]{:S(2)}, u32[]{:S(2)}) collective-permute-start(f32[8,2048]{1,0:T(8,128)S(1)} %slice_bitcast_fusion), channel_id=1, source_target_pairs={{0,16},{16,0},{1,17},{17,1},{2,18},{18,2},{3,19},{19,3},{4,20},{20... | collective-permute-start | bytes 196616 | tf_op jit(solution)/shard_map/ppermute | solution.py:460
  37.9 7.7 %copy-start.6 = (f32[128]{0:T(128)S(1)}, f32[128]{0:T(128)}, u32[]{:S(2)}) copy-start(f32[128]{0:T(128)} %param.12) | copy-start | bytes 1540
